TPU v7x, 32 devices: a whole 2x2x4 slice. The times are simulated.
32 devices in a mesh: elem: 16 (over z, x, core), band: 2 (over y).
Axes of the slice: x: 2, y: 2, z: 4, core: 2. Of those that a mesh axis runs over, the one named last changes fastest.
Arguments:
- start_bands: bfloat16 [96, 256, 1024], P('elem', None, 'band'), may hold values from -6 to 6
- blocks: bfloat16 [96, 5, 256, 256], P('elem'), may hold values from -0.125 to 0.125
- neighbours: int32 [96, 5], P('elem'), may hold values from 0 to 95, as said below
- band_order: int32 [1024], replicated, may hold values from 0 to 1023, each once
- rotation: bfloat16 [1024, 1024], P('elem', 'band'), may hold values from -0.1875 to 0.1875
Outputs:
- final_bands: bfloat16 [96, 256, 1024], P('elem', None, 'band')
Inputs may be any that keep to these rules, and one draw needn't show every extreme that they name: `neighbours`: the elements form a periodic grid of 32 columns of 3 elements; column c holds the ids c * 3 to c * 3 + 2 in a drawn order. Row e lists e, the element at the same place in the previous column, the one in the next column, then the previous and the next element within e's column, periodically, in that order. `band_order`: A permutation of the band numbers.
All inputs are finite; a program needn't handle non-finite values.
Results may differ from a plain program's by a relative error of at most 0.01.
Values may be sent and summed in bfloat16 or wider, within the bound.
No kernel may reach another device: no remote copies, remote signals or barrier semaphores. Data moves between devices by JAX's collectives and lax.ppermute only.
A program may use at most 64 MiB of HBM per device.

v0:
```python
import jax
import jax.numpy as jnp
from jax import lax
from jax.sharding import PartitionSpec as P

GY = 3


def extended_2(cells, sides, width):
    for axis, dim in sides:
        count = lax.axis_size(axis)
        head = lax.slice_in_dim(cells, 0, width, axis=dim)
        tail = lax.slice_in_dim(cells, cells.shape[dim] - width, cells.shape[dim], axis=dim)
        cells = jnp.concatenate(
            [
                lax.ppermute(tail, axis, [(i, (i + 1) % count) for i in range(count)]),
                cells,
                lax.ppermute(head, axis, [((i + 1) % count, i) for i in range(count)]),
            ],
            axis=dim,
        )
    return cells


def apply_blocks(current, blocks, local_links):
    extended = extended_2(current, (("elem", 0),), GY)
    picked = jnp.take(extended, local_links, axis=0)
    return jnp.einsum("esij,esjm->eim", blocks, picked, preferred_element_type=jnp.float32)


def chebyshev(initial, blocks, local_links):
    first_term = apply_blocks(initial, blocks, local_links).astype(jnp.bfloat16)
    second_term = (
        2.0 * apply_blocks(first_term, blocks, local_links) - initial.astype(jnp.float32)
    ).astype(jnp.bfloat16)
    third_term = (
        2.0 * apply_blocks(second_term, blocks, local_links) - first_term.astype(jnp.float32)
    ).astype(jnp.bfloat16)
    return third_term


def body(start_bands, blocks, neighbours, band_order, rotation):
    elem_count = start_bands.shape[0]
    basis = start_bands.shape[1]
    width = start_bands.shape[2]
    everything = elem_count * lax.axis_size("elem")
    first_id = lax.axis_index("elem") * elem_count
    local_links = jnp.mod(neighbours - first_id + GY, everything)
    filtered = chebyshev(start_bands, blocks, local_links)
    rotation_cols = lax.all_gather(rotation, "elem", axis=0, tiled=True)
    rotation_full = lax.all_gather(rotation_cols, "band", axis=1, tiled=True)
    permuted_full = jnp.zeros_like(rotation_full).at[band_order].set(rotation_full)
    flat_rows = filtered.reshape(elem_count * basis, width)
    band_rows = lax.all_to_all(flat_rows, "band", split_axis=0, concat_axis=1, tiled=True)
    mixed_rows = jnp.dot(band_rows, permuted_full, preferred_element_type=jnp.float32).astype(
        jnp.bfloat16
    )
    returned = lax.all_to_all(mixed_rows, "band", split_axis=1, concat_axis=0, tiled=True)
    rotated = returned.reshape(elem_count, basis, width)
    return chebyshev(rotated, blocks, local_links)


def solution(mesh):
    return jax.shard_map(
        body,
        mesh=mesh,
        in_specs=(
            P("elem", None, "band"),
            P("elem", None, None, None),
            P("elem", None),
            P(),
            P("elem", "band"),
        ),
        out_specs=P("elem", None, "band"),
        check_vma=False,
    )
```

profile of v0, /device:TPU:1, one launch (start us, length us, event | category | flops | bytes accessed | tf_op | source)
XLA Modules:
  0.0 296.8 jit_solution(7967829592516730766)
XLA Ops:
  8.0 2.7 collective-permute-start
  10.8 17.2 %collective-permute-done = bf16[3,256,512]{2,1,0:T(8,128)(2,1)S(1)} collective-permute-done((bf16[3,256,512]{2,1,0:T(8,128)(2,1)S(1)}, bf16[3,256,512]{2,1,0:T(8,128)(2,1)S(1)}, u32[]{:S(2)}, u32[]{:S(2)}) %collective-permute-start) | collective-permute-done | bytes 786464 | tf_op jit(solution)/shard_map/ppermute | solution.py:16
  32.7 4.8 %gather_fusion = bf16[30,256,512]{2,1,0:T(8,128)(2,1)} fusion(bf16[12,256,512]{2,1,0:T(8,128)(2,1)S(1)} %pad_maximum_fusion, s32[1024]{0:T(1024)S(1)} %pad_clamp_fusion), kind=kCustom, calls=%fused_computation.clone | custom fusion | bytes 15728760 | tf_op jit(solution)/shard_map/jit(_take)/gather | solution.py:27
  37.5 6.7 %fusion.40 = bf16[6,256,512]{2,1,0:T(8,128)(2,1)S(1)} fusion(bf16[6,5,256,256]{3,2,1,0:T(8,128)(2,1)} %param.8, bf16[6,5,256,512]{3,2,1,0:T(8,128)(2,1)} %bitcast.80, pred[6,5]{1,0:T(8,128)(4,1)S(1)} %get-tuple-element.6), kind=kOutput, calls=%fused_computation.53 | convolution fusion | flops 2017984512 | bytes 13369374 | tf_op jit(solution)/shard_map/esij,esjm->eim/dot_general | solution.py:28
  46.4 18.0 %collective-permute-done.2 = bf16[3,256,512]{2,1,0:T(8,128)(2,1)S(1)} collective-permute-done((bf16[3,256,512]{2,1,0:T(8,128)(2,1)S(1)}, bf16[3,256,512]{2,1,0:T(8,128)(2,1)S(1)}, u32[]{:S(2)}, u32[]{:S(2)}) %collective-permute-start.2) | collective-permute-done | bytes 786464 | tf_op jit(solution)/shard_map/ppermute | solution.py:16
  67.3 4.9 %gather_fusion.1 = bf16[30,256,512]{2,1,0:T(8,128)(2,1)} fusion(bf16[12,256,512]{2,1,0:T(8,128)(2,1)S(1)} %pad_maximum_fusion.1, s32[1024]{0:T(1024)S(1)} %pad_clamp_fusion), kind=kCustom, calls=%fused_computation.1.clone | custom fusion | bytes 15728760 | tf_op jit(solution)/shard_map/jit(_take)/gather | solution.py:27
  72.3 10.8 %copy.15 = bf16[6,5,256,512]{2,3,1,0:T(8,128)(2,1)} copy(bf16[6,5,256,512]{3,2,1,0:T(8,128)(2,1)} %bitcast.74) | data formatting | bytes 15728640 | tf_op jit(solution)/shard_map/jit(_take)/gather | solution.py:27
  83.0 6.7 %fusion.27 = bf16[6,256,512]{2,1,0:T(8,128)(2,1)S(1)} fusion(bf16[6,256,512]{2,1,0:T(8,128)(2,1)S(1)} %copy-done.2, bf16[6,5,256,256]{3,2,1,0:T(8,128)(2,1)} %param.8, bf16[6,5,256,512]{2,3,1,0:T(8,128)(2,1)} %copy.15, pred[6,5]{1,0:T(8,128)(4,1)S(1)} %get-tuple-element.6), kind=kOutput, calls=%fused_computation.48 | convolution fusion | flops 2020343808 | bytes 14942238 | tf_op jit(solution)/shard_map/esij,esjm->eim/dot_general | solution.py:28
  91.0 2.5 collective-permute-start.4
  93.6 16.4 %collective-permute-done.4 = bf16[3,256,512]{2,1,0:T(8,128)(2,1)S(1)} collective-permute-done((bf16[3,256,512]{2,1,0:T(8,128)(2,1)S(1)}, bf16[3,256,512]{2,1,0:T(8,128)(2,1)S(1)}, u32[]{:S(2)}, u32[]{:S(2)}) %collective-permute-start.4) | collective-permute-done | bytes 786464 | tf_op jit(solution)/shard_map/ppermute | solution.py:16
  110.9 2.0 pad_maximum_fusion.2
  112.9 4.8 %gather_fusion.2 = bf16[30,256,512]{2,1,0:T(8,128)(2,1)} fusion(bf16[12,256,512]{2,1,0:T(8,128)(2,1)S(1)} %pad_maximum_fusion.2, s32[1024]{0:T(1024)S(1)} %pad_clamp_fusion), kind=kCustom, calls=%fused_computation.2.clone | custom fusion | bytes 15728760 | tf_op jit(solution)/shard_map/jit(_take)/gather | solution.py:27
  117.8 7.1 %fusion.26 = bf16[6,256,512]{2,1,0:T(8,128)(2,1)S(1)} fusion(bf16[6,256,512]{2,1,0:T(8,128)(2,1)} %copy-done.3, bf16[6,5,256,256]{3,2,1,0:T(8,128)(2,1)} %param.8, bf16[6,5,256,512]{3,2,1,0:T(8,128)(2,1)} %bitcast.81, pred[6,5]{1,0:T(8,128)(4,1)S(1)} %get-tuple-element.6), kind=kOutput, calls=%fused_computation.45 | convolution fusion | flops 2020343808 | bytes 14942238 | tf_op jit(solution)/shard_map/esij,esjm->eim/dot_general | solution.py:28
  126.5 4.8 %all-to-all-start = ((bf16[2,768,512]{1,2,0:T(8,128)(2,1)}), bf16[2,768,512]{1,2,0:T(8,128)(2,1)}, u32[]{:S(2)}, u32[]{:S(2)}) async-start(bf16[2,768,512]{1,2,0:T(8,128)(2,1)} %copy.17), calls=%async_computation | async-start | bytes 3145728 | tf_op jit(solution)/shard_map/all_to_all | solution.py:54
  131.4 6.6 %scatter_custom_fusion = bf16[1024,1024]{1,0:T(8,128)(2,1)S(1)} fusion(s32[1024]{0:T(1024)S(1)} %compare_select_fusion.1, bf16[1024,1024]{1,0:T(8,128)(2,1)} %all-gather.5.cloned.1.call-done, bf16[]{:T(256)} %constant.37.clone.1), kind=kCustom, calls=%fused_computation.55 | custom fusion | bytes 2097664 | tf_op jit(solution)/shard_map/scatter | solution.py:52
  137.9 6.4 %all-to-all-done = bf16[2,768,512]{1,2,0:T(8,128)(2,1)} async-done(((bf16[2,768,512]{1,2,0:T(8,128)(2,1)}), bf16[2,768,512]{1,2,0:T(8,128)(2,1)}, u32[]{:S(2)}, u32[]{:S(2)}) %all-to-all-start) | async-done | bytes 1572896 | tf_op jit(solution)/shard_map/all_to_all | solution.py:54
  144.4 3.2 %convolution_convert_fusion = bf16[768,1024]{1,0:T(8,128)(2,1)S(1)} fusion(bf16[768,1024]{0,1:T(8,128)(2,1)} %bitcast.13, bf16[1024,1024]{1,0:T(8,128)(2,1)S(1)} %scatter_custom_fusion), kind=kOutput, calls=%fused_computation.51 | convolution fusion | flops 1611399168 | bytes 5242880 | tf_op jit(solution)/shard_map/dot_general | solution.py:55
  147.7 16.7 %all_to_all.35 = bf16[768,2,512]{2,0,1:T(8,128)(2,1)S(1)} all-to-all(bf16[768,2,512]{2,0,1:T(8,128)(2,1)S(1)} %bitcast.82), channel_id=1, replica_groups=mesh['elem'=16,'band'=2] {'band'}, dimensions={1} | all-to-all | bytes 3145728 | tf_op jit(solution)/shard_map/all_to_all | solution.py:58
  165.1 16.9 %collective-permute-done.6 = bf16[3,256,512]{2,1,0:T(8,128)(2,1)S(1)} collective-permute-done((bf16[3,256,512]{2,1,0:T(8,128)(2,1)S(1)}, bf16[3,256,512]{2,1,0:T(8,128)(2,1)S(1)}, u32[]{:S(2)}, u32[]{:S(2)}) %collective-permute-start.6) | collective-permute-done | bytes 786464 | tf_op jit(solution)/shard_map/ppermute | solution.py:16
  182.4 4.8 %gather_fusion.3 = bf16[30,256,512]{2,1,0:T(8,128)(2,1)} fusion(bf16[12,256,512]{2,1,0:T(8,128)(2,1)S(1)} %pad_maximum_fusion.3, s32[1024]{0:T(1024)S(1)} %pad_clamp_fusion), kind=kCustom, calls=%fused_computation.3.clone | custom fusion | bytes 15728760 | tf_op jit(solution)/shard_map/jit(_take)/gather | solution.py:27
  187.2 10.6 %copy.19 = bf16[6,5,256,512]{2,3,1,0:T(8,128)(2,1)} copy(bf16[6,5,256,512]{3,2,1,0:T(8,128)(2,1)} %bitcast.75) | data formatting | bytes 15728640 | tf_op jit(solution)/shard_map/jit(_take)/gather | solution.py:27
  197.9 6.6 %fusion.43 = bf16[6,256,512]{2,1,0:T(8,128)(2,1)S(1)} fusion(bf16[6,5,256,256]{3,2,1,0:T(8,128)(2,1)} %param.8, bf16[6,5,256,512]{2,3,1,0:T(8,128)(2,1)} %copy.19, pred[6,5]{1,0:T(8,128)(4,1)S(1)} %get-tuple-element.6), kind=kOutput, calls=%fused_computation.54 | convolution fusion | flops 2017984512 | bytes 13369374 | tf_op jit(solution)/shard_map/esij,esjm->eim/dot_general | solution.py:28
  204.6 2.5 collective-permute-start.8
  207.2 16.7 %collective-permute-done.8 = bf16[3,256,512]{2,1,0:T(8,128)(2,1)S(1)} collective-permute-done((bf16[3,256,512]{2,1,0:T(8,128)(2,1)S(1)}, bf16[3,256,512]{2,1,0:T(8,128)(2,1)S(1)}, u32[]{:S(2)}, u32[]{:S(2)}) %collective-permute-start.8) | collective-permute-done | bytes 786464 | tf_op jit(solution)/shard_map/ppermute | solution.py:16
  224.3 4.9 %gather_fusion.4 = bf16[30,256,512]{2,1,0:T(8,128)(2,1)} fusion(bf16[12,256,512]{2,1,0:T(8,128)(2,1)S(1)} %pad_maximum_fusion.4, s32[1024]{0:T(1024)S(1)} %pad_clamp_fusion), kind=kCustom, calls=%fused_computation.4.clone | custom fusion | bytes 15728760 | tf_op jit(solution)/shard_map/jit(_take)/gather | solution.py:27
  229.1 10.8 %copy.21 = bf16[6,5,256,512]{2,3,1,0:T(8,128)(2,1)} copy(bf16[6,5,256,512]{3,2,1,0:T(8,128)(2,1)} %bitcast.76) | data formatting | bytes 15728640 | tf_op jit(solution)/shard_map/jit(_take)/gather | solution.py:27
  239.9 6.7 %fusion.25 = bf16[6,256,512]{2,1,0:T(8,128)(2,1)S(1)} fusion(bf16[6,256,512]{2,1,0:T(8,128)(2,1)S(1)} %bitcast.79, bf16[6,5,256,256]{3,2,1,0:T(8,128)(2,1)} %param.8, bf16[6,5,256,512]{2,3,1,0:T(8,128)(2,1)} %copy.21, pred[6,5]{1,0:T(8,128)(4,1)S(1)} %get-tuple-element.6), kind=kOutput, calls=%fused_computation.41 | convolution fusion | flops 2020343808 | bytes 14942238 | tf_op jit(solution)/shard_map/esij,esjm->eim/dot_general | solution.py:28
  246.7 2.5 collective-permute-start.10
  249.3 16.9 %collective-permute-done.10 = bf16[3,256,512]{2,1,0:T(8,128)(2,1)S(1)} collective-permute-done((bf16[3,256,512]{2,1,0:T(8,128)(2,1)S(1)}, bf16[3,256,512]{2,1,0:T(8,128)(2,1)S(1)}, u32[]{:S(2)}, u32[]{:S(2)}) %collective-permute-start.10) | collective-permute-done | bytes 786464 | tf_op jit(solution)/shard_map/ppermute | solution.py:16
  266.5 4.8 %gather_fusion.5 = bf16[30,256,512]{2,1,0:T(8,128)(2,1)} fusion(bf16[12,256,512]{2,1,0:T(8,128)(2,1)S(1)} %pad_maximum_fusion.5, s32[1024]{0:T(1024)S(1)} %pad_clamp_fusion), kind=kCustom, calls=%fused_computation.5.clone | custom fusion | bytes 15728760 | tf_op jit(solution)/shard_map/jit(_take)/gather | solution.py:27
  271.4 10.8 %copy.23 = bf16[6,5,256,512]{2,3,1,0:T(8,128)(2,1)} copy(bf16[6,5,256,512]{3,2,1,0:T(8,128)(2,1)} %bitcast.73) | data formatting | bytes 15728640 | tf_op jit(solution)/shard_map/jit(_take)/gather | solution.py:27
  282.1 7.8 %fusion.24 = bf16[6,256,512]{2,1,0:T(8,128)(2,1)} fusion(bf16[6,256,512]{2,1,0:T(8,128)(2,1)S(1)} %copy-done.5, bf16[6,5,256,256]{3,2,1,0:T(8,128)(2,1)} %param.8, bf16[6,5,256,512]{2,3,1,0:T(8,128)(2,1)} %copy.23, pred[6,5]{1,0:T(8,128)(4,1)S(1)} %get-tuple-element.6), kind=kOutput, calls=%fused_computation.38 | convolution fusion | flops 2020343808 | bytes 14942238 | tf_op jit(solution)/shard_map/esij,esjm->eim/dot_general | solution.py:28
  (61 shorter events, 17.2 us)
Async XLA Ops:
  6.5 4.1 %copy-start.10 = (s32[6,5]{1,0:T(8,128)S(1)}, s32[6,5]{1,0:T(8,128)}, u32[]{:S(2)}) copy-start(s32[6,5]{1,0:T(8,128)} %param.9) | copy-start | bytes 364
  6.5 87.1 %all-gather.3.cloned.1.call-start = ((), (), s32[]{:S(2)}) async-start(), calls=%async_computation.2 | async-start | bytes 1114112 | tf_op jit(solution)/shard_map/all_gather | solution.py:50
  8.0 20.0 %collective-permute-start = (bf16[3,256,512]{2,1,0:T(8,128)(2,1)S(1)}, bf16[3,256,512]{2,1,0:T(8,128)(2,1)S(1)}, u32[]{:S(2)}, u32[]{:S(2)}) collective-permute-start(bf16[3,256,512]{2,1,0:T(8,128)(2,1)S(1)} %get-tuple-element.18), channel_id=1, source_target_pairs={{0,2},{2,4},{4,6},{6,8},{8,10},{10,12},{12,14},{14,16},{16,18},{18... | collective-permute-start | bytes 2359304 | tf_op jit(solution)/shard_map/ppermute | solution.py:16
  10.7 19.9 %collective-permute-start.1 = (bf16[3,256,512]{2,1,0:T(8,128)(2,1)S(1)}, bf16[3,256,512]{2,1,0:T(8,128)(2,1)}, u32[]{:S(2)}, u32[]{:S(2)}) collective-permute-start(bf16[3,256,512]{2,1,0:T(8,128)(2,1)S(1)} %get-tuple-element.19), channel_id=1, source_target_pairs={{2,0},{4,2},{6,4},{8,6},{10,8},{12,10},{14,12},{16,14},{18,16},{20... | collective-permute-start | bytes 2359304 | tf_op jit(solution)/shard_map/ppermute | solution.py:18
  28.0 0.9 copy-start.7
  44.2 1.1 copy-start.3
  45.5 18.9 %collective-permute-start.2 = (bf16[3,256,512]{2,1,0:T(8,128)(2,1)S(1)}, bf16[3,256,512]{2,1,0:T(8,128)(2,1)S(1)}, u32[]{:S(2)}, u32[]{:S(2)}) collective-permute-start(bf16[3,256,512]{2,1,0:T(8,128)(2,1)S(1)} %get-tuple-element.16), channel_id=1, source_target_pairs={{0,2},{2,4},{4,6},{6,8},{8,10},{10,12},{12,14},{14,16},{16,18},{18... | collective-permute-start | bytes 2359304 | tf_op jit(solution)/shard_map/ppermute | solution.py:16
  46.3 19.0 %collective-permute-start.3 = (bf16[3,256,512]{2,1,0:T(8,128)(2,1)S(1)}, bf16[3,256,512]{2,1,0:T(8,128)(2,1)}, u32[]{:S(2)}, u32[]{:S(2)}) collective-permute-start(bf16[3,256,512]{2,1,0:T(8,128)(2,1)S(1)} %get-tuple-element.17), channel_id=1, source_target_pairs={{2,0},{4,2},{6,4},{8,6},{10,8},{12,10},{14,12},{16,14},{18,16},{20... | collective-permute-start | bytes 2359304 | tf_op jit(solution)/shard_map/ppermute | solution.py:18
  46.3 85.0 %all-gather.5.cloned.1.call-start = ((), (), s32[]{:S(2)}) async-start(), calls=%async_computation.3 | async-start | bytes 3145728 | tf_op jit(solution)/shard_map/all_gather | solution.py:51
  64.4 0.9 copy-start.9
  72.3 10.8 %copy-start.2 = (bf16[6,256,512]{2,1,0:T(8,128)(2,1)S(1)}, bf16[6,256,512]{2,1,0:T(8,128)(2,1)}, u32[]{:S(2)}) copy-start(bf16[6,256,512]{2,1,0:T(8,128)(2,1)} %param.7) | copy-start | bytes 4718596
  89.8 1.2 copy-start.6
  91.0 19.0 %collective-permute-start.4 = (bf16[3,256,512]{2,1,0:T(8,128)(2,1)S(1)}, bf16[3,256,512]{2,1,0:T(8,128)(2,1)S(1)}, u32[]{:S(2)}, u32[]{:S(2)}) collective-permute-start(bf16[3,256,512]{2,1,0:T(8,128)(2,1)S(1)} %get-tuple-element.14), channel_id=1, source_target_pairs={{0,2},{2,4},{4,6},{6,8},{8,10},{10,12},{12,14},{14,16},{16,18},{18... | collective-permute-start | bytes 2359304 | tf_op jit(solution)/shard_map/ppermute | solution.py:16
  93.6 17.3 %collective-permute-start.5 = (bf16[3,256,512]{2,1,0:T(8,128)(2,1)S(1)}, bf16[3,256,512]{2,1,0:T(8,128)(2,1)}, u32[]{:S(2)}, u32[]{:S(2)}) collective-permute-start(bf16[3,256,512]{2,1,0:T(8,128)(2,1)S(1)} %get-tuple-element.15), channel_id=1, source_target_pairs={{2,0},{4,2},{6,4},{8,6},{10,8},{12,10},{14,12},{16,14},{18,16},{20... | collective-permute-start | bytes 2359304 | tf_op jit(solution)/shard_map/ppermute | solution.py:18
  110.0 0.9 copy-start.8
  124.9 6.4 %copy-start.11 = (s32[1024]{0:T(1024)S(1)}, s32[1024]{0:T(1024)}, u32[]{:S(2)}) copy-start(s32[1024]{0:T(1024)} %param.10) | copy-start | bytes 12292
  126.5 17.9 %all-to-all-start = ((bf16[2,768,512]{1,2,0:T(8,128)(2,1)}), bf16[2,768,512]{1,2,0:T(8,128)(2,1)}, u32[]{:S(2)}, u32[]{:S(2)}) async-start(bf16[2,768,512]{1,2,0:T(8,128)(2,1)} %copy.17), calls=%async_computation | async-start | bytes 3145728 | tf_op jit(solution)/shard_map/all_to_all | solution.py:54
  164.5 17.5 %copy-start = (bf16[768,2,512]{2,0,1:T(8,128)(2,1)}, bf16[768,2,512]{2,0,1:T(8,128)(2,1)S(1)}, u32[]{:S(2)}) copy-start(bf16[768,2,512]{2,0,1:T(8,128)(2,1)S(1)} %all_to_all.35) | copy-start | bytes 4718596
  164.6 17.4 %collective-permute-start.6 = (bf16[3,256,512]{2,1,0:T(8,128)(2,1)S(1)}, bf16[3,256,512]{2,1,0:T(8,128)(2,1)S(1)}, u32[]{:S(2)}, u32[]{:S(2)}) collective-permute-start(bf16[3,256,512]{2,1,0:T(8,128)(2,1)S(1)} %bitcast.86), channel_id=1, source_target_pairs={{0,2},{2,4},{4,6},{6,8},{8,10},{10,12},{12,14},{14,16},{16,18},{18... | collective-permute-start | bytes 2359304 | tf_op jit(solution)/shard_map/ppermute | solution.py:16
  164.7 17.4 %collective-permute-start.7 = (bf16[3,256,512]{2,1,0:T(8,128)(2,1)S(1)}, bf16[3,256,512]{2,1,0:T(8,128)(2,1)S(1)}, u32[]{:S(2)}, u32[]{:S(2)}) collective-permute-start(bf16[3,256,512]{2,1,0:T(8,128)(2,1)S(1)} %bitcast.85), channel_id=1, source_target_pairs={{2,0},{4,2},{6,4},{8,6},{10,8},{12,10},{14,12},{16,14},{18,16},{20... | collective-permute-start | bytes 2359304 | tf_op jit(solution)/shard_map/ppermute | solution.py:18
  204.5 19.4 %copy-start.4 = (bf16[6,256,512]{2,1,0:T(8,128)(2,1)}, bf16[6,256,512]{2,1,0:T(8,128)(2,1)S(1)}, u32[]{:S(2)}) copy-start(bf16[6,256,512]{2,1,0:T(8,128)(2,1)S(1)} %fusion.43) | copy-start | bytes 4718596
  204.6 19.2 %collective-permute-start.8 = (bf16[3,256,512]{2,1,0:T(8,128)(2,1)S(1)}, bf16[3,256,512]{2,1,0:T(8,128)(2,1)S(1)}, u32[]{:S(2)}, u32[]{:S(2)}) collective-permute-start(bf16[3,256,512]{2,1,0:T(8,128)(2,1)S(1)} %get-tuple-element.10), channel_id=1, source_target_pairs={{0,2},{2,4},{4,6},{6,8},{8,10},{10,12},{12,14},{14,16},{16,18},{18... | collective-permute-start | bytes 2359304 | tf_op jit(solution)/shard_map/ppermute | solution.py:16
  207.2 16.7 %collective-permute-start.9 = (bf16[3,256,512]{2,1,0:T(8,128)(2,1)S(1)}, bf16[3,256,512]{2,1,0:T(8,128)(2,1)S(1)}, u32[]{:S(2)}, u32[]{:S(2)}) collective-permute-start(bf16[3,256,512]{2,1,0:T(8,128)(2,1)S(1)} %get-tuple-element.11), channel_id=1, source_target_pairs={{2,0},{4,2},{6,4},{8,6},{10,8},{12,10},{14,12},{16,14},{18,16},{20... | collective-permute-start | bytes 2359304 | tf_op jit(solution)/shard_map/ppermute | solution.py:18
  229.1 10.8 %copy-start.1 = (bf16[768,2,512]{2,0,1:T(8,128)(2,1)S(1)}, bf16[768,2,512]{2,0,1:T(8,128)(2,1)}, u32[]{:S(2)}) copy-start(bf16[768,2,512]{2,0,1:T(8,128)(2,1)} %copy-done) | copy-start | bytes 4718596
  246.7 19.4 %collective-permute-start.10 = (bf16[3,256,512]{2,1,0:T(8,128)(2,1)S(1)}, bf16[3,256,512]{2,1,0:T(8,128)(2,1)S(1)}, u32[]{:S(2)}, u32[]{:S(2)}) collective-permute-start(bf16[3,256,512]{2,1,0:T(8,128)(2,1)S(1)} %get-tuple-element.8), channel_id=1, source_target_pairs={{0,2},{2,4},{4,6},{6,8},{8,10},{10,12},{12,14},{14,16},{16,18},{18... | collective-permute-start | bytes 2359304 | tf_op jit(solution)/shard_map/ppermute | solution.py:16
  249.3 16.9 %collective-permute-start.11 = (bf16[3,256,512]{2,1,0:T(8,128)(2,1)S(1)}, bf16[3,256,512]{2,1,0:T(8,128)(2,1)S(1)}, u32[]{:S(2)}, u32[]{:S(2)}) collective-permute-start(bf16[3,256,512]{2,1,0:T(8,128)(2,1)S(1)} %get-tuple-element.9), channel_id=1, source_target_pairs={{2,0},{4,2},{6,4},{8,6},{10,8},{12,10},{14,12},{16,14},{18,16},{20... | collective-permute-start | bytes 2359304 | tf_op jit(solution)/shard_map/ppermute | solution.py:18
  271.4 10.8 %copy-start.5 = (bf16[6,256,512]{2,1,0:T(8,128)(2,1)S(1)}, bf16[6,256,512]{2,1,0:T(8,128)(2,1)}, u32[]{:S(2)}) copy-start(bf16[6,256,512]{2,1,0:T(8,128)(2,1)} %copy-done.4) | copy-start | bytes 4718596
Sparse Core Ops, SparseCore 0:
  46.5 39.5 all-gather.2
  93.7 35.1 all-gather.4
where the time goes:
time: 298 us; the launch traced here: 297 us
  waiting for transfers between devices  110 us (37%)
  local copies, waits for them, and re-layouts  87.4 us (29%)
  matrix products  45 us (15%)
  blocking collectives  16.7 us (6%)
  starting transfers between devices  16.5 us (6%)
  between operations  13.6 us (5%)
  other arithmetic  7.28 us (2%)
    ppermute x6, waiting for transfers between devices, extended_2(): lax.ppermute(tail, axis, [(i, (i + 1) % count) for i in range(count)])  102 us
    gather x10, local copies, waits for them, and re-layouts, apply_blocks(): picked = jnp.take(extended, local_links, axis=0)  72 us
    dot_general x6, matrix products, apply_blocks(): jnp.einsum('esij,esjm->eim', blocks, picked, preferred_element_type=jnp.f...  41.8 us
    all_to_all x1, blocking collectives, body(): lax.all_to_all(mixed_rows, 'band', split_axis=1, concat_axis=0, tiled=True)  16.7 us
    ppermute x6, starting transfers between devices, extended_2(): lax.ppermute(tail, axis, [(i, (i + 1) % count) for i in range(count)])  11.2 us
    concatenate x6, other arithmetic, extended_2(): jnp.concatenate([lax.ppermute(tail, axis, [(i, (i + 1) % count) for i in...  7.25 us
    scatter x1, local copies, waits for them, and re-layouts, body(): jnp.zeros_like(rotation_full).at[band_order].set(rotation_full)  6.58 us
    all_to_all x1, waiting for transfers between devices, body(): lax.all_to_all(flat_rows, 'band', split_axis=0, concat_axis=1, tiled=True)  6.43 us
  transfers between devices with their start and end apart: 15, of which 8 were waited for; matrix products, arithmetic and copies ran while one was open for 16% of the time, Pallas kernels for 0%

commit v1 on v0

v1 whole, which is shorter than its diff:
```python
import functools

import jax
import jax.numpy as jnp
from jax import lax
from jax.experimental import pallas as pl
from jax.experimental.pallas import tpu as pltpu
from jax.sharding import PartitionSpec as P

GY = 3
CHUNK = 256
MIB = 1024 * 1024


def step_kernel(first, last, column, *refs):
    refs = list(refs)
    odd_ref, links_ref, blocks_ref, far_outer, outer, inner, far_inner = refs[:7]
    refs = refs[7:]
    before = None
    if not first:
        before, refs = refs[:2], refs[2:]
    if last and column > 0:
        refs = refs[1:]
    if last:
        out_ref, held, arrived, made, left = refs
    else:
        new_outer, new_inner, held, arrived = refs
    odd = odd_ref[0]
    rows, copies = [], []
    for k in range(2 * GY):
        row = odd * GY + k if k < GY else (1 - odd) * GY + (k - GY)
        copy = pltpu.make_async_copy(blocks_ref.at[row], held.at[k], arrived.at[k])
        copy.start()
        rows.append(row)
        copies.append(copy)
    sent = []
    for k in range(2 * GY):
        row = rows[k]
        own, near, far = (outer, inner, far_outer) if k < GY else (inner, outer, far_inner)
        far_side = 1 + odd if k < GY else 2 - odd
        near_side = 3 - far_side

        def slot(side):
            return lax.rem(links_ref[row, side], GY)

        copies[k].wait()
        total = jnp.dot(held[k, 0], own[slot(0)], preferred_element_type=jnp.float32)
        total += jnp.dot(held[k, 3], own[slot(3)], preferred_element_type=jnp.float32)
        total += jnp.dot(held[k, 4], own[slot(4)], preferred_element_type=jnp.float32)
        total += jnp.dot(held[k, near_side], near[slot(near_side)], preferred_element_type=jnp.float32)
        total += jnp.dot(held[k, far_side], far[slot(far_side)], preferred_element_type=jnp.float32)
        if not first:
            total = 2.0 * total - before[k // GY][k % GY].astype(jnp.float32)
        if last:
            made[k] = total.astype(jnp.bfloat16)
            width = made.shape[2]
            copy = pltpu.make_async_copy(
                made.at[k], out_ref.at[row, :, pl.ds(column, width)], left.at[k]
            )
            copy.start()
            sent.append(copy)
        else:
            target = new_outer if k < GY else new_inner
            target[k % GY] = total.astype(jnp.bfloat16)
    for copy in sent:
        copy.wait()


def apply_step(odd, links, blocks, halos, current, before, out=None, column=0, out_shape=None):
    basis, width = current[0].shape[1:]
    last = out_shape is not None
    smem = pl.BlockSpec(memory_space=pltpu.SMEM)
    vmem = pl.BlockSpec(memory_space=pltpu.VMEM)
    anywhere = pl.BlockSpec(memory_space=pl.ANY)
    operands = [odd, links, blocks, halos[0], current[0], current[1], halos[1]]
    specs = [smem, smem, anywhere] + [vmem] * 4
    if before is not None:
        operands += list(before)
        specs += [vmem] * 2
    aliases = {}
    scratch = [
        pltpu.VMEM((2 * GY,) + blocks.shape[1:], blocks.dtype),
        pltpu.SemaphoreType.DMA((2 * GY,)),
    ]
    if last:
        if out is not None:
            aliases = {len(operands): 0}
            operands.append(out)
            specs.append(anywhere)
        shapes = jax.ShapeDtypeStruct(out_shape, jnp.bfloat16)
        out_specs = anywhere
        scratch += [
            pltpu.VMEM((2 * GY, basis, width), jnp.bfloat16),
            pltpu.SemaphoreType.DMA((2 * GY,)),
        ]
    else:
        shapes = [jax.ShapeDtypeStruct((GY, basis, width), jnp.bfloat16)] * 2
        out_specs = [vmem, vmem]
    flops = 2 * 2 * GY * blocks.shape[1] * basis * basis * width
    moved = 2 * blocks.size + 2 * 10 * GY * basis * width
    return pl.pallas_call(
        functools.partial(step_kernel, before is None, last, column),
        out_shape=shapes,
        in_specs=specs,
        out_specs=out_specs,
        scratch_shapes=scratch,
        input_output_aliases=aliases,
        compiler_params=pltpu.CompilerParams(vmem_limit_bytes=24 * MIB),
        cost_estimate=pl.CostEstimate(flops=flops, bytes_accessed=moved, transcendentals=0),
    )(*operands)


def rotate_kernel(count, *refs):
    pieces, matrix, outs = refs[:count], refs[count], refs[count + 1 :]
    for k in range(GY):
        row = 0
        total = None
        for piece in pieces:
            width = piece.shape[2]
            part = jnp.dot(piece[k], matrix[row : row + width, :], preferred_element_type=jnp.float32)
            total = part if total is None else total + part
            row += width
        column = 0
        for out in outs:
            width = out.shape[2]
            out[k] = total[:, column : column + width].astype(jnp.bfloat16)
            column += width


def rotate(pieces, matrix, widths):
    basis = pieces[0].shape[1]
    vmem = pl.BlockSpec(memory_space=pltpu.VMEM)
    flops = 2 * GY * basis * matrix.shape[0] * matrix.shape[1]
    moved = 2 * (matrix.size + GY * basis * (matrix.shape[0] + matrix.shape[1]))
    return pl.pallas_call(
        functools.partial(rotate_kernel, len(pieces)),
        out_shape=[jax.ShapeDtypeStruct((GY, basis, width), jnp.bfloat16) for width in widths],
        in_specs=[vmem] * (len(pieces) + 1),
        out_specs=[vmem] * len(widths),
        compiler_params=pltpu.CompilerParams(vmem_limit_bytes=24 * MIB),
        cost_estimate=pl.CostEstimate(flops=flops, bytes_accessed=moved, transcendentals=0),
    )(*pieces, matrix)


def exchange(array, axis, partner):
    return lax.ppermute(array, axis, [(i, partner(i)) for i in range(lax.axis_size(axis))])


def gathered_rotation(rotation, band_order):
    elems, bands = lax.axis_size("elem"), lax.axis_size("band")
    me = lax.axis_index("elem")
    bits = [1 << b for b in range(elems.bit_length() - 1)]
    bits = bits[1:] + bits[:1]
    owners = [0]
    rows = rotation
    for bit in bits:
        rows = jnp.concatenate([rows, exchange(rows, "elem", lambda i: i ^ bit)], axis=0)
        owners = owners + [owner ^ bit for owner in owners]
    share = rotation.shape[0]
    order = band_order.reshape(elems, share)[jnp.bitwise_xor(me, jnp.array(owners))].reshape(-1)
    total = order.shape[0]
    width = total // bands
    place = lax.iota(jnp.int32, total)
    band = jnp.bitwise_xor(place // width, lax.axis_index("band")) * width + place % width
    choice = (band[:, None] == order[None, :]).astype(jnp.bfloat16)
    return jnp.dot(choice, rows, preferred_element_type=jnp.float32).astype(jnp.bfloat16)


def body(start_bands, blocks, neighbours, band_order, rotation):
    elem_count, basis, width = start_bands.shape
    assert elem_count == 2 * GY
    elems, bands = lax.axis_size("elem"), lax.axis_size("band")
    odd = lax.axis_index("elem") % 2
    odd_flag = odd.astype(jnp.int32).reshape(1)
    chunk = min(CHUNK, width)
    starts = list(range(0, width, chunk))
    widths = [chunk] * len(starts)

    def cross(array):
        return exchange(array, "elem", lambda i: (i - 1) % elems if i % 2 == 0 else (i + 1) % elems)

    def intra(array):
        return exchange(array, "elem", lambda i: i ^ 1)

    def step(current, before, **output):
        halos = (cross(current[0]), intra(current[1]))
        return apply_step(odd_flag, neighbours, blocks, halos, current, before, **output)

    matrix = gathered_rotation(rotation, band_order)

    state = []
    for column in starts:
        part = lax.slice_in_dim(start_bands, column, column + chunk, axis=2)
        state.append(
            (
                lax.dynamic_slice_in_dim(part, odd * GY, GY, axis=0),
                lax.dynamic_slice_in_dim(part, (1 - odd) * GY, GY, axis=0),
            )
        )
    before = [None] * len(starts)
    for _ in range(3):
        for c in range(len(starts)):
            new = step(state[c], before[c])
            before[c], state[c] = state[c], tuple(new)

    rotated = []
    for side in range(2):
        own = [state[c][side] for c in range(len(starts))]
        pieces = list(own)
        for shift in range(1, bands):
            pieces += [exchange(piece, "band", lambda i: i ^ shift) for piece in own]
        rotated.append(rotate(pieces, matrix, widths))
    state = [(rotated[0][c], rotated[1][c]) for c in range(len(starts))]

    before = [None] * len(starts)
    for _ in range(2):
        for c in range(len(starts)):
            new = step(state[c], before[c])
            before[c], state[c] = state[c], tuple(new)
    out = None
    for c in range(len(starts)):
        out = step(state[c], before[c], out=out, column=starts[c], out_shape=start_bands.shape)
    return out


def solution(mesh):
    return jax.shard_map(
        body,
        mesh=mesh,
        in_specs=(
            P("elem", None, "band"),
            P("elem", None, None, None),
            P("elem", None),
            P(),
            P("elem", "band"),
        ),
        out_specs=P("elem", None, "band"),
        check_vma=False,
    )
```

time: 298 us -> 173 us (0.58)
  local copies, waits for them, and re-layouts: 87.4 us -> 6.17 us
  Pallas kernels: 0 us -> 62.1 us
  waiting for transfers between devices: 110 us -> 52.6 us
  matrix products: 45 us -> 1.3 us
  starting transfers between devices: 16.5 us -> 47 us
  blocking collectives: 16.7 us -> 0 us
  between operations: 13.6 us -> 0.48 us
  other arithmetic: 7.28 us -> 2.69 us
    gather x10 -> x1, local copies, waits for them, and re-layouts: 72 us -> 0.56 us  [gathered_rotation(): band_order.reshape(elems, share)[jnp.bitwise_xor(me, jnp.array(owners))]]
    pallas_call x0 -> x14, Pallas kernels: none -> 62.1 us  [the longest x12 60.2 us: apply_step(): pl.pallas_call(functools.partial(step_kernel, before is None, last, colum...]
    ppermute x12 -> x32, waiting for transfers between devices: 104 us -> 52.6 us  [exchange(): lax.ppermute(array, axis, [(i, partner(i)) for i in range(lax.axis_size(a...]
    dot_general x7 -> x1, matrix products: 45 us -> 1.3 us  [gathered_rotation(): jnp.dot(choice, rows, preferred_element_type=jnp.float32)]
    ppermute x12 -> x32, starting transfers between devices: 11.7 us -> 47 us  [exchange(): lax.ppermute(array, axis, [(i, partner(i)) for i in range(lax.axis_size(a...]
    all_to_all x1 -> x0, blocking collectives: 16.7 us -> none  [body(): lax.all_to_all(mixed_rows, 'band', split_axis=1, concat_axis=0, tiled=True)]
    scatter x1 -> x0, local copies, waits for them, and re-layouts: 6.58 us -> none  [body(): jnp.zeros_like(rotation_full).at[band_order].set(rotation_full)]
    all_to_all x1 -> x0, waiting for transfers between devices: 6.43 us -> none  [body(): lax.all_to_all(flat_rows, 'band', split_axis=0, concat_axis=1, tiled=True)]
  transfers between devices with their start and end apart: 15 -> 32, of which waited for: 8 -> 11; matrix products, arithmetic and copies ran while one was open for 16% -> 4% of each run, Pallas kernels for 0% -> 33%
where the time goes in v1:
time: 173 us; the launch traced here: 172 us
  Pallas kernels  62.1 us (36%)
  waiting for transfers between devices  52.6 us (30%)
  starting transfers between devices  47 us (27%)
  local copies, waits for them, and re-layouts  6.17 us (4%)
  other arithmetic  2.69 us (2%)
    pallas_call x12, Pallas kernels, apply_step(): pl.pallas_call(functools.partial(step_kernel, before is None, last, colum...  60.2 us
    ppermute x32, waiting for transfers between devices, exchange(): lax.ppermute(array, axis, [(i, partner(i)) for i in range(lax.axis_size(a...  52.6 us
    ppermute x32, starting transfers between devices, exchange(): lax.ppermute(array, axis, [(i, partner(i)) for i in range(lax.axis_size(a...  47 us
    unnamed x14, local copies, waits for them, and re-layouts  3.85 us
  transfers between devices with their start and end apart: 32, of which 11 were waited for; matrix products, arithmetic and copies ran while one was open for 4% of the time, Pallas kernels for 33%

profile of v1, /device:TPU:1, one launch (start us, length us, event | category | flops | bytes accessed | tf_op | source)
XLA Modules:
  0.0 172.4 jit_solution(3577458641356296110)
XLA Ops:
  1.6 2.7 %collective-permute-start.6 = (bf16[3,256,256]{2,1,0:T(8,128)(2,1)S(1)}, bf16[3,256,256]{2,1,0:T(8,128)(2,1)S(1)}, u32[]{:S(2)}, u32[]{:S(2)}) collective-permute-start(bf16[3,256,256]{2,1,0:T(8,128)(2,1)S(1)} %get-tuple-element.56.refs_4_.refs_7_), channel_id=1, source_target_pairs={{0,30},{2,4},{4,2},{6,8},{8,6},{10,12},{12,10},{14,16},{16,14},{18... | collective-permute-start | bytes 1179656 | tf_op jit(solution)/shard_map/ppermute | solution.py:146
  4.3 2.9 %collective-permute-start.7 = (bf16[3,256,256]{2,1,0:T(8,128)(2,1)S(1)}, bf16[3,256,256]{2,1,0:T(8,128)(2,1)S(1)}, u32[]{:S(2)}, u32[]{:S(2)}) collective-permute-start(bf16[3,256,256]{2,1,0:T(8,128)(2,1)S(1)} %get-tuple-element.55.refs_5_.refs_8_), channel_id=1, source_target_pairs={{0,2},{2,0},{4,6},{6,4},{8,10},{10,8},{12,14},{14,12},{16,18},{18,... | collective-permute-start | bytes 1179656 | tf_op jit(solution)/shard_map/ppermute | solution.py:146
  7.2 1.7 collective-permute-start
  9.3 9.6 %collective-permute-done.14 = bf16[64,512]{1,0:T(8,128)(2,1)} collective-permute-done((bf16[64,512]{1,0:T(8,128)(2,1)}, bf16[64,512]{1,0:T(8,128)(2,1)}, u32[]{:S(2)}, u32[]{:S(2)}) %collective-permute-start.14) | collective-permute-done | bytes 65568 | tf_op jit(solution)/shard_map/ppermute | solution.py:146
  21.9 1.8 %collective-permute-done.15 = bf16[128,512]{1,0:T(8,128)(2,1)S(1)} collective-permute-done((bf16[128,512]{1,0:T(8,128)(2,1)S(1)}, bf16[128,512]{1,0:T(8,128)(2,1)S(1)}, u32[]{:S(2)}, u32[]{:S(2)}) %collective-permute-start.15) | collective-permute-done | bytes 131104 | tf_op jit(solution)/shard_map/ppermute | solution.py:146
  24.6 2.4 %collective-permute-start.16 = (bf16[256,512]{1,0:T(8,128)(2,1)S(1)}, bf16[256,512]{1,0:T(8,128)(2,1)S(1)}, u32[]{:S(2)}, u32[]{:S(2)}) collective-permute-start(bf16[256,512]{1,0:T(8,128)(2,1)S(1)} %pad_maximum_fusion.1), channel_id=1, source_target_pairs={{0,16},{2,18},{4,20},{6,22},{8,24},{10,26},{12,28},{14,30},{16,0},... | collective-permute-start | bytes 786440 | tf_op jit(solution)/shard_map/ppermute | solution.py:146
  27.0 2.1 %copy-done = bf16[6,5,256,256]{3,2,1,0:T(8,128)(2,1)S(1)} copy-done((bf16[6,5,256,256]{3,2,1,0:T(8,128)(2,1)S(1)}, bf16[6,5,256,256]{3,2,1,0:T(8,128)(2,1)}, u32[]{:S(2)}) %copy-start) | copy-done | bytes 3932184
  29.1 4.8 %shard_map.67 = (bf16[3,256,256]{2,1,0:T(8,128)(2,1)S(1)}, bf16[3,256,256]{2,1,0:T(8,128)(2,1)S(1)}) custom-call(s32[1]{0:T(128)} %bitcast.refs_0_, s32[6,5]{1,0:T(8,128)S(1)} %copy-done.2, bf16[6,5,256,256]{3,2,1,0:T(8,128)(2,1)S(1)} %copy-done, bf16[3,256,256]{2,1,0:T(8,128)(2,1)S(1)} %collective-permute-done.6.refs_3_, ...), custom_call_target="tpu_custom_call" | custom-call | flops 1006632960 | bytes 7864320 | tf_op jit(solution)/shard_map/pallas_call | solution.py:101
  33.9 2.8 %collective-permute-start.8 = (bf16[3,256,256]{2,1,0:T(8,128)(2,1)S(1)}, bf16[3,256,256]{2,1,0:T(8,128)(2,1)S(1)}, u32[]{:S(2)}, u32[]{:S(2)}) collective-permute-start(bf16[3,256,256]{2,1,0:T(8,128)(2,1)S(1)} %get-tuple-element.34.refs_4_.refs_7_), channel_id=1, source_target_pairs={{0,30},{2,4},{4,2},{6,8},{8,6},{10,12},{12,10},{14,16},{16,14},{18... | collective-permute-start | bytes 1179656 | tf_op jit(solution)/shard_map/ppermute | solution.py:146
  37.7 4.8 %shard_map.64 = (bf16[3,256,256]{2,1,0:T(8,128)(2,1)S(1)}, bf16[3,256,256]{2,1,0:T(8,128)(2,1)S(1)}) custom-call(s32[1]{0:T(128)} %bitcast.refs_0_, s32[6,5]{1,0:T(8,128)S(1)} %copy-done.2, bf16[6,5,256,256]{3,2,1,0:T(8,128)(2,1)S(1)} %copy-done, bf16[3,256,256]{2,1,0:T(8,128)(2,1)S(1)} %collective-permute-done.refs_3_, ...), custom_call_target="tpu_custom_call" | custom-call | flops 1006632960 | bytes 7864320 | tf_op jit(solution)/shard_map/pallas_call | solution.py:101
  42.6 1.9 %collective-permute-start.2 = (bf16[3,256,256]{2,1,0:T(8,128)(2,1)S(1)}, bf16[3,256,256]{2,1,0:T(8,128)(2,1)S(1)}, u32[]{:S(2)}, u32[]{:S(2)}) collective-permute-start(bf16[3,256,256]{2,1,0:T(8,128)(2,1)S(1)} %get-tuple-element.29.refs_4_.refs_7_), channel_id=1, source_target_pairs={{0,30},{2,4},{4,2},{6,8},{8,6},{10,12},{12,10},{14,16},{16,14},{18... | collective-permute-start | bytes 1179656 | tf_op jit(solution)/shard_map/ppermute | solution.py:146
  48.1 4.9 %shard_map.68 = (bf16[3,256,256]{2,1,0:T(8,128)(2,1)S(1)}, bf16[3,256,256]{2,1,0:T(8,128)(2,1)S(1)}) custom-call(s32[1]{0:T(128)} %bitcast.refs_0_, s32[6,5]{1,0:T(8,128)S(1)} %copy-done.2, bf16[6,5,256,256]{3,2,1,0:T(8,128)(2,1)S(1)} %copy-done, bf16[3,256,256]{2,1,0:T(8,128)(2,1)S(1)} %collective-permute-done.8.refs_3_, ...), custom_call_target="tpu_custom_call" | custom-call | flops 1006632960 | bytes 7864320 | tf_op jit(solution)/shard_map/pallas_call | solution.py:101
  54.8 4.9 %shard_map.65 = (bf16[3,256,256]{2,1,0:T(8,128)(2,1)S(1)}, bf16[3,256,256]{2,1,0:T(8,128)(2,1)S(1)}) custom-call(s32[1]{0:T(128)} %bitcast.refs_0_, s32[6,5]{1,0:T(8,128)S(1)} %copy-done.2, bf16[6,5,256,256]{3,2,1,0:T(8,128)(2,1)S(1)} %copy-done, bf16[3,256,256]{2,1,0:T(8,128)(2,1)S(1)} %collective-permute-done.2.refs_3_, ...), custom_call_target="tpu_custom_call" | custom-call | flops 1006632960 | bytes 7864320 | tf_op jit(solution)/shard_map/pallas_call | solution.py:101
  59.7 6.0 %collective-permute-start.4 = (bf16[3,256,256]{2,1,0:T(8,128)(2,1)S(1)}, bf16[3,256,256]{2,1,0:T(8,128)(2,1)S(1)}, u32[]{:S(2)}, u32[]{:S(2)}) collective-permute-start(bf16[3,256,256]{2,1,0:T(8,128)(2,1)S(1)} %get-tuple-element.31.refs_4_), channel_id=1, source_target_pairs={{0,30},{2,4},{4,2},{6,8},{8,6},{10,12},{12,10},{14,16},{16,14},{18... | collective-permute-start | bytes 1179656 | tf_op jit(solution)/shard_map/ppermute | solution.py:146
  66.6 4.9 %shard_map.69 = (bf16[3,256,256]{2,1,0:T(8,128)(2,1)S(1)}, bf16[3,256,256]{2,1,0:T(8,128)(2,1)S(1)}) custom-call(s32[1]{0:T(128)} %bitcast.refs_0_, s32[6,5]{1,0:T(8,128)S(1)} %copy-done.2, bf16[6,5,256,256]{3,2,1,0:T(8,128)(2,1)S(1)} %copy-done, bf16[3,256,256]{2,1,0:T(8,128)(2,1)S(1)} %collective-permute-done.10.refs_3_, ...), custom_call_target="tpu_custom_call" | custom-call | flops 1006632960 | bytes 7864320 | tf_op jit(solution)/shard_map/pallas_call | solution.py:101
  72.9 5.0 %shard_map.66 = (bf16[3,256,256]{2,1,0:T(8,128)(2,1)S(1)}, bf16[3,256,256]{2,1,0:T(8,128)(2,1)S(1)}) custom-call(s32[1]{0:T(128)} %bitcast.refs_0_, s32[6,5]{1,0:T(8,128)S(1)} %copy-done.2, bf16[6,5,256,256]{3,2,1,0:T(8,128)(2,1)S(1)} %copy-done, bf16[3,256,256]{2,1,0:T(8,128)(2,1)S(1)} %collective-permute-done.4.refs_3_, ...), custom_call_target="tpu_custom_call" | custom-call | flops 1006632960 | bytes 7864320 | tf_op jit(solution)/shard_map/pallas_call | solution.py:101
  82.1 8.1 %collective-permute-done.19.refs_2_ = bf16[3,256,256]{2,1,0:T(8,128)(2,1)S(1)} collective-permute-done((bf16[3,256,256]{2,1,0:T(8,128)(2,1)S(1)}, bf16[3,256,256]{2,1,0:T(8,128)(2,1)S(1)}, u32[]{:S(2)}, u32[]{:S(2)}) %collective-permute-start.19) | collective-permute-done | bytes 393248 | tf_op jit(solution)/shard_map/ppermute | solution.py:146
  91.1 2.4 %collective-permute-start.27 = (bf16[3,256,256]{2,1,0:T(8,128)(2,1)S(1)}, bf16[3,256,256]{2,1,0:T(8,128)(2,1)S(1)}, u32[]{:S(2)}, u32[]{:S(2)}) collective-permute-start(bf16[3,256,256]{2,1,0:T(8,128)(2,1)S(1)} %get-tuple-element.48.refs_5_.refs_8_), channel_id=1, source_target_pairs={{0,2},{2,0},{4,6},{6,4},{8,10},{10,8},{12,14},{14,12},{16,18},{18,... | collective-permute-start | bytes 1179656 | tf_op jit(solution)/shard_map/ppermute | solution.py:146
  93.5 5.1 %collective-permute-done.13.refs_3_ = bf16[3,256,256]{2,1,0:T(8,128)(2,1)S(1)} collective-permute-done((bf16[3,256,256]{2,1,0:T(8,128)(2,1)S(1)}, bf16[3,256,256]{2,1,0:T(8,128)(2,1)S(1)}, u32[]{:S(2)}, u32[]{:S(2)}) %collective-permute-start.13) | collective-permute-done | bytes 393248 | tf_op jit(solution)/shard_map/ppermute | solution.py:146
  98.6 8.4 %collective-permute-done.12.refs_2_ = bf16[3,256,256]{2,1,0:T(8,128)(2,1)S(1)} collective-permute-done((bf16[3,256,256]{2,1,0:T(8,128)(2,1)S(1)}, bf16[3,256,256]{2,1,0:T(8,128)(2,1)S(1)}, u32[]{:S(2)}, u32[]{:S(2)}) %collective-permute-start.12) | collective-permute-done | bytes 393248 | tf_op jit(solution)/shard_map/ppermute | solution.py:146
  109.5 2.7 %collective-permute-start.18 = (bf16[3,256,256]{2,1,0:T(8,128)(2,1)S(1)}, bf16[3,256,256]{2,1,0:T(8,128)(2,1)S(1)}, u32[]{:S(2)}, u32[]{:S(2)}) collective-permute-start(bf16[3,256,256]{2,1,0:T(8,128)(2,1)S(1)} %get-tuple-element.39.refs_4_.refs_7_), channel_id=1, source_target_pairs={{0,30},{2,4},{4,2},{6,8},{8,6},{10,12},{12,10},{14,16},{16,14},{18... | collective-permute-start | bytes 1179656 | tf_op jit(solution)/shard_map/ppermute | solution.py:146
  112.2 11.5 %collective-permute-done.26.refs_3_ = bf16[3,256,256]{2,1,0:T(8,128)(2,1)S(1)} collective-permute-done((bf16[3,256,256]{2,1,0:T(8,128)(2,1)S(1)}, bf16[3,256,256]{2,1,0:T(8,128)(2,1)S(1)}, u32[]{:S(2)}, u32[]{:S(2)}) %collective-permute-start.26) | collective-permute-done | bytes 393248 | tf_op jit(solution)/shard_map/ppermute | solution.py:146
  123.7 4.9 %shard_map.74 = (bf16[3,256,256]{2,1,0:T(8,128)(2,1)S(1)}, bf16[3,256,256]{2,1,0:T(8,128)(2,1)S(1)}) custom-call(s32[1]{0:T(128)} %bitcast.refs_0_, s32[6,5]{1,0:T(8,128)S(1)} %copy-done.2, bf16[6,5,256,256]{3,2,1,0:T(8,128)(2,1)S(1)} %copy-done.1, bf16[3,256,256]{2,1,0:T(8,128)(2,1)S(1)} %collective-permute-done.26.refs_3_, ...), custom_call_target="tpu_custom_call" | custom-call | flops 1006632960 | bytes 7864320 | tf_op jit(solution)/shard_map/pallas_call | solution.py:101
  131.1 4.8 %shard_map.72 = (bf16[3,256,256]{2,1,0:T(8,128)(2,1)S(1)}, bf16[3,256,256]{2,1,0:T(8,128)(2,1)S(1)}) custom-call(s32[1]{0:T(128)} %bitcast.refs_0_, s32[6,5]{1,0:T(8,128)S(1)} %copy-done.2, bf16[6,5,256,256]{3,2,1,0:T(8,128)(2,1)S(1)} %copy-done.1, bf16[3,256,256]{2,1,0:T(8,128)(2,1)S(1)} %collective-permute-done.18.refs_3_, ...), custom_call_target="tpu_custom_call" | custom-call | flops 1006632960 | bytes 7864320 | tf_op jit(solution)/shard_map/pallas_call | solution.py:101
  135.9 2.5 %collective-permute-start.22 = (bf16[3,256,256]{2,1,0:T(8,128)(2,1)S(1)}, bf16[3,256,256]{2,1,0:T(8,128)(2,1)S(1)}, u32[]{:S(2)}, u32[]{:S(2)}) collective-permute-start(bf16[3,256,256]{2,1,0:T(8,128)(2,1)S(1)} %get-tuple-element.43.refs_4_.refs_7_), channel_id=1, source_target_pairs={{0,30},{2,4},{4,2},{6,8},{8,6},{10,12},{12,10},{14,16},{16,14},{18... | collective-permute-start | bytes 1179656 | tf_op jit(solution)/shard_map/ppermute | solution.py:146
  138.5 4.9 %shard_map.75 = (bf16[3,256,256]{2,1,0:T(8,128)(2,1)S(1)}, bf16[3,256,256]{2,1,0:T(8,128)(2,1)S(1)}) custom-call(s32[1]{0:T(128)} %bitcast.refs_0_, s32[6,5]{1,0:T(8,128)S(1)} %copy-done.2, bf16[6,5,256,256]{3,2,1,0:T(8,128)(2,1)S(1)} %copy-done.1, bf16[3,256,256]{2,1,0:T(8,128)(2,1)S(1)} %collective-permute-done.28.refs_3_, ...), custom_call_target="tpu_custom_call" | custom-call | flops 1006632960 | bytes 7864320 | tf_op jit(solution)/shard_map/pallas_call | solution.py:101
  144.9 3.3 %collective-permute-done.22.refs_3_ = bf16[3,256,256]{2,1,0:T(8,128)(2,1)S(1)} collective-permute-done((bf16[3,256,256]{2,1,0:T(8,128)(2,1)S(1)}, bf16[3,256,256]{2,1,0:T(8,128)(2,1)S(1)}, u32[]{:S(2)}, u32[]{:S(2)}) %collective-permute-start.22) | collective-permute-done | bytes 393248 | tf_op jit(solution)/shard_map/ppermute | solution.py:146
  148.1 4.9 %shard_map.73 = (bf16[3,256,256]{2,1,0:T(8,128)(2,1)S(1)}, bf16[3,256,256]{2,1,0:T(8,128)(2,1)S(1)}) custom-call(s32[1]{0:T(128)} %bitcast.refs_0_, s32[6,5]{1,0:T(8,128)S(1)} %copy-done.2, bf16[6,5,256,256]{3,2,1,0:T(8,128)(2,1)S(1)} %copy-done.1, bf16[3,256,256]{2,1,0:T(8,128)(2,1)S(1)} %collective-permute-done.22.refs_3_, ...), custom_call_target="tpu_custom_call" | custom-call | flops 1006632960 | bytes 7864320 | tf_op jit(solution)/shard_map/pallas_call | solution.py:101
  153.0 4.4 %collective-permute-start.24 = (bf16[3,256,256]{2,1,0:T(8,128)(2,1)S(1)}, bf16[3,256,256]{2,1,0:T(8,128)(2,1)S(1)}, u32[]{:S(2)}, u32[]{:S(2)}) collective-permute-start(bf16[3,256,256]{2,1,0:T(8,128)(2,1)S(1)} %get-tuple-element.45.refs_4_), channel_id=1, source_target_pairs={{0,30},{2,4},{4,2},{6,8},{8,6},{10,12},{12,10},{14,16},{16,14},{18... | collective-permute-start | bytes 1179656 | tf_op jit(solution)/shard_map/ppermute | solution.py:146
  157.5 3.3 %collective-permute-done.30.refs_3_ = bf16[3,256,256]{2,1,0:T(8,128)(2,1)S(1)} collective-permute-done((bf16[3,256,256]{2,1,0:T(8,128)(2,1)S(1)}, bf16[3,256,256]{2,1,0:T(8,128)(2,1)S(1)}, u32[]{:S(2)}, u32[]{:S(2)}) %collective-permute-start.30) | collective-permute-done | bytes 393248 | tf_op jit(solution)/shard_map/ppermute | solution.py:146
  160.8 5.8 %shard_map.76.refs_9_ = bf16[6,256,512]{2,1,0:T(8,128)(2,1)} custom-call(s32[1]{0:T(128)} %bitcast.refs_0_, s32[6,5]{1,0:T(8,128)S(1)} %copy-done.2, bf16[6,5,256,256]{3,2,1,0:T(8,128)(2,1)S(1)} %copy-done.1, bf16[3,256,256]{2,1,0:T(8,128)(2,1)S(1)} %collective-permute-done.30.refs_3_, bf16[3,256,256]{2,1,0:T(8,128)(2,1)S(1)} %get-tuple-element.51.refs_4_, ...), custom_call_target="tpu_custom_call" | custom-call | flops 1006632960 | bytes 7864320 | tf_op jit(solution)/shard_map/pallas_call | solution.py:101
  166.6 5.6 %shard_map.77 = bf16[6,256,512]{2,1,0:T(8,128)(2,1)} custom-call(s32[1]{0:T(128)} %bitcast.refs_0_, s32[6,5]{1,0:T(8,128)S(1)} %copy-done.2, bf16[6,5,256,256]{3,2,1,0:T(8,128)(2,1)S(1)} %copy-done.1, bf16[3,256,256]{2,1,0:T(8,128)(2,1)S(1)} %collective-permute-done.24.refs_3_, ...), custom_call_target="tpu_custom_call", output_to_operand_aliasing={{}: (9, {})} | custom-call | flops 1006632960 | bytes 7864320 | tf_op jit(solution)/shard_map/pallas_call | solution.py:101
  (74 shorter events, 26.1 us)
Async XLA Ops:
  1.6 25.4 %collective-permute-start.6 = (bf16[3,256,256]{2,1,0:T(8,128)(2,1)S(1)}, bf16[3,256,256]{2,1,0:T(8,128)(2,1)S(1)}, u32[]{:S(2)}, u32[]{:S(2)}) collective-permute-start(bf16[3,256,256]{2,1,0:T(8,128)(2,1)S(1)} %get-tuple-element.56.refs_4_.refs_7_), channel_id=1, source_target_pairs={{0,30},{2,4},{4,2},{6,8},{8,6},{10,12},{12,10},{14,16},{16,14},{18... | collective-permute-start | bytes 1179656 | tf_op jit(solution)/shard_map/ppermute | solution.py:146
  4.3 22.7 %collective-permute-start.7 = (bf16[3,256,256]{2,1,0:T(8,128)(2,1)S(1)}, bf16[3,256,256]{2,1,0:T(8,128)(2,1)S(1)}, u32[]{:S(2)}, u32[]{:S(2)}) collective-permute-start(bf16[3,256,256]{2,1,0:T(8,128)(2,1)S(1)} %get-tuple-element.55.refs_5_.refs_8_), channel_id=1, source_target_pairs={{0,2},{2,0},{4,6},{6,4},{8,10},{10,8},{12,14},{14,12},{16,18},{18,... | collective-permute-start | bytes 1179656 | tf_op jit(solution)/shard_map/ppermute | solution.py:146
  7.1 11.8 %collective-permute-start.14 = (bf16[64,512]{1,0:T(8,128)(2,1)}, bf16[64,512]{1,0:T(8,128)(2,1)}, u32[]{:S(2)}, u32[]{:S(2)}) collective-permute-start(bf16[64,512]{1,0:T(8,128)(2,1)} %param.10), channel_id=1, source_target_pairs={{0,4},{2,6},{4,0},{6,2},{8,12},{10,14},{12,8},{14,10},{16,20},{18,... | collective-permute-start | bytes 196616 | tf_op jit(solution)/shard_map/ppermute | solution.py:146
  7.2 30.6 %collective-permute-start = (bf16[3,256,256]{2,1,0:T(8,128)(2,1)S(1)}, bf16[3,256,256]{2,1,0:T(8,128)(2,1)S(1)}, u32[]{:S(2)}, u32[]{:S(2)}) collective-permute-start(bf16[3,256,256]{2,1,0:T(8,128)(2,1)S(1)} %get-tuple-element.58.refs_4_.refs_7_), channel_id=1, source_target_pairs={{0,30},{2,4},{4,2},{6,8},{8,6},{10,12},{12,10},{14,16},{16,14},{18... | collective-permute-start | bytes 1179656 | tf_op jit(solution)/shard_map/ppermute | solution.py:146
  8.9 28.9 %collective-permute-start.1 = (bf16[3,256,256]{2,1,0:T(8,128)(2,1)S(1)}, bf16[3,256,256]{2,1,0:T(8,128)(2,1)S(1)}, u32[]{:S(2)}, u32[]{:S(2)}) collective-permute-start(bf16[3,256,256]{2,1,0:T(8,128)(2,1)S(1)} %get-tuple-element.57.refs_5_.refs_8_), channel_id=1, source_target_pairs={{0,2},{2,0},{4,6},{6,4},{8,10},{10,8},{12,14},{14,12},{16,18},{18,... | collective-permute-start | bytes 1179656 | tf_op jit(solution)/shard_map/ppermute | solution.py:146
  19.8 3.9 %collective-permute-start.15 = (bf16[128,512]{1,0:T(8,128)(2,1)S(1)}, bf16[128,512]{1,0:T(8,128)(2,1)S(1)}, u32[]{:S(2)}, u32[]{:S(2)}) collective-permute-start(bf16[128,512]{1,0:T(8,128)(2,1)S(1)} %pad_maximum_fusion.2), channel_id=1, source_target_pairs={{0,8},{2,10},{4,12},{6,14},{8,0},{10,2},{12,4},{14,6},{16,24},{18,... | collective-permute-start | bytes 393224 | tf_op jit(solution)/shard_map/ppermute | solution.py:146
  24.6 22.5 %collective-permute-start.16 = (bf16[256,512]{1,0:T(8,128)(2,1)S(1)}, bf16[256,512]{1,0:T(8,128)(2,1)S(1)}, u32[]{:S(2)}, u32[]{:S(2)}) collective-permute-start(bf16[256,512]{1,0:T(8,128)(2,1)S(1)} %pad_maximum_fusion.1), channel_id=1, source_target_pairs={{0,16},{2,18},{4,20},{6,22},{8,24},{10,26},{12,28},{14,30},{16,0},... | collective-permute-start | bytes 786440 | tf_op jit(solution)/shard_map/ppermute | solution.py:146
  33.9 14.2 %collective-permute-start.8 = (bf16[3,256,256]{2,1,0:T(8,128)(2,1)S(1)}, bf16[3,256,256]{2,1,0:T(8,128)(2,1)S(1)}, u32[]{:S(2)}, u32[]{:S(2)}) collective-permute-start(bf16[3,256,256]{2,1,0:T(8,128)(2,1)S(1)} %get-tuple-element.34.refs_4_.refs_7_), channel_id=1, source_target_pairs={{0,30},{2,4},{4,2},{6,8},{8,6},{10,12},{12,10},{14,16},{16,14},{18... | collective-permute-start | bytes 1179656 | tf_op jit(solution)/shard_map/ppermute | solution.py:146
  36.7 11.4 %collective-permute-start.9 = (bf16[3,256,256]{2,1,0:T(8,128)(2,1)S(1)}, bf16[3,256,256]{2,1,0:T(8,128)(2,1)S(1)}, u32[]{:S(2)}, u32[]{:S(2)}) collective-permute-start(bf16[3,256,256]{2,1,0:T(8,128)(2,1)S(1)} %get-tuple-element.35.refs_5_.refs_8_), channel_id=1, source_target_pairs={{0,2},{2,0},{4,6},{6,4},{8,10},{10,8},{12,14},{14,12},{16,18},{18,... | collective-permute-start | bytes 1179656 | tf_op jit(solution)/shard_map/ppermute | solution.py:146
  42.6 12.2 %collective-permute-start.2 = (bf16[3,256,256]{2,1,0:T(8,128)(2,1)S(1)}, bf16[3,256,256]{2,1,0:T(8,128)(2,1)S(1)}, u32[]{:S(2)}, u32[]{:S(2)}) collective-permute-start(bf16[3,256,256]{2,1,0:T(8,128)(2,1)S(1)} %get-tuple-element.29.refs_4_.refs_7_), channel_id=1, source_target_pairs={{0,30},{2,4},{4,2},{6,8},{8,6},{10,12},{12,10},{14,16},{16,14},{18... | collective-permute-start | bytes 1179656 | tf_op jit(solution)/shard_map/ppermute | solution.py:146
  44.5 10.3 %collective-permute-start.3 = (bf16[3,256,256]{2,1,0:T(8,128)(2,1)S(1)}, bf16[3,256,256]{2,1,0:T(8,128)(2,1)S(1)}, u32[]{:S(2)}, u32[]{:S(2)}) collective-permute-start(bf16[3,256,256]{2,1,0:T(8,128)(2,1)S(1)} %get-tuple-element.30.refs_5_.refs_8_), channel_id=1, source_target_pairs={{0,2},{2,0},{4,6},{6,4},{8,10},{10,8},{12,14},{14,12},{16,18},{18,... | collective-permute-start | bytes 1179656 | tf_op jit(solution)/shard_map/ppermute | solution.py:146
  48.0 32.7 %collective-permute-start.17 = (bf16[512,512]{1,0:T(8,128)(2,1)S(1)}, bf16[512,512]{1,0:T(8,128)(2,1)S(1)}, u32[]{:S(2)}, u32[]{:S(2)}) collective-permute-start(bf16[512,512]{1,0:T(8,128)(2,1)S(1)} %pad_maximum_fusion), channel_id=1, source_target_pairs={{0,2},{2,0},{4,6},{6,4},{8,10},{10,8},{12,14},{14,12},{16,18},{18,... | collective-permute-start | bytes 1572872 | tf_op jit(solution)/shard_map/ppermute | solution.py:146
  53.0 13.6 %collective-permute-start.10 = (bf16[3,256,256]{2,1,0:T(8,128)(2,1)S(1)}, bf16[3,256,256]{2,1,0:T(8,128)(2,1)S(1)}, u32[]{:S(2)}, u32[]{:S(2)}) collective-permute-start(bf16[3,256,256]{2,1,0:T(8,128)(2,1)S(1)} %get-tuple-element.36.refs_4_), channel_id=1, source_target_pairs={{0,30},{2,4},{4,2},{6,8},{8,6},{10,12},{12,10},{14,16},{16,14},{18... | collective-permute-start | bytes 1179656 | tf_op jit(solution)/shard_map/ppermute | solution.py:146
  53.1 13.5 %collective-permute-start.11 = (bf16[3,256,256]{2,1,0:T(8,128)(2,1)S(1)}, bf16[3,256,256]{2,1,0:T(8,128)(2,1)S(1)}, u32[]{:S(2)}, u32[]{:S(2)}) collective-permute-start(bf16[3,256,256]{2,1,0:T(8,128)(2,1)S(1)} %get-tuple-element.37.refs_5_), channel_id=1, source_target_pairs={{0,2},{2,0},{4,6},{6,4},{8,10},{10,8},{12,14},{14,12},{16,18},{18,... | collective-permute-start | bytes 1179656 | tf_op jit(solution)/shard_map/ppermute | solution.py:146
  59.7 13.2 %collective-permute-start.4 = (bf16[3,256,256]{2,1,0:T(8,128)(2,1)S(1)}, bf16[3,256,256]{2,1,0:T(8,128)(2,1)S(1)}, u32[]{:S(2)}, u32[]{:S(2)}) collective-permute-start(bf16[3,256,256]{2,1,0:T(8,128)(2,1)S(1)} %get-tuple-element.31.refs_4_), channel_id=1, source_target_pairs={{0,30},{2,4},{4,2},{6,8},{8,6},{10,12},{12,10},{14,16},{16,14},{18... | collective-permute-start | bytes 1179656 | tf_op jit(solution)/shard_map/ppermute | solution.py:146
  65.7 7.2 %collective-permute-start.5 = (bf16[3,256,256]{2,1,0:T(8,128)(2,1)S(1)}, bf16[3,256,256]{2,1,0:T(8,128)(2,1)S(1)}, u32[]{:S(2)}, u32[]{:S(2)}) collective-permute-start(bf16[3,256,256]{2,1,0:T(8,128)(2,1)S(1)} %get-tuple-element.32.refs_5_), channel_id=1, source_target_pairs={{0,2},{2,0},{4,6},{6,4},{8,10},{10,8},{12,14},{14,12},{16,18},{18,... | collective-permute-start | bytes 1179656 | tf_op jit(solution)/shard_map/ppermute | solution.py:146
  71.5 10.6 %collective-permute-start.20 = (bf16[3,256,256]{2,1,0:T(8,128)(2,1)S(1)}, bf16[3,256,256]{2,1,0:T(8,128)(2,1)S(1)}, u32[]{:S(2)}, u32[]{:S(2)}) collective-permute-start(bf16[3,256,256]{2,1,0:T(8,128)(2,1)S(1)} %get-tuple-element.41.refs_1_), channel_id=1, source_target_pairs={{0,1},{1,0},{2,3},{3,2},{4,5},{5,4},{6,7},{7,6},{8,9},{9,8},{10,11... | collective-permute-start | bytes 1179656 | tf_op jit(solution)/shard_map/ppermute | solution.py:146
  78.0 12.2 %collective-permute-start.19 = (bf16[3,256,256]{2,1,0:T(8,128)(2,1)S(1)}, bf16[3,256,256]{2,1,0:T(8,128)(2,1)S(1)}, u32[]{:S(2)}, u32[]{:S(2)}) collective-permute-start(bf16[3,256,256]{2,1,0:T(8,128)(2,1)S(1)} %get-tuple-element.40.refs_0_), channel_id=1, source_target_pairs={{0,1},{1,0},{2,3},{3,2},{4,5},{5,4},{6,7},{7,6},{8,9},{9,8},{10,11... | collective-permute-start | bytes 1179656 | tf_op jit(solution)/shard_map/ppermute | solution.py:146
  79.3 19.3 %collective-permute-start.13 = (bf16[3,256,256]{2,1,0:T(8,128)(2,1)S(1)}, bf16[3,256,256]{2,1,0:T(8,128)(2,1)S(1)}, u32[]{:S(2)}, u32[]{:S(2)}) collective-permute-start(bf16[3,256,256]{2,1,0:T(8,128)(2,1)S(1)} %get-tuple-element.38.refs_1_), channel_id=1, source_target_pairs={{0,1},{1,0},{2,3},{3,2},{4,5},{5,4},{6,7},{7,6},{8,9},{9,8},{10,11... | collective-permute-start | bytes 1179656 | tf_op jit(solution)/shard_map/ppermute | solution.py:146
  79.5 27.5 %collective-permute-start.12 = (bf16[3,256,256]{2,1,0:T(8,128)(2,1)S(1)}, bf16[3,256,256]{2,1,0:T(8,128)(2,1)S(1)}, u32[]{:S(2)}, u32[]{:S(2)}) collective-permute-start(bf16[3,256,256]{2,1,0:T(8,128)(2,1)S(1)} %get-tuple-element.33.refs_0_), channel_id=1, source_target_pairs={{0,1},{1,0},{2,3},{3,2},{4,5},{5,4},{6,7},{7,6},{8,9},{9,8},{10,11... | collective-permute-start | bytes 1179656 | tf_op jit(solution)/shard_map/ppermute | solution.py:146
  91.1 21.0 %collective-permute-start.27 = (bf16[3,256,256]{2,1,0:T(8,128)(2,1)S(1)}, bf16[3,256,256]{2,1,0:T(8,128)(2,1)S(1)}, u32[]{:S(2)}, u32[]{:S(2)}) collective-permute-start(bf16[3,256,256]{2,1,0:T(8,128)(2,1)S(1)} %get-tuple-element.48.refs_5_.refs_8_), channel_id=1, source_target_pairs={{0,2},{2,0},{4,6},{6,4},{8,10},{10,8},{12,14},{14,12},{16,18},{18,... | collective-permute-start | bytes 1179656 | tf_op jit(solution)/shard_map/ppermute | solution.py:146
  108.0 15.7 %collective-permute-start.26 = (bf16[3,256,256]{2,1,0:T(8,128)(2,1)S(1)}, bf16[3,256,256]{2,1,0:T(8,128)(2,1)S(1)}, u32[]{:S(2)}, u32[]{:S(2)}) collective-permute-start(bf16[3,256,256]{2,1,0:T(8,128)(2,1)S(1)} %get-tuple-element.47.refs_4_.refs_7_), channel_id=1, source_target_pairs={{0,30},{2,4},{4,2},{6,8},{8,6},{10,12},{12,10},{14,16},{16,14},{18... | collective-permute-start | bytes 1179656 | tf_op jit(solution)/shard_map/ppermute | solution.py:146
  109.5 20.6 %collective-permute-start.21 = (bf16[3,256,256]{2,1,0:T(8,128)(2,1)S(1)}, bf16[3,256,256]{2,1,0:T(8,128)(2,1)S(1)}, u32[]{:S(2)}, u32[]{:S(2)}) collective-permute-start(bf16[3,256,256]{2,1,0:T(8,128)(2,1)S(1)} %get-tuple-element.42.refs_5_.refs_8_), channel_id=1, source_target_pairs={{0,2},{2,0},{4,6},{6,4},{8,10},{10,8},{12,14},{14,12},{16,18},{18,... | collective-permute-start | bytes 1179656 | tf_op jit(solution)/shard_map/ppermute | solution.py:146
  109.5 21.6 %collective-permute-start.18 = (bf16[3,256,256]{2,1,0:T(8,128)(2,1)S(1)}, bf16[3,256,256]{2,1,0:T(8,128)(2,1)S(1)}, u32[]{:S(2)}, u32[]{:S(2)}) collective-permute-start(bf16[3,256,256]{2,1,0:T(8,128)(2,1)S(1)} %get-tuple-element.39.refs_4_.refs_7_), channel_id=1, source_target_pairs={{0,30},{2,4},{4,2},{6,8},{8,6},{10,12},{12,10},{14,16},{16,14},{18... | collective-permute-start | bytes 1179656 | tf_op jit(solution)/shard_map/ppermute | solution.py:146
  128.5 9.9 %collective-permute-start.28 = (bf16[3,256,256]{2,1,0:T(8,128)(2,1)S(1)}, bf16[3,256,256]{2,1,0:T(8,128)(2,1)S(1)}, u32[]{:S(2)}, u32[]{:S(2)}) collective-permute-start(bf16[3,256,256]{2,1,0:T(8,128)(2,1)S(1)} %get-tuple-element.49.refs_4_.refs_7_), channel_id=1, source_target_pairs={{0,30},{2,4},{4,2},{6,8},{8,6},{10,12},{12,10},{14,16},{16,14},{18... | collective-permute-start | bytes 1179656 | tf_op jit(solution)/shard_map/ppermute | solution.py:146
  130.0 8.4 %collective-permute-start.29 = (bf16[3,256,256]{2,1,0:T(8,128)(2,1)S(1)}, bf16[3,256,256]{2,1,0:T(8,128)(2,1)S(1)}, u32[]{:S(2)}, u32[]{:S(2)}) collective-permute-start(bf16[3,256,256]{2,1,0:T(8,128)(2,1)S(1)} %get-tuple-element.50.refs_5_.refs_8_), channel_id=1, source_target_pairs={{0,2},{2,0},{4,6},{6,4},{8,10},{10,8},{12,14},{14,12},{16,18},{18,... | collective-permute-start | bytes 1179656 | tf_op jit(solution)/shard_map/ppermute | solution.py:146
  135.9 12.2 %collective-permute-start.22 = (bf16[3,256,256]{2,1,0:T(8,128)(2,1)S(1)}, bf16[3,256,256]{2,1,0:T(8,128)(2,1)S(1)}, u32[]{:S(2)}, u32[]{:S(2)}) collective-permute-start(bf16[3,256,256]{2,1,0:T(8,128)(2,1)S(1)} %get-tuple-element.43.refs_4_.refs_7_), channel_id=1, source_target_pairs={{0,30},{2,4},{4,2},{6,8},{8,6},{10,12},{12,10},{14,16},{16,14},{18... | collective-permute-start | bytes 1179656 | tf_op jit(solution)/shard_map/ppermute | solution.py:146
  138.5 9.7 %collective-permute-start.23 = (bf16[3,256,256]{2,1,0:T(8,128)(2,1)S(1)}, bf16[3,256,256]{2,1,0:T(8,128)(2,1)S(1)}, u32[]{:S(2)}, u32[]{:S(2)}) collective-permute-start(bf16[3,256,256]{2,1,0:T(8,128)(2,1)S(1)} %get-tuple-element.44.refs_5_.refs_8_), channel_id=1, source_target_pairs={{0,2},{2,0},{4,6},{6,4},{8,10},{10,8},{12,14},{14,12},{16,18},{18,... | collective-permute-start | bytes 1179656 | tf_op jit(solution)/shard_map/ppermute | solution.py:146
  143.4 17.4 %collective-permute-start.30 = (bf16[3,256,256]{2,1,0:T(8,128)(2,1)S(1)}, bf16[3,256,256]{2,1,0:T(8,128)(2,1)S(1)}, u32[]{:S(2)}, u32[]{:S(2)}) collective-permute-start(bf16[3,256,256]{2,1,0:T(8,128)(2,1)S(1)} %get-tuple-element.51.refs_4_), channel_id=1, source_target_pairs={{0,30},{2,4},{4,2},{6,8},{8,6},{10,12},{12,10},{14,16},{16,14},{18... | collective-permute-start | bytes 1179656 | tf_op jit(solution)/shard_map/ppermute | solution.py:146
  143.5 17.3 %collective-permute-start.31 = (bf16[3,256,256]{2,1,0:T(8,128)(2,1)S(1)}, bf16[3,256,256]{2,1,0:T(8,128)(2,1)S(1)}, u32[]{:S(2)}, u32[]{:S(2)}) collective-permute-start(bf16[3,256,256]{2,1,0:T(8,128)(2,1)S(1)} %get-tuple-element.52.refs_5_), channel_id=1, source_target_pairs={{0,2},{2,0},{4,6},{6,4},{8,10},{10,8},{12,14},{14,12},{16,18},{18,... | collective-permute-start | bytes 1179656 | tf_op jit(solution)/shard_map/ppermute | solution.py:146
  153.0 13.6 %collective-permute-start.24 = (bf16[3,256,256]{2,1,0:T(8,128)(2,1)S(1)}, bf16[3,256,256]{2,1,0:T(8,128)(2,1)S(1)}, u32[]{:S(2)}, u32[]{:S(2)}) collective-permute-start(bf16[3,256,256]{2,1,0:T(8,128)(2,1)S(1)} %get-tuple-element.45.refs_4_), channel_id=1, source_target_pairs={{0,30},{2,4},{4,2},{6,8},{8,6},{10,12},{12,10},{14,16},{16,14},{18... | collective-permute-start | bytes 1179656 | tf_op jit(solution)/shard_map/ppermute | solution.py:146
  157.5 9.1 %collective-permute-start.25 = (bf16[3,256,256]{2,1,0:T(8,128)(2,1)S(1)}, bf16[3,256,256]{2,1,0:T(8,128)(2,1)S(1)}, u32[]{:S(2)}, u32[]{:S(2)}) collective-permute-start(bf16[3,256,256]{2,1,0:T(8,128)(2,1)S(1)} %get-tuple-element.46.refs_5_), channel_id=1, source_target_pairs={{0,2},{2,0},{4,6},{6,4},{8,10},{10,8},{12,14},{14,12},{16,18},{18,... | collective-permute-start | bytes 1179656 | tf_op jit(solution)/shard_map/ppermute | solution.py:146
  (5 other events, 100.5 us)

commit v2 on v1

--- a/solution.py
+++ b/solution.py
@@ -22,20 +22,13 @@
     if last and column > 0:
         refs = refs[1:]
     if last:
-        out_ref, held, arrived, made, left = refs
+        out_ref, made, left = refs
     else:
-        new_outer, new_inner, held, arrived = refs
+        new_outer, new_inner = refs
     odd = odd_ref[0]
-    rows, copies = [], []
+    sent = []
     for k in range(2 * GY):
         row = odd * GY + k if k < GY else (1 - odd) * GY + (k - GY)
-        copy = pltpu.make_async_copy(blocks_ref.at[row], held.at[k], arrived.at[k])
-        copy.start()
-        rows.append(row)
-        copies.append(copy)
-    sent = []
-    for k in range(2 * GY):
-        row = rows[k]
         own, near, far = (outer, inner, far_outer) if k < GY else (inner, outer, far_inner)
         far_side = 1 + odd if k < GY else 2 - odd
         near_side = 3 - far_side
@@ -43,12 +36,11 @@
         def slot(side):
             return lax.rem(links_ref[row, side], GY)
 
-        copies[k].wait()
-        total = jnp.dot(held[k, 0], own[slot(0)], preferred_element_type=jnp.float32)
-        total += jnp.dot(held[k, 3], own[slot(3)], preferred_element_type=jnp.float32)
-        total += jnp.dot(held[k, 4], own[slot(4)], preferred_element_type=jnp.float32)
-        total += jnp.dot(held[k, near_side], near[slot(near_side)], preferred_element_type=jnp.float32)
-        total += jnp.dot(held[k, far_side], far[slot(far_side)], preferred_element_type=jnp.float32)
+        total = jnp.dot(blocks_ref[row, 0], own[slot(0)], preferred_element_type=jnp.float32)
+        total += jnp.dot(blocks_ref[row, 3], own[slot(3)], preferred_element_type=jnp.float32)
+        total += jnp.dot(blocks_ref[row, 4], own[slot(4)], preferred_element_type=jnp.float32)
+        total += jnp.dot(blocks_ref[row, near_side], near[slot(near_side)], preferred_element_type=jnp.float32)
+        total += jnp.dot(blocks_ref[row, far_side], far[slot(far_side)], preferred_element_type=jnp.float32)
         if not first:
             total = 2.0 * total - before[k // GY][k % GY].astype(jnp.float32)
         if last:
@@ -73,15 +65,12 @@
     vmem = pl.BlockSpec(memory_space=pltpu.VMEM)
     anywhere = pl.BlockSpec(memory_space=pl.ANY)
     operands = [odd, links, blocks, halos[0], current[0], current[1], halos[1]]
-    specs = [smem, smem, anywhere] + [vmem] * 4
+    specs = [smem, smem] + [vmem] * 5
     if before is not None:
         operands += list(before)
         specs += [vmem] * 2
     aliases = {}
-    scratch = [
-        pltpu.VMEM((2 * GY,) + blocks.shape[1:], blocks.dtype),
-        pltpu.SemaphoreType.DMA((2 * GY,)),
-    ]
+    scratch = []
     if last:
         if out is not None:
             aliases = {len(operands): 0}
@@ -105,7 +94,7 @@
         out_specs=out_specs,
         scratch_shapes=scratch,
         input_output_aliases=aliases,
-        compiler_params=pltpu.CompilerParams(vmem_limit_bytes=24 * MIB),
+        compiler_params=pltpu.CompilerParams(vmem_limit_bytes=16 * MIB),
         cost_estimate=pl.CostEstimate(flops=flops, bytes_accessed=moved, transcendentals=0),
     )(*operands)
 
@@ -137,7 +126,7 @@
         out_shape=[jax.ShapeDtypeStruct((GY, basis, width), jnp.bfloat16) for width in widths],
         in_specs=[vmem] * (len(pieces) + 1),
         out_specs=[vmem] * len(widths),
-        compiler_params=pltpu.CompilerParams(vmem_limit_bytes=24 * MIB),
+        compiler_params=pltpu.CompilerParams(vmem_limit_bytes=16 * MIB),
         cost_estimate=pl.CostEstimate(flops=flops, bytes_accessed=moved, transcendentals=0),
     )(*pieces, matrix)
 

time: 173 us -> 158 us (0.913)
  waiting for transfers between devices: 52.6 us -> 91.2 us
  Pallas kernels: 62.1 us -> 25.5 us
  starting transfers between devices: 47 us -> 30.1 us
    ppermute x32, waiting for transfers between devices: 52.6 us -> 91.2 us  [exchange(): lax.ppermute(array, axis, [(i, partner(i)) for i in range(lax.axis_size(a...]
    pallas_call x12, Pallas kernels: 60.2 us -> 23.5 us  [apply_step(): pl.pallas_call(functools.partial(step_kernel, before is None, last, colum...]
    ppermute x32, starting transfers between devices: 47 us -> 30.1 us  [exchange(): lax.ppermute(array, axis, [(i, partner(i)) for i in range(lax.axis_size(a...]
  transfers between devices with their start and end apart: 32 -> 32, of which waited for: 11 -> 16; matrix products, arithmetic and copies ran while one was open for 4% -> 4% of each run, Pallas kernels for 33% -> 15%
where the time goes in v2:
time: 158 us; the launch traced here: 157 us
  waiting for transfers between devices  91.2 us (58%)
  starting transfers between devices  30.1 us (19%)
  Pallas kernels  25.5 us (16%)
  local copies, waits for them, and re-layouts  6.17 us (4%)
  other arithmetic  2.69 us (2%)
    ppermute x32, waiting for transfers between devices, exchange(): lax.ppermute(array, axis, [(i, partner(i)) for i in range(lax.axis_size(a...  91.2 us
    ppermute x32, starting transfers between devices, exchange(): lax.ppermute(array, axis, [(i, partner(i)) for i in range(lax.axis_size(a...  30.1 us
    pallas_call x12, Pallas kernels, apply_step(): pl.pallas_call(functools.partial(step_kernel, before is None, last, colum...  23.5 us
    unnamed x14, local copies, waits for them, and re-layouts  3.85 us
  transfers between devices with their start and end apart: 32, of which 16 were waited for; matrix products, arithmetic and copies ran while one was open for 4% of the time, Pallas kernels for 15%

profile of v2, /device:TPU:1, one launch (start us, length us, event | category | flops | bytes accessed | tf_op | source)
XLA Modules:
  0.0 157.4 jit_solution(15092443957603067127)
XLA Ops:
  1.6 2.7 %collective-permute-start.6 = (bf16[3,256,256]{2,1,0:T(8,128)(2,1)S(1)}, bf16[3,256,256]{2,1,0:T(8,128)(2,1)S(1)}, u32[]{:S(2)}, u32[]{:S(2)}) collective-permute-start(bf16[3,256,256]{2,1,0:T(8,128)(2,1)S(1)} %get-tuple-element.56.refs_4_.refs_7_), channel_id=1, source_target_pairs={{0,30},{2,4},{4,2},{6,8},{8,6},{10,12},{12,10},{14,16},{16,14},{18... | collective-permute-start | bytes 1179656 | tf_op jit(solution)/shard_map/ppermute | solution.py:135
  4.3 2.9 %collective-permute-start.7 = (bf16[3,256,256]{2,1,0:T(8,128)(2,1)S(1)}, bf16[3,256,256]{2,1,0:T(8,128)(2,1)S(1)}, u32[]{:S(2)}, u32[]{:S(2)}) collective-permute-start(bf16[3,256,256]{2,1,0:T(8,128)(2,1)S(1)} %get-tuple-element.55.refs_5_.refs_8_), channel_id=1, source_target_pairs={{0,2},{2,0},{4,6},{6,4},{8,10},{10,8},{12,14},{14,12},{16,18},{18,... | collective-permute-start | bytes 1179656 | tf_op jit(solution)/shard_map/ppermute | solution.py:135
  9.3 9.6 %collective-permute-done.14 = bf16[64,512]{1,0:T(8,128)(2,1)} collective-permute-done((bf16[64,512]{1,0:T(8,128)(2,1)}, bf16[64,512]{1,0:T(8,128)(2,1)}, u32[]{:S(2)}, u32[]{:S(2)}) %collective-permute-start.14) | collective-permute-done | bytes 65568 | tf_op jit(solution)/shard_map/ppermute | solution.py:135
  24.6 2.4 %collective-permute-start.16 = (bf16[256,512]{1,0:T(8,128)(2,1)S(1)}, bf16[256,512]{1,0:T(8,128)(2,1)S(1)}, u32[]{:S(2)}, u32[]{:S(2)}) collective-permute-start(bf16[256,512]{1,0:T(8,128)(2,1)S(1)} %pad_maximum_fusion.1), channel_id=1, source_target_pairs={{0,16},{2,18},{4,20},{6,22},{8,24},{10,26},{12,28},{14,30},{16,0},... | collective-permute-start | bytes 786440 | tf_op jit(solution)/shard_map/ppermute | solution.py:135
  27.0 2.1 %copy-done = bf16[6,5,256,256]{3,2,1,0:T(8,128)(2,1)S(1)} copy-done((bf16[6,5,256,256]{3,2,1,0:T(8,128)(2,1)S(1)}, bf16[6,5,256,256]{3,2,1,0:T(8,128)(2,1)}, u32[]{:S(2)}) %copy-start) | copy-done | bytes 3932184
  29.1 1.8 %shard_map.67 = (bf16[3,256,256]{2,1,0:T(8,128)(2,1)S(1)}, bf16[3,256,256]{2,1,0:T(8,128)(2,1)S(1)}) custom-call(s32[1]{0:T(128)} %bitcast.refs_0_, s32[6,5]{1,0:T(8,128)S(1)} %copy-done.2, bf16[6,5,256,256]{3,2,1,0:T(8,128)(2,1)S(1)} %copy-done, bf16[3,256,256]{2,1,0:T(8,128)(2,1)S(1)} %collective-permute-done.6.refs_3_, ...), custom_call_target="tpu_custom_call" | custom-call | flops 1006632960 | bytes 7864320 | tf_op jit(solution)/shard_map/pallas_call | solution.py:90
  30.9 2.8 %collective-permute-start.8 = (bf16[3,256,256]{2,1,0:T(8,128)(2,1)S(1)}, bf16[3,256,256]{2,1,0:T(8,128)(2,1)S(1)}, u32[]{:S(2)}, u32[]{:S(2)}) collective-permute-start(bf16[3,256,256]{2,1,0:T(8,128)(2,1)S(1)} %get-tuple-element.34.refs_4_.refs_7_), channel_id=1, source_target_pairs={{0,30},{2,4},{4,2},{6,8},{8,6},{10,12},{12,10},{14,16},{16,14},{18... | collective-permute-start | bytes 1179656 | tf_op jit(solution)/shard_map/ppermute | solution.py:135
  34.7 1.8 %shard_map.64 = (bf16[3,256,256]{2,1,0:T(8,128)(2,1)S(1)}, bf16[3,256,256]{2,1,0:T(8,128)(2,1)S(1)}) custom-call(s32[1]{0:T(128)} %bitcast.refs_0_, s32[6,5]{1,0:T(8,128)S(1)} %copy-done.2, bf16[6,5,256,256]{3,2,1,0:T(8,128)(2,1)S(1)} %copy-done, bf16[3,256,256]{2,1,0:T(8,128)(2,1)S(1)} %collective-permute-done.refs_3_, ...), custom_call_target="tpu_custom_call" | custom-call | flops 1006632960 | bytes 7864320 | tf_op jit(solution)/shard_map/pallas_call | solution.py:90
  36.5 1.9 %collective-permute-start.2 = (bf16[3,256,256]{2,1,0:T(8,128)(2,1)S(1)}, bf16[3,256,256]{2,1,0:T(8,128)(2,1)S(1)}, u32[]{:S(2)}, u32[]{:S(2)}) collective-permute-start(bf16[3,256,256]{2,1,0:T(8,128)(2,1)S(1)} %get-tuple-element.29.refs_4_.refs_7_), channel_id=1, source_target_pairs={{0,30},{2,4},{4,2},{6,8},{8,6},{10,12},{12,10},{14,16},{16,14},{18... | collective-permute-start | bytes 1179656 | tf_op jit(solution)/shard_map/ppermute | solution.py:135
  42.0 5.6 %collective-permute-done.8.refs_3_ = bf16[3,256,256]{2,1,0:T(8,128)(2,1)S(1)} collective-permute-done((bf16[3,256,256]{2,1,0:T(8,128)(2,1)S(1)}, bf16[3,256,256]{2,1,0:T(8,128)(2,1)S(1)}, u32[]{:S(2)}, u32[]{:S(2)}) %collective-permute-start.8) | collective-permute-done | bytes 393248 | tf_op jit(solution)/shard_map/ppermute | solution.py:135
  47.6 1.8 %shard_map.68 = (bf16[3,256,256]{2,1,0:T(8,128)(2,1)S(1)}, bf16[3,256,256]{2,1,0:T(8,128)(2,1)S(1)}) custom-call(s32[1]{0:T(128)} %bitcast.refs_0_, s32[6,5]{1,0:T(8,128)S(1)} %copy-done.2, bf16[6,5,256,256]{3,2,1,0:T(8,128)(2,1)S(1)} %copy-done, bf16[3,256,256]{2,1,0:T(8,128)(2,1)S(1)} %collective-permute-done.8.refs_3_, ...), custom_call_target="tpu_custom_call" | custom-call | flops 1006632960 | bytes 7864320 | tf_op jit(solution)/shard_map/pallas_call | solution.py:90
  49.4 4.2 %collective-permute-start.10 = (bf16[3,256,256]{2,1,0:T(8,128)(2,1)S(1)}, bf16[3,256,256]{2,1,0:T(8,128)(2,1)S(1)}, u32[]{:S(2)}, u32[]{:S(2)}) collective-permute-start(bf16[3,256,256]{2,1,0:T(8,128)(2,1)S(1)} %get-tuple-element.36.refs_4_), channel_id=1, source_target_pairs={{0,30},{2,4},{4,2},{6,8},{8,6},{10,12},{12,10},{14,16},{16,14},{18... | collective-permute-start | bytes 1179656 | tf_op jit(solution)/shard_map/ppermute | solution.py:135
  53.7 2.3 %collective-permute-done.2.refs_3_ = bf16[3,256,256]{2,1,0:T(8,128)(2,1)S(1)} collective-permute-done((bf16[3,256,256]{2,1,0:T(8,128)(2,1)S(1)}, bf16[3,256,256]{2,1,0:T(8,128)(2,1)S(1)}, u32[]{:S(2)}, u32[]{:S(2)}) %collective-permute-start.2) | collective-permute-done | bytes 393248 | tf_op jit(solution)/shard_map/ppermute | solution.py:135
  56.0 1.8 %shard_map.65 = (bf16[3,256,256]{2,1,0:T(8,128)(2,1)S(1)}, bf16[3,256,256]{2,1,0:T(8,128)(2,1)S(1)}) custom-call(s32[1]{0:T(128)} %bitcast.refs_0_, s32[6,5]{1,0:T(8,128)S(1)} %copy-done.2, bf16[6,5,256,256]{3,2,1,0:T(8,128)(2,1)S(1)} %copy-done, bf16[3,256,256]{2,1,0:T(8,128)(2,1)S(1)} %collective-permute-done.2.refs_3_, ...), custom_call_target="tpu_custom_call" | custom-call | flops 1006632960 | bytes 7864320 | tf_op jit(solution)/shard_map/pallas_call | solution.py:90
  59.2 7.7 %collective-permute-done.10.refs_3_ = bf16[3,256,256]{2,1,0:T(8,128)(2,1)S(1)} collective-permute-done((bf16[3,256,256]{2,1,0:T(8,128)(2,1)S(1)}, bf16[3,256,256]{2,1,0:T(8,128)(2,1)S(1)}, u32[]{:S(2)}, u32[]{:S(2)}) %collective-permute-start.10) | collective-permute-done | bytes 393248 | tf_op jit(solution)/shard_map/ppermute | solution.py:135
  71.0 1.8 %shard_map.66 = (bf16[3,256,256]{2,1,0:T(8,128)(2,1)S(1)}, bf16[3,256,256]{2,1,0:T(8,128)(2,1)S(1)}) custom-call(s32[1]{0:T(128)} %bitcast.refs_0_, s32[6,5]{1,0:T(8,128)S(1)} %copy-done.2, bf16[6,5,256,256]{3,2,1,0:T(8,128)(2,1)S(1)} %copy-done, bf16[3,256,256]{2,1,0:T(8,128)(2,1)S(1)} %collective-permute-done.4.refs_3_, ...), custom_call_target="tpu_custom_call" | custom-call | flops 1006632960 | bytes 7864320 | tf_op jit(solution)/shard_map/pallas_call | solution.py:90
  77.0 2.9 %collective-permute-done.20.refs_3_ = bf16[3,256,256]{2,1,0:T(8,128)(2,1)S(1)} collective-permute-done((bf16[3,256,256]{2,1,0:T(8,128)(2,1)S(1)}, bf16[3,256,256]{2,1,0:T(8,128)(2,1)S(1)}, u32[]{:S(2)}, u32[]{:S(2)}) %collective-permute-start.20) | collective-permute-done | bytes 393248 | tf_op jit(solution)/shard_map/ppermute | solution.py:135
  79.8 8.4 %collective-permute-done.19.refs_2_ = bf16[3,256,256]{2,1,0:T(8,128)(2,1)S(1)} collective-permute-done((bf16[3,256,256]{2,1,0:T(8,128)(2,1)S(1)}, bf16[3,256,256]{2,1,0:T(8,128)(2,1)S(1)}, u32[]{:S(2)}, u32[]{:S(2)}) %collective-permute-start.19) | collective-permute-done | bytes 393248 | tf_op jit(solution)/shard_map/ppermute | solution.py:135
  89.3 6.9 %collective-permute-done.13.refs_3_ = bf16[3,256,256]{2,1,0:T(8,128)(2,1)S(1)} collective-permute-done((bf16[3,256,256]{2,1,0:T(8,128)(2,1)S(1)}, bf16[3,256,256]{2,1,0:T(8,128)(2,1)S(1)}, u32[]{:S(2)}, u32[]{:S(2)}) %collective-permute-start.13) | collective-permute-done | bytes 393248 | tf_op jit(solution)/shard_map/ppermute | solution.py:135
  96.2 4.2 %collective-permute-done.12.refs_2_ = bf16[3,256,256]{2,1,0:T(8,128)(2,1)S(1)} collective-permute-done((bf16[3,256,256]{2,1,0:T(8,128)(2,1)S(1)}, bf16[3,256,256]{2,1,0:T(8,128)(2,1)S(1)}, u32[]{:S(2)}, u32[]{:S(2)}) %collective-permute-start.12) | collective-permute-done | bytes 393248 | tf_op jit(solution)/shard_map/ppermute | solution.py:135
  103.1 16.3 %collective-permute-done.26.refs_3_ = bf16[3,256,256]{2,1,0:T(8,128)(2,1)S(1)} collective-permute-done((bf16[3,256,256]{2,1,0:T(8,128)(2,1)S(1)}, bf16[3,256,256]{2,1,0:T(8,128)(2,1)S(1)}, u32[]{:S(2)}, u32[]{:S(2)}) %collective-permute-start.26) | collective-permute-done | bytes 393248 | tf_op jit(solution)/shard_map/ppermute | solution.py:135
  119.5 1.8 %shard_map.74 = (bf16[3,256,256]{2,1,0:T(8,128)(2,1)S(1)}, bf16[3,256,256]{2,1,0:T(8,128)(2,1)S(1)}) custom-call(s32[1]{0:T(128)} %bitcast.refs_0_, s32[6,5]{1,0:T(8,128)S(1)} %copy-done.2, bf16[6,5,256,256]{3,2,1,0:T(8,128)(2,1)S(1)} %copy-done.1, bf16[3,256,256]{2,1,0:T(8,128)(2,1)S(1)} %collective-permute-done.26.refs_3_, ...), custom_call_target="tpu_custom_call" | custom-call | flops 1006632960 | bytes 7864320 | tf_op jit(solution)/shard_map/pallas_call | solution.py:90
  121.4 2.2 %collective-permute-done.18.refs_3_ = bf16[3,256,256]{2,1,0:T(8,128)(2,1)S(1)} collective-permute-done((bf16[3,256,256]{2,1,0:T(8,128)(2,1)S(1)}, bf16[3,256,256]{2,1,0:T(8,128)(2,1)S(1)}, u32[]{:S(2)}, u32[]{:S(2)}) %collective-permute-start.18) | collective-permute-done | bytes 393248 | tf_op jit(solution)/shard_map/ppermute | solution.py:135
  123.7 2.0 %shard_map.72 = (bf16[3,256,256]{2,1,0:T(8,128)(2,1)S(1)}, bf16[3,256,256]{2,1,0:T(8,128)(2,1)S(1)}) custom-call(s32[1]{0:T(128)} %bitcast.refs_0_, s32[6,5]{1,0:T(8,128)S(1)} %copy-done.2, bf16[6,5,256,256]{3,2,1,0:T(8,128)(2,1)S(1)} %copy-done.1, bf16[3,256,256]{2,1,0:T(8,128)(2,1)S(1)} %collective-permute-done.18.refs_3_, ...), custom_call_target="tpu_custom_call" | custom-call | flops 1006632960 | bytes 7864320 | tf_op jit(solution)/shard_map/pallas_call | solution.py:90
  125.8 2.7 %collective-permute-done.28.refs_3_ = bf16[3,256,256]{2,1,0:T(8,128)(2,1)S(1)} collective-permute-done((bf16[3,256,256]{2,1,0:T(8,128)(2,1)S(1)}, bf16[3,256,256]{2,1,0:T(8,128)(2,1)S(1)}, u32[]{:S(2)}, u32[]{:S(2)}) %collective-permute-start.28) | collective-permute-done | bytes 393248 | tf_op jit(solution)/shard_map/ppermute | solution.py:135
  128.6 1.8 %shard_map.75 = (bf16[3,256,256]{2,1,0:T(8,128)(2,1)S(1)}, bf16[3,256,256]{2,1,0:T(8,128)(2,1)S(1)}) custom-call(s32[1]{0:T(128)} %bitcast.refs_0_, s32[6,5]{1,0:T(8,128)S(1)} %copy-done.2, bf16[6,5,256,256]{3,2,1,0:T(8,128)(2,1)S(1)} %copy-done.1, bf16[3,256,256]{2,1,0:T(8,128)(2,1)S(1)} %collective-permute-done.28.refs_3_, ...), custom_call_target="tpu_custom_call" | custom-call | flops 1006632960 | bytes 7864320 | tf_op jit(solution)/shard_map/pallas_call | solution.py:90
  130.5 15.1 %collective-permute-done.22.refs_3_ = bf16[3,256,256]{2,1,0:T(8,128)(2,1)S(1)} collective-permute-done((bf16[3,256,256]{2,1,0:T(8,128)(2,1)S(1)}, bf16[3,256,256]{2,1,0:T(8,128)(2,1)S(1)}, u32[]{:S(2)}, u32[]{:S(2)}) %collective-permute-start.22) | collective-permute-done | bytes 393248 | tf_op jit(solution)/shard_map/ppermute | solution.py:135
  145.6 1.8 %shard_map.73 = (bf16[3,256,256]{2,1,0:T(8,128)(2,1)S(1)}, bf16[3,256,256]{2,1,0:T(8,128)(2,1)S(1)}) custom-call(s32[1]{0:T(128)} %bitcast.refs_0_, s32[6,5]{1,0:T(8,128)S(1)} %copy-done.2, bf16[6,5,256,256]{3,2,1,0:T(8,128)(2,1)S(1)} %copy-done.1, bf16[3,256,256]{2,1,0:T(8,128)(2,1)S(1)} %collective-permute-done.22.refs_3_, ...), custom_call_target="tpu_custom_call" | custom-call | flops 1006632960 | bytes 7864320 | tf_op jit(solution)/shard_map/pallas_call | solution.py:90
  147.6 2.2 %collective-permute-done.30.refs_3_ = bf16[3,256,256]{2,1,0:T(8,128)(2,1)S(1)} collective-permute-done((bf16[3,256,256]{2,1,0:T(8,128)(2,1)S(1)}, bf16[3,256,256]{2,1,0:T(8,128)(2,1)S(1)}, u32[]{:S(2)}, u32[]{:S(2)}) %collective-permute-start.30) | collective-permute-done | bytes 393248 | tf_op jit(solution)/shard_map/ppermute | solution.py:135
  149.8 2.6 %shard_map.76.refs_9_ = bf16[6,256,512]{2,1,0:T(8,128)(2,1)} custom-call(s32[1]{0:T(128)} %bitcast.refs_0_, s32[6,5]{1,0:T(8,128)S(1)} %copy-done.2, bf16[6,5,256,256]{3,2,1,0:T(8,128)(2,1)S(1)} %copy-done.1, bf16[3,256,256]{2,1,0:T(8,128)(2,1)S(1)} %collective-permute-done.30.refs_3_, bf16[3,256,256]{2,1,0:T(8,128)(2,1)S(1)} %get-tuple-element.51.refs_4_, ...), custom_call_target="tpu_custom_call" | custom-call | flops 1006632960 | bytes 7864320 | tf_op jit(solution)/shard_map/pallas_call | solution.py:90
  152.4 2.3 %collective-permute-done.24.refs_3_ = bf16[3,256,256]{2,1,0:T(8,128)(2,1)S(1)} collective-permute-done((bf16[3,256,256]{2,1,0:T(8,128)(2,1)S(1)}, bf16[3,256,256]{2,1,0:T(8,128)(2,1)S(1)}, u32[]{:S(2)}, u32[]{:S(2)}) %collective-permute-start.24) | collective-permute-done | bytes 393248 | tf_op jit(solution)/shard_map/ppermute | solution.py:135
  154.7 2.6 %shard_map.77 = bf16[6,256,512]{2,1,0:T(8,128)(2,1)} custom-call(s32[1]{0:T(128)} %bitcast.refs_0_, s32[6,5]{1,0:T(8,128)S(1)} %copy-done.2, bf16[6,5,256,256]{3,2,1,0:T(8,128)(2,1)S(1)} %copy-done.1, bf16[3,256,256]{2,1,0:T(8,128)(2,1)S(1)} %collective-permute-done.24.refs_3_, ...), custom_call_target="tpu_custom_call", output_to_operand_aliasing={{}: (9, {})} | custom-call | flops 1006632960 | bytes 7864320 | tf_op jit(solution)/shard_map/pallas_call | solution.py:90
  (74 shorter events, 28.0 us)
Async XLA Ops:
  1.6 25.4 %collective-permute-start.6 = (bf16[3,256,256]{2,1,0:T(8,128)(2,1)S(1)}, bf16[3,256,256]{2,1,0:T(8,128)(2,1)S(1)}, u32[]{:S(2)}, u32[]{:S(2)}) collective-permute-start(bf16[3,256,256]{2,1,0:T(8,128)(2,1)S(1)} %get-tuple-element.56.refs_4_.refs_7_), channel_id=1, source_target_pairs={{0,30},{2,4},{4,2},{6,8},{8,6},{10,12},{12,10},{14,16},{16,14},{18... | collective-permute-start | bytes 1179656 | tf_op jit(solution)/shard_map/ppermute | solution.py:135
  4.3 22.7 %collective-permute-start.7 = (bf16[3,256,256]{2,1,0:T(8,128)(2,1)S(1)}, bf16[3,256,256]{2,1,0:T(8,128)(2,1)S(1)}, u32[]{:S(2)}, u32[]{:S(2)}) collective-permute-start(bf16[3,256,256]{2,1,0:T(8,128)(2,1)S(1)} %get-tuple-element.55.refs_5_.refs_8_), channel_id=1, source_target_pairs={{0,2},{2,0},{4,6},{6,4},{8,10},{10,8},{12,14},{14,12},{16,18},{18,... | collective-permute-start | bytes 1179656 | tf_op jit(solution)/shard_map/ppermute | solution.py:135
  7.1 11.8 %collective-permute-start.14 = (bf16[64,512]{1,0:T(8,128)(2,1)}, bf16[64,512]{1,0:T(8,128)(2,1)}, u32[]{:S(2)}, u32[]{:S(2)}) collective-permute-start(bf16[64,512]{1,0:T(8,128)(2,1)} %param.10), channel_id=1, source_target_pairs={{0,4},{2,6},{4,0},{6,2},{8,12},{10,14},{12,8},{14,10},{16,20},{18,... | collective-permute-start | bytes 196616 | tf_op jit(solution)/shard_map/ppermute | solution.py:135
  7.2 27.5 %collective-permute-start = (bf16[3,256,256]{2,1,0:T(8,128)(2,1)S(1)}, bf16[3,256,256]{2,1,0:T(8,128)(2,1)S(1)}, u32[]{:S(2)}, u32[]{:S(2)}) collective-permute-start(bf16[3,256,256]{2,1,0:T(8,128)(2,1)S(1)} %get-tuple-element.58.refs_4_.refs_7_), channel_id=1, source_target_pairs={{0,30},{2,4},{4,2},{6,8},{8,6},{10,12},{12,10},{14,16},{16,14},{18... | collective-permute-start | bytes 1179656 | tf_op jit(solution)/shard_map/ppermute | solution.py:135
  8.9 25.8 %collective-permute-start.1 = (bf16[3,256,256]{2,1,0:T(8,128)(2,1)S(1)}, bf16[3,256,256]{2,1,0:T(8,128)(2,1)S(1)}, u32[]{:S(2)}, u32[]{:S(2)}) collective-permute-start(bf16[3,256,256]{2,1,0:T(8,128)(2,1)S(1)} %get-tuple-element.57.refs_5_.refs_8_), channel_id=1, source_target_pairs={{0,2},{2,0},{4,6},{6,4},{8,10},{10,8},{12,14},{14,12},{16,18},{18,... | collective-permute-start | bytes 1179656 | tf_op jit(solution)/shard_map/ppermute | solution.py:135
  19.8 3.9 %collective-permute-start.15 = (bf16[128,512]{1,0:T(8,128)(2,1)S(1)}, bf16[128,512]{1,0:T(8,128)(2,1)S(1)}, u32[]{:S(2)}, u32[]{:S(2)}) collective-permute-start(bf16[128,512]{1,0:T(8,128)(2,1)S(1)} %pad_maximum_fusion.2), channel_id=1, source_target_pairs={{0,8},{2,10},{4,12},{6,14},{8,0},{10,2},{12,4},{14,6},{16,24},{18,... | collective-permute-start | bytes 393224 | tf_op jit(solution)/shard_map/ppermute | solution.py:135
  24.6 16.4 %collective-permute-start.16 = (bf16[256,512]{1,0:T(8,128)(2,1)S(1)}, bf16[256,512]{1,0:T(8,128)(2,1)S(1)}, u32[]{:S(2)}, u32[]{:S(2)}) collective-permute-start(bf16[256,512]{1,0:T(8,128)(2,1)S(1)} %pad_maximum_fusion.1), channel_id=1, source_target_pairs={{0,16},{2,18},{4,20},{6,22},{8,24},{10,26},{12,28},{14,30},{16,0},... | collective-permute-start | bytes 786440 | tf_op jit(solution)/shard_map/ppermute | solution.py:135
  30.9 16.7 %collective-permute-start.8 = (bf16[3,256,256]{2,1,0:T(8,128)(2,1)S(1)}, bf16[3,256,256]{2,1,0:T(8,128)(2,1)S(1)}, u32[]{:S(2)}, u32[]{:S(2)}) collective-permute-start(bf16[3,256,256]{2,1,0:T(8,128)(2,1)S(1)} %get-tuple-element.34.refs_4_.refs_7_), channel_id=1, source_target_pairs={{0,30},{2,4},{4,2},{6,8},{8,6},{10,12},{12,10},{14,16},{16,14},{18... | collective-permute-start | bytes 1179656 | tf_op jit(solution)/shard_map/ppermute | solution.py:135
  33.7 13.9 %collective-permute-start.9 = (bf16[3,256,256]{2,1,0:T(8,128)(2,1)S(1)}, bf16[3,256,256]{2,1,0:T(8,128)(2,1)S(1)}, u32[]{:S(2)}, u32[]{:S(2)}) collective-permute-start(bf16[3,256,256]{2,1,0:T(8,128)(2,1)S(1)} %get-tuple-element.35.refs_5_.refs_8_), channel_id=1, source_target_pairs={{0,2},{2,0},{4,6},{6,4},{8,10},{10,8},{12,14},{14,12},{16,18},{18,... | collective-permute-start | bytes 1179656 | tf_op jit(solution)/shard_map/ppermute | solution.py:135
  36.5 19.5 %collective-permute-start.2 = (bf16[3,256,256]{2,1,0:T(8,128)(2,1)S(1)}, bf16[3,256,256]{2,1,0:T(8,128)(2,1)S(1)}, u32[]{:S(2)}, u32[]{:S(2)}) collective-permute-start(bf16[3,256,256]{2,1,0:T(8,128)(2,1)S(1)} %get-tuple-element.29.refs_4_.refs_7_), channel_id=1, source_target_pairs={{0,30},{2,4},{4,2},{6,8},{8,6},{10,12},{12,10},{14,16},{16,14},{18... | collective-permute-start | bytes 1179656 | tf_op jit(solution)/shard_map/ppermute | solution.py:135
  38.5 17.5 %collective-permute-start.3 = (bf16[3,256,256]{2,1,0:T(8,128)(2,1)S(1)}, bf16[3,256,256]{2,1,0:T(8,128)(2,1)S(1)}, u32[]{:S(2)}, u32[]{:S(2)}) collective-permute-start(bf16[3,256,256]{2,1,0:T(8,128)(2,1)S(1)} %get-tuple-element.30.refs_5_.refs_8_), channel_id=1, source_target_pairs={{0,2},{2,0},{4,6},{6,4},{8,10},{10,8},{12,14},{14,12},{16,18},{18,... | collective-permute-start | bytes 1179656 | tf_op jit(solution)/shard_map/ppermute | solution.py:135
  41.9 33.7 %collective-permute-start.17 = (bf16[512,512]{1,0:T(8,128)(2,1)S(1)}, bf16[512,512]{1,0:T(8,128)(2,1)S(1)}, u32[]{:S(2)}, u32[]{:S(2)}) collective-permute-start(bf16[512,512]{1,0:T(8,128)(2,1)S(1)} %pad_maximum_fusion), channel_id=1, source_target_pairs={{0,2},{2,0},{4,6},{6,4},{8,10},{10,8},{12,14},{14,12},{16,18},{18,... | collective-permute-start | bytes 1572872 | tf_op jit(solution)/shard_map/ppermute | solution.py:135
  49.4 17.4 %collective-permute-start.10 = (bf16[3,256,256]{2,1,0:T(8,128)(2,1)S(1)}, bf16[3,256,256]{2,1,0:T(8,128)(2,1)S(1)}, u32[]{:S(2)}, u32[]{:S(2)}) collective-permute-start(bf16[3,256,256]{2,1,0:T(8,128)(2,1)S(1)} %get-tuple-element.36.refs_4_), channel_id=1, source_target_pairs={{0,30},{2,4},{4,2},{6,8},{8,6},{10,12},{12,10},{14,16},{16,14},{18... | collective-permute-start | bytes 1179656 | tf_op jit(solution)/shard_map/ppermute | solution.py:135
  53.7 13.2 %collective-permute-start.11 = (bf16[3,256,256]{2,1,0:T(8,128)(2,1)S(1)}, bf16[3,256,256]{2,1,0:T(8,128)(2,1)S(1)}, u32[]{:S(2)}, u32[]{:S(2)}) collective-permute-start(bf16[3,256,256]{2,1,0:T(8,128)(2,1)S(1)} %get-tuple-element.37.refs_5_), channel_id=1, source_target_pairs={{0,2},{2,0},{4,6},{6,4},{8,10},{10,8},{12,14},{14,12},{16,18},{18,... | collective-permute-start | bytes 1179656 | tf_op jit(solution)/shard_map/ppermute | solution.py:135
  57.8 13.2 %collective-permute-start.4 = (bf16[3,256,256]{2,1,0:T(8,128)(2,1)S(1)}, bf16[3,256,256]{2,1,0:T(8,128)(2,1)S(1)}, u32[]{:S(2)}, u32[]{:S(2)}) collective-permute-start(bf16[3,256,256]{2,1,0:T(8,128)(2,1)S(1)} %get-tuple-element.31.refs_4_), channel_id=1, source_target_pairs={{0,30},{2,4},{4,2},{6,8},{8,6},{10,12},{12,10},{14,16},{16,14},{18... | collective-permute-start | bytes 1179656 | tf_op jit(solution)/shard_map/ppermute | solution.py:135
  57.9 13.1 %collective-permute-start.5 = (bf16[3,256,256]{2,1,0:T(8,128)(2,1)S(1)}, bf16[3,256,256]{2,1,0:T(8,128)(2,1)S(1)}, u32[]{:S(2)}, u32[]{:S(2)}) collective-permute-start(bf16[3,256,256]{2,1,0:T(8,128)(2,1)S(1)} %get-tuple-element.32.refs_5_), channel_id=1, source_target_pairs={{0,2},{2,0},{4,6},{6,4},{8,10},{10,8},{12,14},{14,12},{16,18},{18,... | collective-permute-start | bytes 1179656 | tf_op jit(solution)/shard_map/ppermute | solution.py:135
  68.6 11.2 %collective-permute-start.20 = (bf16[3,256,256]{2,1,0:T(8,128)(2,1)S(1)}, bf16[3,256,256]{2,1,0:T(8,128)(2,1)S(1)}, u32[]{:S(2)}, u32[]{:S(2)}) collective-permute-start(bf16[3,256,256]{2,1,0:T(8,128)(2,1)S(1)} %get-tuple-element.41.refs_1_), channel_id=1, source_target_pairs={{0,1},{1,0},{2,3},{3,2},{4,5},{5,4},{6,7},{7,6},{8,9},{9,8},{10,11... | collective-permute-start | bytes 1179656 | tf_op jit(solution)/shard_map/ppermute | solution.py:135
  72.9 15.4 %collective-permute-start.19 = (bf16[3,256,256]{2,1,0:T(8,128)(2,1)S(1)}, bf16[3,256,256]{2,1,0:T(8,128)(2,1)S(1)}, u32[]{:S(2)}, u32[]{:S(2)}) collective-permute-start(bf16[3,256,256]{2,1,0:T(8,128)(2,1)S(1)} %get-tuple-element.40.refs_0_), channel_id=1, source_target_pairs={{0,1},{1,0},{2,3},{3,2},{4,5},{5,4},{6,7},{7,6},{8,9},{9,8},{10,11... | collective-permute-start | bytes 1179656 | tf_op jit(solution)/shard_map/ppermute | solution.py:135
  74.2 22.0 %collective-permute-start.13 = (bf16[3,256,256]{2,1,0:T(8,128)(2,1)S(1)}, bf16[3,256,256]{2,1,0:T(8,128)(2,1)S(1)}, u32[]{:S(2)}, u32[]{:S(2)}) collective-permute-start(bf16[3,256,256]{2,1,0:T(8,128)(2,1)S(1)} %get-tuple-element.38.refs_1_), channel_id=1, source_target_pairs={{0,1},{1,0},{2,3},{3,2},{4,5},{5,4},{6,7},{7,6},{8,9},{9,8},{10,11... | collective-permute-start | bytes 1179656 | tf_op jit(solution)/shard_map/ppermute | solution.py:135
  74.4 26.0 %collective-permute-start.12 = (bf16[3,256,256]{2,1,0:T(8,128)(2,1)S(1)}, bf16[3,256,256]{2,1,0:T(8,128)(2,1)S(1)}, u32[]{:S(2)}, u32[]{:S(2)}) collective-permute-start(bf16[3,256,256]{2,1,0:T(8,128)(2,1)S(1)} %get-tuple-element.33.refs_0_), channel_id=1, source_target_pairs={{0,1},{1,0},{2,3},{3,2},{4,5},{5,4},{6,7},{7,6},{8,9},{9,8},{10,11... | collective-permute-start | bytes 1179656 | tf_op jit(solution)/shard_map/ppermute | solution.py:135
  89.2 13.9 %collective-permute-start.27 = (bf16[3,256,256]{2,1,0:T(8,128)(2,1)S(1)}, bf16[3,256,256]{2,1,0:T(8,128)(2,1)S(1)}, u32[]{:S(2)}, u32[]{:S(2)}) collective-permute-start(bf16[3,256,256]{2,1,0:T(8,128)(2,1)S(1)} %get-tuple-element.48.refs_5_.refs_8_), channel_id=1, source_target_pairs={{0,2},{2,0},{4,6},{6,4},{8,10},{10,8},{12,14},{14,12},{16,18},{18,... | collective-permute-start | bytes 1179656 | tf_op jit(solution)/shard_map/ppermute | solution.py:135
  101.3 18.1 %collective-permute-start.26 = (bf16[3,256,256]{2,1,0:T(8,128)(2,1)S(1)}, bf16[3,256,256]{2,1,0:T(8,128)(2,1)S(1)}, u32[]{:S(2)}, u32[]{:S(2)}) collective-permute-start(bf16[3,256,256]{2,1,0:T(8,128)(2,1)S(1)} %get-tuple-element.47.refs_4_.refs_7_), channel_id=1, source_target_pairs={{0,30},{2,4},{4,2},{6,8},{8,6},{10,12},{12,10},{14,16},{16,14},{18... | collective-permute-start | bytes 1179656 | tf_op jit(solution)/shard_map/ppermute | solution.py:135
  101.6 19.8 %collective-permute-start.21 = (bf16[3,256,256]{2,1,0:T(8,128)(2,1)S(1)}, bf16[3,256,256]{2,1,0:T(8,128)(2,1)S(1)}, u32[]{:S(2)}, u32[]{:S(2)}) collective-permute-start(bf16[3,256,256]{2,1,0:T(8,128)(2,1)S(1)} %get-tuple-element.42.refs_5_.refs_8_), channel_id=1, source_target_pairs={{0,2},{2,0},{4,6},{6,4},{8,10},{10,8},{12,14},{14,12},{16,18},{18,... | collective-permute-start | bytes 1179656 | tf_op jit(solution)/shard_map/ppermute | solution.py:135
  101.6 22.1 %collective-permute-start.18 = (bf16[3,256,256]{2,1,0:T(8,128)(2,1)S(1)}, bf16[3,256,256]{2,1,0:T(8,128)(2,1)S(1)}, u32[]{:S(2)}, u32[]{:S(2)}) collective-permute-start(bf16[3,256,256]{2,1,0:T(8,128)(2,1)S(1)} %get-tuple-element.39.refs_4_.refs_7_), channel_id=1, source_target_pairs={{0,30},{2,4},{4,2},{6,8},{8,6},{10,12},{12,10},{14,16},{16,14},{18... | collective-permute-start | bytes 1179656 | tf_op jit(solution)/shard_map/ppermute | solution.py:135
  121.3 7.3 %collective-permute-start.28 = (bf16[3,256,256]{2,1,0:T(8,128)(2,1)S(1)}, bf16[3,256,256]{2,1,0:T(8,128)(2,1)S(1)}, u32[]{:S(2)}, u32[]{:S(2)}) collective-permute-start(bf16[3,256,256]{2,1,0:T(8,128)(2,1)S(1)} %get-tuple-element.49.refs_4_.refs_7_), channel_id=1, source_target_pairs={{0,30},{2,4},{4,2},{6,8},{8,6},{10,12},{12,10},{14,16},{16,14},{18... | collective-permute-start | bytes 1179656 | tf_op jit(solution)/shard_map/ppermute | solution.py:135
  121.4 7.2 %collective-permute-start.29 = (bf16[3,256,256]{2,1,0:T(8,128)(2,1)S(1)}, bf16[3,256,256]{2,1,0:T(8,128)(2,1)S(1)}, u32[]{:S(2)}, u32[]{:S(2)}) collective-permute-start(bf16[3,256,256]{2,1,0:T(8,128)(2,1)S(1)} %get-tuple-element.50.refs_5_.refs_8_), channel_id=1, source_target_pairs={{0,2},{2,0},{4,6},{6,4},{8,10},{10,8},{12,14},{14,12},{16,18},{18,... | collective-permute-start | bytes 1179656 | tf_op jit(solution)/shard_map/ppermute | solution.py:135
  125.7 19.9 %collective-permute-start.22 = (bf16[3,256,256]{2,1,0:T(8,128)(2,1)S(1)}, bf16[3,256,256]{2,1,0:T(8,128)(2,1)S(1)}, u32[]{:S(2)}, u32[]{:S(2)}) collective-permute-start(bf16[3,256,256]{2,1,0:T(8,128)(2,1)S(1)} %get-tuple-element.43.refs_4_.refs_7_), channel_id=1, source_target_pairs={{0,30},{2,4},{4,2},{6,8},{8,6},{10,12},{12,10},{14,16},{16,14},{18... | collective-permute-start | bytes 1179656 | tf_op jit(solution)/shard_map/ppermute | solution.py:135
  125.8 19.8 %collective-permute-start.23 = (bf16[3,256,256]{2,1,0:T(8,128)(2,1)S(1)}, bf16[3,256,256]{2,1,0:T(8,128)(2,1)S(1)}, u32[]{:S(2)}, u32[]{:S(2)}) collective-permute-start(bf16[3,256,256]{2,1,0:T(8,128)(2,1)S(1)} %get-tuple-element.44.refs_5_.refs_8_), channel_id=1, source_target_pairs={{0,2},{2,0},{4,6},{6,4},{8,10},{10,8},{12,14},{14,12},{16,18},{18,... | collective-permute-start | bytes 1179656 | tf_op jit(solution)/shard_map/ppermute | solution.py:135
  130.4 19.4 %collective-permute-start.30 = (bf16[3,256,256]{2,1,0:T(8,128)(2,1)S(1)}, bf16[3,256,256]{2,1,0:T(8,128)(2,1)S(1)}, u32[]{:S(2)}, u32[]{:S(2)}) collective-permute-start(bf16[3,256,256]{2,1,0:T(8,128)(2,1)S(1)} %get-tuple-element.51.refs_4_), channel_id=1, source_target_pairs={{0,30},{2,4},{4,2},{6,8},{8,6},{10,12},{12,10},{14,16},{16,14},{18... | collective-permute-start | bytes 1179656 | tf_op jit(solution)/shard_map/ppermute | solution.py:135
  130.5 19.4 %collective-permute-start.31 = (bf16[3,256,256]{2,1,0:T(8,128)(2,1)S(1)}, bf16[3,256,256]{2,1,0:T(8,128)(2,1)S(1)}, u32[]{:S(2)}, u32[]{:S(2)}) collective-permute-start(bf16[3,256,256]{2,1,0:T(8,128)(2,1)S(1)} %get-tuple-element.52.refs_5_), channel_id=1, source_target_pairs={{0,2},{2,0},{4,6},{6,4},{8,10},{10,8},{12,14},{14,12},{16,18},{18,... | collective-permute-start | bytes 1179656 | tf_op jit(solution)/shard_map/ppermute | solution.py:135
  147.4 7.3 %collective-permute-start.24 = (bf16[3,256,256]{2,1,0:T(8,128)(2,1)S(1)}, bf16[3,256,256]{2,1,0:T(8,128)(2,1)S(1)}, u32[]{:S(2)}, u32[]{:S(2)}) collective-permute-start(bf16[3,256,256]{2,1,0:T(8,128)(2,1)S(1)} %get-tuple-element.45.refs_4_), channel_id=1, source_target_pairs={{0,30},{2,4},{4,2},{6,8},{8,6},{10,12},{12,10},{14,16},{16,14},{18... | collective-permute-start | bytes 1179656 | tf_op jit(solution)/shard_map/ppermute | solution.py:135
  147.5 7.2 %collective-permute-start.25 = (bf16[3,256,256]{2,1,0:T(8,128)(2,1)S(1)}, bf16[3,256,256]{2,1,0:T(8,128)(2,1)S(1)}, u32[]{:S(2)}, u32[]{:S(2)}) collective-permute-start(bf16[3,256,256]{2,1,0:T(8,128)(2,1)S(1)} %get-tuple-element.46.refs_5_), channel_id=1, source_target_pairs={{0,2},{2,0},{4,6},{6,4},{8,10},{10,8},{12,14},{14,12},{16,18},{18,... | collective-permute-start | bytes 1179656 | tf_op jit(solution)/shard_map/ppermute | solution.py:135
  (5 other events, 98.2 us)

commit v3 on v0

v3 whole, which is shorter than its diff:
```python
import functools

import jax
import jax.numpy as jnp
from jax import lax
from jax.experimental import pallas as pl
from jax.experimental.pallas import tpu as pltpu
from jax.sharding import PartitionSpec as P

GY = 3
CHUNK = 256
MIB = 1024 * 1024
LONG = 4 * 10**9
PARAMS = pltpu.CompilerParams(vmem_limit_bytes=16 * MIB)
SMEM = pl.BlockSpec(memory_space=pltpu.SMEM)
VMEM = pl.BlockSpec(memory_space=pltpu.VMEM)
ANYWHERE = pl.BlockSpec(memory_space=pl.ANY)
HBM = pl.BlockSpec(memory_space=pltpu.HBM)


def cost(flops):
    return pl.CostEstimate(flops=flops, bytes_accessed=1024, transcendentals=0)


def like(array):
    return jax.ShapeDtypeStruct(array.shape, array.dtype)


def bands_of(count, basis, width):
    return jax.ShapeDtypeStruct((count, basis, width), jnp.bfloat16)


def first_row(side, odd):
    return odd * GY if side == 0 else (1 - odd) * GY


def run_copies(pairs, sems):
    copies = [pltpu.make_async_copy(source, target, sems.at[n]) for n, (source, target) in enumerate(pairs)]
    for copy in copies:
        copy.start()
    return copies


def split_kernel(starts, width, held, waits, odd_ref, start_ref, *refs):
    refs = list(refs)
    pairs = []
    if held:
        blocks_ref, refs = refs[0], refs[1:]
    refs = refs[waits:]
    sems = refs.pop()
    if held:
        pairs.append((blocks_ref, refs.pop(0)))
    for n, target in enumerate(refs):
        rows = pl.ds(first_row(n % 2, odd_ref[0]), GY)
        pairs.append((start_ref.at[rows, :, pl.ds(starts[n // 2], width)], target))
    for copy in run_copies(pairs, sems):
        copy.wait()


def split(odd, start_bands, starts, width, blocks=None, later=()):
    basis = start_bands.shape[1]
    held = [] if blocks is None else [blocks]
    shapes = [pltpu.VMEM(b.shape, b.dtype) for b in held] + [bands_of(GY, basis, width)] * (2 * len(starts))
    result = pl.pallas_call(
        functools.partial(split_kernel, starts, width, len(held), len(later)),
        out_shape=shapes,
        in_specs=[SMEM, HBM] + [HBM] * len(held) + [ANYWHERE] * len(later),
        out_specs=[VMEM] * len(shapes),
        scratch_shapes=[pltpu.SemaphoreType.DMA((len(shapes),))],
        compiler_params=PARAMS,
        cost_estimate=cost(LONG),
    )(odd, start_bands, *held, *later)
    parts = result[len(held) :]
    return result[: len(held)], [[parts[2 * n], parts[2 * n + 1]] for n in range(len(starts))]


def step_kernel(sides, firsts, out_column, has_out, waits, joined, odd_ref, links_ref, blocks_ref, *refs):
    refs = list(refs)

    def take(count):
        taken = refs[:count]
        del refs[:count]
        return taken

    current = take(2)
    halos = take(len(sides))
    before = [None if first else take(1)[0] for first in firsts]
    join = take(2 * joined)
    take(waits + has_out)
    results = take(1 if out_column is not None else len(sides))
    join_out = take(joined)
    if out_column is not None:
        made, left = take(2)
    copies = []
    if joined:
        rows = join[0].shape[0]
        copies = run_copies([(join[0], join_out[0].at[:rows]), (join[1], join_out[0].at[rows:])], refs[0])
    odd = odd_ref[0]
    for i, side in enumerate(sides):
        far_side = 1 + odd if side == 0 else 2 - odd
        near_side = 3 - far_side
        for k in range(GY):
            row = first_row(side, odd) + k

            def term(s, column):
                slot = lax.rem(links_ref[row, s], GY)
                return jnp.dot(blocks_ref[row, s], column[slot], preferred_element_type=jnp.float32)

            total = term(0, current[side])
            total += term(3, current[side])
            total += term(4, current[side])
            total += term(near_side, current[1 - side])
            total += term(far_side, halos[i])
            if before[i] is not None:
                total = 2.0 * total - before[i][k].astype(jnp.float32)
            if out_column is None:
                results[i][k] = total.astype(jnp.bfloat16)
            else:
                n = i * GY + k
                made[n] = total.astype(jnp.bfloat16)
                place = results[0].at[row, :, pl.ds(out_column, made.shape[2])]
                copy = pltpu.make_async_copy(made.at[n], place, left.at[n])
                copy.start()
                copies.append(copy)
    for copy in copies:
        copy.wait()


def apply_step(shared, sides, current, halos, before, out=None, out_column=None, out_shape=None, later=(), join=()):
    basis, width = current[0].shape[1:]
    operands = list(shared) + list(current) + list(halos) + [b for b in before if b is not None] + list(join)
    specs = [SMEM, SMEM] + [VMEM] * (len(operands) - 2) + [ANYWHERE] * len(later)
    operands += list(later)
    aliases, scratch = {}, []
    if out_column is None:
        shapes = [bands_of(GY, basis, width)] * len(sides)
        out_specs = [VMEM] * len(sides)
    else:
        if out is not None:
            aliases = {len(operands): 0}
            operands.append(out)
            specs.append(ANYWHERE)
        shapes, out_specs = [jax.ShapeDtypeStruct(out_shape, jnp.bfloat16)], [ANYWHERE]
        parts = len(sides) * GY
        scratch = [pltpu.VMEM((parts, basis, width), jnp.bfloat16), pltpu.SemaphoreType.DMA((parts,))]
    if join:
        rows = join[0].shape[0] + join[1].shape[0]
        shapes.append(jax.ShapeDtypeStruct((rows,) + join[0].shape[1:], join[0].dtype))
        out_specs.append(VMEM)
        scratch.append(pltpu.SemaphoreType.DMA((2,)))
    firsts = [b is None for b in before]
    return pl.pallas_call(
        functools.partial(step_kernel, sides, firsts, out_column, out is not None, len(later), int(bool(join))),
        out_shape=shapes,
        in_specs=specs,
        out_specs=out_specs,
        scratch_shapes=scratch,
        input_output_aliases=aliases,
        compiler_params=PARAMS,
        cost_estimate=cost(LONG),
    )(*operands)


def rotate_kernel(count, column, extra, passed, *refs):
    pieces, matrix = refs[:count], refs[count]
    outs = refs[count + 1 + extra : len(refs) - passed]
    for k in range(GY):
        rows = jnp.concatenate([piece[k] for piece in pieces], axis=1)
        start = column
        for out in outs:
            width = out.shape[2]
            out[k] = jnp.dot(
                rows, matrix[:, start : start + width], preferred_element_type=jnp.float32
            ).astype(jnp.bfloat16)
            start += width


def rotate(pieces, matrix, column, widths, passed=(), later=()):
    basis = pieces[0].shape[1]
    count = len(pieces) + 1
    result = pl.pallas_call(
        functools.partial(rotate_kernel, len(pieces), column, len(passed) + len(later), len(passed)),
        out_shape=[bands_of(GY, basis, width) for width in widths] + [like(p) for p in passed],
        in_specs=[VMEM] * count + [ANYWHERE] * (len(passed) + len(later)),
        out_specs=[VMEM] * len(widths) + [ANYWHERE] * len(passed),
        input_output_aliases={count + i: len(widths) + i for i in range(len(passed))},
        compiler_params=PARAMS,
        cost_estimate=cost(LONG // 2),
    )(*pieces, matrix, *passed, *later)
    return list(result[: len(widths)]), list(result[len(widths) :])


def ordered_kernel(bands, own_ref, order_ref, *refs):
    rows, out_ref = refs[:-1], refs[-1]
    total = out_ref.shape[0]
    width = total // bands
    for shift in range(bands):
        for start in range(0, width, 256):
            size = min(256, width - start)
            first = jnp.bitwise_xor(own_ref[0], shift) * width + start
            band = lax.broadcasted_iota(jnp.int32, (size, total), 0) + first
            choice = (band == order_ref[...]).astype(jnp.float32).astype(jnp.bfloat16)
            result, column = None, 0
            for part in rows:
                held = choice[:, column : column + part.shape[0]]
                found = jnp.dot(held, part[...], preferred_element_type=jnp.float32)
                result = found if result is None else result + found
                column += part.shape[0]
            place = shift * width + start
            out_ref[place : place + size, :] = result.astype(jnp.bfloat16)


def ordered_rows(own, order, rows, bands):
    total = order.shape[1]
    return pl.pallas_call(
        functools.partial(ordered_kernel, bands),
        out_shape=jax.ShapeDtypeStruct((total, rows[0].shape[1]), rows[0].dtype),
        in_specs=[SMEM] + [VMEM] * (1 + len(rows)),
        out_specs=VMEM,
        compiler_params=PARAMS,
        cost_estimate=cost(LONG // 2),
    )(own, order, *rows)


def exchange(array, axis, partner):
    return lax.ppermute(array, axis, [(i, partner(i)) for i in range(lax.axis_size(axis))])


class Gather:
    def __init__(self, rows):
        elems = lax.axis_size("elem")
        bits = [1 << b for b in range(elems.bit_length() - 1)]
        self.bits = bits[1:2] + bits[:1:-1] + bits[:1]
        self.owners = [0]
        self.held = rows
        self.received = self.send()

    def send(self):
        bit = self.bits.pop(0)
        self.owners = self.owners + [owner ^ bit for owner in self.owners]
        return exchange(self.held, "elem", lambda i: i ^ bit)

    def parts(self):
        return [self.held, self.received]

    def step(self, *args, **kwargs):
        if not self.bits:
            return apply_step(*args, **kwargs)
        result = apply_step(*args, join=self.parts(), **kwargs)
        self.held = result[-1]
        self.received = self.send()
        return result[:-1]

    def finish(self):
        while self.bits:
            self.held = jnp.concatenate(self.parts(), axis=0)
            self.received = self.send()
        return self.parts(), jnp.array(self.owners)


def body(start_bands, blocks, neighbours, band_order, rotation):
    elem_count, basis, width = start_bands.shape
    assert elem_count == 2 * GY
    elems, bands = lax.axis_size("elem"), lax.axis_size("band")
    me = lax.axis_index("elem")
    odd = (me % 2).astype(jnp.int32).reshape(1)
    chunk = min(CHUNK, width)
    starts = list(range(0, width, chunk))
    chunks = range(len(starts))
    nothing = [None, None]

    def cross(array):
        return exchange(array, "elem", lambda i: (i - 1) % elems if i % 2 == 0 else (i + 1) % elems)

    def intra(array):
        return exchange(array, "elem", lambda i: i ^ 1)

    def halos(columns):
        return [cross(columns[0]), intra(columns[1])]

    def over_band(piece):
        return [exchange(piece, "band", lambda i: i ^ shift) for shift in range(1, bands)]

    _, state = split(odd, start_bands, starts[:1], chunk)
    beside = [halos(state[0])]
    (held,), rest = split(odd, start_bands, starts[1:], chunk, blocks, later=beside[0][1:])
    state += rest
    beside += [halos(columns) for columns in rest]
    shared = (odd, neighbours, held)
    gather = Gather(rotation)

    before = [nothing for _ in chunks]
    for _ in range(2):
        for c in chunks:
            step = gather.step if c == 0 else apply_step
            new = step(shared, (0, 1), state[c], beside[c], before[c], later=state[c - 1][:1] if c or before[0][0] is not None else ())
            before[c], state[c] = state[c], new
            beside[c] = halos(new)

    inner, inner_others, outer, outer_others = [], [], [], []
    waits = []
    for c in chunks:
        step = gather.step if c == 0 else apply_step
        inner += apply_step(shared, (1,), state[c], beside[c][1:], before[c][1:], later=outer[-1:])
        outer += step(shared, (0,), state[c], beside[c][:1], before[c][:1], later=waits + inner[-1:])
        outer_others.append(over_band(outer[-1]))
        if c != chunks[-1]:
            inner_others.append(over_band(inner[-1]))
            waits = inner_others[-1]
    rows, owners = gather.finish()
    order = band_order.reshape(elems, -1)[jnp.bitwise_xor(me, owners)].reshape(1, -1)
    matrix = ordered_rows(lax.axis_index("band").astype(jnp.int32).reshape(1), order, rows, bands)

    def by_band(own, others):
        return list(own) + [other[shift] for shift in range(bands - 1) for other in others]

    pieces = by_band(outer, outer_others)
    rotated, last = rotate(pieces, matrix, 0, [chunk], passed=inner[-1:])
    far = [cross(rotated[0])]
    inner[-1] = last[0]
    inner_others.append(over_band(inner[-1]))
    for c in chunks[1:]:
        rotated += rotate(pieces, matrix, starts[c], [chunk], later=inner_others[-1])[0]
        far.append(cross(rotated[c]))
    rotated_inner, _ = rotate(by_band(inner, inner_others), matrix, 0, [chunk for _ in chunks])
    state = [[rotated[c], rotated_inner[c]] for c in chunks]
    beside = [[far[c], intra(rotated_inner[c])] for c in chunks]

    before = [nothing for _ in chunks]
    for _ in range(2):
        for c in chunks:
            new = apply_step(shared, (0, 1), state[c], beside[c], before[c])
            before[c], state[c] = state[c], new
            beside[c] = halos(new)
    out = None
    for c in chunks:
        (out,) = apply_step(
            shared, (0, 1), state[c], beside[c], before[c],
            out=out, out_column=starts[c], out_shape=start_bands.shape,
        )
    return out


def solution(mesh):
    return jax.shard_map(
        body,
        mesh=mesh,
        in_specs=(
            P("elem", None, "band"),
            P("elem", None, None, None),
            P("elem", None),
            P(),
            P("elem", "band"),
        ),
        out_specs=P("elem", None, "band"),
        check_vma=False,
    )
```

time: 298 us -> 144 us (0.48)
  local copies, waits for them, and re-layouts: 87.4 us -> 2.16 us
  waiting for transfers between devices: 110 us -> 53.5 us
  matrix products: 45 us -> 0 us
  starting transfers between devices: 16.5 us -> 57.7 us
  Pallas kernels: 0 us -> 29.3 us
  blocking collectives: 16.7 us -> 0 us
  between operations: 13.6 us -> 0.41 us
  other arithmetic: 7.28 us -> 0.01 us
    gather x10 -> x1, local copies, waits for them, and re-layouts: 72 us -> 0.56 us  [body(): band_order.reshape(elems, -1)[jnp.bitwise_xor(me, owners)].reshape(1, -1)]
    ppermute x12 -> x32, waiting for transfers between devices: 104 us -> 53.5 us  [exchange(): lax.ppermute(array, axis, [(i, partner(i)) for i in range(lax.axis_size(a...]
    ppermute x12 -> x32, starting transfers between devices: 11.7 us -> 57.7 us  [exchange(): lax.ppermute(array, axis, [(i, partner(i)) for i in range(lax.axis_size(a...]
    dot_general x7 -> x0, matrix products: 45 us -> none  [the longest x6 41.8 us: apply_blocks(): jnp.einsum('esij,esjm->eim', blocks, picked, preferred_element_type=jnp.f...]
    pallas_call x0 -> x20, Pallas kernels: none -> 29.3 us  [the longest x14 25.6 us: apply_step(): pl.pallas_call(functools.partial(step_kernel, sides, firsts, out_column,...]
    all_to_all x1 -> x0, blocking collectives: 16.7 us -> none  [body(): lax.all_to_all(mixed_rows, 'band', split_axis=1, concat_axis=0, tiled=True)]
    concatenate x6 -> x0, other arithmetic: 7.25 us -> none  [extended_2(): jnp.concatenate([lax.ppermute(tail, axis, [(i, (i + 1) % count) for i in...]
    scatter x1 -> x0, local copies, waits for them, and re-layouts: 6.58 us -> none  [body(): jnp.zeros_like(rotation_full).at[band_order].set(rotation_full)]
  transfers between devices with their start and end apart: 15 -> 32, of which waited for: 8 -> 11; matrix products, arithmetic and copies ran while one was open for 16% -> 1% of each run, Pallas kernels for 0% -> 18%
where the time goes in v3:
time: 144 us; the launch traced here: 143 us
  starting transfers between devices  57.7 us (40%)
  waiting for transfers between devices  53.5 us (37%)
  Pallas kernels  29.3 us (20%)
  local copies, waits for them, and re-layouts  2.16 us (2%)
    ppermute x32, starting transfers between devices, exchange(): lax.ppermute(array, axis, [(i, partner(i)) for i in range(lax.axis_size(a...  57.7 us
    ppermute x32, waiting for transfers between devices, exchange(): lax.ppermute(array, axis, [(i, partner(i)) for i in range(lax.axis_size(a...  53.5 us
    pallas_call x14, Pallas kernels, apply_step(): pl.pallas_call(functools.partial(step_kernel, sides, firsts, out_column,...  25.6 us
  transfers between devices with their start and end apart: 32, of which 11 were waited for; matrix products, arithmetic and copies ran while one was open for 1% of the time, Pallas kernels for 18%

profile of v3, /device:TPU:1, one launch (start us, length us, event | category | flops | bytes accessed | tf_op | source)
XLA Modules:
  0.0 143.2 jit_solution(3485677528562472369)
XLA Ops:
  1.6 2.6 %collective-permute-start.1 = (bf16[3,256,256]{2,1,0:T(8,128)(2,1)S(1)}, bf16[3,256,256]{2,1,0:T(8,128)(2,1)S(1)}, u32[]{:S(2)}, u32[]{:S(2)}) collective-permute-start(bf16[3,256,256]{2,1,0:T(8,128)(2,1)S(1)} %get-tuple-element.36.refs_0_.refs_4_), channel_id=1, source_target_pairs={{0,30},{2,4},{4,2},{6,8},{8,6},{10,12},{12,10},{14,16},{16,14},{18... | collective-permute-start | bytes 1179656 | tf_op jit(solution)/shard_map/ppermute | solution.py:226
  5.9 3.9 %collective-permute-start.6 = (bf16[3,256,256]{2,1,0:T(8,128)(2,1)S(1)}, bf16[3,256,256]{2,1,0:T(8,128)(2,1)S(1)}, u32[]{:S(2)}, u32[]{:S(2)}) collective-permute-start(bf16[3,256,256]{2,1,0:T(8,128)(2,1)S(1)} %get-tuple-element.40.refs_0_.refs_4_), channel_id=1, source_target_pairs={{0,30},{2,4},{4,2},{6,8},{8,6},{10,12},{12,10},{14,16},{16,14},{18... | collective-permute-start | bytes 1179656 | tf_op jit(solution)/shard_map/ppermute | solution.py:226
  9.8 9.0 %collective-permute-done.2.refs_5_ = bf16[64,512]{1,0:T(8,128)(2,1)S(1)} collective-permute-done((bf16[64,512]{1,0:T(8,128)(2,1)S(1)}, bf16[64,512]{1,0:T(8,128)(2,1)S(1)}, u32[]{:S(2)}, u32[]{:S(2)}) %collective-permute-start.2) | collective-permute-done | bytes 65568 | tf_op jit(solution)/shard_map/ppermute | solution.py:226
  18.8 2.0 %shard_map.66 = (bf16[3,256,256]{2,1,0:T(8,128)(2,1)S(1)}, bf16[3,256,256]{2,1,0:T(8,128)(2,1)S(1)}, bf16[128,512]{1,0:T(8,128)(2,1)S(1)}) custom-call(s32[1]{0:T(128)} %bitcast.odd_ref, s32[6,5]{1,0:T(8,128)S(1)} %copy-done.5, bf16[6,5,256,256]{3,2,1,0:T(8,128)(2,1)S(1)} %get-tuple-element.35.blocks_ref, ...), custom_call_target="tpu_custom_call" | custom-call | flops 4000000000 | bytes 1024 | tf_op jit(solution)/shard_map/pallas_call | solution.py:152
  23.2 2.3 %collective-permute-start.5 = (bf16[128,512]{1,0:T(8,128)(2,1)S(1)}, bf16[128,512]{1,0:T(8,128)(2,1)S(1)}, u32[]{:S(2)}, u32[]{:S(2)}) collective-permute-start(bf16[128,512]{1,0:T(8,128)(2,1)S(1)} %get-tuple-element.39.refs_6_), channel_id=1, source_target_pairs={{0,16},{2,18},{4,20},{6,22},{8,24},{10,26},{12,28},{14,30},{16,0},... | collective-permute-start | bytes 393224 | tf_op jit(solution)/shard_map/ppermute | solution.py:226
  25.5 1.8 %shard_map.67 = (bf16[3,256,256]{2,1,0:T(8,128)(2,1)S(1)}, bf16[3,256,256]{2,1,0:T(8,128)(2,1)S(1)}) custom-call(s32[1]{0:T(128)} %bitcast.odd_ref, s32[6,5]{1,0:T(8,128)S(1)} %copy-done.5, bf16[6,5,256,256]{3,2,1,0:T(8,128)(2,1)S(1)} %get-tuple-element.35.blocks_ref, bf16[3,256,256]{2,1,0:T(8,128)(2,1)S(1)} %get-tuple-element.40.refs_0_.refs_4_, ...), custom_call_target="tpu_custom_call" | custom-call | flops 4000000000 | bytes 1024 | tf_op jit(solution)/shard_map/pallas_call | solution.py:152
  28.2 1.7 %collective-permute-start.11 = (bf16[3,256,256]{2,1,0:T(8,128)(2,1)S(1)}, bf16[3,256,256]{2,1,0:T(8,128)(2,1)S(1)}, u32[]{:S(2)}, u32[]{:S(2)}) collective-permute-start(bf16[3,256,256]{2,1,0:T(8,128)(2,1)S(1)} %get-tuple-element.42.refs_8_.refs_0_.refs_3_), channel_id=1, source_target_pairs={{0,30},{2,4},{4,2},{6,8},{8,6},{10,12},{12,10},{14,16},{16,14},{18... | collective-permute-start | bytes 1179656 | tf_op jit(solution)/shard_map/ppermute | solution.py:226
  30.9 3.9 %collective-permute-done.3.refs_2_ = bf16[3,256,256]{2,1,0:T(8,128)(2,1)S(1)} collective-permute-done((bf16[3,256,256]{2,1,0:T(8,128)(2,1)S(1)}, bf16[3,256,256]{2,1,0:T(8,128)(2,1)S(1)}, u32[]{:S(2)}, u32[]{:S(2)}) %collective-permute-start.3) | collective-permute-done | bytes 393248 | tf_op jit(solution)/shard_map/ppermute | solution.py:226
  34.9 2.2 %shard_map.68 = (bf16[3,256,256]{2,1,0:T(8,128)(2,1)S(1)}, bf16[3,256,256]{2,1,0:T(8,128)(2,1)S(1)}, bf16[256,512]{1,0:T(8,128)(2,1)S(1)}) custom-call(s32[1]{0:T(128)} %bitcast.odd_ref, s32[6,5]{1,0:T(8,128)S(1)} %copy-done.5, bf16[6,5,256,256]{3,2,1,0:T(8,128)(2,1)S(1)} %get-tuple-element.35.blocks_ref, ...), custom_call_target="tpu_custom_call" | custom-call | flops 4000000000 | bytes 1024 | tf_op jit(solution)/shard_map/pallas_call | solution.py:152
  37.1 2.4 %collective-permute-start.10 = (bf16[3,256,256]{2,1,0:T(8,128)(2,1)S(1)}, bf16[3,256,256]{2,1,0:T(8,128)(2,1)S(1)}, u32[]{:S(2)}, u32[]{:S(2)}) collective-permute-start(bf16[3,256,256]{2,1,0:T(8,128)(2,1)S(1)} %get-tuple-element.44.refs_1_), channel_id=1, source_target_pairs={{0,2},{2,0},{4,6},{6,4},{8,10},{10,8},{12,14},{14,12},{16,18},{18,... | collective-permute-start | bytes 1179656 | tf_op jit(solution)/shard_map/ppermute | solution.py:226
  39.4 4.5 %collective-permute-start.9 = (bf16[256,512]{1,0:T(8,128)(2,1)S(1)}, bf16[256,512]{1,0:T(8,128)(2,1)S(1)}, u32[]{:S(2)}, u32[]{:S(2)}) collective-permute-start(bf16[256,512]{1,0:T(8,128)(2,1)S(1)} %get-tuple-element.45.refs_4_), channel_id=1, source_target_pairs={{0,8},{2,10},{4,12},{6,14},{8,0},{10,2},{12,4},{14,6},{16,24},{18,... | collective-permute-start | bytes 786440 | tf_op jit(solution)/shard_map/ppermute | solution.py:226
  44.7 1.8 %shard_map.71 = (bf16[3,256,256]{2,1,0:T(8,128)(2,1)S(1)}, bf16[3,256,256]{2,1,0:T(8,128)(2,1)S(1)}) custom-call(s32[1]{0:T(128)} %bitcast.odd_ref, s32[6,5]{1,0:T(8,128)S(1)} %copy-done.5, bf16[6,5,256,256]{3,2,1,0:T(8,128)(2,1)S(1)} %get-tuple-element.35.blocks_ref, bf16[3,256,256]{2,1,0:T(8,128)(2,1)S(1)} %get-tuple-element.42.refs_8_.refs_0_.refs_3_, ...), custom_call_target="tpu_custom_call" | custom-call | flops 4000000000 | bytes 1024 | tf_op jit(solution)/shard_map/pallas_call | solution.py:152
  48.4 1.9 %collective-permute-start.14 = (bf16[3,256,256]{2,1,0:T(8,128)(2,1)S(1)}, bf16[3,256,256]{2,1,0:T(8,128)(2,1)S(1)}, u32[]{:S(2)}, u32[]{:S(2)}) collective-permute-start(bf16[3,256,256]{2,1,0:T(8,128)(2,1)S(1)} %shard_map.69.refs_6_.refs_0_), channel_id=1, source_target_pairs={{0,1},{1,0},{2,3},{3,2},{4,5},{5,4},{6,7},{7,6},{8,9},{9,8},{10,11... | collective-permute-start | bytes 1179656 | tf_op jit(solution)/shard_map/ppermute | solution.py:226
  54.0 6.1 %collective-permute-start.18 = (bf16[512,512]{1,0:T(8,128)(2,1)S(1)}, bf16[512,512]{1,0:T(8,128)(2,1)S(1)}, u32[]{:S(2)}, u32[]{:S(2)}) collective-permute-start(bf16[512,512]{1,0:T(8,128)(2,1)S(1)} %get-tuple-element.50.refs_0_), channel_id=1, source_target_pairs={{0,2},{2,0},{4,6},{6,4},{8,10},{10,8},{12,14},{14,12},{16,18},{18,... | collective-permute-start | bytes 1572872 | tf_op jit(solution)/shard_map/ppermute | solution.py:226
  61.5 2.9 %collective-permute-done.13.refs_2_ = bf16[3,256,256]{2,1,0:T(8,128)(2,1)S(1)} collective-permute-done((bf16[3,256,256]{2,1,0:T(8,128)(2,1)S(1)}, bf16[3,256,256]{2,1,0:T(8,128)(2,1)S(1)}, u32[]{:S(2)}, u32[]{:S(2)}) %collective-permute-start.13) | collective-permute-done | bytes 393248 | tf_op jit(solution)/shard_map/ppermute | solution.py:226
  65.7 1.6 %collective-permute-start.17 = (bf16[3,256,256]{2,1,0:T(8,128)(2,1)S(1)}, bf16[3,256,256]{2,1,0:T(8,128)(2,1)S(1)}, u32[]{:S(2)}, u32[]{:S(2)}) collective-permute-start(bf16[3,256,256]{2,1,0:T(8,128)(2,1)S(1)} %shard_map.73.refs_1_), channel_id=1, source_target_pairs={{0,1},{1,0},{2,3},{3,2},{4,5},{5,4},{6,7},{7,6},{8,9},{9,8},{10,11... | collective-permute-start | bytes 1179656 | tf_op jit(solution)/shard_map/ppermute | solution.py:226
  69.3 7.3 %collective-permute-done.17.refs_3_ = bf16[3,256,256]{2,1,0:T(8,128)(2,1)S(1)} collective-permute-done((bf16[3,256,256]{2,1,0:T(8,128)(2,1)S(1)}, bf16[3,256,256]{2,1,0:T(8,128)(2,1)S(1)}, u32[]{:S(2)}, u32[]{:S(2)}) %collective-permute-start.17) | collective-permute-done | bytes 393248 | tf_op jit(solution)/shard_map/ppermute | solution.py:226
  78.7 6.5 %collective-permute-start.26 = (bf16[3,256,256]{2,1,0:T(8,128)(2,1)S(1)}, bf16[3,256,256]{2,1,0:T(8,128)(2,1)S(1)}, u32[]{:S(2)}, u32[]{:S(2)}) collective-permute-start(bf16[3,256,256]{2,1,0:T(8,128)(2,1)S(1)} %get-tuple-element.57.refs_0_.refs_4_), channel_id=1, source_target_pairs={{0,30},{2,4},{4,2},{6,8},{8,6},{10,12},{12,10},{14,16},{16,14},{18... | collective-permute-start | bytes 1179656 | tf_op jit(solution)/shard_map/ppermute | solution.py:226
  85.2 2.3 %collective-permute-done.19.refs_5_.refs_3_ = bf16[3,256,256]{2,1,0:T(8,128)(2,1)S(1)} collective-permute-done((bf16[3,256,256]{2,1,0:T(8,128)(2,1)S(1)}, bf16[3,256,256]{2,1,0:T(8,128)(2,1)S(1)}, u32[]{:S(2)}, u32[]{:S(2)}) %collective-permute-start.19) | collective-permute-done | bytes 393248 | tf_op jit(solution)/shard_map/ppermute | solution.py:226
  90.5 5.3 %collective-permute-start.20 = (bf16[3,256,256]{2,1,0:T(8,128)(2,1)S(1)}, bf16[3,256,256]{2,1,0:T(8,128)(2,1)S(1)}, u32[]{:S(2)}, u32[]{:S(2)}) collective-permute-start(bf16[3,256,256]{2,1,0:T(8,128)(2,1)S(1)} %shard_map.76.refs_0_.refs_4_), channel_id=1, source_target_pairs={{0,30},{2,4},{4,2},{6,8},{8,6},{10,12},{12,10},{14,16},{16,14},{18... | collective-permute-start | bytes 1179656 | tf_op jit(solution)/shard_map/ppermute | solution.py:226
  95.8 1.8 %shard_map.80 = (bf16[3,256,256]{2,1,0:T(8,128)(2,1)S(1)}, bf16[3,256,256]{2,1,0:T(8,128)(2,1)S(1)}) custom-call(s32[1]{0:T(128)} %bitcast.odd_ref, s32[6,5]{1,0:T(8,128)S(1)} %copy-done.5, bf16[6,5,256,256]{3,2,1,0:T(8,128)(2,1)S(1)} %copy-done.7, bf16[3,256,256]{2,1,0:T(8,128)(2,1)S(1)} %get-tuple-element.57.refs_0_.refs_4_, ...), custom_call_target="tpu_custom_call" | custom-call | flops 4000000000 | bytes 1024 | tf_op jit(solution)/shard_map/pallas_call | solution.py:152
  98.6 14.5 %collective-permute-done.20.refs_2_ = bf16[3,256,256]{2,1,0:T(8,128)(2,1)S(1)} collective-permute-done((bf16[3,256,256]{2,1,0:T(8,128)(2,1)S(1)}, bf16[3,256,256]{2,1,0:T(8,128)(2,1)S(1)}, u32[]{:S(2)}, u32[]{:S(2)}) %collective-permute-start.20) | collective-permute-done | bytes 393248 | tf_op jit(solution)/shard_map/ppermute | solution.py:226
  113.1 1.8 %shard_map.78 = (bf16[3,256,256]{2,1,0:T(8,128)(2,1)S(1)}, bf16[3,256,256]{2,1,0:T(8,128)(2,1)S(1)}) custom-call(s32[1]{0:T(128)} %bitcast.odd_ref, s32[6,5]{1,0:T(8,128)S(1)} %copy-done.5, bf16[6,5,256,256]{3,2,1,0:T(8,128)(2,1)S(1)} %copy-done.7, bf16[3,256,256]{2,1,0:T(8,128)(2,1)S(1)} %shard_map.76.refs_0_.refs_4_, ...), custom_call_target="tpu_custom_call" | custom-call | flops 4000000000 | bytes 1024 | tf_op jit(solution)/shard_map/pallas_call | solution.py:152
  114.9 2.5 %collective-permute-start.22 = (bf16[3,256,256]{2,1,0:T(8,128)(2,1)S(1)}, bf16[3,256,256]{2,1,0:T(8,128)(2,1)S(1)}, u32[]{:S(2)}, u32[]{:S(2)}) collective-permute-start(bf16[3,256,256]{2,1,0:T(8,128)(2,1)S(1)} %get-tuple-element.53.refs_0_.refs_4_), channel_id=1, source_target_pairs={{0,30},{2,4},{4,2},{6,8},{8,6},{10,12},{12,10},{14,16},{16,14},{18... | collective-permute-start | bytes 1179656 | tf_op jit(solution)/shard_map/ppermute | solution.py:226
  117.5 1.8 %shard_map.81 = (bf16[3,256,256]{2,1,0:T(8,128)(2,1)S(1)}, bf16[3,256,256]{2,1,0:T(8,128)(2,1)S(1)}) custom-call(s32[1]{0:T(128)} %bitcast.odd_ref, s32[6,5]{1,0:T(8,128)S(1)} %copy-done.5, bf16[6,5,256,256]{3,2,1,0:T(8,128)(2,1)S(1)} %copy-done.7, bf16[3,256,256]{2,1,0:T(8,128)(2,1)S(1)} %get-tuple-element.59.refs_0_.refs_4_, ...), custom_call_target="tpu_custom_call" | custom-call | flops 4000000000 | bytes 1024 | tf_op jit(solution)/shard_map/pallas_call | solution.py:152
  119.3 2.4 %collective-permute-start.30 = (bf16[3,256,256]{2,1,0:T(8,128)(2,1)S(1)}, bf16[3,256,256]{2,1,0:T(8,128)(2,1)S(1)}, u32[]{:S(2)}, u32[]{:S(2)}) collective-permute-start(bf16[3,256,256]{2,1,0:T(8,128)(2,1)S(1)} %get-tuple-element.61.refs_0_), channel_id=1, source_target_pairs={{0,30},{2,4},{4,2},{6,8},{8,6},{10,12},{12,10},{14,16},{16,14},{18... | collective-permute-start | bytes 1179656 | tf_op jit(solution)/shard_map/ppermute | solution.py:226
  122.4 8.2 %collective-permute-done.22.refs_2_ = bf16[3,256,256]{2,1,0:T(8,128)(2,1)S(1)} collective-permute-done((bf16[3,256,256]{2,1,0:T(8,128)(2,1)S(1)}, bf16[3,256,256]{2,1,0:T(8,128)(2,1)S(1)}, u32[]{:S(2)}, u32[]{:S(2)}) %collective-permute-start.22) | collective-permute-done | bytes 393248 | tf_op jit(solution)/shard_map/ppermute | solution.py:226
  130.6 1.8 %shard_map.79 = (bf16[3,256,256]{2,1,0:T(8,128)(2,1)S(1)}, bf16[3,256,256]{2,1,0:T(8,128)(2,1)S(1)}) custom-call(s32[1]{0:T(128)} %bitcast.odd_ref, s32[6,5]{1,0:T(8,128)S(1)} %copy-done.5, bf16[6,5,256,256]{3,2,1,0:T(8,128)(2,1)S(1)} %copy-done.7, bf16[3,256,256]{2,1,0:T(8,128)(2,1)S(1)} %get-tuple-element.53.refs_0_.refs_4_, ...), custom_call_target="tpu_custom_call" | custom-call | flops 4000000000 | bytes 1024 | tf_op jit(solution)/shard_map/pallas_call | solution.py:152
  132.4 2.6 %collective-permute-start.24 = (bf16[3,256,256]{2,1,0:T(8,128)(2,1)S(1)}, bf16[3,256,256]{2,1,0:T(8,128)(2,1)S(1)}, u32[]{:S(2)}, u32[]{:S(2)}) collective-permute-start(bf16[3,256,256]{2,1,0:T(8,128)(2,1)S(1)} %get-tuple-element.55.refs_0_), channel_id=1, source_target_pairs={{0,30},{2,4},{4,2},{6,8},{8,6},{10,12},{12,10},{14,16},{16,14},{18... | collective-permute-start | bytes 1179656 | tf_op jit(solution)/shard_map/ppermute | solution.py:226
  135.6 2.5 %shard_map.82.refs_6_ = bf16[6,256,512]{2,1,0:T(8,128)(2,1)} custom-call(s32[1]{0:T(128)} %bitcast.odd_ref, s32[6,5]{1,0:T(8,128)S(1)} %copy-done.5, bf16[6,5,256,256]{3,2,1,0:T(8,128)(2,1)S(1)} %copy-done.7, bf16[3,256,256]{2,1,0:T(8,128)(2,1)S(1)} %get-tuple-element.61.refs_0_, bf16[3,256,256]{2,1,0:T(8,128)(2,1)S(1)} %get-tuple-element.62.refs_1_, ...), custom_call_target="tpu_custom_call" | custom-call | flops 4000000000 | bytes 1024 | tf_op jit(solution)/shard_map/pallas_call | solution.py:152
  138.2 2.3 %collective-permute-done.24.refs_2_ = bf16[3,256,256]{2,1,0:T(8,128)(2,1)S(1)} collective-permute-done((bf16[3,256,256]{2,1,0:T(8,128)(2,1)S(1)}, bf16[3,256,256]{2,1,0:T(8,128)(2,1)S(1)}, u32[]{:S(2)}, u32[]{:S(2)}) %collective-permute-start.24) | collective-permute-done | bytes 393248 | tf_op jit(solution)/shard_map/ppermute | solution.py:226
  140.5 2.6 %shard_map.83 = bf16[6,256,512]{2,1,0:T(8,128)(2,1)} custom-call(s32[1]{0:T(128)} %bitcast.odd_ref, s32[6,5]{1,0:T(8,128)S(1)} %copy-done.5, bf16[6,5,256,256]{3,2,1,0:T(8,128)(2,1)S(1)} %copy-done.7, bf16[3,256,256]{2,1,0:T(8,128)(2,1)S(1)} %get-tuple-element.55.refs_0_, ...), custom_call_target="tpu_custom_call", output_to_operand_aliasing={{}: (9, {})} | custom-call | flops 4000000000 | bytes 1024 | tf_op jit(solution)/shard_map/pallas_call | solution.py:152
  (77 shorter events, 25.8 us)
Async XLA Ops:
  1.5 4.0 %collective-permute-start = (bf16[3,256,256]{2,1,0:T(8,128)(2,1)S(1)}, bf16[3,256,256]{2,1,0:T(8,128)(2,1)S(1)}, u32[]{:S(2)}, u32[]{:S(2)}) collective-permute-start(bf16[3,256,256]{2,1,0:T(8,128)(2,1)S(1)} %get-tuple-element.34.refs_1_.refs_5_), channel_id=1, source_target_pairs={{0,2},{2,0},{4,6},{6,4},{8,10},{10,8},{12,14},{14,12},{16,18},{18,... | collective-permute-start | bytes 1179656 | tf_op jit(solution)/shard_map/ppermute | solution.py:226
  1.6 17.2 %collective-permute-start.1 = (bf16[3,256,256]{2,1,0:T(8,128)(2,1)S(1)}, bf16[3,256,256]{2,1,0:T(8,128)(2,1)S(1)}, u32[]{:S(2)}, u32[]{:S(2)}) collective-permute-start(bf16[3,256,256]{2,1,0:T(8,128)(2,1)S(1)} %get-tuple-element.36.refs_0_.refs_4_), channel_id=1, source_target_pairs={{0,30},{2,4},{4,2},{6,8},{8,6},{10,12},{12,10},{14,16},{16,14},{18... | collective-permute-start | bytes 1179656 | tf_op jit(solution)/shard_map/ppermute | solution.py:226
  4.3 14.6 %collective-permute-start.2 = (bf16[64,512]{1,0:T(8,128)(2,1)S(1)}, bf16[64,512]{1,0:T(8,128)(2,1)S(1)}, u32[]{:S(2)}, u32[]{:S(2)}) collective-permute-start(bf16[64,512]{1,0:T(8,128)(2,1)S(1)} %copy-done.4), channel_id=1, source_target_pairs={{0,4},{2,6},{4,0},{6,2},{8,12},{10,14},{12,8},{14,10},{16,20},{18,... | collective-permute-start | bytes 196616 | tf_op jit(solution)/shard_map/ppermute | solution.py:226
  5.9 19.6 %collective-permute-start.6 = (bf16[3,256,256]{2,1,0:T(8,128)(2,1)S(1)}, bf16[3,256,256]{2,1,0:T(8,128)(2,1)S(1)}, u32[]{:S(2)}, u32[]{:S(2)}) collective-permute-start(bf16[3,256,256]{2,1,0:T(8,128)(2,1)S(1)} %get-tuple-element.40.refs_0_.refs_4_), channel_id=1, source_target_pairs={{0,30},{2,4},{4,2},{6,8},{8,6},{10,12},{12,10},{14,16},{16,14},{18... | collective-permute-start | bytes 1179656 | tf_op jit(solution)/shard_map/ppermute | solution.py:226
  9.8 15.7 %collective-permute-start.7 = (bf16[3,256,256]{2,1,0:T(8,128)(2,1)S(1)}, bf16[3,256,256]{2,1,0:T(8,128)(2,1)S(1)}, u32[]{:S(2)}, u32[]{:S(2)}) collective-permute-start(bf16[3,256,256]{2,1,0:T(8,128)(2,1)S(1)} %get-tuple-element.41.refs_1_.refs_5_), channel_id=1, source_target_pairs={{0,2},{2,0},{4,6},{6,4},{8,10},{10,8},{12,14},{14,12},{16,18},{18,... | collective-permute-start | bytes 1179656 | tf_op jit(solution)/shard_map/ppermute | solution.py:226
  20.8 10.1 %collective-permute-start.4 = (bf16[3,256,256]{2,1,0:T(8,128)(2,1)S(1)}, bf16[3,256,256]{2,1,0:T(8,128)(2,1)S(1)}, u32[]{:S(2)}, u32[]{:S(2)}) collective-permute-start(bf16[3,256,256]{2,1,0:T(8,128)(2,1)S(1)} %get-tuple-element.38.refs_1_.refs_3_), channel_id=1, source_target_pairs={{0,2},{2,0},{4,6},{6,4},{8,10},{10,8},{12,14},{14,12},{16,18},{18,... | collective-permute-start | bytes 1179656 | tf_op jit(solution)/shard_map/ppermute | solution.py:226
  22.3 12.6 %collective-permute-start.3 = (bf16[3,256,256]{2,1,0:T(8,128)(2,1)S(1)}, bf16[3,256,256]{2,1,0:T(8,128)(2,1)S(1)}, u32[]{:S(2)}, u32[]{:S(2)}) collective-permute-start(bf16[3,256,256]{2,1,0:T(8,128)(2,1)S(1)} %get-tuple-element.37.refs_4_.refs_0_.refs_3_), channel_id=1, source_target_pairs={{0,30},{2,4},{4,2},{6,8},{8,6},{10,12},{12,10},{14,16},{16,14},{18... | collective-permute-start | bytes 1179656 | tf_op jit(solution)/shard_map/ppermute | solution.py:226
  23.2 7.7 %collective-permute-start.5 = (bf16[128,512]{1,0:T(8,128)(2,1)S(1)}, bf16[128,512]{1,0:T(8,128)(2,1)S(1)}, u32[]{:S(2)}, u32[]{:S(2)}) collective-permute-start(bf16[128,512]{1,0:T(8,128)(2,1)S(1)} %get-tuple-element.39.refs_6_), channel_id=1, source_target_pairs={{0,16},{2,18},{4,20},{6,22},{8,24},{10,26},{12,28},{14,30},{16,0},... | collective-permute-start | bytes 393224 | tf_op jit(solution)/shard_map/ppermute | solution.py:226
  27.3 17.4 %collective-permute-start.12 = (bf16[3,256,256]{2,1,0:T(8,128)(2,1)S(1)}, bf16[3,256,256]{2,1,0:T(8,128)(2,1)S(1)}, u32[]{:S(2)}, u32[]{:S(2)}) collective-permute-start(bf16[3,256,256]{2,1,0:T(8,128)(2,1)S(1)} %get-tuple-element.47.refs_1_.refs_3_), channel_id=1, source_target_pairs={{0,2},{2,0},{4,6},{6,4},{8,10},{10,8},{12,14},{14,12},{16,18},{18,... | collective-permute-start | bytes 1179656 | tf_op jit(solution)/shard_map/ppermute | solution.py:226
  28.2 16.5 %collective-permute-start.11 = (bf16[3,256,256]{2,1,0:T(8,128)(2,1)S(1)}, bf16[3,256,256]{2,1,0:T(8,128)(2,1)S(1)}, u32[]{:S(2)}, u32[]{:S(2)}) collective-permute-start(bf16[3,256,256]{2,1,0:T(8,128)(2,1)S(1)} %get-tuple-element.42.refs_8_.refs_0_.refs_3_), channel_id=1, source_target_pairs={{0,30},{2,4},{4,2},{6,8},{8,6},{10,12},{12,10},{14,16},{16,14},{18... | collective-permute-start | bytes 1179656 | tf_op jit(solution)/shard_map/ppermute | solution.py:226
  37.1 10.0 %collective-permute-start.10 = (bf16[3,256,256]{2,1,0:T(8,128)(2,1)S(1)}, bf16[3,256,256]{2,1,0:T(8,128)(2,1)S(1)}, u32[]{:S(2)}, u32[]{:S(2)}) collective-permute-start(bf16[3,256,256]{2,1,0:T(8,128)(2,1)S(1)} %get-tuple-element.44.refs_1_), channel_id=1, source_target_pairs={{0,2},{2,0},{4,6},{6,4},{8,10},{10,8},{12,14},{14,12},{16,18},{18,... | collective-permute-start | bytes 1179656 | tf_op jit(solution)/shard_map/ppermute | solution.py:226
  39.4 11.1 %collective-permute-start.9 = (bf16[256,512]{1,0:T(8,128)(2,1)S(1)}, bf16[256,512]{1,0:T(8,128)(2,1)S(1)}, u32[]{:S(2)}, u32[]{:S(2)}) collective-permute-start(bf16[256,512]{1,0:T(8,128)(2,1)S(1)} %get-tuple-element.45.refs_4_), channel_id=1, source_target_pairs={{0,8},{2,10},{4,12},{6,14},{8,0},{10,2},{12,4},{14,6},{16,24},{18,... | collective-permute-start | bytes 786440 | tf_op jit(solution)/shard_map/ppermute | solution.py:226
  43.9 7.9 %collective-permute-start.8 = (bf16[3,256,256]{2,1,0:T(8,128)(2,1)S(1)}, bf16[3,256,256]{2,1,0:T(8,128)(2,1)S(1)}, u32[]{:S(2)}, u32[]{:S(2)}) collective-permute-start(bf16[3,256,256]{2,1,0:T(8,128)(2,1)S(1)} %get-tuple-element.43.refs_0_.refs_6_), channel_id=1, source_target_pairs={{0,30},{2,4},{4,2},{6,8},{8,6},{10,12},{12,10},{14,16},{16,14},{18... | collective-permute-start | bytes 1179656 | tf_op jit(solution)/shard_map/ppermute | solution.py:226
  46.6 13.6 %collective-permute-start.15 = (bf16[3,256,256]{2,1,0:T(8,128)(2,1)S(1)}, bf16[3,256,256]{2,1,0:T(8,128)(2,1)S(1)}, u32[]{:S(2)}, u32[]{:S(2)}) collective-permute-start(bf16[3,256,256]{2,1,0:T(8,128)(2,1)S(1)} %get-tuple-element.49.refs_1_), channel_id=1, source_target_pairs={{0,2},{2,0},{4,6},{6,4},{8,10},{10,8},{12,14},{14,12},{16,18},{18,... | collective-permute-start | bytes 1179656 | tf_op jit(solution)/shard_map/ppermute | solution.py:226
  48.4 13.1 %collective-permute-start.14 = (bf16[3,256,256]{2,1,0:T(8,128)(2,1)S(1)}, bf16[3,256,256]{2,1,0:T(8,128)(2,1)S(1)}, u32[]{:S(2)}, u32[]{:S(2)}) collective-permute-start(bf16[3,256,256]{2,1,0:T(8,128)(2,1)S(1)} %shard_map.69.refs_6_.refs_0_), channel_id=1, source_target_pairs={{0,1},{1,0},{2,3},{3,2},{4,5},{5,4},{6,7},{7,6},{8,9},{9,8},{10,11... | collective-permute-start | bytes 1179656 | tf_op jit(solution)/shard_map/ppermute | solution.py:226
  50.3 14.1 %collective-permute-start.13 = (bf16[3,256,256]{2,1,0:T(8,128)(2,1)S(1)}, bf16[3,256,256]{2,1,0:T(8,128)(2,1)S(1)}, u32[]{:S(2)}, u32[]{:S(2)}) collective-permute-start(bf16[3,256,256]{2,1,0:T(8,128)(2,1)S(1)} %get-tuple-element.48.refs_0_), channel_id=1, source_target_pairs={{0,30},{2,4},{4,2},{6,8},{8,6},{10,12},{12,10},{14,16},{16,14},{18... | collective-permute-start | bytes 1179656 | tf_op jit(solution)/shard_map/ppermute | solution.py:226
  53.4 15.9 %collective-permute-start.16 = (bf16[3,256,256]{2,1,0:T(8,128)(2,1)S(1)}, bf16[3,256,256]{2,1,0:T(8,128)(2,1)S(1)}, u32[]{:S(2)}, u32[]{:S(2)}) collective-permute-start(bf16[3,256,256]{2,1,0:T(8,128)(2,1)S(1)} %get-tuple-element.46.refs_4_.refs_0_), channel_id=1, source_target_pairs={{0,1},{1,0},{2,3},{3,2},{4,5},{5,4},{6,7},{7,6},{8,9},{9,8},{10,11... | collective-permute-start | bytes 1179656 | tf_op jit(solution)/shard_map/ppermute | solution.py:226
  54.0 14.1 %collective-permute-start.18 = (bf16[512,512]{1,0:T(8,128)(2,1)S(1)}, bf16[512,512]{1,0:T(8,128)(2,1)S(1)}, u32[]{:S(2)}, u32[]{:S(2)}) collective-permute-start(bf16[512,512]{1,0:T(8,128)(2,1)S(1)} %get-tuple-element.50.refs_0_), channel_id=1, source_target_pairs={{0,2},{2,0},{4,6},{6,4},{8,10},{10,8},{12,14},{14,12},{16,18},{18,... | collective-permute-start | bytes 1572872 | tf_op jit(solution)/shard_map/ppermute | solution.py:226
  65.7 10.9 %collective-permute-start.17 = (bf16[3,256,256]{2,1,0:T(8,128)(2,1)S(1)}, bf16[3,256,256]{2,1,0:T(8,128)(2,1)S(1)}, u32[]{:S(2)}, u32[]{:S(2)}) collective-permute-start(bf16[3,256,256]{2,1,0:T(8,128)(2,1)S(1)} %shard_map.73.refs_1_), channel_id=1, source_target_pairs={{0,1},{1,0},{2,3},{3,2},{4,5},{5,4},{6,7},{7,6},{8,9},{9,8},{10,11... | collective-permute-start | bytes 1179656 | tf_op jit(solution)/shard_map/ppermute | solution.py:226
  77.2 10.4 %collective-permute-start.19 = (bf16[3,256,256]{2,1,0:T(8,128)(2,1)S(1)}, bf16[3,256,256]{2,1,0:T(8,128)(2,1)S(1)}, u32[]{:S(2)}, u32[]{:S(2)}) collective-permute-start(bf16[3,256,256]{2,1,0:T(8,128)(2,1)S(1)} %get-tuple-element.51.refs_1_), channel_id=1, source_target_pairs={{0,1},{1,0},{2,3},{3,2},{4,5},{5,4},{6,7},{7,6},{8,9},{9,8},{10,11... | collective-permute-start | bytes 1179656 | tf_op jit(solution)/shard_map/ppermute | solution.py:226
  78.7 17.1 %collective-permute-start.26 = (bf16[3,256,256]{2,1,0:T(8,128)(2,1)S(1)}, bf16[3,256,256]{2,1,0:T(8,128)(2,1)S(1)}, u32[]{:S(2)}, u32[]{:S(2)}) collective-permute-start(bf16[3,256,256]{2,1,0:T(8,128)(2,1)S(1)} %get-tuple-element.57.refs_0_.refs_4_), channel_id=1, source_target_pairs={{0,30},{2,4},{4,2},{6,8},{8,6},{10,12},{12,10},{14,16},{16,14},{18... | collective-permute-start | bytes 1179656 | tf_op jit(solution)/shard_map/ppermute | solution.py:226
  88.5 7.3 %collective-permute-start.27 = (bf16[3,256,256]{2,1,0:T(8,128)(2,1)S(1)}, bf16[3,256,256]{2,1,0:T(8,128)(2,1)S(1)}, u32[]{:S(2)}, u32[]{:S(2)}) collective-permute-start(bf16[3,256,256]{2,1,0:T(8,128)(2,1)S(1)} %get-tuple-element.58.refs_1_.refs_5_), channel_id=1, source_target_pairs={{0,2},{2,0},{4,6},{6,4},{8,10},{10,8},{12,14},{14,12},{16,18},{18,... | collective-permute-start | bytes 1179656 | tf_op jit(solution)/shard_map/ppermute | solution.py:226
  89.8 8.8 %collective-permute-start.21 = (bf16[3,256,256]{2,1,0:T(8,128)(2,1)S(1)}, bf16[3,256,256]{2,1,0:T(8,128)(2,1)S(1)}, u32[]{:S(2)}, u32[]{:S(2)}) collective-permute-start(bf16[3,256,256]{2,1,0:T(8,128)(2,1)S(1)} %get-tuple-element.52.refs_1_.refs_5_), channel_id=1, source_target_pairs={{0,2},{2,0},{4,6},{6,4},{8,10},{10,8},{12,14},{14,12},{16,18},{18,... | collective-permute-start | bytes 1179656 | tf_op jit(solution)/shard_map/ppermute | solution.py:226
  90.5 22.7 %collective-permute-start.20 = (bf16[3,256,256]{2,1,0:T(8,128)(2,1)S(1)}, bf16[3,256,256]{2,1,0:T(8,128)(2,1)S(1)}, u32[]{:S(2)}, u32[]{:S(2)}) collective-permute-start(bf16[3,256,256]{2,1,0:T(8,128)(2,1)S(1)} %shard_map.76.refs_0_.refs_4_), channel_id=1, source_target_pairs={{0,30},{2,4},{4,2},{6,8},{8,6},{10,12},{12,10},{14,16},{16,14},{18... | collective-permute-start | bytes 1179656 | tf_op jit(solution)/shard_map/ppermute | solution.py:226
  97.6 19.9 %collective-permute-start.28 = (bf16[3,256,256]{2,1,0:T(8,128)(2,1)S(1)}, bf16[3,256,256]{2,1,0:T(8,128)(2,1)S(1)}, u32[]{:S(2)}, u32[]{:S(2)}) collective-permute-start(bf16[3,256,256]{2,1,0:T(8,128)(2,1)S(1)} %get-tuple-element.59.refs_0_.refs_4_), channel_id=1, source_target_pairs={{0,30},{2,4},{4,2},{6,8},{8,6},{10,12},{12,10},{14,16},{16,14},{18... | collective-permute-start | bytes 1179656 | tf_op jit(solution)/shard_map/ppermute | solution.py:226
  98.6 18.9 %collective-permute-start.29 = (bf16[3,256,256]{2,1,0:T(8,128)(2,1)S(1)}, bf16[3,256,256]{2,1,0:T(8,128)(2,1)S(1)}, u32[]{:S(2)}, u32[]{:S(2)}) collective-permute-start(bf16[3,256,256]{2,1,0:T(8,128)(2,1)S(1)} %get-tuple-element.60.refs_1_.refs_5_), channel_id=1, source_target_pairs={{0,2},{2,0},{4,6},{6,4},{8,10},{10,8},{12,14},{14,12},{16,18},{18,... | collective-permute-start | bytes 1179656 | tf_op jit(solution)/shard_map/ppermute | solution.py:226
  114.9 15.7 %collective-permute-start.22 = (bf16[3,256,256]{2,1,0:T(8,128)(2,1)S(1)}, bf16[3,256,256]{2,1,0:T(8,128)(2,1)S(1)}, u32[]{:S(2)}, u32[]{:S(2)}) collective-permute-start(bf16[3,256,256]{2,1,0:T(8,128)(2,1)S(1)} %get-tuple-element.53.refs_0_.refs_4_), channel_id=1, source_target_pairs={{0,30},{2,4},{4,2},{6,8},{8,6},{10,12},{12,10},{14,16},{16,14},{18... | collective-permute-start | bytes 1179656 | tf_op jit(solution)/shard_map/ppermute | solution.py:226
  117.5 13.2 %collective-permute-start.23 = (bf16[3,256,256]{2,1,0:T(8,128)(2,1)S(1)}, bf16[3,256,256]{2,1,0:T(8,128)(2,1)S(1)}, u32[]{:S(2)}, u32[]{:S(2)}) collective-permute-start(bf16[3,256,256]{2,1,0:T(8,128)(2,1)S(1)} %get-tuple-element.54.refs_1_.refs_5_), channel_id=1, source_target_pairs={{0,2},{2,0},{4,6},{6,4},{8,10},{10,8},{12,14},{14,12},{16,18},{18,... | collective-permute-start | bytes 1179656 | tf_op jit(solution)/shard_map/ppermute | solution.py:226
  119.3 16.3 %collective-permute-start.30 = (bf16[3,256,256]{2,1,0:T(8,128)(2,1)S(1)}, bf16[3,256,256]{2,1,0:T(8,128)(2,1)S(1)}, u32[]{:S(2)}, u32[]{:S(2)}) collective-permute-start(bf16[3,256,256]{2,1,0:T(8,128)(2,1)S(1)} %get-tuple-element.61.refs_0_), channel_id=1, source_target_pairs={{0,30},{2,4},{4,2},{6,8},{8,6},{10,12},{12,10},{14,16},{16,14},{18... | collective-permute-start | bytes 1179656 | tf_op jit(solution)/shard_map/ppermute | solution.py:226
  121.7 13.9 %collective-permute-start.31 = (bf16[3,256,256]{2,1,0:T(8,128)(2,1)S(1)}, bf16[3,256,256]{2,1,0:T(8,128)(2,1)S(1)}, u32[]{:S(2)}, u32[]{:S(2)}) collective-permute-start(bf16[3,256,256]{2,1,0:T(8,128)(2,1)S(1)} %get-tuple-element.62.refs_1_), channel_id=1, source_target_pairs={{0,2},{2,0},{4,6},{6,4},{8,10},{10,8},{12,14},{14,12},{16,18},{18,... | collective-permute-start | bytes 1179656 | tf_op jit(solution)/shard_map/ppermute | solution.py:226
  132.4 8.0 %collective-permute-start.24 = (bf16[3,256,256]{2,1,0:T(8,128)(2,1)S(1)}, bf16[3,256,256]{2,1,0:T(8,128)(2,1)S(1)}, u32[]{:S(2)}, u32[]{:S(2)}) collective-permute-start(bf16[3,256,256]{2,1,0:T(8,128)(2,1)S(1)} %get-tuple-element.55.refs_0_), channel_id=1, source_target_pairs={{0,30},{2,4},{4,2},{6,8},{8,6},{10,12},{12,10},{14,16},{16,14},{18... | collective-permute-start | bytes 1179656 | tf_op jit(solution)/shard_map/ppermute | solution.py:226
  135.0 5.5 %collective-permute-start.25 = (bf16[3,256,256]{2,1,0:T(8,128)(2,1)S(1)}, bf16[3,256,256]{2,1,0:T(8,128)(2,1)S(1)}, u32[]{:S(2)}, u32[]{:S(2)}) collective-permute-start(bf16[3,256,256]{2,1,0:T(8,128)(2,1)S(1)} %get-tuple-element.56.refs_1_), channel_id=1, source_target_pairs={{0,2},{2,0},{4,6},{6,4},{8,10},{10,8},{12,14},{14,12},{16,18},{18,... | collective-permute-start | bytes 1179656 | tf_op jit(solution)/shard_map/ppermute | solution.py:226
  (10 other events, 114.6 us)

commit v4 on v3

--- a/solution.py
+++ b/solution.py
@@ -190,8 +190,8 @@
     return list(result[: len(widths)]), list(result[len(widths) :])
 
 
-def ordered_kernel(bands, own_ref, order_ref, *refs):
-    rows, out_ref = refs[:-1], refs[-1]
+def ordered_kernel(bands, count, own_ref, order_ref, *refs):
+    rows, out_ref = refs[:count], refs[-1]
     total = out_ref.shape[0]
     width = total // bands
     for shift in range(bands):
@@ -210,16 +210,16 @@
             out_ref[place : place + size, :] = result.astype(jnp.bfloat16)
 
 
-def ordered_rows(own, order, rows, bands):
+def ordered_rows(own, order, rows, bands, later):
     total = order.shape[1]
     return pl.pallas_call(
-        functools.partial(ordered_kernel, bands),
+        functools.partial(ordered_kernel, bands, len(rows)),
         out_shape=jax.ShapeDtypeStruct((total, rows[0].shape[1]), rows[0].dtype),
-        in_specs=[SMEM] + [VMEM] * (1 + len(rows)),
+        in_specs=[SMEM] + [VMEM] * (1 + len(rows)) + [ANYWHERE] * len(later),
         out_specs=VMEM,
         compiler_params=PARAMS,
-        cost_estimate=cost(LONG // 2),
-    )(own, order, *rows)
+        cost_estimate=cost(LONG),
+    )(own, order, *rows, *later)
 
 
 def exchange(array, axis, partner):
@@ -244,7 +244,7 @@
         return [self.held, self.received]
 
     def step(self, *args, **kwargs):
-        if not self.bits:
+        if len(self.bits) < 2:
             return apply_step(*args, **kwargs)
         result = apply_step(*args, join=self.parts(), **kwargs)
         self.held = result[-1]
@@ -252,10 +252,14 @@
         return result[:-1]
 
     def finish(self):
-        while self.bits:
+        while len(self.bits) > 1:
             self.held = jnp.concatenate(self.parts(), axis=0)
             self.received = self.send()
-        return self.parts(), jnp.array(self.owners)
+        parts = self.parts()
+        for bit in self.bits:
+            parts = parts + [exchange(part, "elem", lambda i: i ^ bit) for part in parts]
+            self.owners = self.owners + [owner ^ bit for owner in self.owners]
+        return parts, jnp.array(self.owners)
 
 
 def body(start_bands, blocks, neighbours, band_order, rotation):
@@ -281,7 +285,13 @@
     def over_band(piece):
         return [exchange(piece, "band", lambda i: i ^ shift) for shift in range(1, bands)]
 
-    _, state = split(odd, start_bands, starts[:1], chunk)
+    place = (me % 2) * GY
+    state = [
+        [
+            lax.dynamic_slice(start_bands, (first, 0, starts[0]), (GY, basis, chunk))
+            for first in (place, GY - place)
+        ]
+    ]
     beside = [halos(state[0])]
     (held,), rest = split(odd, start_bands, starts[1:], chunk, blocks, later=beside[0][1:])
     state += rest
@@ -290,9 +300,9 @@
     gather = Gather(rotation)
 
     before = [nothing for _ in chunks]
-    for _ in range(2):
+    for n in range(2):
         for c in chunks:
-            step = gather.step if c == 0 else apply_step
+            step = gather.step if c == (chunks[0], chunks[-1])[n] else apply_step
             new = step(shared, (0, 1), state[c], beside[c], before[c], later=state[c - 1][:1] if c or before[0][0] is not None else ())
             before[c], state[c] = state[c], new
             beside[c] = halos(new)
@@ -300,16 +310,17 @@
     inner, inner_others, outer, outer_others = [], [], [], []
     waits = []
     for c in chunks:
-        step = gather.step if c == 0 else apply_step
+        step = gather.step if c == chunks[-1] else apply_step
         inner += apply_step(shared, (1,), state[c], beside[c][1:], before[c][1:], later=outer[-1:])
         outer += step(shared, (0,), state[c], beside[c][:1], before[c][:1], later=waits + inner[-1:])
         outer_others.append(over_band(outer[-1]))
         if c != chunks[-1]:
             inner_others.append(over_band(inner[-1]))
             waits = inner_others[-1]
-    rows, owners = gather.finish()
+        if c == 0:
+            rows, owners = gather.finish()
     order = band_order.reshape(elems, -1)[jnp.bitwise_xor(me, owners)].reshape(1, -1)
-    matrix = ordered_rows(lax.axis_index("band").astype(jnp.int32).reshape(1), order, rows, bands)
+    matrix = ordered_rows(lax.axis_index("band").astype(jnp.int32).reshape(1), order, rows, bands, later=outer_others[0])
 
     def by_band(own, others):
         return list(own) + [other[shift] for shift in range(bands - 1) for other in others]

time: 144 us -> 142 us (0.986)
  the two profiles are of different devices: /device:TPU:1 before, /device:TPU:25 now
where the time goes in v4:
time: 142 us; the launch traced here: 141 us
  waiting for transfers between devices  80.9 us (57%)
  Pallas kernels  30.2 us (21%)
  starting transfers between devices  22.9 us (16%)
  local copies, waits for them, and re-layouts  6.86 us (5%)
    ppermute x33, waiting for transfers between devices, exchange(): lax.ppermute(array, axis, [(i, partner(i)) for i in range(lax.axis_size(a...  80.9 us
    pallas_call x14, Pallas kernels, apply_step(): pl.pallas_call(functools.partial(step_kernel, sides, firsts, out_column,...  25.5 us
    ppermute x33, starting transfers between devices, exchange(): lax.ppermute(array, axis, [(i, partner(i)) for i in range(lax.axis_size(a...  22.9 us
    unnamed x14, local copies, waits for them, and re-layouts  2.9 us
  transfers between devices with their start and end apart: 33, of which 18 were waited for; matrix products, arithmetic and copies ran while one was open for 2% of the time, Pallas kernels for 19%

profile of v4, /device:TPU:25, one launch (start us, length us, event | category | flops | bytes accessed | tf_op | source)
XLA Modules:
  0.0 141.4 jit_solution(830288474468186092)
XLA Ops:
  3.4 2.1 %copy-done.1 = bf16[6,5,256,256]{3,2,1,0:T(8,128)(2,1)S(1)} copy-done((bf16[6,5,256,256]{3,2,1,0:T(8,128)(2,1)S(1)}, bf16[6,5,256,256]{3,2,1,0:T(8,128)(2,1)}, u32[]{:S(2)}) %copy-start.1) | copy-done | bytes 3932184
  5.9 1.8 %collective-permute-start.5 = (bf16[3,256,256]{2,1,0:T(8,128)(2,1)S(1)}, bf16[3,256,256]{2,1,0:T(8,128)(2,1)S(1)}, u32[]{:S(2)}, u32[]{:S(2)}) collective-permute-start(bf16[3,256,256]{2,1,0:T(8,128)(2,1)S(1)} %get-tuple-element.33.refs_0_.refs_4_), channel_id=1, source_target_pairs={{0,30},{2,4},{4,2},{6,8},{8,6},{10,12},{12,10},{14,16},{16,14},{18... | collective-permute-start | bytes 1179656 | tf_op jit(solution)/shard_map/ppermute | solution.py:226
  7.7 10.2 %collective-permute-done.2.refs_5_ = bf16[64,512]{1,0:T(8,128)(2,1)S(1)} collective-permute-done((bf16[64,512]{1,0:T(8,128)(2,1)}, bf16[64,512]{1,0:T(8,128)(2,1)S(1)}, u32[]{:S(2)}, u32[]{:S(2)}) %collective-permute-start.2) | collective-permute-done | bytes 65568 | tf_op jit(solution)/shard_map/ppermute | solution.py:226
  18.4 2.0 %shard_map.65 = (bf16[3,256,256]{2,1,0:T(8,128)(2,1)S(1)}, bf16[3,256,256]{2,1,0:T(8,128)(2,1)S(1)}, bf16[128,512]{1,0:T(8,128)(2,1)S(1)}) custom-call(s32[1]{0:T(128)} %bitcast.odd_ref, s32[6,5]{1,0:T(8,128)S(1)} %copy-done.3, bf16[6,5,256,256]{3,2,1,0:T(8,128)(2,1)S(1)} %get-tuple-element.30.blocks_ref, ...), custom_call_target="tpu_custom_call" | custom-call | flops 4000000000 | bytes 1024 | tf_op jit(solution)/shard_map/pallas_call | solution.py:152
  20.4 1.5 %collective-permute-start.4 = (bf16[3,256,256]{2,1,0:T(8,128)(2,1)S(1)}, bf16[3,256,256]{2,1,0:T(8,128)(2,1)S(1)}, u32[]{:S(2)}, u32[]{:S(2)}) collective-permute-start(bf16[3,256,256]{2,1,0:T(8,128)(2,1)S(1)} %get-tuple-element.32.refs_1_.refs_3_), channel_id=1, source_target_pairs={{0,2},{2,0},{4,6},{6,4},{8,10},{10,8},{12,14},{14,12},{16,18},{18,... | collective-permute-start | bytes 1179656 | tf_op jit(solution)/shard_map/ppermute | solution.py:226
  23.3 1.8 %shard_map.66 = (bf16[3,256,256]{2,1,0:T(8,128)(2,1)S(1)}, bf16[3,256,256]{2,1,0:T(8,128)(2,1)S(1)}) custom-call(s32[1]{0:T(128)} %bitcast.odd_ref, s32[6,5]{1,0:T(8,128)S(1)} %copy-done.3, bf16[6,5,256,256]{3,2,1,0:T(8,128)(2,1)S(1)} %get-tuple-element.30.blocks_ref, bf16[3,256,256]{2,1,0:T(8,128)(2,1)S(1)} %get-tuple-element.33.refs_0_.refs_4_, ...), custom_call_target="tpu_custom_call" | custom-call | flops 4000000000 | bytes 1024 | tf_op jit(solution)/shard_map/pallas_call | solution.py:152
  25.2 1.4 %collective-permute-start.9 = (bf16[3,256,256]{2,1,0:T(8,128)(2,1)S(1)}, bf16[3,256,256]{2,1,0:T(8,128)(2,1)S(1)}, u32[]{:S(2)}, u32[]{:S(2)}) collective-permute-start(bf16[3,256,256]{2,1,0:T(8,128)(2,1)S(1)} %get-tuple-element.35.refs_6_.refs_0_.refs_3_), channel_id=1, source_target_pairs={{0,30},{2,4},{4,2},{6,8},{8,6},{10,12},{12,10},{14,16},{16,14},{18... | collective-permute-start | bytes 1179656 | tf_op jit(solution)/shard_map/ppermute | solution.py:226
  26.6 11.2 %collective-permute-done.3.refs_2_ = bf16[3,256,256]{2,1,0:T(8,128)(2,1)S(1)} collective-permute-done((bf16[3,256,256]{2,1,0:T(8,128)(2,1)S(1)}, bf16[3,256,256]{2,1,0:T(8,128)(2,1)S(1)}, u32[]{:S(2)}, u32[]{:S(2)}) %collective-permute-start.3) | collective-permute-done | bytes 393248 | tf_op jit(solution)/shard_map/ppermute | solution.py:226
  37.8 1.8 %shard_map.67 = (bf16[3,256,256]{2,1,0:T(8,128)(2,1)S(1)}, bf16[3,256,256]{2,1,0:T(8,128)(2,1)S(1)}) custom-call(s32[1]{0:T(128)} %bitcast.odd_ref, s32[6,5]{1,0:T(8,128)S(1)} %copy-done.3, bf16[6,5,256,256]{3,2,1,0:T(8,128)(2,1)S(1)} %get-tuple-element.30.blocks_ref, bf16[3,256,256]{2,1,0:T(8,128)(2,1)S(1)} %get-tuple-element.31.refs_4_.refs_0_.refs_3_, ...), custom_call_target="tpu_custom_call" | custom-call | flops 4000000000 | bytes 1024 | tf_op jit(solution)/shard_map/pallas_call | solution.py:152
  39.8 1.9 %collective-permute-done.9.refs_2_ = bf16[3,256,256]{2,1,0:T(8,128)(2,1)S(1)} collective-permute-done((bf16[3,256,256]{2,1,0:T(8,128)(2,1)S(1)}, bf16[3,256,256]{2,1,0:T(8,128)(2,1)S(1)}, u32[]{:S(2)}, u32[]{:S(2)}) %collective-permute-start.9) | collective-permute-done | bytes 393248 | tf_op jit(solution)/shard_map/ppermute | solution.py:226
  41.7 2.3 %shard_map.70 = (bf16[3,256,256]{2,1,0:T(8,128)(2,1)S(1)}, bf16[3,256,256]{2,1,0:T(8,128)(2,1)S(1)}, bf16[256,512]{1,0:T(8,128)(2,1)S(1)}) custom-call(s32[1]{0:T(128)} %bitcast.odd_ref, s32[6,5]{1,0:T(8,128)S(1)} %copy-done.3, bf16[6,5,256,256]{3,2,1,0:T(8,128)(2,1)S(1)} %get-tuple-element.30.blocks_ref, ...), custom_call_target="tpu_custom_call" | custom-call | flops 4000000000 | bytes 1024 | tf_op jit(solution)/shard_map/pallas_call | solution.py:152
  44.1 4.4 %collective-permute-start.17 = (bf16[256,512]{1,0:T(8,128)(2,1)S(1)}, bf16[256,512]{1,0:T(8,128)(2,1)S(1)}, u32[]{:S(2)}, u32[]{:S(2)}) collective-permute-start(bf16[256,512]{1,0:T(8,128)(2,1)S(1)} %get-tuple-element.42.refs_0_), channel_id=1, source_target_pairs={{0,8},{2,10},{4,12},{6,14},{8,0},{10,2},{12,4},{14,6},{16,24},{18,... | collective-permute-start | bytes 786440 | tf_op jit(solution)/shard_map/ppermute | solution.py:226
  53.2 1.8 %collective-permute-done.17.refs_1_ = bf16[256,512]{1,0:T(8,128)(2,1)S(1)} collective-permute-done((bf16[256,512]{1,0:T(8,128)(2,1)S(1)}, bf16[256,512]{1,0:T(8,128)(2,1)S(1)}, u32[]{:S(2)}, u32[]{:S(2)}) %collective-permute-start.17) | collective-permute-done | bytes 262176 | tf_op jit(solution)/shard_map/ppermute | solution.py:226
  58.7 2.7 %collective-permute-done.13.refs_4_.refs_2_ = bf16[3,256,256]{2,1,0:T(8,128)(2,1)S(1)} collective-permute-done((bf16[3,256,256]{2,1,0:T(8,128)(2,1)S(1)}, bf16[3,256,256]{2,1,0:T(8,128)(2,1)S(1)}, u32[]{:S(2)}, u32[]{:S(2)}) %collective-permute-start.13) | collective-permute-done | bytes 393248 | tf_op jit(solution)/shard_map/ppermute | solution.py:226
  61.4 2.2 %collective-permute-done.12.refs_2_ = bf16[3,256,256]{2,1,0:T(8,128)(2,1)S(1)} collective-permute-done((bf16[3,256,256]{2,1,0:T(8,128)(2,1)S(1)}, bf16[3,256,256]{2,1,0:T(8,128)(2,1)S(1)}, u32[]{:S(2)}, u32[]{:S(2)}) %collective-permute-start.12) | collective-permute-done | bytes 393248 | tf_op jit(solution)/shard_map/ppermute | solution.py:226
  68.4 1.4 collective-permute-done.15.refs_4_.refs_2_
  69.8 2.2 %shard_map.73.refs_4_ = bf16[1024,512]{1,0:T(8,128)(2,1)S(1)} custom-call(s32[1]{0:T(128)} %bitcast.1.own_ref, s32[1,1024]{1,0:T(1,128)S(1)} %reshape.15.order_ref, bf16[256,512]{1,0:T(8,128)(2,1)S(1)} %get-tuple-element.42.refs_0_, bf16[256,512]{1,0:T(8,128)(2,1)S(1)} %collective-permute-done.17.refs_1_, ...), custom_call_target="tpu_custom_call" | custom-call | flops 4000000000 | bytes 1024 | tf_op jit(solution)/shard_map/pallas_call | solution.py:215
  72.0 6.2 %collective-permute-done.16.refs_3_ = bf16[3,256,256]{2,1,0:T(8,128)(2,1)S(1)} collective-permute-done((bf16[3,256,256]{2,1,0:T(8,128)(2,1)S(1)}, bf16[3,256,256]{2,1,0:T(8,128)(2,1)S(1)}, u32[]{:S(2)}, u32[]{:S(2)}) %collective-permute-start.16) | collective-permute-done | bytes 393248 | tf_op jit(solution)/shard_map/ppermute | solution.py:226
  80.6 8.1 %collective-permute-done.20.refs_5_.refs_3_ = bf16[3,256,256]{2,1,0:T(8,128)(2,1)S(1)} collective-permute-done((bf16[3,256,256]{2,1,0:T(8,128)(2,1)S(1)}, bf16[3,256,256]{2,1,0:T(8,128)(2,1)S(1)}, u32[]{:S(2)}, u32[]{:S(2)}) %collective-permute-start.20) | collective-permute-done | bytes 393248 | tf_op jit(solution)/shard_map/ppermute | solution.py:226
  89.7 1.7 %collective-permute-start.28 = (bf16[3,256,256]{2,1,0:T(8,128)(2,1)S(1)}, bf16[3,256,256]{2,1,0:T(8,128)(2,1)S(1)}, u32[]{:S(2)}, u32[]{:S(2)}) collective-permute-start(bf16[3,256,256]{2,1,0:T(8,128)(2,1)S(1)} %get-tuple-element.50.refs_1_.refs_5_), channel_id=1, source_target_pairs={{0,2},{2,0},{4,6},{6,4},{8,10},{10,8},{12,14},{14,12},{16,18},{18,... | collective-permute-start | bytes 1179656 | tf_op jit(solution)/shard_map/ppermute | solution.py:226
  93.6 1.8 %shard_map.79 = (bf16[3,256,256]{2,1,0:T(8,128)(2,1)S(1)}, bf16[3,256,256]{2,1,0:T(8,128)(2,1)S(1)}) custom-call(s32[1]{0:T(128)} %bitcast.odd_ref, s32[6,5]{1,0:T(8,128)S(1)} %copy-done.3, bf16[6,5,256,256]{3,2,1,0:T(8,128)(2,1)S(1)} %copy-done.5, bf16[3,256,256]{2,1,0:T(8,128)(2,1)S(1)} %get-tuple-element.49.refs_0_.refs_4_, ...), custom_call_target="tpu_custom_call" | custom-call | flops 4000000000 | bytes 1024 | tf_op jit(solution)/shard_map/pallas_call | solution.py:152
  95.8 1.3 collective-permute-start.30
  97.2 14.9 %collective-permute-done.21.refs_2_ = bf16[3,256,256]{2,1,0:T(8,128)(2,1)S(1)} collective-permute-done((bf16[3,256,256]{2,1,0:T(8,128)(2,1)S(1)}, bf16[3,256,256]{2,1,0:T(8,128)(2,1)S(1)}, u32[]{:S(2)}, u32[]{:S(2)}) %collective-permute-start.21) | collective-permute-done | bytes 393248 | tf_op jit(solution)/shard_map/ppermute | solution.py:226
  112.0 1.8 %shard_map.77 = (bf16[3,256,256]{2,1,0:T(8,128)(2,1)S(1)}, bf16[3,256,256]{2,1,0:T(8,128)(2,1)S(1)}) custom-call(s32[1]{0:T(128)} %bitcast.odd_ref, s32[6,5]{1,0:T(8,128)S(1)} %copy-done.3, bf16[6,5,256,256]{3,2,1,0:T(8,128)(2,1)S(1)} %copy-done.5, bf16[3,256,256]{2,1,0:T(8,128)(2,1)S(1)} %shard_map.75.refs_0_.refs_4_, ...), custom_call_target="tpu_custom_call" | custom-call | flops 4000000000 | bytes 1024 | tf_op jit(solution)/shard_map/pallas_call | solution.py:152
  114.0 2.2 %collective-permute-done.29.refs_2_ = bf16[3,256,256]{2,1,0:T(8,128)(2,1)S(1)} collective-permute-done((bf16[3,256,256]{2,1,0:T(8,128)(2,1)S(1)}, bf16[3,256,256]{2,1,0:T(8,128)(2,1)S(1)}, u32[]{:S(2)}, u32[]{:S(2)}) %collective-permute-start.29) | collective-permute-done | bytes 393248 | tf_op jit(solution)/shard_map/ppermute | solution.py:226
  116.3 1.8 %shard_map.80 = (bf16[3,256,256]{2,1,0:T(8,128)(2,1)S(1)}, bf16[3,256,256]{2,1,0:T(8,128)(2,1)S(1)}) custom-call(s32[1]{0:T(128)} %bitcast.odd_ref, s32[6,5]{1,0:T(8,128)S(1)} %copy-done.3, bf16[6,5,256,256]{3,2,1,0:T(8,128)(2,1)S(1)} %copy-done.5, bf16[3,256,256]{2,1,0:T(8,128)(2,1)S(1)} %get-tuple-element.51.refs_0_.refs_4_, ...), custom_call_target="tpu_custom_call" | custom-call | flops 4000000000 | bytes 1024 | tf_op jit(solution)/shard_map/pallas_call | solution.py:152
  118.2 11.3 %collective-permute-done.23.refs_2_ = bf16[3,256,256]{2,1,0:T(8,128)(2,1)S(1)} collective-permute-done((bf16[3,256,256]{2,1,0:T(8,128)(2,1)S(1)}, bf16[3,256,256]{2,1,0:T(8,128)(2,1)S(1)}, u32[]{:S(2)}, u32[]{:S(2)}) %collective-permute-start.23) | collective-permute-done | bytes 393248 | tf_op jit(solution)/shard_map/ppermute | solution.py:226
  129.6 1.8 %shard_map.78 = (bf16[3,256,256]{2,1,0:T(8,128)(2,1)S(1)}, bf16[3,256,256]{2,1,0:T(8,128)(2,1)S(1)}) custom-call(s32[1]{0:T(128)} %bitcast.odd_ref, s32[6,5]{1,0:T(8,128)S(1)} %copy-done.3, bf16[6,5,256,256]{3,2,1,0:T(8,128)(2,1)S(1)} %copy-done.5, bf16[3,256,256]{2,1,0:T(8,128)(2,1)S(1)} %get-tuple-element.45.refs_0_.refs_4_, ...), custom_call_target="tpu_custom_call" | custom-call | flops 4000000000 | bytes 1024 | tf_op jit(solution)/shard_map/pallas_call | solution.py:152
  131.5 2.2 %collective-permute-done.31.refs_2_ = bf16[3,256,256]{2,1,0:T(8,128)(2,1)S(1)} collective-permute-done((bf16[3,256,256]{2,1,0:T(8,128)(2,1)S(1)}, bf16[3,256,256]{2,1,0:T(8,128)(2,1)S(1)}, u32[]{:S(2)}, u32[]{:S(2)}) %collective-permute-start.31) | collective-permute-done | bytes 393248 | tf_op jit(solution)/shard_map/ppermute | solution.py:226
  133.8 2.6 %shard_map.81.refs_6_ = bf16[6,256,512]{2,1,0:T(8,128)(2,1)} custom-call(s32[1]{0:T(128)} %bitcast.odd_ref, s32[6,5]{1,0:T(8,128)S(1)} %copy-done.3, bf16[6,5,256,256]{3,2,1,0:T(8,128)(2,1)S(1)} %copy-done.5, bf16[3,256,256]{2,1,0:T(8,128)(2,1)S(1)} %get-tuple-element.53.refs_0_, bf16[3,256,256]{2,1,0:T(8,128)(2,1)S(1)} %get-tuple-element.54.refs_1_, ...), custom_call_target="tpu_custom_call" | custom-call | flops 4000000000 | bytes 1024 | tf_op jit(solution)/shard_map/pallas_call | solution.py:152
  136.4 2.3 %collective-permute-done.25.refs_2_ = bf16[3,256,256]{2,1,0:T(8,128)(2,1)S(1)} collective-permute-done((bf16[3,256,256]{2,1,0:T(8,128)(2,1)S(1)}, bf16[3,256,256]{2,1,0:T(8,128)(2,1)S(1)}, u32[]{:S(2)}, u32[]{:S(2)}) %collective-permute-start.25) | collective-permute-done | bytes 393248 | tf_op jit(solution)/shard_map/ppermute | solution.py:226
  138.7 2.6 %shard_map.82 = bf16[6,256,512]{2,1,0:T(8,128)(2,1)} custom-call(s32[1]{0:T(128)} %bitcast.odd_ref, s32[6,5]{1,0:T(8,128)S(1)} %copy-done.3, bf16[6,5,256,256]{3,2,1,0:T(8,128)(2,1)S(1)} %copy-done.5, bf16[3,256,256]{2,1,0:T(8,128)(2,1)S(1)} %get-tuple-element.47.refs_0_, ...), custom_call_target="tpu_custom_call", output_to_operand_aliasing={{}: (9, {})} | custom-call | flops 4000000000 | bytes 1024 | tf_op jit(solution)/shard_map/pallas_call | solution.py:152
  (73 shorter events, 25.5 us)
Async XLA Ops:
  2.0 16.3 %collective-permute-start.1 = (bf16[3,256,256]{2,1,0:T(8,128)(2,1)S(1)}, bf16[3,256,256]{2,1,0:T(8,128)(2,1)S(1)}, u32[]{:S(2)}, u32[]{:S(2)}) collective-permute-start(bf16[3,256,256]{2,1,0:T(8,128)(2,1)S(1)} %get-tuple-element.55.refs_0_.refs_4_), channel_id=1, source_target_pairs={{0,30},{2,4},{4,2},{6,8},{8,6},{10,12},{12,10},{14,16},{16,14},{18... | collective-permute-start | bytes 1179656 | tf_op jit(solution)/shard_map/ppermute | solution.py:226
  3.2 14.7 %collective-permute-start.2 = (bf16[64,512]{1,0:T(8,128)(2,1)}, bf16[64,512]{1,0:T(8,128)(2,1)S(1)}, u32[]{:S(2)}, u32[]{:S(2)}) collective-permute-start(bf16[64,512]{1,0:T(8,128)(2,1)} %refs_4_.1), channel_id=1, source_target_pairs={{0,4},{2,6},{4,0},{6,2},{8,12},{10,14},{12,8},{14,10},{16,20},{18,... | collective-permute-start | bytes 196616 | tf_op jit(solution)/shard_map/ppermute | solution.py:226
  5.9 17.4 %collective-permute-start.5 = (bf16[3,256,256]{2,1,0:T(8,128)(2,1)S(1)}, bf16[3,256,256]{2,1,0:T(8,128)(2,1)S(1)}, u32[]{:S(2)}, u32[]{:S(2)}) collective-permute-start(bf16[3,256,256]{2,1,0:T(8,128)(2,1)S(1)} %get-tuple-element.33.refs_0_.refs_4_), channel_id=1, source_target_pairs={{0,30},{2,4},{4,2},{6,8},{8,6},{10,12},{12,10},{14,16},{16,14},{18... | collective-permute-start | bytes 1179656 | tf_op jit(solution)/shard_map/ppermute | solution.py:226
  7.7 15.6 %collective-permute-start.6 = (bf16[3,256,256]{2,1,0:T(8,128)(2,1)S(1)}, bf16[3,256,256]{2,1,0:T(8,128)(2,1)S(1)}, u32[]{:S(2)}, u32[]{:S(2)}) collective-permute-start(bf16[3,256,256]{2,1,0:T(8,128)(2,1)S(1)} %get-tuple-element.34.refs_1_.refs_5_), channel_id=1, source_target_pairs={{0,2},{2,0},{4,6},{6,4},{8,10},{10,8},{12,14},{14,12},{16,18},{18,... | collective-permute-start | bytes 1179656 | tf_op jit(solution)/shard_map/ppermute | solution.py:226
  20.4 6.2 %collective-permute-start.4 = (bf16[3,256,256]{2,1,0:T(8,128)(2,1)S(1)}, bf16[3,256,256]{2,1,0:T(8,128)(2,1)S(1)}, u32[]{:S(2)}, u32[]{:S(2)}) collective-permute-start(bf16[3,256,256]{2,1,0:T(8,128)(2,1)S(1)} %get-tuple-element.32.refs_1_.refs_3_), channel_id=1, source_target_pairs={{0,2},{2,0},{4,6},{6,4},{8,10},{10,8},{12,14},{14,12},{16,18},{18,... | collective-permute-start | bytes 1179656 | tf_op jit(solution)/shard_map/ppermute | solution.py:226
  21.8 15.9 %collective-permute-start.3 = (bf16[3,256,256]{2,1,0:T(8,128)(2,1)S(1)}, bf16[3,256,256]{2,1,0:T(8,128)(2,1)S(1)}, u32[]{:S(2)}, u32[]{:S(2)}) collective-permute-start(bf16[3,256,256]{2,1,0:T(8,128)(2,1)S(1)} %get-tuple-element.31.refs_4_.refs_0_.refs_3_), channel_id=1, source_target_pairs={{0,30},{2,4},{4,2},{6,8},{8,6},{10,12},{12,10},{14,16},{16,14},{18... | collective-permute-start | bytes 1179656 | tf_op jit(solution)/shard_map/ppermute | solution.py:226
  22.1 17.6 %collective-permute-start.11 = (bf16[128,512]{1,0:T(8,128)(2,1)S(1)}, bf16[128,512]{1,0:T(8,128)(2,1)S(1)}, u32[]{:S(2)}, u32[]{:S(2)}) collective-permute-start(bf16[128,512]{1,0:T(8,128)(2,1)S(1)} %get-tuple-element.39.refs_6_), channel_id=1, source_target_pairs={{0,16},{2,18},{4,20},{6,22},{8,24},{10,26},{12,28},{14,30},{16,0},... | collective-permute-start | bytes 393224 | tf_op jit(solution)/shard_map/ppermute | solution.py:226
  25.1 14.7 %collective-permute-start.10 = (bf16[3,256,256]{2,1,0:T(8,128)(2,1)S(1)}, bf16[3,256,256]{2,1,0:T(8,128)(2,1)S(1)}, u32[]{:S(2)}, u32[]{:S(2)}) collective-permute-start(bf16[3,256,256]{2,1,0:T(8,128)(2,1)S(1)} %get-tuple-element.38.refs_1_.refs_3_), channel_id=1, source_target_pairs={{0,2},{2,0},{4,6},{6,4},{8,10},{10,8},{12,14},{14,12},{16,18},{18,... | collective-permute-start | bytes 1179656 | tf_op jit(solution)/shard_map/ppermute | solution.py:226
  25.2 16.5 %collective-permute-start.9 = (bf16[3,256,256]{2,1,0:T(8,128)(2,1)S(1)}, bf16[3,256,256]{2,1,0:T(8,128)(2,1)S(1)}, u32[]{:S(2)}, u32[]{:S(2)}) collective-permute-start(bf16[3,256,256]{2,1,0:T(8,128)(2,1)S(1)} %get-tuple-element.35.refs_6_.refs_0_.refs_3_), channel_id=1, source_target_pairs={{0,30},{2,4},{4,2},{6,8},{8,6},{10,12},{12,10},{14,16},{16,14},{18... | collective-permute-start | bytes 1179656 | tf_op jit(solution)/shard_map/ppermute | solution.py:226
  39.6 9.7 %collective-permute-start.8 = (bf16[3,256,256]{2,1,0:T(8,128)(2,1)S(1)}, bf16[3,256,256]{2,1,0:T(8,128)(2,1)S(1)}, u32[]{:S(2)}, u32[]{:S(2)}) collective-permute-start(bf16[3,256,256]{2,1,0:T(8,128)(2,1)S(1)} %get-tuple-element.37.refs_1_), channel_id=1, source_target_pairs={{0,2},{2,0},{4,6},{6,4},{8,10},{10,8},{12,14},{14,12},{16,18},{18,... | collective-permute-start | bytes 1179656 | tf_op jit(solution)/shard_map/ppermute | solution.py:226
  39.7 12.2 %collective-permute-start.7 = (bf16[3,256,256]{2,1,0:T(8,128)(2,1)S(1)}, bf16[3,256,256]{2,1,0:T(8,128)(2,1)S(1)}, u32[]{:S(2)}, u32[]{:S(2)}) collective-permute-start(bf16[3,256,256]{2,1,0:T(8,128)(2,1)S(1)} %get-tuple-element.36.refs_0_.refs_8_), channel_id=1, source_target_pairs={{0,30},{2,4},{4,2},{6,8},{8,6},{10,12},{12,10},{14,16},{16,14},{18... | collective-permute-start | bytes 1179656 | tf_op jit(solution)/shard_map/ppermute | solution.py:226
  44.0 24.4 %collective-permute-start.18 = (bf16[256,512]{1,0:T(8,128)(2,1)S(1)}, bf16[256,512]{1,0:T(8,128)(2,1)S(1)}, u32[]{:S(2)}, u32[]{:S(2)}) collective-permute-start(bf16[256,512]{1,0:T(8,128)(2,1)S(1)} %get-tuple-element.42.refs_0_), channel_id=1, source_target_pairs={{0,2},{2,0},{4,6},{6,4},{8,10},{10,8},{12,14},{14,12},{16,18},{18,... | collective-permute-start | bytes 786440 | tf_op jit(solution)/shard_map/ppermute | solution.py:226
  44.1 10.9 %collective-permute-start.17 = (bf16[256,512]{1,0:T(8,128)(2,1)S(1)}, bf16[256,512]{1,0:T(8,128)(2,1)S(1)}, u32[]{:S(2)}, u32[]{:S(2)}) collective-permute-start(bf16[256,512]{1,0:T(8,128)(2,1)S(1)} %get-tuple-element.42.refs_0_), channel_id=1, source_target_pairs={{0,8},{2,10},{4,12},{6,14},{8,0},{10,2},{12,4},{14,6},{16,24},{18,... | collective-permute-start | bytes 786440 | tf_op jit(solution)/shard_map/ppermute | solution.py:226
  48.6 7.6 %collective-permute-start.14 = (bf16[3,256,256]{2,1,0:T(8,128)(2,1)S(1)}, bf16[3,256,256]{2,1,0:T(8,128)(2,1)S(1)}, u32[]{:S(2)}, u32[]{:S(2)}) collective-permute-start(bf16[3,256,256]{2,1,0:T(8,128)(2,1)S(1)} %get-tuple-element.41.refs_1_), channel_id=1, source_target_pairs={{0,2},{2,0},{4,6},{6,4},{8,10},{10,8},{12,14},{14,12},{16,18},{18,... | collective-permute-start | bytes 1179656 | tf_op jit(solution)/shard_map/ppermute | solution.py:226
  50.6 10.8 %collective-permute-start.13 = (bf16[3,256,256]{2,1,0:T(8,128)(2,1)S(1)}, bf16[3,256,256]{2,1,0:T(8,128)(2,1)S(1)}, u32[]{:S(2)}, u32[]{:S(2)}) collective-permute-start(bf16[3,256,256]{2,1,0:T(8,128)(2,1)S(1)} %shard_map.68.refs_4_.refs_0_), channel_id=1, source_target_pairs={{0,1},{1,0},{2,3},{3,2},{4,5},{5,4},{6,7},{7,6},{8,9},{9,8},{10,11... | collective-permute-start | bytes 1179656 | tf_op jit(solution)/shard_map/ppermute | solution.py:226
  51.9 11.7 %collective-permute-start.12 = (bf16[3,256,256]{2,1,0:T(8,128)(2,1)S(1)}, bf16[3,256,256]{2,1,0:T(8,128)(2,1)S(1)}, u32[]{:S(2)}, u32[]{:S(2)}) collective-permute-start(bf16[3,256,256]{2,1,0:T(8,128)(2,1)S(1)} %get-tuple-element.40.refs_0_), channel_id=1, source_target_pairs={{0,30},{2,4},{4,2},{6,8},{8,6},{10,12},{12,10},{14,16},{16,14},{18... | collective-permute-start | bytes 1179656 | tf_op jit(solution)/shard_map/ppermute | solution.py:226
  55.0 14.8 %collective-permute-start.15 = (bf16[3,256,256]{2,1,0:T(8,128)(2,1)S(1)}, bf16[3,256,256]{2,1,0:T(8,128)(2,1)S(1)}, u32[]{:S(2)}, u32[]{:S(2)}) collective-permute-start(bf16[3,256,256]{2,1,0:T(8,128)(2,1)S(1)} %shard_map.69.refs_4_.refs_0_), channel_id=1, source_target_pairs={{0,1},{1,0},{2,3},{3,2},{4,5},{5,4},{6,7},{7,6},{8,9},{9,8},{10,11... | collective-permute-start | bytes 1179656 | tf_op jit(solution)/shard_map/ppermute | solution.py:226
  56.2 13.6 %collective-permute-start.19 = (bf16[256,512]{1,0:T(8,128)(2,1)S(1)}, bf16[256,512]{1,0:T(8,128)(2,1)}, u32[]{:S(2)}, u32[]{:S(2)}) collective-permute-start(bf16[256,512]{1,0:T(8,128)(2,1)S(1)} %collective-permute-done.17.refs_1_), channel_id=1, source_target_pairs={{0,2},{2,0},{4,6},{6,4},{8,10},{10,8},{12,14},{14,12},{16,18},{18,... | collective-permute-start | bytes 786440 | tf_op jit(solution)/shard_map/ppermute | solution.py:226
  64.9 13.3 %collective-permute-start.16 = (bf16[3,256,256]{2,1,0:T(8,128)(2,1)S(1)}, bf16[3,256,256]{2,1,0:T(8,128)(2,1)S(1)}, u32[]{:S(2)}, u32[]{:S(2)}) collective-permute-start(bf16[3,256,256]{2,1,0:T(8,128)(2,1)S(1)} %shard_map.72.refs_1_), channel_id=1, source_target_pairs={{0,1},{1,0},{2,3},{3,2},{4,5},{5,4},{6,7},{7,6},{8,9},{9,8},{10,11... | collective-permute-start | bytes 1179656 | tf_op jit(solution)/shard_map/ppermute | solution.py:226
  78.8 9.9 %collective-permute-start.20 = (bf16[3,256,256]{2,1,0:T(8,128)(2,1)S(1)}, bf16[3,256,256]{2,1,0:T(8,128)(2,1)S(1)}, u32[]{:S(2)}, u32[]{:S(2)}) collective-permute-start(bf16[3,256,256]{2,1,0:T(8,128)(2,1)S(1)} %get-tuple-element.43.refs_1_), channel_id=1, source_target_pairs={{0,1},{1,0},{2,3},{3,2},{4,5},{5,4},{6,7},{7,6},{8,9},{9,8},{10,11... | collective-permute-start | bytes 1179656 | tf_op jit(solution)/shard_map/ppermute | solution.py:226
  80.1 12.1 %collective-permute-start.27 = (bf16[3,256,256]{2,1,0:T(8,128)(2,1)S(1)}, bf16[3,256,256]{2,1,0:T(8,128)(2,1)S(1)}, u32[]{:S(2)}, u32[]{:S(2)}) collective-permute-start(bf16[3,256,256]{2,1,0:T(8,128)(2,1)S(1)} %get-tuple-element.49.refs_0_.refs_4_), channel_id=1, source_target_pairs={{0,30},{2,4},{4,2},{6,8},{8,6},{10,12},{12,10},{14,16},{16,14},{18... | collective-permute-start | bytes 1179656 | tf_op jit(solution)/shard_map/ppermute | solution.py:226
  89.7 3.1 %collective-permute-start.28 = (bf16[3,256,256]{2,1,0:T(8,128)(2,1)S(1)}, bf16[3,256,256]{2,1,0:T(8,128)(2,1)S(1)}, u32[]{:S(2)}, u32[]{:S(2)}) collective-permute-start(bf16[3,256,256]{2,1,0:T(8,128)(2,1)S(1)} %get-tuple-element.50.refs_1_.refs_5_), channel_id=1, source_target_pairs={{0,2},{2,0},{4,6},{6,4},{8,10},{10,8},{12,14},{14,12},{16,18},{18,... | collective-permute-start | bytes 1179656 | tf_op jit(solution)/shard_map/ppermute | solution.py:226
  91.5 5.7 %collective-permute-start.22 = (bf16[3,256,256]{2,1,0:T(8,128)(2,1)S(1)}, bf16[3,256,256]{2,1,0:T(8,128)(2,1)S(1)}, u32[]{:S(2)}, u32[]{:S(2)}) collective-permute-start(bf16[3,256,256]{2,1,0:T(8,128)(2,1)S(1)} %get-tuple-element.44.refs_1_.refs_5_), channel_id=1, source_target_pairs={{0,2},{2,0},{4,6},{6,4},{8,10},{10,8},{12,14},{14,12},{16,18},{18,... | collective-permute-start | bytes 1179656 | tf_op jit(solution)/shard_map/ppermute | solution.py:226
  92.1 19.9 %collective-permute-start.21 = (bf16[3,256,256]{2,1,0:T(8,128)(2,1)S(1)}, bf16[3,256,256]{2,1,0:T(8,128)(2,1)S(1)}, u32[]{:S(2)}, u32[]{:S(2)}) collective-permute-start(bf16[3,256,256]{2,1,0:T(8,128)(2,1)S(1)} %shard_map.75.refs_0_.refs_4_), channel_id=1, source_target_pairs={{0,30},{2,4},{4,2},{6,8},{8,6},{10,12},{12,10},{14,16},{16,14},{18... | collective-permute-start | bytes 1179656 | tf_op jit(solution)/shard_map/ppermute | solution.py:226
  95.4 20.9 %collective-permute-start.29 = (bf16[3,256,256]{2,1,0:T(8,128)(2,1)S(1)}, bf16[3,256,256]{2,1,0:T(8,128)(2,1)S(1)}, u32[]{:S(2)}, u32[]{:S(2)}) collective-permute-start(bf16[3,256,256]{2,1,0:T(8,128)(2,1)S(1)} %get-tuple-element.51.refs_0_.refs_4_), channel_id=1, source_target_pairs={{0,30},{2,4},{4,2},{6,8},{8,6},{10,12},{12,10},{14,16},{16,14},{18... | collective-permute-start | bytes 1179656 | tf_op jit(solution)/shard_map/ppermute | solution.py:226
  95.8 20.4 %collective-permute-start.30 = (bf16[3,256,256]{2,1,0:T(8,128)(2,1)S(1)}, bf16[3,256,256]{2,1,0:T(8,128)(2,1)S(1)}, u32[]{:S(2)}, u32[]{:S(2)}) collective-permute-start(bf16[3,256,256]{2,1,0:T(8,128)(2,1)S(1)} %get-tuple-element.52.refs_1_.refs_5_), channel_id=1, source_target_pairs={{0,2},{2,0},{4,6},{6,4},{8,10},{10,8},{12,14},{14,12},{16,18},{18,... | collective-permute-start | bytes 1179656 | tf_op jit(solution)/shard_map/ppermute | solution.py:226
  113.9 15.7 %collective-permute-start.23 = (bf16[3,256,256]{2,1,0:T(8,128)(2,1)S(1)}, bf16[3,256,256]{2,1,0:T(8,128)(2,1)S(1)}, u32[]{:S(2)}, u32[]{:S(2)}) collective-permute-start(bf16[3,256,256]{2,1,0:T(8,128)(2,1)S(1)} %get-tuple-element.45.refs_0_.refs_4_), channel_id=1, source_target_pairs={{0,30},{2,4},{4,2},{6,8},{8,6},{10,12},{12,10},{14,16},{16,14},{18... | collective-permute-start | bytes 1179656 | tf_op jit(solution)/shard_map/ppermute | solution.py:226
  113.9 15.6 %collective-permute-start.24 = (bf16[3,256,256]{2,1,0:T(8,128)(2,1)S(1)}, bf16[3,256,256]{2,1,0:T(8,128)(2,1)S(1)}, u32[]{:S(2)}, u32[]{:S(2)}) collective-permute-start(bf16[3,256,256]{2,1,0:T(8,128)(2,1)S(1)} %get-tuple-element.46.refs_1_.refs_5_), channel_id=1, source_target_pairs={{0,2},{2,0},{4,6},{6,4},{8,10},{10,8},{12,14},{14,12},{16,18},{18,... | collective-permute-start | bytes 1179656 | tf_op jit(solution)/shard_map/ppermute | solution.py:226
  118.1 15.7 %collective-permute-start.31 = (bf16[3,256,256]{2,1,0:T(8,128)(2,1)S(1)}, bf16[3,256,256]{2,1,0:T(8,128)(2,1)S(1)}, u32[]{:S(2)}, u32[]{:S(2)}) collective-permute-start(bf16[3,256,256]{2,1,0:T(8,128)(2,1)S(1)} %get-tuple-element.53.refs_0_), channel_id=1, source_target_pairs={{0,30},{2,4},{4,2},{6,8},{8,6},{10,12},{12,10},{14,16},{16,14},{18... | collective-permute-start | bytes 1179656 | tf_op jit(solution)/shard_map/ppermute | solution.py:226
  118.1 15.6 %collective-permute-start.32 = (bf16[3,256,256]{2,1,0:T(8,128)(2,1)S(1)}, bf16[3,256,256]{2,1,0:T(8,128)(2,1)S(1)}, u32[]{:S(2)}, u32[]{:S(2)}) collective-permute-start(bf16[3,256,256]{2,1,0:T(8,128)(2,1)S(1)} %get-tuple-element.54.refs_1_), channel_id=1, source_target_pairs={{0,2},{2,0},{4,6},{6,4},{8,10},{10,8},{12,14},{14,12},{16,18},{18,... | collective-permute-start | bytes 1179656 | tf_op jit(solution)/shard_map/ppermute | solution.py:226
  131.4 7.3 %collective-permute-start.25 = (bf16[3,256,256]{2,1,0:T(8,128)(2,1)S(1)}, bf16[3,256,256]{2,1,0:T(8,128)(2,1)S(1)}, u32[]{:S(2)}, u32[]{:S(2)}) collective-permute-start(bf16[3,256,256]{2,1,0:T(8,128)(2,1)S(1)} %get-tuple-element.47.refs_0_), channel_id=1, source_target_pairs={{0,30},{2,4},{4,2},{6,8},{8,6},{10,12},{12,10},{14,16},{16,14},{18... | collective-permute-start | bytes 1179656 | tf_op jit(solution)/shard_map/ppermute | solution.py:226
  131.5 7.2 %collective-permute-start.26 = (bf16[3,256,256]{2,1,0:T(8,128)(2,1)S(1)}, bf16[3,256,256]{2,1,0:T(8,128)(2,1)S(1)}, u32[]{:S(2)}, u32[]{:S(2)}) collective-permute-start(bf16[3,256,256]{2,1,0:T(8,128)(2,1)S(1)} %get-tuple-element.48.refs_1_), channel_id=1, source_target_pairs={{0,2},{2,0},{4,6},{6,4},{8,10},{10,8},{12,14},{14,12},{16,18},{18,... | collective-permute-start | bytes 1179656 | tf_op jit(solution)/shard_map/ppermute | solution.py:226
  (8 other events, 107.7 us)

commit v5 on v4

--- a/solution.py
+++ b/solution.py
@@ -190,6 +190,23 @@
     return list(result[: len(widths)]), list(result[len(widths) :])
 
 
+def wait_kernel(*refs):
+    del refs
+
+
+def after(arrays, later):
+    count = len(arrays)
+    return pl.pallas_call(
+        wait_kernel,
+        out_shape=[like(array) for array in arrays],
+        in_specs=[ANYWHERE] * (count + len(later)),
+        out_specs=[ANYWHERE] * count,
+        input_output_aliases={i: i for i in range(count)},
+        compiler_params=PARAMS,
+        cost_estimate=cost(LONG),
+    )(*arrays, *later)
+
+
 def ordered_kernel(bands, count, own_ref, order_ref, *refs):
     rows, out_ref = refs[:count], refs[-1]
     total = out_ref.shape[0]
@@ -302,38 +319,33 @@
     before = [nothing for _ in chunks]
     for n in range(2):
         for c in chunks:
-            step = gather.step if c == (chunks[0], chunks[-1])[n] else apply_step
+            step = gather.step if (n, c) in ((0, 0), (1, chunks[-1])) else apply_step
             new = step(shared, (0, 1), state[c], beside[c], before[c], later=state[c - 1][:1] if c or before[0][0] is not None else ())
             before[c], state[c] = state[c], new
             beside[c] = halos(new)
 
-    inner, inner_others, outer, outer_others = [], [], [], []
-    waits = []
+    inner, outer, outer_others = [], [], []
     for c in chunks:
-        step = gather.step if c == chunks[-1] else apply_step
-        inner += apply_step(shared, (1,), state[c], beside[c][1:], before[c][1:], later=outer[-1:])
-        outer += step(shared, (0,), state[c], beside[c][:1], before[c][:1], later=waits + inner[-1:])
-        outer_others.append(over_band(outer[-1]))
-        if c != chunks[-1]:
-            inner_others.append(over_band(inner[-1]))
-            waits = inner_others[-1]
-        if c == 0:
-            rows, owners = gather.finish()
+        made = apply_step(shared, (0, 1), state[c], beside[c], before[c], later=state[c - 1][:1] if c == 0 else outer[-1:])
+        outer.append(made[0])
+        inner.append(made[1])
+        outer_others.append(over_band(made[0]))
+    rows, owners = gather.finish()
+    inner = after(inner, outer_others[0])
     order = band_order.reshape(elems, -1)[jnp.bitwise_xor(me, owners)].reshape(1, -1)
-    matrix = ordered_rows(lax.axis_index("band").astype(jnp.int32).reshape(1), order, rows, bands, later=outer_others[0])
+    matrix = ordered_rows(lax.axis_index("band").astype(jnp.int32).reshape(1), order, rows, bands, later=outer_others[-1] + list(inner[:1]))
 
     def by_band(own, others):
         return list(own) + [other[shift] for shift in range(bands - 1) for other in others]
 
     pieces = by_band(outer, outer_others)
-    rotated, last = rotate(pieces, matrix, 0, [chunk], passed=inner[-1:])
+    rotated, inner = rotate(pieces, matrix, 0, [chunk], passed=inner)
     far = [cross(rotated[0])]
-    inner[-1] = last[0]
-    inner_others.append(over_band(inner[-1]))
+    inner_others = [over_band(part) for part in inner]
     for c in chunks[1:]:
-        rotated += rotate(pieces, matrix, starts[c], [chunk], later=inner_others[-1])[0]
+        rotated += rotate(pieces, matrix, starts[c], [chunk], later=())[0]
         far.append(cross(rotated[c]))
-    rotated_inner, _ = rotate(by_band(inner, inner_others), matrix, 0, [chunk for _ in chunks])
+    rotated_inner, _ = rotate(by_band(inner, inner_others), matrix, 0, [chunk for _ in chunks], later=far[1:])
     state = [[rotated[c], rotated_inner[c]] for c in chunks]
     beside = [[far[c], intra(rotated_inner[c])] for c in chunks]
 
@@ -345,10 +357,11 @@
             beside[c] = halos(new)
     out = None
     for c in chunks:
-        (out,) = apply_step(
-            shared, (0, 1), state[c], beside[c], before[c],
-            out=out, out_column=starts[c], out_shape=start_bands.shape,
-        )
+        for sides in ((0, 1),) if c < chunks[-1] else ((1,), (0,)):
+            (out,) = apply_step(
+                shared, sides, state[c], [beside[c][side] for side in sides], [before[c][side] for side in sides],
+                out=out, out_column=starts[c], out_shape=start_bands.shape,
+            )
     return out
 
 

time: 142 us -> 136 us (0.958)
  the two profiles are of different devices: /device:TPU:25 before, /device:TPU:1 now
where the time goes in v5:
time: 136 us
  waiting for transfers between devices  62.2 us (46%)
  starting transfers between devices  40.1 us (29%)
  Pallas kernels  29.2 us (21%)
  local copies, waits for them, and re-layouts  4.13 us (3%)
    ppermute x33, waiting for transfers between devices, exchange(): lax.ppermute(array, axis, [(i, partner(i)) for i in range(lax.axis_size(a...  62.2 us
    ppermute x33, starting transfers between devices, exchange(): lax.ppermute(array, axis, [(i, partner(i)) for i in range(lax.axis_size(a...  40.1 us
    pallas_call x13, Pallas kernels, apply_step(): pl.pallas_call(functools.partial(step_kernel, sides, firsts, out_column,...  25.5 us
  transfers between devices with their start and end apart: 33, of which 14 were waited for; matrix products, arithmetic and copies ran while one was open for 1% of the time, Pallas kernels for 19%

profile of v5, /device:TPU:1, one launch (start us, length us, event | category | flops | bytes accessed | tf_op | source)
XLA Modules:
  0.0 136.0 jit_solution(13103544489636191145)
XLA Ops:
  1.4 2.6 %collective-permute-start.1 = (bf16[3,256,256]{2,1,0:T(8,128)(2,1)S(1)}, bf16[3,256,256]{2,1,0:T(8,128)(2,1)S(1)}, u32[]{:S(2)}, u32[]{:S(2)}) collective-permute-start(bf16[3,256,256]{2,1,0:T(8,128)(2,1)S(1)} %get-tuple-element.69.refs_0_.refs_4_), channel_id=1, source_target_pairs={{0,30},{2,4},{4,2},{6,8},{8,6},{10,12},{12,10},{14,16},{16,14},{18... | collective-permute-start | bytes 1179656 | tf_op jit(solution)/shard_map/ppermute | solution.py:243
  5.3 2.1 %copy-done.1 = bf16[6,5,256,256]{3,2,1,0:T(8,128)(2,1)S(1)} copy-done((bf16[6,5,256,256]{3,2,1,0:T(8,128)(2,1)S(1)}, bf16[6,5,256,256]{3,2,1,0:T(8,128)(2,1)}, u32[]{:S(2)}) %copy-start.1) | copy-done | bytes 3932184
  7.8 3.9 %collective-permute-start.5 = (bf16[3,256,256]{2,1,0:T(8,128)(2,1)S(1)}, bf16[3,256,256]{2,1,0:T(8,128)(2,1)S(1)}, u32[]{:S(2)}, u32[]{:S(2)}) collective-permute-start(bf16[3,256,256]{2,1,0:T(8,128)(2,1)S(1)} %get-tuple-element.40.refs_0_.refs_4_), channel_id=1, source_target_pairs={{0,30},{2,4},{4,2},{6,8},{8,6},{10,12},{12,10},{14,16},{16,14},{18... | collective-permute-start | bytes 1179656 | tf_op jit(solution)/shard_map/ppermute | solution.py:243
  11.7 7.0 %collective-permute-done.2.refs_5_ = bf16[64,512]{1,0:T(8,128)(2,1)S(1)} collective-permute-done((bf16[64,512]{1,0:T(8,128)(2,1)}, bf16[64,512]{1,0:T(8,128)(2,1)S(1)}, u32[]{:S(2)}, u32[]{:S(2)}) %collective-permute-start.2) | collective-permute-done | bytes 65568 | tf_op jit(solution)/shard_map/ppermute | solution.py:243
  18.7 2.0 %shard_map.65 = (bf16[3,256,256]{2,1,0:T(8,128)(2,1)S(1)}, bf16[3,256,256]{2,1,0:T(8,128)(2,1)S(1)}, bf16[128,512]{1,0:T(8,128)(2,1)S(1)}) custom-call(s32[1]{0:T(128)} %bitcast.odd_ref, s32[6,5]{1,0:T(8,128)S(1)} %copy-done.3, bf16[6,5,256,256]{3,2,1,0:T(8,128)(2,1)S(1)} %get-tuple-element.37.blocks_ref, ...), custom_call_target="tpu_custom_call" | custom-call | flops 4000000000 | bytes 1024 | tf_op jit(solution)/shard_map/pallas_call | solution.py:152
  22.4 3.6 %collective-permute-start.4 = (bf16[3,256,256]{2,1,0:T(8,128)(2,1)S(1)}, bf16[3,256,256]{2,1,0:T(8,128)(2,1)S(1)}, u32[]{:S(2)}, u32[]{:S(2)}) collective-permute-start(bf16[3,256,256]{2,1,0:T(8,128)(2,1)S(1)} %get-tuple-element.39.refs_1_.refs_5_), channel_id=1, source_target_pairs={{0,2},{2,0},{4,6},{6,4},{8,10},{10,8},{12,14},{14,12},{16,18},{18,... | collective-permute-start | bytes 1179656 | tf_op jit(solution)/shard_map/ppermute | solution.py:243
  26.0 1.8 %shard_map.66 = (bf16[3,256,256]{2,1,0:T(8,128)(2,1)S(1)}, bf16[3,256,256]{2,1,0:T(8,128)(2,1)S(1)}) custom-call(s32[1]{0:T(128)} %bitcast.odd_ref, s32[6,5]{1,0:T(8,128)S(1)} %copy-done.3, bf16[6,5,256,256]{3,2,1,0:T(8,128)(2,1)S(1)} %get-tuple-element.37.blocks_ref, bf16[3,256,256]{2,1,0:T(8,128)(2,1)S(1)} %get-tuple-element.40.refs_0_.refs_4_, ...), custom_call_target="tpu_custom_call" | custom-call | flops 4000000000 | bytes 1024 | tf_op jit(solution)/shard_map/pallas_call | solution.py:152
  29.7 9.8 %collective-permute-done.3.refs_2_ = bf16[3,256,256]{2,1,0:T(8,128)(2,1)S(1)} collective-permute-done((bf16[3,256,256]{2,1,0:T(8,128)(2,1)S(1)}, bf16[3,256,256]{2,1,0:T(8,128)(2,1)S(1)}, u32[]{:S(2)}, u32[]{:S(2)}) %collective-permute-start.3) | collective-permute-done | bytes 393248 | tf_op jit(solution)/shard_map/ppermute | solution.py:243
  39.5 1.8 %shard_map.67 = (bf16[3,256,256]{2,1,0:T(8,128)(2,1)S(1)}, bf16[3,256,256]{2,1,0:T(8,128)(2,1)S(1)}) custom-call(s32[1]{0:T(128)} %bitcast.odd_ref, s32[6,5]{1,0:T(8,128)S(1)} %copy-done.3, bf16[6,5,256,256]{3,2,1,0:T(8,128)(2,1)S(1)} %get-tuple-element.37.blocks_ref, bf16[3,256,256]{2,1,0:T(8,128)(2,1)S(1)} %get-tuple-element.38.refs_4_.refs_0_, ...), custom_call_target="tpu_custom_call" | custom-call | flops 4000000000 | bytes 1024 | tf_op jit(solution)/shard_map/pallas_call | solution.py:152
  41.4 2.5 %collective-permute-start.7 = (bf16[3,256,256]{2,1,0:T(8,128)(2,1)S(1)}, bf16[3,256,256]{2,1,0:T(8,128)(2,1)S(1)}, u32[]{:S(2)}, u32[]{:S(2)}) collective-permute-start(bf16[3,256,256]{2,1,0:T(8,128)(2,1)S(1)} %get-tuple-element.43.refs_8_.refs_0_), channel_id=1, source_target_pairs={{0,30},{2,4},{4,2},{6,8},{8,6},{10,12},{12,10},{14,16},{16,14},{18... | collective-permute-start | bytes 1179656 | tf_op jit(solution)/shard_map/ppermute | solution.py:243
  44.8 2.4 %shard_map.68 = (bf16[3,256,256]{2,1,0:T(8,128)(2,1)S(1)}, bf16[3,256,256]{2,1,0:T(8,128)(2,1)S(1)}, bf16[256,512]{1,0:T(8,128)(2,1)S(1)}) custom-call(s32[1]{0:T(128)} %bitcast.odd_ref, s32[6,5]{1,0:T(8,128)S(1)} %copy-done.3, bf16[6,5,256,256]{3,2,1,0:T(8,128)(2,1)S(1)} %get-tuple-element.37.blocks_ref, ...), custom_call_target="tpu_custom_call" | custom-call | flops 4000000000 | bytes 1024 | tf_op jit(solution)/shard_map/pallas_call | solution.py:152
  47.2 2.1 %collective-permute-start.12 = (bf16[3,256,256]{2,1,0:T(8,128)(2,1)S(1)}, bf16[3,256,256]{2,1,0:T(8,128)(2,1)S(1)}, u32[]{:S(2)}, u32[]{:S(2)}) collective-permute-start(bf16[3,256,256]{2,1,0:T(8,128)(2,1)S(1)} %get-tuple-element.47.refs_6_.refs_0_), channel_id=1, source_target_pairs={{0,30},{2,4},{4,2},{6,8},{8,6},{10,12},{12,10},{14,16},{16,14},{18... | collective-permute-start | bytes 1179656 | tf_op jit(solution)/shard_map/ppermute | solution.py:243
  49.5 1.8 %shard_map.69 = (bf16[3,256,256]{2,1,0:T(8,128)(2,1)S(1)}, bf16[3,256,256]{2,1,0:T(8,128)(2,1)S(1)}) custom-call(s32[1]{0:T(128)} %bitcast.odd_ref, s32[6,5]{1,0:T(8,128)S(1)} %copy-done.3, bf16[6,5,256,256]{3,2,1,0:T(8,128)(2,1)S(1)} %get-tuple-element.37.blocks_ref, bf16[3,256,256]{2,1,0:T(8,128)(2,1)S(1)} %get-tuple-element.43.refs_8_.refs_0_, ...), custom_call_target="tpu_custom_call" | custom-call | flops 4000000000 | bytes 1024 | tf_op jit(solution)/shard_map/pallas_call | solution.py:152
  52.6 4.3 %collective-permute-start.16 = (bf16[256,512]{1,0:T(8,128)(2,1)S(1)}, bf16[256,512]{1,0:T(8,128)(2,1)S(1)}, u32[]{:S(2)}, u32[]{:S(2)}) collective-permute-start(bf16[256,512]{1,0:T(8,128)(2,1)S(1)} %get-tuple-element.51.refs_0_), channel_id=1, source_target_pairs={{0,8},{2,10},{4,12},{6,14},{8,0},{10,2},{12,4},{14,6},{16,24},{18,... | collective-permute-start | bytes 786440 | tf_op jit(solution)/shard_map/ppermute | solution.py:243
  56.9 2.4 %collective-permute-done.12.refs_2_ = bf16[3,256,256]{2,1,0:T(8,128)(2,1)S(1)} collective-permute-done((bf16[3,256,256]{2,1,0:T(8,128)(2,1)S(1)}, bf16[3,256,256]{2,1,0:T(8,128)(2,1)S(1)}, u32[]{:S(2)}, u32[]{:S(2)}) %collective-permute-start.12) | collective-permute-done | bytes 393248 | tf_op jit(solution)/shard_map/ppermute | solution.py:243
  59.3 1.8 %shard_map.70 = (bf16[3,256,256]{2,1,0:T(8,128)(2,1)S(1)}, bf16[3,256,256]{2,1,0:T(8,128)(2,1)S(1)}) custom-call(s32[1]{0:T(128)} %bitcast.odd_ref, s32[6,5]{1,0:T(8,128)S(1)} %copy-done.3, bf16[6,5,256,256]{3,2,1,0:T(8,128)(2,1)S(1)} %get-tuple-element.37.blocks_ref, bf16[3,256,256]{2,1,0:T(8,128)(2,1)S(1)} %get-tuple-element.47.refs_6_.refs_0_, ...), custom_call_target="tpu_custom_call" | custom-call | flops 4000000000 | bytes 1024 | tf_op jit(solution)/shard_map/pallas_call | solution.py:152
  65.1 5.5 %collective-permute-done.15.refs_4_.refs_3_ = bf16[3,256,256]{2,1,0:T(8,128)(2,1)S(1)} collective-permute-done((bf16[3,256,256]{2,1,0:T(8,128)(2,1)S(1)}, bf16[3,256,256]{2,1,0:T(8,128)(2,1)S(1)}, u32[]{:S(2)}, u32[]{:S(2)}) %collective-permute-start.15) | collective-permute-done | bytes 393248 | tf_op jit(solution)/shard_map/ppermute | solution.py:243
  74.6 1.8 %collective-permute-start.21 = (bf16[3,256,256]{2,1,0:T(8,128)(2,1)S(1)}, bf16[3,256,256]{2,1,0:T(8,128)(2,1)S(1)}, u32[]{:S(2)}, u32[]{:S(2)}) collective-permute-start(bf16[3,256,256]{2,1,0:T(8,128)(2,1)S(1)} %shard_map.73.refs_0_.refs_4_), channel_id=1, source_target_pairs={{0,30},{2,4},{4,2},{6,8},{8,6},{10,12},{12,10},{14,16},{16,14},{18... | collective-permute-start | bytes 1179656 | tf_op jit(solution)/shard_map/ppermute | solution.py:243
  76.5 7.2 %collective-permute-done.19.refs_2_ = bf16[3,256,256]{2,1,0:T(8,128)(2,1)S(1)} collective-permute-done((bf16[3,256,256]{2,1,0:T(8,128)(2,1)S(1)}, bf16[3,256,256]{2,1,0:T(8,128)(2,1)S(1)}, u32[]{:S(2)}, u32[]{:S(2)}) %collective-permute-start.19) | collective-permute-done | bytes 393248 | tf_op jit(solution)/shard_map/ppermute | solution.py:243
  83.7 7.8 %collective-permute-done.20.refs_3_ = bf16[3,256,256]{2,1,0:T(8,128)(2,1)S(1)} collective-permute-done((bf16[3,256,256]{2,1,0:T(8,128)(2,1)S(1)}, bf16[3,256,256]{2,1,0:T(8,128)(2,1)S(1)}, u32[]{:S(2)}, u32[]{:S(2)}) %collective-permute-start.20) | collective-permute-done | bytes 393248 | tf_op jit(solution)/shard_map/ppermute | solution.py:243
  94.5 1.8 %shard_map.78 = (bf16[3,256,256]{2,1,0:T(8,128)(2,1)S(1)}, bf16[3,256,256]{2,1,0:T(8,128)(2,1)S(1)}) custom-call(s32[1]{0:T(128)} %bitcast.odd_ref, s32[6,5]{1,0:T(8,128)S(1)} %copy-done.3, bf16[6,5,256,256]{3,2,1,0:T(8,128)(2,1)S(1)} %copy-done.5, bf16[3,256,256]{2,1,0:T(8,128)(2,1)S(1)} %get-tuple-element.63.refs_0_.refs_4_, ...), custom_call_target="tpu_custom_call" | custom-call | flops 4000000000 | bytes 1024 | tf_op jit(solution)/shard_map/pallas_call | solution.py:152
  97.3 2.2 %collective-permute-start.30 = (bf16[3,256,256]{2,1,0:T(8,128)(2,1)S(1)}, bf16[3,256,256]{2,1,0:T(8,128)(2,1)S(1)}, u32[]{:S(2)}, u32[]{:S(2)}) collective-permute-start(bf16[3,256,256]{2,1,0:T(8,128)(2,1)S(1)} %get-tuple-element.66.refs_1_.refs_5_), channel_id=1, source_target_pairs={{0,2},{2,0},{4,6},{6,4},{8,10},{10,8},{12,14},{14,12},{16,18},{18,... | collective-permute-start | bytes 1179656 | tf_op jit(solution)/shard_map/ppermute | solution.py:243
  99.6 1.8 %shard_map.76 = (bf16[3,256,256]{2,1,0:T(8,128)(2,1)S(1)}, bf16[3,256,256]{2,1,0:T(8,128)(2,1)S(1)}) custom-call(s32[1]{0:T(128)} %bitcast.odd_ref, s32[6,5]{1,0:T(8,128)S(1)} %copy-done.3, bf16[6,5,256,256]{3,2,1,0:T(8,128)(2,1)S(1)} %copy-done.5, bf16[3,256,256]{2,1,0:T(8,128)(2,1)S(1)} %shard_map.73.refs_0_.refs_4_, ...), custom_call_target="tpu_custom_call" | custom-call | flops 4000000000 | bytes 1024 | tf_op jit(solution)/shard_map/pallas_call | solution.py:152
  101.4 1.9 %collective-permute-start.24 = (bf16[3,256,256]{2,1,0:T(8,128)(2,1)S(1)}, bf16[3,256,256]{2,1,0:T(8,128)(2,1)S(1)}, u32[]{:S(2)}, u32[]{:S(2)}) collective-permute-start(bf16[3,256,256]{2,1,0:T(8,128)(2,1)S(1)} %get-tuple-element.60.refs_1_.refs_3_), channel_id=1, source_target_pairs={{0,2},{2,0},{4,6},{6,4},{8,10},{10,8},{12,14},{14,12},{16,18},{18,... | collective-permute-start | bytes 1179656 | tf_op jit(solution)/shard_map/ppermute | solution.py:243
  103.3 11.4 %collective-permute-done.29.refs_2_ = bf16[3,256,256]{2,1,0:T(8,128)(2,1)S(1)} collective-permute-done((bf16[3,256,256]{2,1,0:T(8,128)(2,1)S(1)}, bf16[3,256,256]{2,1,0:T(8,128)(2,1)S(1)}, u32[]{:S(2)}, u32[]{:S(2)}) %collective-permute-start.29) | collective-permute-done | bytes 393248 | tf_op jit(solution)/shard_map/ppermute | solution.py:243
  114.7 1.8 %shard_map.79 = (bf16[3,256,256]{2,1,0:T(8,128)(2,1)S(1)}, bf16[3,256,256]{2,1,0:T(8,128)(2,1)S(1)}) custom-call(s32[1]{0:T(128)} %bitcast.odd_ref, s32[6,5]{1,0:T(8,128)S(1)} %copy-done.3, bf16[6,5,256,256]{3,2,1,0:T(8,128)(2,1)S(1)} %copy-done.5, bf16[3,256,256]{2,1,0:T(8,128)(2,1)S(1)} %get-tuple-element.65.refs_0_.refs_4_, ...), custom_call_target="tpu_custom_call" | custom-call | flops 4000000000 | bytes 1024 | tf_op jit(solution)/shard_map/pallas_call | solution.py:152
  116.5 2.5 %collective-permute-start.31 = (bf16[3,256,256]{2,1,0:T(8,128)(2,1)S(1)}, bf16[3,256,256]{2,1,0:T(8,128)(2,1)S(1)}, u32[]{:S(2)}, u32[]{:S(2)}) collective-permute-start(bf16[3,256,256]{2,1,0:T(8,128)(2,1)S(1)} %get-tuple-element.67.refs_0_), channel_id=1, source_target_pairs={{0,30},{2,4},{4,2},{6,8},{8,6},{10,12},{12,10},{14,16},{16,14},{18... | collective-permute-start | bytes 1179656 | tf_op jit(solution)/shard_map/ppermute | solution.py:243
  120.5 1.8 %shard_map.77 = (bf16[3,256,256]{2,1,0:T(8,128)(2,1)S(1)}, bf16[3,256,256]{2,1,0:T(8,128)(2,1)S(1)}) custom-call(s32[1]{0:T(128)} %bitcast.odd_ref, s32[6,5]{1,0:T(8,128)S(1)} %copy-done.3, bf16[6,5,256,256]{3,2,1,0:T(8,128)(2,1)S(1)} %copy-done.5, bf16[3,256,256]{2,1,0:T(8,128)(2,1)S(1)} %get-tuple-element.59.refs_0_.refs_3_, ...), custom_call_target="tpu_custom_call" | custom-call | flops 4000000000 | bytes 1024 | tf_op jit(solution)/shard_map/pallas_call | solution.py:152
  124.7 2.6 %shard_map.80.refs_4_ = bf16[6,256,512]{2,1,0:T(8,128)(2,1)} custom-call(s32[1]{0:T(128)} %bitcast.odd_ref, s32[6,5]{1,0:T(8,128)S(1)} %copy-done.3, bf16[6,5,256,256]{3,2,1,0:T(8,128)(2,1)S(1)} %copy-done.5, bf16[3,256,256]{2,1,0:T(8,128)(2,1)S(1)} %get-tuple-element.67.refs_0_, bf16[3,256,256]{2,1,0:T(8,128)(2,1)S(1)} %get-tuple-element.68.refs_1_, ...), custom_call_target="tpu_custom_call" | custom-call | flops 4000000000 | bytes 1024 | tf_op jit(solution)/shard_map/pallas_call | solution.py:152
  127.2 2.0 %shard_map.81.refs_4_ = bf16[6,256,512]{2,1,0:T(8,128)(2,1)} custom-call(s32[1]{0:T(128)} %bitcast.odd_ref, s32[6,5]{1,0:T(8,128)S(1)} %copy-done.3, bf16[6,5,256,256]{3,2,1,0:T(8,128)(2,1)S(1)} %copy-done.5, bf16[3,256,256]{2,1,0:T(8,128)(2,1)S(1)} %get-tuple-element.61.refs_0_, ...), custom_call_target="tpu_custom_call", output_to_operand_aliasing={{}: (7, {})} | custom-call | flops 4000000000 | bytes 1024 | tf_op jit(solution)/shard_map/pallas_call | solution.py:152
  129.3 4.5 %collective-permute-done.25.refs_2_ = bf16[3,256,256]{2,1,0:T(8,128)(2,1)S(1)} collective-permute-done((bf16[3,256,256]{2,1,0:T(8,128)(2,1)S(1)}, bf16[3,256,256]{2,1,0:T(8,128)(2,1)S(1)}, u32[]{:S(2)}, u32[]{:S(2)}) %collective-permute-start.25) | collective-permute-done | bytes 393248 | tf_op jit(solution)/shard_map/ppermute | solution.py:243
  133.8 2.0 %shard_map.82 = bf16[6,256,512]{2,1,0:T(8,128)(2,1)} custom-call(s32[1]{0:T(128)} %bitcast.odd_ref, s32[6,5]{1,0:T(8,128)S(1)} %copy-done.3, bf16[6,5,256,256]{3,2,1,0:T(8,128)(2,1)S(1)} %copy-done.5, bf16[3,256,256]{2,1,0:T(8,128)(2,1)S(1)} %get-tuple-element.61.refs_0_, ...), custom_call_target="tpu_custom_call", output_to_operand_aliasing={{}: (7, {})} | custom-call | flops 4000000000 | bytes 1024 | tf_op jit(solution)/shard_map/pallas_call | solution.py:152
  (75 shorter events, 24.9 us)
Async XLA Ops:
  1.3 4.0 %collective-permute-start = (bf16[3,256,256]{2,1,0:T(8,128)(2,1)S(1)}, bf16[3,256,256]{2,1,0:T(8,128)(2,1)S(1)}, u32[]{:S(2)}, u32[]{:S(2)}) collective-permute-start(bf16[3,256,256]{2,1,0:T(8,128)(2,1)S(1)} %get-tuple-element.70.refs_1_.refs_5_), channel_id=1, source_target_pairs={{0,2},{2,0},{4,6},{6,4},{8,10},{10,8},{12,14},{14,12},{16,18},{18,... | collective-permute-start | bytes 1179656 | tf_op jit(solution)/shard_map/ppermute | solution.py:243
  1.4 17.3 %collective-permute-start.1 = (bf16[3,256,256]{2,1,0:T(8,128)(2,1)S(1)}, bf16[3,256,256]{2,1,0:T(8,128)(2,1)S(1)}, u32[]{:S(2)}, u32[]{:S(2)}) collective-permute-start(bf16[3,256,256]{2,1,0:T(8,128)(2,1)S(1)} %get-tuple-element.69.refs_0_.refs_4_), channel_id=1, source_target_pairs={{0,30},{2,4},{4,2},{6,8},{8,6},{10,12},{12,10},{14,16},{16,14},{18... | collective-permute-start | bytes 1179656 | tf_op jit(solution)/shard_map/ppermute | solution.py:243
  4.0 14.7 %collective-permute-start.2 = (bf16[64,512]{1,0:T(8,128)(2,1)}, bf16[64,512]{1,0:T(8,128)(2,1)S(1)}, u32[]{:S(2)}, u32[]{:S(2)}) collective-permute-start(bf16[64,512]{1,0:T(8,128)(2,1)} %refs_4_.1), channel_id=1, source_target_pairs={{0,4},{2,6},{4,0},{6,2},{8,12},{10,14},{12,8},{14,10},{16,20},{18,... | collective-permute-start | bytes 196616 | tf_op jit(solution)/shard_map/ppermute | solution.py:243
  7.8 18.2 %collective-permute-start.5 = (bf16[3,256,256]{2,1,0:T(8,128)(2,1)S(1)}, bf16[3,256,256]{2,1,0:T(8,128)(2,1)S(1)}, u32[]{:S(2)}, u32[]{:S(2)}) collective-permute-start(bf16[3,256,256]{2,1,0:T(8,128)(2,1)S(1)} %get-tuple-element.40.refs_0_.refs_4_), channel_id=1, source_target_pairs={{0,30},{2,4},{4,2},{6,8},{8,6},{10,12},{12,10},{14,16},{16,14},{18... | collective-permute-start | bytes 1179656 | tf_op jit(solution)/shard_map/ppermute | solution.py:243
  11.7 14.3 %collective-permute-start.6 = (bf16[3,256,256]{2,1,0:T(8,128)(2,1)S(1)}, bf16[3,256,256]{2,1,0:T(8,128)(2,1)S(1)}, u32[]{:S(2)}, u32[]{:S(2)}) collective-permute-start(bf16[3,256,256]{2,1,0:T(8,128)(2,1)S(1)} %get-tuple-element.41.refs_1_.refs_5_), channel_id=1, source_target_pairs={{0,2},{2,0},{4,6},{6,4},{8,10},{10,8},{12,14},{14,12},{16,18},{18,... | collective-permute-start | bytes 1179656 | tf_op jit(solution)/shard_map/ppermute | solution.py:243
  20.7 18.8 %collective-permute-start.3 = (bf16[3,256,256]{2,1,0:T(8,128)(2,1)S(1)}, bf16[3,256,256]{2,1,0:T(8,128)(2,1)S(1)}, u32[]{:S(2)}, u32[]{:S(2)}) collective-permute-start(bf16[3,256,256]{2,1,0:T(8,128)(2,1)S(1)} %get-tuple-element.38.refs_4_.refs_0_), channel_id=1, source_target_pairs={{0,30},{2,4},{4,2},{6,8},{8,6},{10,12},{12,10},{14,16},{16,14},{18... | collective-permute-start | bytes 1179656 | tf_op jit(solution)/shard_map/ppermute | solution.py:243
  22.4 17.1 %collective-permute-start.4 = (bf16[3,256,256]{2,1,0:T(8,128)(2,1)S(1)}, bf16[3,256,256]{2,1,0:T(8,128)(2,1)S(1)}, u32[]{:S(2)}, u32[]{:S(2)}) collective-permute-start(bf16[3,256,256]{2,1,0:T(8,128)(2,1)S(1)} %get-tuple-element.39.refs_1_.refs_5_), channel_id=1, source_target_pairs={{0,2},{2,0},{4,6},{6,4},{8,10},{10,8},{12,14},{14,12},{16,18},{18,... | collective-permute-start | bytes 1179656 | tf_op jit(solution)/shard_map/ppermute | solution.py:243
  27.8 16.1 %collective-permute-start.10 = (bf16[3,256,256]{2,1,0:T(8,128)(2,1)S(1)}, bf16[3,256,256]{2,1,0:T(8,128)(2,1)S(1)}, u32[]{:S(2)}, u32[]{:S(2)}) collective-permute-start(bf16[3,256,256]{2,1,0:T(8,128)(2,1)S(1)} %get-tuple-element.45.refs_1_.refs_5_), channel_id=1, source_target_pairs={{0,2},{2,0},{4,6},{6,4},{8,10},{10,8},{12,14},{14,12},{16,18},{18,... | collective-permute-start | bytes 1179656 | tf_op jit(solution)/shard_map/ppermute | solution.py:243
  27.9 16.9 %collective-permute-start.9 = (bf16[3,256,256]{2,1,0:T(8,128)(2,1)S(1)}, bf16[3,256,256]{2,1,0:T(8,128)(2,1)S(1)}, u32[]{:S(2)}, u32[]{:S(2)}) collective-permute-start(bf16[3,256,256]{2,1,0:T(8,128)(2,1)S(1)} %get-tuple-element.42.refs_6_.refs_0_.refs_4_), channel_id=1, source_target_pairs={{0,30},{2,4},{4,2},{6,8},{8,6},{10,12},{12,10},{14,16},{16,14},{18... | collective-permute-start | bytes 1179656 | tf_op jit(solution)/shard_map/ppermute | solution.py:243
  28.0 15.9 %collective-permute-start.11 = (bf16[128,512]{1,0:T(8,128)(2,1)S(1)}, bf16[128,512]{1,0:T(8,128)(2,1)S(1)}, u32[]{:S(2)}, u32[]{:S(2)}) collective-permute-start(bf16[128,512]{1,0:T(8,128)(2,1)S(1)} %get-tuple-element.46.refs_6_), channel_id=1, source_target_pairs={{0,16},{2,18},{4,20},{6,22},{8,24},{10,26},{12,28},{14,30},{16,0},... | collective-permute-start | bytes 393224 | tf_op jit(solution)/shard_map/ppermute | solution.py:243
  41.4 8.1 %collective-permute-start.7 = (bf16[3,256,256]{2,1,0:T(8,128)(2,1)S(1)}, bf16[3,256,256]{2,1,0:T(8,128)(2,1)S(1)}, u32[]{:S(2)}, u32[]{:S(2)}) collective-permute-start(bf16[3,256,256]{2,1,0:T(8,128)(2,1)S(1)} %get-tuple-element.43.refs_8_.refs_0_), channel_id=1, source_target_pairs={{0,30},{2,4},{4,2},{6,8},{8,6},{10,12},{12,10},{14,16},{16,14},{18... | collective-permute-start | bytes 1179656 | tf_op jit(solution)/shard_map/ppermute | solution.py:243
  43.9 5.6 %collective-permute-start.8 = (bf16[3,256,256]{2,1,0:T(8,128)(2,1)S(1)}, bf16[3,256,256]{2,1,0:T(8,128)(2,1)S(1)}, u32[]{:S(2)}, u32[]{:S(2)}) collective-permute-start(bf16[3,256,256]{2,1,0:T(8,128)(2,1)S(1)} %get-tuple-element.44.refs_1_), channel_id=1, source_target_pairs={{0,2},{2,0},{4,6},{6,4},{8,10},{10,8},{12,14},{14,12},{16,18},{18,... | collective-permute-start | bytes 1179656 | tf_op jit(solution)/shard_map/ppermute | solution.py:243
  47.2 12.1 %collective-permute-start.12 = (bf16[3,256,256]{2,1,0:T(8,128)(2,1)S(1)}, bf16[3,256,256]{2,1,0:T(8,128)(2,1)S(1)}, u32[]{:S(2)}, u32[]{:S(2)}) collective-permute-start(bf16[3,256,256]{2,1,0:T(8,128)(2,1)S(1)} %get-tuple-element.47.refs_6_.refs_0_), channel_id=1, source_target_pairs={{0,30},{2,4},{4,2},{6,8},{8,6},{10,12},{12,10},{14,16},{16,14},{18... | collective-permute-start | bytes 1179656 | tf_op jit(solution)/shard_map/ppermute | solution.py:243
  49.3 10.0 %collective-permute-start.13 = (bf16[3,256,256]{2,1,0:T(8,128)(2,1)S(1)}, bf16[3,256,256]{2,1,0:T(8,128)(2,1)S(1)}, u32[]{:S(2)}, u32[]{:S(2)}) collective-permute-start(bf16[3,256,256]{2,1,0:T(8,128)(2,1)S(1)} %get-tuple-element.49.refs_1_), channel_id=1, source_target_pairs={{0,2},{2,0},{4,6},{6,4},{8,10},{10,8},{12,14},{14,12},{16,18},{18,... | collective-permute-start | bytes 1179656 | tf_op jit(solution)/shard_map/ppermute | solution.py:243
  51.3 12.4 %collective-permute-start.14 = (bf16[3,256,256]{2,1,0:T(8,128)(2,1)S(1)}, bf16[3,256,256]{2,1,0:T(8,128)(2,1)S(1)}, u32[]{:S(2)}, u32[]{:S(2)}) collective-permute-start(bf16[3,256,256]{2,1,0:T(8,128)(2,1)S(1)} %get-tuple-element.48.refs_6_.refs_0_), channel_id=1, source_target_pairs={{0,1},{1,0},{2,3},{3,2},{4,5},{5,4},{6,7},{7,6},{8,9},{9,8},{10,11... | collective-permute-start | bytes 1179656 | tf_op jit(solution)/shard_map/ppermute | solution.py:243
  52.6 10.6 %collective-permute-start.16 = (bf16[256,512]{1,0:T(8,128)(2,1)S(1)}, bf16[256,512]{1,0:T(8,128)(2,1)S(1)}, u32[]{:S(2)}, u32[]{:S(2)}) collective-permute-start(bf16[256,512]{1,0:T(8,128)(2,1)S(1)} %get-tuple-element.51.refs_0_), channel_id=1, source_target_pairs={{0,8},{2,10},{4,12},{6,14},{8,0},{10,2},{12,4},{14,6},{16,24},{18,... | collective-permute-start | bytes 786440 | tf_op jit(solution)/shard_map/ppermute | solution.py:243
  61.1 9.5 %collective-permute-start.15 = (bf16[3,256,256]{2,1,0:T(8,128)(2,1)S(1)}, bf16[3,256,256]{2,1,0:T(8,128)(2,1)S(1)}, u32[]{:S(2)}, u32[]{:S(2)}) collective-permute-start(bf16[3,256,256]{2,1,0:T(8,128)(2,1)S(1)} %get-tuple-element.50.refs_1_), channel_id=1, source_target_pairs={{0,1},{1,0},{2,3},{3,2},{4,5},{5,4},{6,7},{7,6},{8,9},{9,8},{10,11... | collective-permute-start | bytes 1179656 | tf_op jit(solution)/shard_map/ppermute | solution.py:243
  63.2 1.9 %collective-permute-start.18 = (bf16[256,512]{1,0:T(8,128)(2,1)S(1)}, bf16[256,512]{1,0:T(8,128)(2,1)S(1)}, u32[]{:S(2)}, u32[]{:S(2)}) collective-permute-start(bf16[256,512]{1,0:T(8,128)(2,1)S(1)} %collective-permute-done.16.refs_1_), channel_id=1, source_target_pairs={{0,2},{2,0},{4,6},{6,4},{8,10},{10,8},{12,14},{14,12},{16,18},{18,... | collective-permute-start | bytes 786440 | tf_op jit(solution)/shard_map/ppermute | solution.py:243
  72.5 11.2 %collective-permute-start.19 = (bf16[3,256,256]{2,1,0:T(8,128)(2,1)S(1)}, bf16[3,256,256]{2,1,0:T(8,128)(2,1)S(1)}, u32[]{:S(2)}, u32[]{:S(2)}) collective-permute-start(bf16[3,256,256]{2,1,0:T(8,128)(2,1)S(1)} %get-tuple-element.56.refs_0_), channel_id=1, source_target_pairs={{0,1},{1,0},{2,3},{3,2},{4,5},{5,4},{6,7},{7,6},{8,9},{9,8},{10,11... | collective-permute-start | bytes 1179656 | tf_op jit(solution)/shard_map/ppermute | solution.py:243
  73.8 17.7 %collective-permute-start.20 = (bf16[3,256,256]{2,1,0:T(8,128)(2,1)S(1)}, bf16[3,256,256]{2,1,0:T(8,128)(2,1)S(1)}, u32[]{:S(2)}, u32[]{:S(2)}) collective-permute-start(bf16[3,256,256]{2,1,0:T(8,128)(2,1)S(1)} %get-tuple-element.57.refs_1_), channel_id=1, source_target_pairs={{0,1},{1,0},{2,3},{3,2},{4,5},{5,4},{6,7},{7,6},{8,9},{9,8},{10,11... | collective-permute-start | bytes 1179656 | tf_op jit(solution)/shard_map/ppermute | solution.py:243
  74.6 16.9 %collective-permute-start.21 = (bf16[3,256,256]{2,1,0:T(8,128)(2,1)S(1)}, bf16[3,256,256]{2,1,0:T(8,128)(2,1)S(1)}, u32[]{:S(2)}, u32[]{:S(2)}) collective-permute-start(bf16[3,256,256]{2,1,0:T(8,128)(2,1)S(1)} %shard_map.73.refs_0_.refs_4_), channel_id=1, source_target_pairs={{0,30},{2,4},{4,2},{6,8},{8,6},{10,12},{12,10},{14,16},{16,14},{18... | collective-permute-start | bytes 1179656 | tf_op jit(solution)/shard_map/ppermute | solution.py:243
  76.4 18.1 %collective-permute-start.27 = (bf16[3,256,256]{2,1,0:T(8,128)(2,1)S(1)}, bf16[3,256,256]{2,1,0:T(8,128)(2,1)S(1)}, u32[]{:S(2)}, u32[]{:S(2)}) collective-permute-start(bf16[3,256,256]{2,1,0:T(8,128)(2,1)S(1)} %get-tuple-element.63.refs_0_.refs_4_), channel_id=1, source_target_pairs={{0,30},{2,4},{4,2},{6,8},{8,6},{10,12},{12,10},{14,16},{16,14},{18... | collective-permute-start | bytes 1179656 | tf_op jit(solution)/shard_map/ppermute | solution.py:243
  92.5 2.0 %collective-permute-start.28 = (bf16[3,256,256]{2,1,0:T(8,128)(2,1)S(1)}, bf16[3,256,256]{2,1,0:T(8,128)(2,1)S(1)}, u32[]{:S(2)}, u32[]{:S(2)}) collective-permute-start(bf16[3,256,256]{2,1,0:T(8,128)(2,1)S(1)} %get-tuple-element.64.refs_1_.refs_5_), channel_id=1, source_target_pairs={{0,2},{2,0},{4,6},{6,4},{8,10},{10,8},{12,14},{14,12},{16,18},{18,... | collective-permute-start | bytes 1179656 | tf_op jit(solution)/shard_map/ppermute | solution.py:243
  93.0 6.6 %collective-permute-start.22 = (bf16[3,256,256]{2,1,0:T(8,128)(2,1)S(1)}, bf16[3,256,256]{2,1,0:T(8,128)(2,1)S(1)}, u32[]{:S(2)}, u32[]{:S(2)}) collective-permute-start(bf16[3,256,256]{2,1,0:T(8,128)(2,1)S(1)} %get-tuple-element.58.refs_1_.refs_5_), channel_id=1, source_target_pairs={{0,2},{2,0},{4,6},{6,4},{8,10},{10,8},{12,14},{14,12},{16,18},{18,... | collective-permute-start | bytes 1179656 | tf_op jit(solution)/shard_map/ppermute | solution.py:243
  96.3 18.4 %collective-permute-start.29 = (bf16[3,256,256]{2,1,0:T(8,128)(2,1)S(1)}, bf16[3,256,256]{2,1,0:T(8,128)(2,1)S(1)}, u32[]{:S(2)}, u32[]{:S(2)}) collective-permute-start(bf16[3,256,256]{2,1,0:T(8,128)(2,1)S(1)} %get-tuple-element.65.refs_0_.refs_4_), channel_id=1, source_target_pairs={{0,30},{2,4},{4,2},{6,8},{8,6},{10,12},{12,10},{14,16},{16,14},{18... | collective-permute-start | bytes 1179656 | tf_op jit(solution)/shard_map/ppermute | solution.py:243
  97.3 17.4 %collective-permute-start.30 = (bf16[3,256,256]{2,1,0:T(8,128)(2,1)S(1)}, bf16[3,256,256]{2,1,0:T(8,128)(2,1)S(1)}, u32[]{:S(2)}, u32[]{:S(2)}) collective-permute-start(bf16[3,256,256]{2,1,0:T(8,128)(2,1)S(1)} %get-tuple-element.66.refs_1_.refs_5_), channel_id=1, source_target_pairs={{0,2},{2,0},{4,6},{6,4},{8,10},{10,8},{12,14},{14,12},{16,18},{18,... | collective-permute-start | bytes 1179656 | tf_op jit(solution)/shard_map/ppermute | solution.py:243
  101.4 19.1 %collective-permute-start.23 = (bf16[3,256,256]{2,1,0:T(8,128)(2,1)S(1)}, bf16[3,256,256]{2,1,0:T(8,128)(2,1)S(1)}, u32[]{:S(2)}, u32[]{:S(2)}) collective-permute-start(bf16[3,256,256]{2,1,0:T(8,128)(2,1)S(1)} %get-tuple-element.59.refs_0_.refs_3_), channel_id=1, source_target_pairs={{0,30},{2,4},{4,2},{6,8},{8,6},{10,12},{12,10},{14,16},{16,14},{18... | collective-permute-start | bytes 1179656 | tf_op jit(solution)/shard_map/ppermute | solution.py:243
  101.4 19.0 %collective-permute-start.24 = (bf16[3,256,256]{2,1,0:T(8,128)(2,1)S(1)}, bf16[3,256,256]{2,1,0:T(8,128)(2,1)S(1)}, u32[]{:S(2)}, u32[]{:S(2)}) collective-permute-start(bf16[3,256,256]{2,1,0:T(8,128)(2,1)S(1)} %get-tuple-element.60.refs_1_.refs_3_), channel_id=1, source_target_pairs={{0,2},{2,0},{4,6},{6,4},{8,10},{10,8},{12,14},{14,12},{16,18},{18,... | collective-permute-start | bytes 1179656 | tf_op jit(solution)/shard_map/ppermute | solution.py:243
  116.5 8.2 %collective-permute-start.31 = (bf16[3,256,256]{2,1,0:T(8,128)(2,1)S(1)}, bf16[3,256,256]{2,1,0:T(8,128)(2,1)S(1)}, u32[]{:S(2)}, u32[]{:S(2)}) collective-permute-start(bf16[3,256,256]{2,1,0:T(8,128)(2,1)S(1)} %get-tuple-element.67.refs_0_), channel_id=1, source_target_pairs={{0,30},{2,4},{4,2},{6,8},{8,6},{10,12},{12,10},{14,16},{16,14},{18... | collective-permute-start | bytes 1179656 | tf_op jit(solution)/shard_map/ppermute | solution.py:243
  119.1 5.6 %collective-permute-start.32 = (bf16[3,256,256]{2,1,0:T(8,128)(2,1)S(1)}, bf16[3,256,256]{2,1,0:T(8,128)(2,1)S(1)}, u32[]{:S(2)}, u32[]{:S(2)}) collective-permute-start(bf16[3,256,256]{2,1,0:T(8,128)(2,1)S(1)} %get-tuple-element.68.refs_1_), channel_id=1, source_target_pairs={{0,2},{2,0},{4,6},{6,4},{8,10},{10,8},{12,14},{14,12},{16,18},{18,... | collective-permute-start | bytes 1179656 | tf_op jit(solution)/shard_map/ppermute | solution.py:243
  122.3 5.0 %collective-permute-start.26 = (bf16[3,256,256]{2,1,0:T(8,128)(2,1)S(1)}, bf16[3,256,256]{2,1,0:T(8,128)(2,1)S(1)}, u32[]{:S(2)}, u32[]{:S(2)}) collective-permute-start(bf16[3,256,256]{2,1,0:T(8,128)(2,1)S(1)} %get-tuple-element.62.refs_1_), channel_id=1, source_target_pairs={{0,2},{2,0},{4,6},{6,4},{8,10},{10,8},{12,14},{14,12},{16,18},{18,... | collective-permute-start | bytes 1179656 | tf_op jit(solution)/shard_map/ppermute | solution.py:243
  122.3 11.5 %collective-permute-start.25 = (bf16[3,256,256]{2,1,0:T(8,128)(2,1)S(1)}, bf16[3,256,256]{2,1,0:T(8,128)(2,1)S(1)}, u32[]{:S(2)}, u32[]{:S(2)}) collective-permute-start(bf16[3,256,256]{2,1,0:T(8,128)(2,1)S(1)} %get-tuple-element.61.refs_0_), channel_id=1, source_target_pairs={{0,30},{2,4},{4,2},{6,8},{8,6},{10,12},{12,10},{14,16},{16,14},{18... | collective-permute-start | bytes 1179656 | tf_op jit(solution)/shard_map/ppermute | solution.py:243
  (9 other events, 116.5 us)

commit v6 on v5

--- a/solution.py
+++ b/solution.py
@@ -10,7 +10,7 @@
 GY = 3
 CHUNK = 256
 MIB = 1024 * 1024
-LONG = 4 * 10**9
+LONG, SHORT = 4 * 10**9, 10**8
 PARAMS = pltpu.CompilerParams(vmem_limit_bytes=16 * MIB)
 SMEM = pl.BlockSpec(memory_space=pltpu.SMEM)
 VMEM = pl.BlockSpec(memory_space=pltpu.VMEM)
@@ -41,37 +41,30 @@
     return copies
 
 
-def split_kernel(starts, width, held, waits, odd_ref, start_ref, *refs):
-    refs = list(refs)
+def split_kernel(starts, width, extra, passed, odd_ref, start_ref, *refs):
+    targets, sems = refs[extra : len(refs) - passed - 1], refs[-1]
     pairs = []
-    if held:
-        blocks_ref, refs = refs[0], refs[1:]
-    refs = refs[waits:]
-    sems = refs.pop()
-    if held:
-        pairs.append((blocks_ref, refs.pop(0)))
-    for n, target in enumerate(refs):
+    for n, target in enumerate(targets):
         rows = pl.ds(first_row(n % 2, odd_ref[0]), GY)
         pairs.append((start_ref.at[rows, :, pl.ds(starts[n // 2], width)], target))
     for copy in run_copies(pairs, sems):
         copy.wait()
 
 
-def split(odd, start_bands, starts, width, blocks=None, later=()):
-    basis = start_bands.shape[1]
-    held = [] if blocks is None else [blocks]
-    shapes = [pltpu.VMEM(b.shape, b.dtype) for b in held] + [bands_of(GY, basis, width)] * (2 * len(starts))
+def split(odd, start_bands, starts, width, passed, later):
+    basis, count = start_bands.shape[1], 2 * len(starts)
+    extra = len(passed) + len(later)
     result = pl.pallas_call(
-        functools.partial(split_kernel, starts, width, len(held), len(later)),
-        out_shape=shapes,
-        in_specs=[SMEM, HBM] + [HBM] * len(held) + [ANYWHERE] * len(later),
-        out_specs=[VMEM] * len(shapes),
-        scratch_shapes=[pltpu.SemaphoreType.DMA((len(shapes),))],
+        functools.partial(split_kernel, starts, width, extra, len(passed)),
+        out_shape=[bands_of(GY, basis, width)] * count + [like(p) for p in passed],
+        in_specs=[SMEM, HBM] + [ANYWHERE] * extra,
+        out_specs=[VMEM] * count + [ANYWHERE] * len(passed),
+        scratch_shapes=[pltpu.SemaphoreType.DMA((max(count, 1),))],
+        input_output_aliases={2 + i: count + i for i in range(len(passed))},
         compiler_params=PARAMS,
         cost_estimate=cost(LONG),
-    )(odd, start_bands, *held, *later)
-    parts = result[len(held) :]
-    return result[: len(held)], [[parts[2 * n], parts[2 * n + 1]] for n in range(len(starts))]
+    )(odd, start_bands, *passed, *later)
+    return [[result[2 * n], result[2 * n + 1]] for n in range(len(starts))], list(result[count:])
 
 
 def step_kernel(sides, firsts, out_column, has_out, waits, joined, odd_ref, links_ref, blocks_ref, *refs):
@@ -185,7 +178,7 @@
         out_specs=[VMEM] * len(widths) + [ANYWHERE] * len(passed),
         input_output_aliases={count + i: len(widths) + i for i in range(len(passed))},
         compiler_params=PARAMS,
-        cost_estimate=cost(LONG // 2),
+        cost_estimate=cost(SHORT),
     )(*pieces, matrix, *passed, *later)
     return list(result[: len(widths)]), list(result[len(widths) :])
 
@@ -194,7 +187,7 @@
     del refs
 
 
-def after(arrays, later):
+def after(arrays, later, weight=LONG):
     count = len(arrays)
     return pl.pallas_call(
         wait_kernel,
@@ -203,7 +196,7 @@
         out_specs=[ANYWHERE] * count,
         input_output_aliases={i: i for i in range(count)},
         compiler_params=PARAMS,
-        cost_estimate=cost(LONG),
+        cost_estimate=cost(weight),
     )(*arrays, *later)
 
 
@@ -243,18 +236,26 @@
     return lax.ppermute(array, axis, [(i, partner(i)) for i in range(lax.axis_size(axis))])
 
 
+def bits_of(elems):
+    bits = [1 << b for b in range(elems.bit_length() - 1)]
+    return bits[1:2] + bits[:1:-1] + bits[:1]
+
+
+def owners_of(elems):
+    owners = [0]
+    for bit in bits_of(elems):
+        owners = owners + [owner ^ bit for owner in owners]
+    return owners
+
+
 class Gather:
     def __init__(self, rows):
-        elems = lax.axis_size("elem")
-        bits = [1 << b for b in range(elems.bit_length() - 1)]
-        self.bits = bits[1:2] + bits[:1:-1] + bits[:1]
-        self.owners = [0]
+        self.bits = bits_of(lax.axis_size("elem"))
         self.held = rows
         self.received = self.send()
 
     def send(self):
         bit = self.bits.pop(0)
-        self.owners = self.owners + [owner ^ bit for owner in self.owners]
         return exchange(self.held, "elem", lambda i: i ^ bit)
 
     def parts(self):
@@ -275,8 +276,7 @@
         parts = self.parts()
         for bit in self.bits:
             parts = parts + [exchange(part, "elem", lambda i: i ^ bit) for part in parts]
-            self.owners = self.owners + [owner ^ bit for owner in self.owners]
-        return parts, jnp.array(self.owners)
+            return parts
 
 
 def body(start_bands, blocks, neighbours, band_order, rotation):
@@ -310,10 +310,11 @@
         ]
     ]
     beside = [halos(state[0])]
-    (held,), rest = split(odd, start_bands, starts[1:], chunk, blocks, later=beside[0][1:])
+    order = band_order.reshape(elems, -1)[jnp.bitwise_xor(me, jnp.array(owners_of(elems)))].reshape(1, -1)
+    rest, (order,) = split(odd, start_bands, starts[1:], chunk, [order], later=beside[0][1:])
     state += rest
     beside += [halos(columns) for columns in rest]
-    shared = (odd, neighbours, held)
+    shared = (odd, neighbours, blocks)
     gather = Gather(rotation)
 
     before = [nothing for _ in chunks]
@@ -330,21 +331,24 @@
         outer.append(made[0])
         inner.append(made[1])
         outer_others.append(over_band(made[0]))
-    rows, owners = gather.finish()
+    rows = gather.finish()
     inner = after(inner, outer_others[0])
-    order = band_order.reshape(elems, -1)[jnp.bitwise_xor(me, owners)].reshape(1, -1)
+    inner = after(inner, outer_others[-1], SHORT)
+    inner_others = [over_band(part) for part in inner]
     matrix = ordered_rows(lax.axis_index("band").astype(jnp.int32).reshape(1), order, rows, bands, later=outer_others[-1] + list(inner[:1]))
 
     def by_band(own, others):
         return list(own) + [other[shift] for shift in range(bands - 1) for other in others]
 
     pieces = by_band(outer, outer_others)
-    rotated, inner = rotate(pieces, matrix, 0, [chunk], passed=inner)
+    rotated, _ = rotate(pieces, matrix, 0, [chunk])
     far = [cross(rotated[0])]
-    inner_others = [over_band(part) for part in inner]
     for c in chunks[1:]:
         rotated += rotate(pieces, matrix, starts[c], [chunk], later=())[0]
         far.append(cross(rotated[c]))
+    if bands > 1:
+        arrived = list(after([p for others in inner_others for p in others], []))
+        inner_others = [arrived[n * (bands - 1) : (n + 1) * (bands - 1)] for n in range(len(chunks))]
     rotated_inner, _ = rotate(by_band(inner, inner_others), matrix, 0, [chunk for _ in chunks], later=far[1:])
     state = [[rotated[c], rotated_inner[c]] for c in chunks]
     beside = [[far[c], intra(rotated_inner[c])] for c in chunks]

time: 136 us -> 136 us (level)
  local copies, waits for them, and re-layouts: 4.13 us -> 2.03 us
  waiting for transfers between devices: 62.2 us -> 64 us
    unnamed x16 -> x14, local copies, waits for them, and re-layouts: 2.14 us -> 0.03 us
    ppermute x33, waiting for transfers between devices: 62.2 us -> 64 us  [exchange(): lax.ppermute(array, axis, [(i, partner(i)) for i in range(lax.axis_size(a...]
  transfers between devices with their start and end apart: 33 -> 33, of which waited for: 14 -> 12; matrix products, arithmetic and copies ran while one was open for 1% -> 1% of each run, Pallas kernels for 19% -> 20%
where the time goes in v6:
time: 136 us; the launch traced here: 135 us
  waiting for transfers between devices  64 us (47%)
  starting transfers between devices  40 us (29%)
  Pallas kernels  28.9 us (21%)
  local copies, waits for them, and re-layouts  2.03 us (1%)
    ppermute x33, waiting for transfers between devices, exchange(): lax.ppermute(array, axis, [(i, partner(i)) for i in range(lax.axis_size(a...  64 us
    ppermute x33, starting transfers between devices, exchange(): lax.ppermute(array, axis, [(i, partner(i)) for i in range(lax.axis_size(a...  40 us
    pallas_call x13, Pallas kernels, apply_step(): pl.pallas_call(functools.partial(step_kernel, sides, firsts, out_column,...  25.5 us
  transfers between devices with their start and end apart: 33, of which 12 were waited for; matrix products, arithmetic and copies ran while one was open for 1% of the time, Pallas kernels for 20%

profile of v6, /device:TPU:1, one launch (start us, length us, event | category | flops | bytes accessed | tf_op | source)
XLA Modules:
  0.0 135.4 jit_solution(5528116429922783291)
XLA Ops:
  1.4 2.6 %collective-permute-start = (bf16[3,256,256]{2,1,0:T(8,128)(2,1)S(1)}, bf16[3,256,256]{2,1,0:T(8,128)(2,1)S(1)}, u32[]{:S(2)}, u32[]{:S(2)}) collective-permute-start(bf16[3,256,256]{2,1,0:T(8,128)(2,1)S(1)} %get-tuple-element.72.refs_0_.refs_4_), channel_id=1, source_target_pairs={{0,30},{2,4},{4,2},{6,8},{8,6},{10,12},{12,10},{14,16},{16,14},{18... | collective-permute-start | bytes 1179656 | tf_op jit(solution)/shard_map/ppermute | solution.py:236
  6.2 3.9 %collective-permute-start.5 = (bf16[3,256,256]{2,1,0:T(8,128)(2,1)S(1)}, bf16[3,256,256]{2,1,0:T(8,128)(2,1)S(1)}, u32[]{:S(2)}, u32[]{:S(2)}) collective-permute-start(bf16[3,256,256]{2,1,0:T(8,128)(2,1)S(1)} %get-tuple-element.40.refs_0_.refs_4_), channel_id=1, source_target_pairs={{0,30},{2,4},{4,2},{6,8},{8,6},{10,12},{12,10},{14,16},{16,14},{18... | collective-permute-start | bytes 1179656 | tf_op jit(solution)/shard_map/ppermute | solution.py:236
  10.1 8.6 %collective-permute-done.2.refs_5_ = bf16[64,512]{1,0:T(8,128)(2,1)S(1)} collective-permute-done((bf16[64,512]{1,0:T(8,128)(2,1)}, bf16[64,512]{1,0:T(8,128)(2,1)S(1)}, u32[]{:S(2)}, u32[]{:S(2)}) %collective-permute-start.2) | collective-permute-done | bytes 65568 | tf_op jit(solution)/shard_map/ppermute | solution.py:236
  18.7 2.0 %shard_map.64 = (bf16[3,256,256]{2,1,0:T(8,128)(2,1)S(1)}, bf16[3,256,256]{2,1,0:T(8,128)(2,1)S(1)}, bf16[128,512]{1,0:T(8,128)(2,1)S(1)}) custom-call(s32[1]{0:T(128)} %bitcast.odd_ref, s32[6,5]{1,0:T(8,128)S(1)} %copy-done.4, bf16[6,5,256,256]{3,2,1,0:T(8,128)(2,1)S(1)} %copy-done.1, bf16[3,256,256]{2,1,0:T(8,128)(2,1)S(1)} %get-tuple-element.72.refs_0_.refs_4_, ...), custom_call_target="tpu_custom_call" | custom-call | flops 4000000000 | bytes 1024 | tf_op jit(solution)/shard_map/pallas_call | solution.py:145
  22.5 3.6 %collective-permute-start.4 = (bf16[3,256,256]{2,1,0:T(8,128)(2,1)S(1)}, bf16[3,256,256]{2,1,0:T(8,128)(2,1)S(1)}, u32[]{:S(2)}, u32[]{:S(2)}) collective-permute-start(bf16[3,256,256]{2,1,0:T(8,128)(2,1)S(1)} %get-tuple-element.39.refs_1_.refs_5_), channel_id=1, source_target_pairs={{0,2},{2,0},{4,6},{6,4},{8,10},{10,8},{12,14},{14,12},{16,18},{18,... | collective-permute-start | bytes 1179656 | tf_op jit(solution)/shard_map/ppermute | solution.py:236
  26.1 1.8 %shard_map.66 = (bf16[3,256,256]{2,1,0:T(8,128)(2,1)S(1)}, bf16[3,256,256]{2,1,0:T(8,128)(2,1)S(1)}) custom-call(s32[1]{0:T(128)} %bitcast.odd_ref, s32[6,5]{1,0:T(8,128)S(1)} %copy-done.4, bf16[6,5,256,256]{3,2,1,0:T(8,128)(2,1)S(1)} %copy-done.1, bf16[3,256,256]{2,1,0:T(8,128)(2,1)S(1)} %get-tuple-element.40.refs_0_.refs_4_, ...), custom_call_target="tpu_custom_call" | custom-call | flops 4000000000 | bytes 1024 | tf_op jit(solution)/shard_map/pallas_call | solution.py:145
  29.8 9.8 %collective-permute-done.3.refs_2_ = bf16[3,256,256]{2,1,0:T(8,128)(2,1)S(1)} collective-permute-done((bf16[3,256,256]{2,1,0:T(8,128)(2,1)S(1)}, bf16[3,256,256]{2,1,0:T(8,128)(2,1)S(1)}, u32[]{:S(2)}, u32[]{:S(2)}) %collective-permute-start.3) | collective-permute-done | bytes 393248 | tf_op jit(solution)/shard_map/ppermute | solution.py:236
  39.6 1.8 %shard_map.67 = (bf16[3,256,256]{2,1,0:T(8,128)(2,1)S(1)}, bf16[3,256,256]{2,1,0:T(8,128)(2,1)S(1)}) custom-call(s32[1]{0:T(128)} %bitcast.odd_ref, s32[6,5]{1,0:T(8,128)S(1)} %copy-done.4, bf16[6,5,256,256]{3,2,1,0:T(8,128)(2,1)S(1)} %copy-done.1, bf16[3,256,256]{2,1,0:T(8,128)(2,1)S(1)} %get-tuple-element.38.refs_4_.refs_0_, ...), custom_call_target="tpu_custom_call" | custom-call | flops 4000000000 | bytes 1024 | tf_op jit(solution)/shard_map/pallas_call | solution.py:145
  41.4 2.6 %collective-permute-start.7 = (bf16[3,256,256]{2,1,0:T(8,128)(2,1)S(1)}, bf16[3,256,256]{2,1,0:T(8,128)(2,1)S(1)}, u32[]{:S(2)}, u32[]{:S(2)}) collective-permute-start(bf16[3,256,256]{2,1,0:T(8,128)(2,1)S(1)} %get-tuple-element.43.refs_8_.refs_0_), channel_id=1, source_target_pairs={{0,30},{2,4},{4,2},{6,8},{8,6},{10,12},{12,10},{14,16},{16,14},{18... | collective-permute-start | bytes 1179656 | tf_op jit(solution)/shard_map/ppermute | solution.py:236
  44.9 2.3 %shard_map.68 = (bf16[3,256,256]{2,1,0:T(8,128)(2,1)S(1)}, bf16[3,256,256]{2,1,0:T(8,128)(2,1)S(1)}, bf16[256,512]{1,0:T(8,128)(2,1)S(1)}) custom-call(s32[1]{0:T(128)} %bitcast.odd_ref, s32[6,5]{1,0:T(8,128)S(1)} %copy-done.4, bf16[6,5,256,256]{3,2,1,0:T(8,128)(2,1)S(1)} %copy-done.1, bf16[3,256,256]{2,1,0:T(8,128)(2,1)S(1)} %get-tuple-element.42.refs_6_.refs_0_.refs_4_, ...), custom_call_target="tpu_custom_call" | custom-call | flops 4000000000 | bytes 1024 | tf_op jit(solution)/shard_map/pallas_call | solution.py:145
  47.2 2.0 %collective-permute-start.12 = (bf16[3,256,256]{2,1,0:T(8,128)(2,1)S(1)}, bf16[3,256,256]{2,1,0:T(8,128)(2,1)S(1)}, u32[]{:S(2)}, u32[]{:S(2)}) collective-permute-start(bf16[3,256,256]{2,1,0:T(8,128)(2,1)S(1)} %get-tuple-element.47.refs_6_.refs_0_), channel_id=1, source_target_pairs={{0,30},{2,4},{4,2},{6,8},{8,6},{10,12},{12,10},{14,16},{16,14},{18... | collective-permute-start | bytes 1179656 | tf_op jit(solution)/shard_map/ppermute | solution.py:236
  49.5 1.8 %shard_map.69 = (bf16[3,256,256]{2,1,0:T(8,128)(2,1)S(1)}, bf16[3,256,256]{2,1,0:T(8,128)(2,1)S(1)}) custom-call(s32[1]{0:T(128)} %bitcast.odd_ref, s32[6,5]{1,0:T(8,128)S(1)} %copy-done.4, bf16[6,5,256,256]{3,2,1,0:T(8,128)(2,1)S(1)} %copy-done.1, bf16[3,256,256]{2,1,0:T(8,128)(2,1)S(1)} %get-tuple-element.43.refs_8_.refs_0_, ...), custom_call_target="tpu_custom_call" | custom-call | flops 4000000000 | bytes 1024 | tf_op jit(solution)/shard_map/pallas_call | solution.py:145
  52.7 4.2 %collective-permute-start.16 = (bf16[256,512]{1,0:T(8,128)(2,1)S(1)}, bf16[256,512]{1,0:T(8,128)(2,1)S(1)}, u32[]{:S(2)}, u32[]{:S(2)}) collective-permute-start(bf16[256,512]{1,0:T(8,128)(2,1)S(1)} %get-tuple-element.52.refs_0_), channel_id=1, source_target_pairs={{0,8},{2,10},{4,12},{6,14},{8,0},{10,2},{12,4},{14,6},{16,24},{18,... | collective-permute-start | bytes 786440 | tf_op jit(solution)/shard_map/ppermute | solution.py:236
  56.9 2.3 %collective-permute-done.12.refs_2_ = bf16[3,256,256]{2,1,0:T(8,128)(2,1)S(1)} collective-permute-done((bf16[3,256,256]{2,1,0:T(8,128)(2,1)S(1)}, bf16[3,256,256]{2,1,0:T(8,128)(2,1)S(1)}, u32[]{:S(2)}, u32[]{:S(2)}) %collective-permute-start.12) | collective-permute-done | bytes 393248 | tf_op jit(solution)/shard_map/ppermute | solution.py:236
  59.3 1.8 %shard_map.70 = (bf16[3,256,256]{2,1,0:T(8,128)(2,1)S(1)}, bf16[3,256,256]{2,1,0:T(8,128)(2,1)S(1)}) custom-call(s32[1]{0:T(128)} %bitcast.odd_ref, s32[6,5]{1,0:T(8,128)S(1)} %copy-done.4, bf16[6,5,256,256]{3,2,1,0:T(8,128)(2,1)S(1)} %copy-done.1, bf16[3,256,256]{2,1,0:T(8,128)(2,1)S(1)} %get-tuple-element.47.refs_6_.refs_0_, ...), custom_call_target="tpu_custom_call" | custom-call | flops 4000000000 | bytes 1024 | tf_op jit(solution)/shard_map/pallas_call | solution.py:145
  63.1 7.5 %collective-permute-done.15.refs_2_.refs_4_.refs_3_ = bf16[3,256,256]{2,1,0:T(8,128)(2,1)S(1)} collective-permute-done((bf16[3,256,256]{2,1,0:T(8,128)(2,1)S(1)}, bf16[3,256,256]{2,1,0:T(8,128)(2,1)S(1)}, u32[]{:S(2)}, u32[]{:S(2)}) %collective-permute-start.15) | collective-permute-done | bytes 393248 | tf_op jit(solution)/shard_map/ppermute | solution.py:236
  74.0 1.8 %collective-permute-start.21 = (bf16[3,256,256]{2,1,0:T(8,128)(2,1)S(1)}, bf16[3,256,256]{2,1,0:T(8,128)(2,1)S(1)}, u32[]{:S(2)}, u32[]{:S(2)}) collective-permute-start(bf16[3,256,256]{2,1,0:T(8,128)(2,1)S(1)} %shard_map.74.refs_0_.refs_4_), channel_id=1, source_target_pairs={{0,30},{2,4},{4,2},{6,8},{8,6},{10,12},{12,10},{14,16},{16,14},{18... | collective-permute-start | bytes 1179656 | tf_op jit(solution)/shard_map/ppermute | solution.py:236
  76.5 5.3 %collective-permute-done.19.refs_0_ = bf16[3,256,256]{2,1,0:T(8,128)(2,1)S(1)} collective-permute-done((bf16[3,256,256]{2,1,0:T(8,128)(2,1)S(1)}, bf16[3,256,256]{2,1,0:T(8,128)(2,1)S(1)}, u32[]{:S(2)}, u32[]{:S(2)}) %collective-permute-start.19) | collective-permute-done | bytes 393248 | tf_op jit(solution)/shard_map/ppermute | solution.py:236
  81.8 7.9 %collective-permute-done.20.refs_1_ = bf16[3,256,256]{2,1,0:T(8,128)(2,1)S(1)} collective-permute-done((bf16[3,256,256]{2,1,0:T(8,128)(2,1)S(1)}, bf16[3,256,256]{2,1,0:T(8,128)(2,1)S(1)}, u32[]{:S(2)}, u32[]{:S(2)}) %collective-permute-start.20) | collective-permute-done | bytes 393248 | tf_op jit(solution)/shard_map/ppermute | solution.py:236
  91.3 2.6 %collective-permute-done.27.refs_2_ = bf16[3,256,256]{2,1,0:T(8,128)(2,1)S(1)} collective-permute-done((bf16[3,256,256]{2,1,0:T(8,128)(2,1)S(1)}, bf16[3,256,256]{2,1,0:T(8,128)(2,1)S(1)}, u32[]{:S(2)}, u32[]{:S(2)}) %collective-permute-start.27) | collective-permute-done | bytes 393248 | tf_op jit(solution)/shard_map/ppermute | solution.py:236
  93.9 1.8 %shard_map.80 = (bf16[3,256,256]{2,1,0:T(8,128)(2,1)S(1)}, bf16[3,256,256]{2,1,0:T(8,128)(2,1)S(1)}) custom-call(s32[1]{0:T(128)} %bitcast.odd_ref, s32[6,5]{1,0:T(8,128)S(1)} %copy-done.4, bf16[6,5,256,256]{3,2,1,0:T(8,128)(2,1)S(1)} %copy-done.2, bf16[3,256,256]{2,1,0:T(8,128)(2,1)S(1)} %shard_map.79.refs_0_.refs_4_, ...), custom_call_target="tpu_custom_call" | custom-call | flops 4000000000 | bytes 1024 | tf_op jit(solution)/shard_map/pallas_call | solution.py:145
  96.7 2.2 %collective-permute-start.30 = (bf16[3,256,256]{2,1,0:T(8,128)(2,1)S(1)}, bf16[3,256,256]{2,1,0:T(8,128)(2,1)S(1)}, u32[]{:S(2)}, u32[]{:S(2)}) collective-permute-start(bf16[3,256,256]{2,1,0:T(8,128)(2,1)S(1)} %get-tuple-element.68.refs_1_.refs_5_), channel_id=1, source_target_pairs={{0,2},{2,0},{4,6},{6,4},{8,10},{10,8},{12,14},{14,12},{16,18},{18,... | collective-permute-start | bytes 1179656 | tf_op jit(solution)/shard_map/ppermute | solution.py:236
  98.9 1.8 %shard_map.77 = (bf16[3,256,256]{2,1,0:T(8,128)(2,1)S(1)}, bf16[3,256,256]{2,1,0:T(8,128)(2,1)S(1)}) custom-call(s32[1]{0:T(128)} %bitcast.odd_ref, s32[6,5]{1,0:T(8,128)S(1)} %copy-done.4, bf16[6,5,256,256]{3,2,1,0:T(8,128)(2,1)S(1)} %copy-done.2, bf16[3,256,256]{2,1,0:T(8,128)(2,1)S(1)} %shard_map.74.refs_0_.refs_4_, ...), custom_call_target="tpu_custom_call" | custom-call | flops 4000000000 | bytes 1024 | tf_op jit(solution)/shard_map/pallas_call | solution.py:145
  100.8 1.9 %collective-permute-start.24 = (bf16[3,256,256]{2,1,0:T(8,128)(2,1)S(1)}, bf16[3,256,256]{2,1,0:T(8,128)(2,1)S(1)}, u32[]{:S(2)}, u32[]{:S(2)}) collective-permute-start(bf16[3,256,256]{2,1,0:T(8,128)(2,1)S(1)} %get-tuple-element.63.refs_1_.refs_3_), channel_id=1, source_target_pairs={{0,2},{2,0},{4,6},{6,4},{8,10},{10,8},{12,14},{14,12},{16,18},{18,... | collective-permute-start | bytes 1179656 | tf_op jit(solution)/shard_map/ppermute | solution.py:236
  102.7 11.2 %collective-permute-done.29.refs_2_ = bf16[3,256,256]{2,1,0:T(8,128)(2,1)S(1)} collective-permute-done((bf16[3,256,256]{2,1,0:T(8,128)(2,1)S(1)}, bf16[3,256,256]{2,1,0:T(8,128)(2,1)S(1)}, u32[]{:S(2)}, u32[]{:S(2)}) %collective-permute-start.29) | collective-permute-done | bytes 393248 | tf_op jit(solution)/shard_map/ppermute | solution.py:236
  113.9 1.8 %shard_map.81 = (bf16[3,256,256]{2,1,0:T(8,128)(2,1)S(1)}, bf16[3,256,256]{2,1,0:T(8,128)(2,1)S(1)}) custom-call(s32[1]{0:T(128)} %bitcast.odd_ref, s32[6,5]{1,0:T(8,128)S(1)} %copy-done.4, bf16[6,5,256,256]{3,2,1,0:T(8,128)(2,1)S(1)} %copy-done.2, bf16[3,256,256]{2,1,0:T(8,128)(2,1)S(1)} %get-tuple-element.67.refs_0_.refs_4_, ...), custom_call_target="tpu_custom_call" | custom-call | flops 4000000000 | bytes 1024 | tf_op jit(solution)/shard_map/pallas_call | solution.py:145
  115.7 2.5 %collective-permute-start.31 = (bf16[3,256,256]{2,1,0:T(8,128)(2,1)S(1)}, bf16[3,256,256]{2,1,0:T(8,128)(2,1)S(1)}, u32[]{:S(2)}, u32[]{:S(2)}) collective-permute-start(bf16[3,256,256]{2,1,0:T(8,128)(2,1)S(1)} %get-tuple-element.69.refs_0_), channel_id=1, source_target_pairs={{0,30},{2,4},{4,2},{6,8},{8,6},{10,12},{12,10},{14,16},{16,14},{18... | collective-permute-start | bytes 1179656 | tf_op jit(solution)/shard_map/ppermute | solution.py:236
  119.9 1.8 %shard_map.78 = (bf16[3,256,256]{2,1,0:T(8,128)(2,1)S(1)}, bf16[3,256,256]{2,1,0:T(8,128)(2,1)S(1)}) custom-call(s32[1]{0:T(128)} %bitcast.odd_ref, s32[6,5]{1,0:T(8,128)S(1)} %copy-done.4, bf16[6,5,256,256]{3,2,1,0:T(8,128)(2,1)S(1)} %copy-done.2, bf16[3,256,256]{2,1,0:T(8,128)(2,1)S(1)} %get-tuple-element.62.refs_0_.refs_3_, ...), custom_call_target="tpu_custom_call" | custom-call | flops 4000000000 | bytes 1024 | tf_op jit(solution)/shard_map/pallas_call | solution.py:145
  124.1 2.6 %shard_map.82.refs_4_ = bf16[6,256,512]{2,1,0:T(8,128)(2,1)} custom-call(s32[1]{0:T(128)} %bitcast.odd_ref, s32[6,5]{1,0:T(8,128)S(1)} %copy-done.4, bf16[6,5,256,256]{3,2,1,0:T(8,128)(2,1)S(1)} %copy-done.2, bf16[3,256,256]{2,1,0:T(8,128)(2,1)S(1)} %get-tuple-element.69.refs_0_, bf16[3,256,256]{2,1,0:T(8,128)(2,1)S(1)} %get-tuple-element.70.refs_1_, ...), custom_call_target="tpu_custom_call" | custom-call | flops 4000000000 | bytes 1024 | tf_op jit(solution)/shard_map/pallas_call | solution.py:145
  126.7 2.0 %shard_map.83.refs_4_ = bf16[6,256,512]{2,1,0:T(8,128)(2,1)} custom-call(s32[1]{0:T(128)} %bitcast.odd_ref, s32[6,5]{1,0:T(8,128)S(1)} %copy-done.4, bf16[6,5,256,256]{3,2,1,0:T(8,128)(2,1)S(1)} %copy-done.2, bf16[3,256,256]{2,1,0:T(8,128)(2,1)S(1)} %get-tuple-element.64.refs_0_, ...), custom_call_target="tpu_custom_call", output_to_operand_aliasing={{}: (7, {})} | custom-call | flops 4000000000 | bytes 1024 | tf_op jit(solution)/shard_map/pallas_call | solution.py:145
  128.7 4.5 %collective-permute-done.25.refs_2_ = bf16[3,256,256]{2,1,0:T(8,128)(2,1)S(1)} collective-permute-done((bf16[3,256,256]{2,1,0:T(8,128)(2,1)S(1)}, bf16[3,256,256]{2,1,0:T(8,128)(2,1)S(1)}, u32[]{:S(2)}, u32[]{:S(2)}) %collective-permute-start.25) | collective-permute-done | bytes 393248 | tf_op jit(solution)/shard_map/ppermute | solution.py:236
  133.2 2.0 %shard_map.84 = bf16[6,256,512]{2,1,0:T(8,128)(2,1)} custom-call(s32[1]{0:T(128)} %bitcast.odd_ref, s32[6,5]{1,0:T(8,128)S(1)} %copy-done.4, bf16[6,5,256,256]{3,2,1,0:T(8,128)(2,1)S(1)} %copy-done.2, bf16[3,256,256]{2,1,0:T(8,128)(2,1)S(1)} %get-tuple-element.64.refs_0_, ...), custom_call_target="tpu_custom_call", output_to_operand_aliasing={{}: (7, {})} | custom-call | flops 4000000000 | bytes 1024 | tf_op jit(solution)/shard_map/pallas_call | solution.py:145
  (75 shorter events, 22.3 us)
Async XLA Ops:
  1.3 4.8 %collective-permute-start.1 = (bf16[3,256,256]{2,1,0:T(8,128)(2,1)S(1)}, bf16[3,256,256]{2,1,0:T(8,128)(2,1)S(1)}, u32[]{:S(2)}, u32[]{:S(2)}) collective-permute-start(bf16[3,256,256]{2,1,0:T(8,128)(2,1)S(1)} %get-tuple-element.71.refs_1_.refs_5_), channel_id=1, source_target_pairs={{0,2},{2,0},{4,6},{6,4},{8,10},{10,8},{12,14},{14,12},{16,18},{18,... | collective-permute-start | bytes 1179656 | tf_op jit(solution)/shard_map/ppermute | solution.py:236
  1.4 17.3 %collective-permute-start = (bf16[3,256,256]{2,1,0:T(8,128)(2,1)S(1)}, bf16[3,256,256]{2,1,0:T(8,128)(2,1)S(1)}, u32[]{:S(2)}, u32[]{:S(2)}) collective-permute-start(bf16[3,256,256]{2,1,0:T(8,128)(2,1)S(1)} %get-tuple-element.72.refs_0_.refs_4_), channel_id=1, source_target_pairs={{0,30},{2,4},{4,2},{6,8},{8,6},{10,12},{12,10},{14,16},{16,14},{18... | collective-permute-start | bytes 1179656 | tf_op jit(solution)/shard_map/ppermute | solution.py:236
  4.1 14.7 %collective-permute-start.2 = (bf16[64,512]{1,0:T(8,128)(2,1)}, bf16[64,512]{1,0:T(8,128)(2,1)S(1)}, u32[]{:S(2)}, u32[]{:S(2)}) collective-permute-start(bf16[64,512]{1,0:T(8,128)(2,1)} %refs_4_.1), channel_id=1, source_target_pairs={{0,4},{2,6},{4,0},{6,2},{8,12},{10,14},{12,8},{14,10},{16,20},{18,... | collective-permute-start | bytes 196616 | tf_op jit(solution)/shard_map/ppermute | solution.py:236
  6.2 19.9 %collective-permute-start.5 = (bf16[3,256,256]{2,1,0:T(8,128)(2,1)S(1)}, bf16[3,256,256]{2,1,0:T(8,128)(2,1)S(1)}, u32[]{:S(2)}, u32[]{:S(2)}) collective-permute-start(bf16[3,256,256]{2,1,0:T(8,128)(2,1)S(1)} %get-tuple-element.40.refs_0_.refs_4_), channel_id=1, source_target_pairs={{0,30},{2,4},{4,2},{6,8},{8,6},{10,12},{12,10},{14,16},{16,14},{18... | collective-permute-start | bytes 1179656 | tf_op jit(solution)/shard_map/ppermute | solution.py:236
  10.1 16.0 %collective-permute-start.6 = (bf16[3,256,256]{2,1,0:T(8,128)(2,1)S(1)}, bf16[3,256,256]{2,1,0:T(8,128)(2,1)S(1)}, u32[]{:S(2)}, u32[]{:S(2)}) collective-permute-start(bf16[3,256,256]{2,1,0:T(8,128)(2,1)S(1)} %get-tuple-element.41.refs_1_.refs_5_), channel_id=1, source_target_pairs={{0,2},{2,0},{4,6},{6,4},{8,10},{10,8},{12,14},{14,12},{16,18},{18,... | collective-permute-start | bytes 1179656 | tf_op jit(solution)/shard_map/ppermute | solution.py:236
  20.8 18.8 %collective-permute-start.3 = (bf16[3,256,256]{2,1,0:T(8,128)(2,1)S(1)}, bf16[3,256,256]{2,1,0:T(8,128)(2,1)S(1)}, u32[]{:S(2)}, u32[]{:S(2)}) collective-permute-start(bf16[3,256,256]{2,1,0:T(8,128)(2,1)S(1)} %get-tuple-element.38.refs_4_.refs_0_), channel_id=1, source_target_pairs={{0,30},{2,4},{4,2},{6,8},{8,6},{10,12},{12,10},{14,16},{16,14},{18... | collective-permute-start | bytes 1179656 | tf_op jit(solution)/shard_map/ppermute | solution.py:236
  22.5 17.1 %collective-permute-start.4 = (bf16[3,256,256]{2,1,0:T(8,128)(2,1)S(1)}, bf16[3,256,256]{2,1,0:T(8,128)(2,1)S(1)}, u32[]{:S(2)}, u32[]{:S(2)}) collective-permute-start(bf16[3,256,256]{2,1,0:T(8,128)(2,1)S(1)} %get-tuple-element.39.refs_1_.refs_5_), channel_id=1, source_target_pairs={{0,2},{2,0},{4,6},{6,4},{8,10},{10,8},{12,14},{14,12},{16,18},{18,... | collective-permute-start | bytes 1179656 | tf_op jit(solution)/shard_map/ppermute | solution.py:236
  27.9 16.1 %collective-permute-start.10 = (bf16[3,256,256]{2,1,0:T(8,128)(2,1)S(1)}, bf16[3,256,256]{2,1,0:T(8,128)(2,1)S(1)}, u32[]{:S(2)}, u32[]{:S(2)}) collective-permute-start(bf16[3,256,256]{2,1,0:T(8,128)(2,1)S(1)} %get-tuple-element.45.refs_1_.refs_5_), channel_id=1, source_target_pairs={{0,2},{2,0},{4,6},{6,4},{8,10},{10,8},{12,14},{14,12},{16,18},{18,... | collective-permute-start | bytes 1179656 | tf_op jit(solution)/shard_map/ppermute | solution.py:236
  28.0 16.9 %collective-permute-start.9 = (bf16[3,256,256]{2,1,0:T(8,128)(2,1)S(1)}, bf16[3,256,256]{2,1,0:T(8,128)(2,1)S(1)}, u32[]{:S(2)}, u32[]{:S(2)}) collective-permute-start(bf16[3,256,256]{2,1,0:T(8,128)(2,1)S(1)} %get-tuple-element.42.refs_6_.refs_0_.refs_4_), channel_id=1, source_target_pairs={{0,30},{2,4},{4,2},{6,8},{8,6},{10,12},{12,10},{14,16},{16,14},{18... | collective-permute-start | bytes 1179656 | tf_op jit(solution)/shard_map/ppermute | solution.py:236
  28.0 15.9 %collective-permute-start.11 = (bf16[128,512]{1,0:T(8,128)(2,1)S(1)}, bf16[128,512]{1,0:T(8,128)(2,1)S(1)}, u32[]{:S(2)}, u32[]{:S(2)}) collective-permute-start(bf16[128,512]{1,0:T(8,128)(2,1)S(1)} %get-tuple-element.46.refs_6_), channel_id=1, source_target_pairs={{0,16},{2,18},{4,20},{6,22},{8,24},{10,26},{12,28},{14,30},{16,0},... | collective-permute-start | bytes 393224 | tf_op jit(solution)/shard_map/ppermute | solution.py:236
  41.4 8.1 %collective-permute-start.7 = (bf16[3,256,256]{2,1,0:T(8,128)(2,1)S(1)}, bf16[3,256,256]{2,1,0:T(8,128)(2,1)S(1)}, u32[]{:S(2)}, u32[]{:S(2)}) collective-permute-start(bf16[3,256,256]{2,1,0:T(8,128)(2,1)S(1)} %get-tuple-element.43.refs_8_.refs_0_), channel_id=1, source_target_pairs={{0,30},{2,4},{4,2},{6,8},{8,6},{10,12},{12,10},{14,16},{16,14},{18... | collective-permute-start | bytes 1179656 | tf_op jit(solution)/shard_map/ppermute | solution.py:236
  44.0 5.5 %collective-permute-start.8 = (bf16[3,256,256]{2,1,0:T(8,128)(2,1)S(1)}, bf16[3,256,256]{2,1,0:T(8,128)(2,1)S(1)}, u32[]{:S(2)}, u32[]{:S(2)}) collective-permute-start(bf16[3,256,256]{2,1,0:T(8,128)(2,1)S(1)} %get-tuple-element.44.refs_1_), channel_id=1, source_target_pairs={{0,2},{2,0},{4,6},{6,4},{8,10},{10,8},{12,14},{14,12},{16,18},{18,... | collective-permute-start | bytes 1179656 | tf_op jit(solution)/shard_map/ppermute | solution.py:236
  47.2 12.0 %collective-permute-start.12 = (bf16[3,256,256]{2,1,0:T(8,128)(2,1)S(1)}, bf16[3,256,256]{2,1,0:T(8,128)(2,1)S(1)}, u32[]{:S(2)}, u32[]{:S(2)}) collective-permute-start(bf16[3,256,256]{2,1,0:T(8,128)(2,1)S(1)} %get-tuple-element.47.refs_6_.refs_0_), channel_id=1, source_target_pairs={{0,30},{2,4},{4,2},{6,8},{8,6},{10,12},{12,10},{14,16},{16,14},{18... | collective-permute-start | bytes 1179656 | tf_op jit(solution)/shard_map/ppermute | solution.py:236
  49.3 10.0 %collective-permute-start.13 = (bf16[3,256,256]{2,1,0:T(8,128)(2,1)S(1)}, bf16[3,256,256]{2,1,0:T(8,128)(2,1)S(1)}, u32[]{:S(2)}, u32[]{:S(2)}) collective-permute-start(bf16[3,256,256]{2,1,0:T(8,128)(2,1)S(1)} %get-tuple-element.49.refs_1_), channel_id=1, source_target_pairs={{0,2},{2,0},{4,6},{6,4},{8,10},{10,8},{12,14},{14,12},{16,18},{18,... | collective-permute-start | bytes 1179656 | tf_op jit(solution)/shard_map/ppermute | solution.py:236
  51.3 11.8 %collective-permute-start.14 = (bf16[3,256,256]{2,1,0:T(8,128)(2,1)S(1)}, bf16[3,256,256]{2,1,0:T(8,128)(2,1)S(1)}, u32[]{:S(2)}, u32[]{:S(2)}) collective-permute-start(bf16[3,256,256]{2,1,0:T(8,128)(2,1)S(1)} %get-tuple-element.48.refs_6_.refs_0_), channel_id=1, source_target_pairs={{0,1},{1,0},{2,3},{3,2},{4,5},{5,4},{6,7},{7,6},{8,9},{9,8},{10,11... | collective-permute-start | bytes 1179656 | tf_op jit(solution)/shard_map/ppermute | solution.py:236
  52.7 9.9 %collective-permute-start.16 = (bf16[256,512]{1,0:T(8,128)(2,1)S(1)}, bf16[256,512]{1,0:T(8,128)(2,1)S(1)}, u32[]{:S(2)}, u32[]{:S(2)}) collective-permute-start(bf16[256,512]{1,0:T(8,128)(2,1)S(1)} %get-tuple-element.52.refs_0_), channel_id=1, source_target_pairs={{0,8},{2,10},{4,12},{6,14},{8,0},{10,2},{12,4},{14,6},{16,24},{18,... | collective-permute-start | bytes 786440 | tf_op jit(solution)/shard_map/ppermute | solution.py:236
  61.1 9.6 %collective-permute-start.15 = (bf16[3,256,256]{2,1,0:T(8,128)(2,1)S(1)}, bf16[3,256,256]{2,1,0:T(8,128)(2,1)S(1)}, u32[]{:S(2)}, u32[]{:S(2)}) collective-permute-start(bf16[3,256,256]{2,1,0:T(8,128)(2,1)S(1)} %get-tuple-element.50.refs_1_), channel_id=1, source_target_pairs={{0,1},{1,0},{2,3},{3,2},{4,5},{5,4},{6,7},{7,6},{8,9},{9,8},{10,11... | collective-permute-start | bytes 1179656 | tf_op jit(solution)/shard_map/ppermute | solution.py:236
  62.6 9.5 %collective-permute-start.17 = (bf16[256,512]{1,0:T(8,128)(2,1)S(1)}, bf16[256,512]{1,0:T(8,128)(2,1)S(1)}, u32[]{:S(2)}, u32[]{:S(2)}) collective-permute-start(bf16[256,512]{1,0:T(8,128)(2,1)S(1)} %get-tuple-element.52.refs_0_), channel_id=1, source_target_pairs={{0,2},{2,0},{4,6},{6,4},{8,10},{10,8},{12,14},{14,12},{16,18},{18,... | collective-permute-start | bytes 786440 | tf_op jit(solution)/shard_map/ppermute | solution.py:236
  62.6 9.5 %collective-permute-start.18 = (bf16[256,512]{1,0:T(8,128)(2,1)S(1)}, bf16[256,512]{1,0:T(8,128)(2,1)S(1)}, u32[]{:S(2)}, u32[]{:S(2)}) collective-permute-start(bf16[256,512]{1,0:T(8,128)(2,1)S(1)} %collective-permute-done.16.refs_1_), channel_id=1, source_target_pairs={{0,2},{2,0},{4,6},{6,4},{8,10},{10,8},{12,14},{14,12},{16,18},{18,... | collective-permute-start | bytes 786440 | tf_op jit(solution)/shard_map/ppermute | solution.py:236
  70.7 11.1 %collective-permute-start.19 = (bf16[3,256,256]{2,1,0:T(8,128)(2,1)S(1)}, bf16[3,256,256]{2,1,0:T(8,128)(2,1)S(1)}, u32[]{:S(2)}, u32[]{:S(2)}) collective-permute-start(bf16[3,256,256]{2,1,0:T(8,128)(2,1)S(1)} %get-tuple-element.57.refs_5_.refs_0_), channel_id=1, source_target_pairs={{0,1},{1,0},{2,3},{3,2},{4,5},{5,4},{6,7},{7,6},{8,9},{9,8},{10,11... | collective-permute-start | bytes 1179656 | tf_op jit(solution)/shard_map/ppermute | solution.py:236
  72.0 17.7 %collective-permute-start.20 = (bf16[3,256,256]{2,1,0:T(8,128)(2,1)S(1)}, bf16[3,256,256]{2,1,0:T(8,128)(2,1)S(1)}, u32[]{:S(2)}, u32[]{:S(2)}) collective-permute-start(bf16[3,256,256]{2,1,0:T(8,128)(2,1)S(1)} %get-tuple-element.58.refs_1_), channel_id=1, source_target_pairs={{0,1},{1,0},{2,3},{3,2},{4,5},{5,4},{6,7},{7,6},{8,9},{9,8},{10,11... | collective-permute-start | bytes 1179656 | tf_op jit(solution)/shard_map/ppermute | solution.py:236
  74.0 15.7 %collective-permute-start.21 = (bf16[3,256,256]{2,1,0:T(8,128)(2,1)S(1)}, bf16[3,256,256]{2,1,0:T(8,128)(2,1)S(1)}, u32[]{:S(2)}, u32[]{:S(2)}) collective-permute-start(bf16[3,256,256]{2,1,0:T(8,128)(2,1)S(1)} %shard_map.74.refs_0_.refs_4_), channel_id=1, source_target_pairs={{0,30},{2,4},{4,2},{6,8},{8,6},{10,12},{12,10},{14,16},{16,14},{18... | collective-permute-start | bytes 1179656 | tf_op jit(solution)/shard_map/ppermute | solution.py:236
  76.4 17.5 %collective-permute-start.27 = (bf16[3,256,256]{2,1,0:T(8,128)(2,1)S(1)}, bf16[3,256,256]{2,1,0:T(8,128)(2,1)S(1)}, u32[]{:S(2)}, u32[]{:S(2)}) collective-permute-start(bf16[3,256,256]{2,1,0:T(8,128)(2,1)S(1)} %shard_map.79.refs_0_.refs_4_), channel_id=1, source_target_pairs={{0,30},{2,4},{4,2},{6,8},{8,6},{10,12},{12,10},{14,16},{16,14},{18... | collective-permute-start | bytes 1179656 | tf_op jit(solution)/shard_map/ppermute | solution.py:236
  91.2 7.7 %collective-permute-start.22 = (bf16[3,256,256]{2,1,0:T(8,128)(2,1)S(1)}, bf16[3,256,256]{2,1,0:T(8,128)(2,1)S(1)}, u32[]{:S(2)}, u32[]{:S(2)}) collective-permute-start(bf16[3,256,256]{2,1,0:T(8,128)(2,1)S(1)} %get-tuple-element.61.refs_1_.refs_5_), channel_id=1, source_target_pairs={{0,2},{2,0},{4,6},{6,4},{8,10},{10,8},{12,14},{14,12},{16,18},{18,... | collective-permute-start | bytes 1179656 | tf_op jit(solution)/shard_map/ppermute | solution.py:236
  95.7 18.1 %collective-permute-start.29 = (bf16[3,256,256]{2,1,0:T(8,128)(2,1)S(1)}, bf16[3,256,256]{2,1,0:T(8,128)(2,1)S(1)}, u32[]{:S(2)}, u32[]{:S(2)}) collective-permute-start(bf16[3,256,256]{2,1,0:T(8,128)(2,1)S(1)} %get-tuple-element.67.refs_0_.refs_4_), channel_id=1, source_target_pairs={{0,30},{2,4},{4,2},{6,8},{8,6},{10,12},{12,10},{14,16},{16,14},{18... | collective-permute-start | bytes 1179656 | tf_op jit(solution)/shard_map/ppermute | solution.py:236
  96.7 17.1 %collective-permute-start.30 = (bf16[3,256,256]{2,1,0:T(8,128)(2,1)S(1)}, bf16[3,256,256]{2,1,0:T(8,128)(2,1)S(1)}, u32[]{:S(2)}, u32[]{:S(2)}) collective-permute-start(bf16[3,256,256]{2,1,0:T(8,128)(2,1)S(1)} %get-tuple-element.68.refs_1_.refs_5_), channel_id=1, source_target_pairs={{0,2},{2,0},{4,6},{6,4},{8,10},{10,8},{12,14},{14,12},{16,18},{18,... | collective-permute-start | bytes 1179656 | tf_op jit(solution)/shard_map/ppermute | solution.py:236
  100.7 19.1 %collective-permute-start.23 = (bf16[3,256,256]{2,1,0:T(8,128)(2,1)S(1)}, bf16[3,256,256]{2,1,0:T(8,128)(2,1)S(1)}, u32[]{:S(2)}, u32[]{:S(2)}) collective-permute-start(bf16[3,256,256]{2,1,0:T(8,128)(2,1)S(1)} %get-tuple-element.62.refs_0_.refs_3_), channel_id=1, source_target_pairs={{0,30},{2,4},{4,2},{6,8},{8,6},{10,12},{12,10},{14,16},{16,14},{18... | collective-permute-start | bytes 1179656 | tf_op jit(solution)/shard_map/ppermute | solution.py:236
  100.8 19.1 %collective-permute-start.24 = (bf16[3,256,256]{2,1,0:T(8,128)(2,1)S(1)}, bf16[3,256,256]{2,1,0:T(8,128)(2,1)S(1)}, u32[]{:S(2)}, u32[]{:S(2)}) collective-permute-start(bf16[3,256,256]{2,1,0:T(8,128)(2,1)S(1)} %get-tuple-element.63.refs_1_.refs_3_), channel_id=1, source_target_pairs={{0,2},{2,0},{4,6},{6,4},{8,10},{10,8},{12,14},{14,12},{16,18},{18,... | collective-permute-start | bytes 1179656 | tf_op jit(solution)/shard_map/ppermute | solution.py:236
  115.7 8.4 %collective-permute-start.31 = (bf16[3,256,256]{2,1,0:T(8,128)(2,1)S(1)}, bf16[3,256,256]{2,1,0:T(8,128)(2,1)S(1)}, u32[]{:S(2)}, u32[]{:S(2)}) collective-permute-start(bf16[3,256,256]{2,1,0:T(8,128)(2,1)S(1)} %get-tuple-element.69.refs_0_), channel_id=1, source_target_pairs={{0,30},{2,4},{4,2},{6,8},{8,6},{10,12},{12,10},{14,16},{16,14},{18... | collective-permute-start | bytes 1179656 | tf_op jit(solution)/shard_map/ppermute | solution.py:236
  118.2 5.8 %collective-permute-start.32 = (bf16[3,256,256]{2,1,0:T(8,128)(2,1)S(1)}, bf16[3,256,256]{2,1,0:T(8,128)(2,1)S(1)}, u32[]{:S(2)}, u32[]{:S(2)}) collective-permute-start(bf16[3,256,256]{2,1,0:T(8,128)(2,1)S(1)} %get-tuple-element.70.refs_1_), channel_id=1, source_target_pairs={{0,2},{2,0},{4,6},{6,4},{8,10},{10,8},{12,14},{14,12},{16,18},{18,... | collective-permute-start | bytes 1179656 | tf_op jit(solution)/shard_map/ppermute | solution.py:236
  121.7 5.0 %collective-permute-start.26 = (bf16[3,256,256]{2,1,0:T(8,128)(2,1)S(1)}, bf16[3,256,256]{2,1,0:T(8,128)(2,1)S(1)}, u32[]{:S(2)}, u32[]{:S(2)}) collective-permute-start(bf16[3,256,256]{2,1,0:T(8,128)(2,1)S(1)} %get-tuple-element.65.refs_1_), channel_id=1, source_target_pairs={{0,2},{2,0},{4,6},{6,4},{8,10},{10,8},{12,14},{14,12},{16,18},{18,... | collective-permute-start | bytes 1179656 | tf_op jit(solution)/shard_map/ppermute | solution.py:236
  121.8 11.5 %collective-permute-start.25 = (bf16[3,256,256]{2,1,0:T(8,128)(2,1)S(1)}, bf16[3,256,256]{2,1,0:T(8,128)(2,1)S(1)}, u32[]{:S(2)}, u32[]{:S(2)}) collective-permute-start(bf16[3,256,256]{2,1,0:T(8,128)(2,1)S(1)} %get-tuple-element.64.refs_0_), channel_id=1, source_target_pairs={{0,30},{2,4},{4,2},{6,8},{8,6},{10,12},{12,10},{14,16},{16,14},{18... | collective-permute-start | bytes 1179656 | tf_op jit(solution)/shard_map/ppermute | solution.py:236
  (8 other events, 62.1 us)

commit v7 on v6

--- a/solution.py
+++ b/solution.py
@@ -238,7 +238,7 @@
 
 def bits_of(elems):
     bits = [1 << b for b in range(elems.bit_length() - 1)]
-    return bits[1:2] + bits[:1:-1] + bits[:1]
+    return bits[1:2] + bits[2:] + bits[:1]
 
 
 def owners_of(elems):
@@ -349,19 +349,20 @@
     if bands > 1:
         arrived = list(after([p for others in inner_others for p in others], []))
         inner_others = [arrived[n * (bands - 1) : (n + 1) * (bands - 1)] for n in range(len(chunks))]
-    rotated_inner, _ = rotate(by_band(inner, inner_others), matrix, 0, [chunk for _ in chunks], later=far[1:])
+    rotated_inner, _ = rotate(by_band(inner, inner_others), matrix, 0, [chunk for _ in chunks], later=far[:1])
     state = [[rotated[c], rotated_inner[c]] for c in chunks]
     beside = [[far[c], intra(rotated_inner[c])] for c in chunks]
 
     before = [nothing for _ in chunks]
+    backwards = chunks[::-1]
     for _ in range(2):
-        for c in chunks:
+        for c in backwards:
             new = apply_step(shared, (0, 1), state[c], beside[c], before[c])
             before[c], state[c] = state[c], new
             beside[c] = halos(new)
     out = None
-    for c in chunks:
-        for sides in ((0, 1),) if c < chunks[-1] else ((1,), (0,)):
+    for c in backwards:
+        for sides in ((0, 1),) if c != backwards[-1] else ((1,), (0,)):
             (out,) = apply_step(
                 shared, sides, state[c], [beside[c][side] for side in sides], [before[c][side] for side in sides],
                 out=out, out_column=starts[c], out_shape=start_bands.shape,

time: 136 us -> 136 us (level)
  waiting for transfers between devices: 64 us -> 69.3 us
  starting transfers between devices: 40 us -> 35.1 us
    ppermute x33, waiting for transfers between devices: 64 us -> 69.3 us  [exchange(): lax.ppermute(array, axis, [(i, partner(i)) for i in range(lax.axis_size(a...]
    ppermute x33, starting transfers between devices: 40 us -> 35.1 us  [exchange(): lax.ppermute(array, axis, [(i, partner(i)) for i in range(lax.axis_size(a...]
  transfers between devices with their start and end apart: 33 -> 33, of which waited for: 12 -> 14; matrix products, arithmetic and copies ran while one was open for 1% -> 1% of each run, Pallas kernels for 20% -> 20%
where the time goes in v7:
time: 136 us
  waiting for transfers between devices  69.3 us (51%)
  starting transfers between devices  35.1 us (26%)
  Pallas kernels  28.9 us (21%)
  local copies, waits for them, and re-layouts  2.03 us (1%)
    ppermute x33, waiting for transfers between devices, exchange(): lax.ppermute(array, axis, [(i, partner(i)) for i in range(lax.axis_size(a...  69.3 us
    ppermute x33, starting transfers between devices, exchange(): lax.ppermute(array, axis, [(i, partner(i)) for i in range(lax.axis_size(a...  35.1 us
    pallas_call x13, Pallas kernels, apply_step(): pl.pallas_call(functools.partial(step_kernel, sides, firsts, out_column,...  25.5 us
  transfers between devices with their start and end apart: 33, of which 14 were waited for; matrix products, arithmetic and copies ran while one was open for 1% of the time, Pallas kernels for 20%

profile of v7, /device:TPU:1, one launch (start us, length us, event | category | flops | bytes accessed | tf_op | source)
XLA Modules:
  0.0 135.8 jit_solution(2718779609788822936)
XLA Ops:
  1.4 2.6 %collective-permute-start = (bf16[3,256,256]{2,1,0:T(8,128)(2,1)S(1)}, bf16[3,256,256]{2,1,0:T(8,128)(2,1)S(1)}, u32[]{:S(2)}, u32[]{:S(2)}) collective-permute-start(bf16[3,256,256]{2,1,0:T(8,128)(2,1)S(1)} %get-tuple-element.72.refs_0_.refs_4_), channel_id=1, source_target_pairs={{0,30},{2,4},{4,2},{6,8},{8,6},{10,12},{12,10},{14,16},{16,14},{18... | collective-permute-start | bytes 1179656 | tf_op jit(solution)/shard_map/ppermute | solution.py:236
  6.2 3.9 %collective-permute-start.5 = (bf16[3,256,256]{2,1,0:T(8,128)(2,1)S(1)}, bf16[3,256,256]{2,1,0:T(8,128)(2,1)S(1)}, u32[]{:S(2)}, u32[]{:S(2)}) collective-permute-start(bf16[3,256,256]{2,1,0:T(8,128)(2,1)S(1)} %get-tuple-element.40.refs_0_.refs_4_), channel_id=1, source_target_pairs={{0,30},{2,4},{4,2},{6,8},{8,6},{10,12},{12,10},{14,16},{16,14},{18... | collective-permute-start | bytes 1179656 | tf_op jit(solution)/shard_map/ppermute | solution.py:236
  10.1 8.6 %collective-permute-done.2.refs_5_ = bf16[64,512]{1,0:T(8,128)(2,1)S(1)} collective-permute-done((bf16[64,512]{1,0:T(8,128)(2,1)}, bf16[64,512]{1,0:T(8,128)(2,1)S(1)}, u32[]{:S(2)}, u32[]{:S(2)}) %collective-permute-start.2) | collective-permute-done | bytes 65568 | tf_op jit(solution)/shard_map/ppermute | solution.py:236
  18.7 2.0 %shard_map.64 = (bf16[3,256,256]{2,1,0:T(8,128)(2,1)S(1)}, bf16[3,256,256]{2,1,0:T(8,128)(2,1)S(1)}, bf16[128,512]{1,0:T(8,128)(2,1)S(1)}) custom-call(s32[1]{0:T(128)} %bitcast.odd_ref, s32[6,5]{1,0:T(8,128)S(1)} %copy-done.4, bf16[6,5,256,256]{3,2,1,0:T(8,128)(2,1)S(1)} %copy-done.1, bf16[3,256,256]{2,1,0:T(8,128)(2,1)S(1)} %get-tuple-element.72.refs_0_.refs_4_, ...), custom_call_target="tpu_custom_call" | custom-call | flops 4000000000 | bytes 1024 | tf_op jit(solution)/shard_map/pallas_call | solution.py:145
  22.5 3.6 %collective-permute-start.4 = (bf16[3,256,256]{2,1,0:T(8,128)(2,1)S(1)}, bf16[3,256,256]{2,1,0:T(8,128)(2,1)S(1)}, u32[]{:S(2)}, u32[]{:S(2)}) collective-permute-start(bf16[3,256,256]{2,1,0:T(8,128)(2,1)S(1)} %get-tuple-element.39.refs_1_.refs_5_), channel_id=1, source_target_pairs={{0,2},{2,0},{4,6},{6,4},{8,10},{10,8},{12,14},{14,12},{16,18},{18,... | collective-permute-start | bytes 1179656 | tf_op jit(solution)/shard_map/ppermute | solution.py:236
  26.1 1.8 %shard_map.66 = (bf16[3,256,256]{2,1,0:T(8,128)(2,1)S(1)}, bf16[3,256,256]{2,1,0:T(8,128)(2,1)S(1)}) custom-call(s32[1]{0:T(128)} %bitcast.odd_ref, s32[6,5]{1,0:T(8,128)S(1)} %copy-done.4, bf16[6,5,256,256]{3,2,1,0:T(8,128)(2,1)S(1)} %copy-done.1, bf16[3,256,256]{2,1,0:T(8,128)(2,1)S(1)} %get-tuple-element.40.refs_0_.refs_4_, ...), custom_call_target="tpu_custom_call" | custom-call | flops 4000000000 | bytes 1024 | tf_op jit(solution)/shard_map/pallas_call | solution.py:145
  28.7 6.9 %collective-permute-done.3.refs_2_ = bf16[3,256,256]{2,1,0:T(8,128)(2,1)S(1)} collective-permute-done((bf16[3,256,256]{2,1,0:T(8,128)(2,1)S(1)}, bf16[3,256,256]{2,1,0:T(8,128)(2,1)S(1)}, u32[]{:S(2)}, u32[]{:S(2)}) %collective-permute-start.3) | collective-permute-done | bytes 393248 | tf_op jit(solution)/shard_map/ppermute | solution.py:236
  35.7 1.8 %shard_map.67 = (bf16[3,256,256]{2,1,0:T(8,128)(2,1)S(1)}, bf16[3,256,256]{2,1,0:T(8,128)(2,1)S(1)}) custom-call(s32[1]{0:T(128)} %bitcast.odd_ref, s32[6,5]{1,0:T(8,128)S(1)} %copy-done.4, bf16[6,5,256,256]{3,2,1,0:T(8,128)(2,1)S(1)} %copy-done.1, bf16[3,256,256]{2,1,0:T(8,128)(2,1)S(1)} %get-tuple-element.38.refs_4_.refs_0_, ...), custom_call_target="tpu_custom_call" | custom-call | flops 4000000000 | bytes 1024 | tf_op jit(solution)/shard_map/pallas_call | solution.py:145
  37.5 2.5 %collective-permute-start.7 = (bf16[3,256,256]{2,1,0:T(8,128)(2,1)S(1)}, bf16[3,256,256]{2,1,0:T(8,128)(2,1)S(1)}, u32[]{:S(2)}, u32[]{:S(2)}) collective-permute-start(bf16[3,256,256]{2,1,0:T(8,128)(2,1)S(1)} %get-tuple-element.43.refs_8_.refs_0_), channel_id=1, source_target_pairs={{0,30},{2,4},{4,2},{6,8},{8,6},{10,12},{12,10},{14,16},{16,14},{18... | collective-permute-start | bytes 1179656 | tf_op jit(solution)/shard_map/ppermute | solution.py:236
  40.1 4.8 %collective-permute-done.9.refs_2_ = bf16[3,256,256]{2,1,0:T(8,128)(2,1)S(1)} collective-permute-done((bf16[3,256,256]{2,1,0:T(8,128)(2,1)S(1)}, bf16[3,256,256]{2,1,0:T(8,128)(2,1)S(1)}, u32[]{:S(2)}, u32[]{:S(2)}) %collective-permute-start.9) | collective-permute-done | bytes 393248 | tf_op jit(solution)/shard_map/ppermute | solution.py:236
  44.9 2.3 %shard_map.68 = (bf16[3,256,256]{2,1,0:T(8,128)(2,1)S(1)}, bf16[3,256,256]{2,1,0:T(8,128)(2,1)S(1)}, bf16[256,512]{1,0:T(8,128)(2,1)S(1)}) custom-call(s32[1]{0:T(128)} %bitcast.odd_ref, s32[6,5]{1,0:T(8,128)S(1)} %copy-done.4, bf16[6,5,256,256]{3,2,1,0:T(8,128)(2,1)S(1)} %copy-done.1, bf16[3,256,256]{2,1,0:T(8,128)(2,1)S(1)} %get-tuple-element.42.refs_6_.refs_0_.refs_4_, ...), custom_call_target="tpu_custom_call" | custom-call | flops 4000000000 | bytes 1024 | tf_op jit(solution)/shard_map/pallas_call | solution.py:145
  49.0 4.3 %collective-permute-done.7.refs_2_ = bf16[3,256,256]{2,1,0:T(8,128)(2,1)S(1)} collective-permute-done((bf16[3,256,256]{2,1,0:T(8,128)(2,1)S(1)}, bf16[3,256,256]{2,1,0:T(8,128)(2,1)S(1)}, u32[]{:S(2)}, u32[]{:S(2)}) %collective-permute-start.7) | collective-permute-done | bytes 393248 | tf_op jit(solution)/shard_map/ppermute | solution.py:236
  53.3 1.8 %shard_map.69 = (bf16[3,256,256]{2,1,0:T(8,128)(2,1)S(1)}, bf16[3,256,256]{2,1,0:T(8,128)(2,1)S(1)}) custom-call(s32[1]{0:T(128)} %bitcast.odd_ref, s32[6,5]{1,0:T(8,128)S(1)} %copy-done.4, bf16[6,5,256,256]{3,2,1,0:T(8,128)(2,1)S(1)} %copy-done.1, bf16[3,256,256]{2,1,0:T(8,128)(2,1)S(1)} %get-tuple-element.43.refs_8_.refs_0_, ...), custom_call_target="tpu_custom_call" | custom-call | flops 4000000000 | bytes 1024 | tf_op jit(solution)/shard_map/pallas_call | solution.py:145
  55.1 1.8 %collective-permute-start.14 = (bf16[3,256,256]{2,1,0:T(8,128)(2,1)S(1)}, bf16[3,256,256]{2,1,0:T(8,128)(2,1)S(1)}, u32[]{:S(2)}, u32[]{:S(2)}) collective-permute-start(bf16[3,256,256]{2,1,0:T(8,128)(2,1)S(1)} %get-tuple-element.48.refs_6_.refs_0_), channel_id=1, source_target_pairs={{0,1},{1,0},{2,3},{3,2},{4,5},{5,4},{6,7},{7,6},{8,9},{9,8},{10,11... | collective-permute-start | bytes 1179656 | tf_op jit(solution)/shard_map/ppermute | solution.py:236
  56.9 3.3 %collective-permute-start.16 = (bf16[256,512]{1,0:T(8,128)(2,1)S(1)}, bf16[256,512]{1,0:T(8,128)(2,1)S(1)}, u32[]{:S(2)}, u32[]{:S(2)}) collective-permute-start(bf16[256,512]{1,0:T(8,128)(2,1)S(1)} %get-tuple-element.52.refs_0_), channel_id=1, source_target_pairs={{0,16},{2,18},{4,20},{6,22},{8,24},{10,26},{12,28},{14,30},{16,0},... | collective-permute-start | bytes 786440 | tf_op jit(solution)/shard_map/ppermute | solution.py:236
  60.2 1.8 %shard_map.70 = (bf16[3,256,256]{2,1,0:T(8,128)(2,1)S(1)}, bf16[3,256,256]{2,1,0:T(8,128)(2,1)S(1)}) custom-call(s32[1]{0:T(128)} %bitcast.odd_ref, s32[6,5]{1,0:T(8,128)S(1)} %copy-done.4, bf16[6,5,256,256]{3,2,1,0:T(8,128)(2,1)S(1)} %copy-done.1, bf16[3,256,256]{2,1,0:T(8,128)(2,1)S(1)} %get-tuple-element.47.refs_6_.refs_0_, ...), custom_call_target="tpu_custom_call" | custom-call | flops 4000000000 | bytes 1024 | tf_op jit(solution)/shard_map/pallas_call | solution.py:145
  62.4 5.6 %collective-permute-done.16.refs_1_ = bf16[256,512]{1,0:T(8,128)(2,1)S(1)} collective-permute-done((bf16[256,512]{1,0:T(8,128)(2,1)S(1)}, bf16[256,512]{1,0:T(8,128)(2,1)S(1)}, u32[]{:S(2)}, u32[]{:S(2)}) %collective-permute-start.16) | collective-permute-done | bytes 262176 | tf_op jit(solution)/shard_map/ppermute | solution.py:236
  67.9 3.2 %collective-permute-done.15.refs_2_.refs_4_.refs_3_ = bf16[3,256,256]{2,1,0:T(8,128)(2,1)S(1)} collective-permute-done((bf16[3,256,256]{2,1,0:T(8,128)(2,1)S(1)}, bf16[3,256,256]{2,1,0:T(8,128)(2,1)S(1)}, u32[]{:S(2)}, u32[]{:S(2)}) %collective-permute-start.15) | collective-permute-done | bytes 393248 | tf_op jit(solution)/shard_map/ppermute | solution.py:236
  76.9 5.4 %collective-permute-done.19.refs_0_ = bf16[3,256,256]{2,1,0:T(8,128)(2,1)S(1)} collective-permute-done((bf16[3,256,256]{2,1,0:T(8,128)(2,1)S(1)}, bf16[3,256,256]{2,1,0:T(8,128)(2,1)S(1)}, u32[]{:S(2)}, u32[]{:S(2)}) %collective-permute-start.19) | collective-permute-done | bytes 393248 | tf_op jit(solution)/shard_map/ppermute | solution.py:236
  82.3 6.9 %collective-permute-done.20.refs_1_ = bf16[3,256,256]{2,1,0:T(8,128)(2,1)S(1)} collective-permute-done((bf16[3,256,256]{2,1,0:T(8,128)(2,1)S(1)}, bf16[3,256,256]{2,1,0:T(8,128)(2,1)S(1)}, u32[]{:S(2)}, u32[]{:S(2)}) %collective-permute-start.20) | collective-permute-done | bytes 393248 | tf_op jit(solution)/shard_map/ppermute | solution.py:236
  91.7 2.7 %collective-permute-done.27.refs_2_ = bf16[3,256,256]{2,1,0:T(8,128)(2,1)S(1)} collective-permute-done((bf16[3,256,256]{2,1,0:T(8,128)(2,1)S(1)}, bf16[3,256,256]{2,1,0:T(8,128)(2,1)S(1)}, u32[]{:S(2)}, u32[]{:S(2)}) %collective-permute-start.27) | collective-permute-done | bytes 393248 | tf_op jit(solution)/shard_map/ppermute | solution.py:236
  94.3 1.8 %shard_map.80 = (bf16[3,256,256]{2,1,0:T(8,128)(2,1)S(1)}, bf16[3,256,256]{2,1,0:T(8,128)(2,1)S(1)}) custom-call(s32[1]{0:T(128)} %bitcast.odd_ref, s32[6,5]{1,0:T(8,128)S(1)} %copy-done.4, bf16[6,5,256,256]{3,2,1,0:T(8,128)(2,1)S(1)} %copy-done.2, bf16[3,256,256]{2,1,0:T(8,128)(2,1)S(1)} %shard_map.79.refs_0_.refs_4_, ...), custom_call_target="tpu_custom_call" | custom-call | flops 4000000000 | bytes 1024 | tf_op jit(solution)/shard_map/pallas_call | solution.py:145
  98.1 1.8 %shard_map.77 = (bf16[3,256,256]{2,1,0:T(8,128)(2,1)S(1)}, bf16[3,256,256]{2,1,0:T(8,128)(2,1)S(1)}) custom-call(s32[1]{0:T(128)} %bitcast.odd_ref, s32[6,5]{1,0:T(8,128)S(1)} %copy-done.4, bf16[6,5,256,256]{3,2,1,0:T(8,128)(2,1)S(1)} %copy-done.2, bf16[3,256,256]{2,1,0:T(8,128)(2,1)S(1)} %shard_map.74.refs_0_.refs_4_, ...), custom_call_target="tpu_custom_call" | custom-call | flops 4000000000 | bytes 1024 | tf_op jit(solution)/shard_map/pallas_call | solution.py:145
  100.1 1.8 %collective-permute-start.24 = (bf16[3,256,256]{2,1,0:T(8,128)(2,1)S(1)}, bf16[3,256,256]{2,1,0:T(8,128)(2,1)S(1)}, u32[]{:S(2)}, u32[]{:S(2)}) collective-permute-start(bf16[3,256,256]{2,1,0:T(8,128)(2,1)S(1)} %get-tuple-element.63.refs_1_.refs_3_), channel_id=1, source_target_pairs={{0,2},{2,0},{4,6},{6,4},{8,10},{10,8},{12,14},{14,12},{16,18},{18,... | collective-permute-start | bytes 1179656 | tf_op jit(solution)/shard_map/ppermute | solution.py:236
  101.9 12.5 %collective-permute-done.29.refs_2_ = bf16[3,256,256]{2,1,0:T(8,128)(2,1)S(1)} collective-permute-done((bf16[3,256,256]{2,1,0:T(8,128)(2,1)S(1)}, bf16[3,256,256]{2,1,0:T(8,128)(2,1)S(1)}, u32[]{:S(2)}, u32[]{:S(2)}) %collective-permute-start.29) | collective-permute-done | bytes 393248 | tf_op jit(solution)/shard_map/ppermute | solution.py:236
  114.4 1.8 %shard_map.81 = (bf16[3,256,256]{2,1,0:T(8,128)(2,1)S(1)}, bf16[3,256,256]{2,1,0:T(8,128)(2,1)S(1)}) custom-call(s32[1]{0:T(128)} %bitcast.odd_ref, s32[6,5]{1,0:T(8,128)S(1)} %copy-done.4, bf16[6,5,256,256]{3,2,1,0:T(8,128)(2,1)S(1)} %copy-done.2, bf16[3,256,256]{2,1,0:T(8,128)(2,1)S(1)} %get-tuple-element.67.refs_0_.refs_4_, ...), custom_call_target="tpu_custom_call" | custom-call | flops 4000000000 | bytes 1024 | tf_op jit(solution)/shard_map/pallas_call | solution.py:145
  116.2 2.6 %collective-permute-start.31 = (bf16[3,256,256]{2,1,0:T(8,128)(2,1)S(1)}, bf16[3,256,256]{2,1,0:T(8,128)(2,1)S(1)}, u32[]{:S(2)}, u32[]{:S(2)}) collective-permute-start(bf16[3,256,256]{2,1,0:T(8,128)(2,1)S(1)} %get-tuple-element.69.refs_0_), channel_id=1, source_target_pairs={{0,30},{2,4},{4,2},{6,8},{8,6},{10,12},{12,10},{14,16},{16,14},{18... | collective-permute-start | bytes 1179656 | tf_op jit(solution)/shard_map/ppermute | solution.py:236
  120.3 1.8 %shard_map.78 = (bf16[3,256,256]{2,1,0:T(8,128)(2,1)S(1)}, bf16[3,256,256]{2,1,0:T(8,128)(2,1)S(1)}) custom-call(s32[1]{0:T(128)} %bitcast.odd_ref, s32[6,5]{1,0:T(8,128)S(1)} %copy-done.4, bf16[6,5,256,256]{3,2,1,0:T(8,128)(2,1)S(1)} %copy-done.2, bf16[3,256,256]{2,1,0:T(8,128)(2,1)S(1)} %get-tuple-element.62.refs_0_.refs_3_, ...), custom_call_target="tpu_custom_call" | custom-call | flops 4000000000 | bytes 1024 | tf_op jit(solution)/shard_map/pallas_call | solution.py:145
  124.5 2.6 %shard_map.82.refs_4_ = bf16[6,256,512]{2,1,0:T(8,128)(2,1)} custom-call(s32[1]{0:T(128)} %bitcast.odd_ref, s32[6,5]{1,0:T(8,128)S(1)} %copy-done.4, bf16[6,5,256,256]{3,2,1,0:T(8,128)(2,1)S(1)} %copy-done.2, bf16[3,256,256]{2,1,0:T(8,128)(2,1)S(1)} %get-tuple-element.69.refs_0_, bf16[3,256,256]{2,1,0:T(8,128)(2,1)S(1)} %get-tuple-element.70.refs_1_, ...), custom_call_target="tpu_custom_call" | custom-call | flops 4000000000 | bytes 1024 | tf_op jit(solution)/shard_map/pallas_call | solution.py:145
  127.1 2.0 %shard_map.83.refs_4_ = bf16[6,256,512]{2,1,0:T(8,128)(2,1)} custom-call(s32[1]{0:T(128)} %bitcast.odd_ref, s32[6,5]{1,0:T(8,128)S(1)} %copy-done.4, bf16[6,5,256,256]{3,2,1,0:T(8,128)(2,1)S(1)} %copy-done.2, bf16[3,256,256]{2,1,0:T(8,128)(2,1)S(1)} %get-tuple-element.64.refs_0_, ...), custom_call_target="tpu_custom_call", output_to_operand_aliasing={{}: (7, {})} | custom-call | flops 4000000000 | bytes 1024 | tf_op jit(solution)/shard_map/pallas_call | solution.py:145
  129.1 4.5 %collective-permute-done.25.refs_2_ = bf16[3,256,256]{2,1,0:T(8,128)(2,1)S(1)} collective-permute-done((bf16[3,256,256]{2,1,0:T(8,128)(2,1)S(1)}, bf16[3,256,256]{2,1,0:T(8,128)(2,1)S(1)}, u32[]{:S(2)}, u32[]{:S(2)}) %collective-permute-start.25) | collective-permute-done | bytes 393248 | tf_op jit(solution)/shard_map/ppermute | solution.py:236
  133.6 2.0 %shard_map.84 = bf16[6,256,512]{2,1,0:T(8,128)(2,1)} custom-call(s32[1]{0:T(128)} %bitcast.odd_ref, s32[6,5]{1,0:T(8,128)S(1)} %copy-done.4, bf16[6,5,256,256]{3,2,1,0:T(8,128)(2,1)S(1)} %copy-done.2, bf16[3,256,256]{2,1,0:T(8,128)(2,1)S(1)} %get-tuple-element.64.refs_0_, ...), custom_call_target="tpu_custom_call", output_to_operand_aliasing={{}: (7, {})} | custom-call | flops 4000000000 | bytes 1024 | tf_op jit(solution)/shard_map/pallas_call | solution.py:145
  (75 shorter events, 22.5 us)
Async XLA Ops:
  1.3 4.8 %collective-permute-start.1 = (bf16[3,256,256]{2,1,0:T(8,128)(2,1)S(1)}, bf16[3,256,256]{2,1,0:T(8,128)(2,1)S(1)}, u32[]{:S(2)}, u32[]{:S(2)}) collective-permute-start(bf16[3,256,256]{2,1,0:T(8,128)(2,1)S(1)} %get-tuple-element.71.refs_1_.refs_5_), channel_id=1, source_target_pairs={{0,2},{2,0},{4,6},{6,4},{8,10},{10,8},{12,14},{14,12},{16,18},{18,... | collective-permute-start | bytes 1179656 | tf_op jit(solution)/shard_map/ppermute | solution.py:236
  1.4 17.3 %collective-permute-start = (bf16[3,256,256]{2,1,0:T(8,128)(2,1)S(1)}, bf16[3,256,256]{2,1,0:T(8,128)(2,1)S(1)}, u32[]{:S(2)}, u32[]{:S(2)}) collective-permute-start(bf16[3,256,256]{2,1,0:T(8,128)(2,1)S(1)} %get-tuple-element.72.refs_0_.refs_4_), channel_id=1, source_target_pairs={{0,30},{2,4},{4,2},{6,8},{8,6},{10,12},{12,10},{14,16},{16,14},{18... | collective-permute-start | bytes 1179656 | tf_op jit(solution)/shard_map/ppermute | solution.py:236
  4.1 14.7 %collective-permute-start.2 = (bf16[64,512]{1,0:T(8,128)(2,1)}, bf16[64,512]{1,0:T(8,128)(2,1)S(1)}, u32[]{:S(2)}, u32[]{:S(2)}) collective-permute-start(bf16[64,512]{1,0:T(8,128)(2,1)} %refs_4_.1), channel_id=1, source_target_pairs={{0,4},{2,6},{4,0},{6,2},{8,12},{10,14},{12,8},{14,10},{16,20},{18,... | collective-permute-start | bytes 196616 | tf_op jit(solution)/shard_map/ppermute | solution.py:236
  6.2 19.9 %collective-permute-start.5 = (bf16[3,256,256]{2,1,0:T(8,128)(2,1)S(1)}, bf16[3,256,256]{2,1,0:T(8,128)(2,1)S(1)}, u32[]{:S(2)}, u32[]{:S(2)}) collective-permute-start(bf16[3,256,256]{2,1,0:T(8,128)(2,1)S(1)} %get-tuple-element.40.refs_0_.refs_4_), channel_id=1, source_target_pairs={{0,30},{2,4},{4,2},{6,8},{8,6},{10,12},{12,10},{14,16},{16,14},{18... | collective-permute-start | bytes 1179656 | tf_op jit(solution)/shard_map/ppermute | solution.py:236
  10.1 16.0 %collective-permute-start.6 = (bf16[3,256,256]{2,1,0:T(8,128)(2,1)S(1)}, bf16[3,256,256]{2,1,0:T(8,128)(2,1)S(1)}, u32[]{:S(2)}, u32[]{:S(2)}) collective-permute-start(bf16[3,256,256]{2,1,0:T(8,128)(2,1)S(1)} %get-tuple-element.41.refs_1_.refs_5_), channel_id=1, source_target_pairs={{0,2},{2,0},{4,6},{6,4},{8,10},{10,8},{12,14},{14,12},{16,18},{18,... | collective-permute-start | bytes 1179656 | tf_op jit(solution)/shard_map/ppermute | solution.py:236
  20.8 14.9 %collective-permute-start.3 = (bf16[3,256,256]{2,1,0:T(8,128)(2,1)S(1)}, bf16[3,256,256]{2,1,0:T(8,128)(2,1)S(1)}, u32[]{:S(2)}, u32[]{:S(2)}) collective-permute-start(bf16[3,256,256]{2,1,0:T(8,128)(2,1)S(1)} %get-tuple-element.38.refs_4_.refs_0_), channel_id=1, source_target_pairs={{0,30},{2,4},{4,2},{6,8},{8,6},{10,12},{12,10},{14,16},{16,14},{18... | collective-permute-start | bytes 1179656 | tf_op jit(solution)/shard_map/ppermute | solution.py:236
  22.5 13.2 %collective-permute-start.4 = (bf16[3,256,256]{2,1,0:T(8,128)(2,1)S(1)}, bf16[3,256,256]{2,1,0:T(8,128)(2,1)S(1)}, u32[]{:S(2)}, u32[]{:S(2)}) collective-permute-start(bf16[3,256,256]{2,1,0:T(8,128)(2,1)S(1)} %get-tuple-element.39.refs_1_.refs_5_), channel_id=1, source_target_pairs={{0,2},{2,0},{4,6},{6,4},{8,10},{10,8},{12,14},{14,12},{16,18},{18,... | collective-permute-start | bytes 1179656 | tf_op jit(solution)/shard_map/ppermute | solution.py:236
  27.9 12.2 %collective-permute-start.10 = (bf16[3,256,256]{2,1,0:T(8,128)(2,1)S(1)}, bf16[3,256,256]{2,1,0:T(8,128)(2,1)S(1)}, u32[]{:S(2)}, u32[]{:S(2)}) collective-permute-start(bf16[3,256,256]{2,1,0:T(8,128)(2,1)S(1)} %get-tuple-element.45.refs_1_.refs_5_), channel_id=1, source_target_pairs={{0,2},{2,0},{4,6},{6,4},{8,10},{10,8},{12,14},{14,12},{16,18},{18,... | collective-permute-start | bytes 1179656 | tf_op jit(solution)/shard_map/ppermute | solution.py:236
  28.0 16.9 %collective-permute-start.9 = (bf16[3,256,256]{2,1,0:T(8,128)(2,1)S(1)}, bf16[3,256,256]{2,1,0:T(8,128)(2,1)S(1)}, u32[]{:S(2)}, u32[]{:S(2)}) collective-permute-start(bf16[3,256,256]{2,1,0:T(8,128)(2,1)S(1)} %get-tuple-element.42.refs_6_.refs_0_.refs_4_), channel_id=1, source_target_pairs={{0,30},{2,4},{4,2},{6,8},{8,6},{10,12},{12,10},{14,16},{16,14},{18... | collective-permute-start | bytes 1179656 | tf_op jit(solution)/shard_map/ppermute | solution.py:236
  28.0 12.0 %collective-permute-start.11 = (bf16[128,512]{1,0:T(8,128)(2,1)S(1)}, bf16[128,512]{1,0:T(8,128)(2,1)S(1)}, u32[]{:S(2)}, u32[]{:S(2)}) collective-permute-start(bf16[128,512]{1,0:T(8,128)(2,1)S(1)} %get-tuple-element.46.refs_6_), channel_id=1, source_target_pairs={{0,8},{2,10},{4,12},{6,14},{8,0},{10,2},{12,4},{14,6},{16,24},{18,... | collective-permute-start | bytes 393224 | tf_op jit(solution)/shard_map/ppermute | solution.py:236
  37.5 15.8 %collective-permute-start.7 = (bf16[3,256,256]{2,1,0:T(8,128)(2,1)S(1)}, bf16[3,256,256]{2,1,0:T(8,128)(2,1)S(1)}, u32[]{:S(2)}, u32[]{:S(2)}) collective-permute-start(bf16[3,256,256]{2,1,0:T(8,128)(2,1)S(1)} %get-tuple-element.43.refs_8_.refs_0_), channel_id=1, source_target_pairs={{0,30},{2,4},{4,2},{6,8},{8,6},{10,12},{12,10},{14,16},{16,14},{18... | collective-permute-start | bytes 1179656 | tf_op jit(solution)/shard_map/ppermute | solution.py:236
  40.0 13.3 %collective-permute-start.8 = (bf16[3,256,256]{2,1,0:T(8,128)(2,1)S(1)}, bf16[3,256,256]{2,1,0:T(8,128)(2,1)S(1)}, u32[]{:S(2)}, u32[]{:S(2)}) collective-permute-start(bf16[3,256,256]{2,1,0:T(8,128)(2,1)S(1)} %get-tuple-element.44.refs_1_), channel_id=1, source_target_pairs={{0,2},{2,0},{4,6},{6,4},{8,10},{10,8},{12,14},{14,12},{16,18},{18,... | collective-permute-start | bytes 1179656 | tf_op jit(solution)/shard_map/ppermute | solution.py:236
  47.2 13.0 %collective-permute-start.12 = (bf16[3,256,256]{2,1,0:T(8,128)(2,1)S(1)}, bf16[3,256,256]{2,1,0:T(8,128)(2,1)S(1)}, u32[]{:S(2)}, u32[]{:S(2)}) collective-permute-start(bf16[3,256,256]{2,1,0:T(8,128)(2,1)S(1)} %get-tuple-element.47.refs_6_.refs_0_), channel_id=1, source_target_pairs={{0,30},{2,4},{4,2},{6,8},{8,6},{10,12},{12,10},{14,16},{16,14},{18... | collective-permute-start | bytes 1179656 | tf_op jit(solution)/shard_map/ppermute | solution.py:236
  49.0 11.3 %collective-permute-start.13 = (bf16[3,256,256]{2,1,0:T(8,128)(2,1)S(1)}, bf16[3,256,256]{2,1,0:T(8,128)(2,1)S(1)}, u32[]{:S(2)}, u32[]{:S(2)}) collective-permute-start(bf16[3,256,256]{2,1,0:T(8,128)(2,1)S(1)} %get-tuple-element.49.refs_1_), channel_id=1, source_target_pairs={{0,2},{2,0},{4,6},{6,4},{8,10},{10,8},{12,14},{14,12},{16,18},{18,... | collective-permute-start | bytes 1179656 | tf_op jit(solution)/shard_map/ppermute | solution.py:236
  55.1 12.8 %collective-permute-start.14 = (bf16[3,256,256]{2,1,0:T(8,128)(2,1)S(1)}, bf16[3,256,256]{2,1,0:T(8,128)(2,1)S(1)}, u32[]{:S(2)}, u32[]{:S(2)}) collective-permute-start(bf16[3,256,256]{2,1,0:T(8,128)(2,1)S(1)} %get-tuple-element.48.refs_6_.refs_0_), channel_id=1, source_target_pairs={{0,1},{1,0},{2,3},{3,2},{4,5},{5,4},{6,7},{7,6},{8,9},{9,8},{10,11... | collective-permute-start | bytes 1179656 | tf_op jit(solution)/shard_map/ppermute | solution.py:236
  56.9 11.0 %collective-permute-start.16 = (bf16[256,512]{1,0:T(8,128)(2,1)S(1)}, bf16[256,512]{1,0:T(8,128)(2,1)S(1)}, u32[]{:S(2)}, u32[]{:S(2)}) collective-permute-start(bf16[256,512]{1,0:T(8,128)(2,1)S(1)} %get-tuple-element.52.refs_0_), channel_id=1, source_target_pairs={{0,16},{2,18},{4,20},{6,22},{8,24},{10,26},{12,28},{14,30},{16,0},... | collective-permute-start | bytes 786440 | tf_op jit(solution)/shard_map/ppermute | solution.py:236
  62.1 9.1 %collective-permute-start.15 = (bf16[3,256,256]{2,1,0:T(8,128)(2,1)S(1)}, bf16[3,256,256]{2,1,0:T(8,128)(2,1)S(1)}, u32[]{:S(2)}, u32[]{:S(2)}) collective-permute-start(bf16[3,256,256]{2,1,0:T(8,128)(2,1)S(1)} %get-tuple-element.50.refs_1_), channel_id=1, source_target_pairs={{0,1},{1,0},{2,3},{3,2},{4,5},{5,4},{6,7},{7,6},{8,9},{9,8},{10,11... | collective-permute-start | bytes 1179656 | tf_op jit(solution)/shard_map/ppermute | solution.py:236
  62.3 10.2 %collective-permute-start.17 = (bf16[256,512]{1,0:T(8,128)(2,1)S(1)}, bf16[256,512]{1,0:T(8,128)(2,1)S(1)}, u32[]{:S(2)}, u32[]{:S(2)}) collective-permute-start(bf16[256,512]{1,0:T(8,128)(2,1)S(1)} %get-tuple-element.52.refs_0_), channel_id=1, source_target_pairs={{0,2},{2,0},{4,6},{6,4},{8,10},{10,8},{12,14},{14,12},{16,18},{18,... | collective-permute-start | bytes 786440 | tf_op jit(solution)/shard_map/ppermute | solution.py:236
  67.9 4.7 %collective-permute-start.18 = (bf16[256,512]{1,0:T(8,128)(2,1)S(1)}, bf16[256,512]{1,0:T(8,128)(2,1)S(1)}, u32[]{:S(2)}, u32[]{:S(2)}) collective-permute-start(bf16[256,512]{1,0:T(8,128)(2,1)S(1)} %collective-permute-done.16.refs_1_), channel_id=1, source_target_pairs={{0,2},{2,0},{4,6},{6,4},{8,10},{10,8},{12,14},{14,12},{16,18},{18,... | collective-permute-start | bytes 786440 | tf_op jit(solution)/shard_map/ppermute | solution.py:236
  71.1 11.2 %collective-permute-start.19 = (bf16[3,256,256]{2,1,0:T(8,128)(2,1)S(1)}, bf16[3,256,256]{2,1,0:T(8,128)(2,1)S(1)}, u32[]{:S(2)}, u32[]{:S(2)}) collective-permute-start(bf16[3,256,256]{2,1,0:T(8,128)(2,1)S(1)} %get-tuple-element.57.refs_5_.refs_0_), channel_id=1, source_target_pairs={{0,1},{1,0},{2,3},{3,2},{4,5},{5,4},{6,7},{7,6},{8,9},{9,8},{10,11... | collective-permute-start | bytes 1179656 | tf_op jit(solution)/shard_map/ppermute | solution.py:236
  72.4 16.8 %collective-permute-start.20 = (bf16[3,256,256]{2,1,0:T(8,128)(2,1)S(1)}, bf16[3,256,256]{2,1,0:T(8,128)(2,1)S(1)}, u32[]{:S(2)}, u32[]{:S(2)}) collective-permute-start(bf16[3,256,256]{2,1,0:T(8,128)(2,1)S(1)} %get-tuple-element.58.refs_1_), channel_id=1, source_target_pairs={{0,1},{1,0},{2,3},{3,2},{4,5},{5,4},{6,7},{7,6},{8,9},{9,8},{10,11... | collective-permute-start | bytes 1179656 | tf_op jit(solution)/shard_map/ppermute | solution.py:236
  74.4 15.7 %collective-permute-start.21 = (bf16[3,256,256]{2,1,0:T(8,128)(2,1)S(1)}, bf16[3,256,256]{2,1,0:T(8,128)(2,1)S(1)}, u32[]{:S(2)}, u32[]{:S(2)}) collective-permute-start(bf16[3,256,256]{2,1,0:T(8,128)(2,1)S(1)} %shard_map.74.refs_0_.refs_4_), channel_id=1, source_target_pairs={{0,30},{2,4},{4,2},{6,8},{8,6},{10,12},{12,10},{14,16},{16,14},{18... | collective-permute-start | bytes 1179656 | tf_op jit(solution)/shard_map/ppermute | solution.py:236
  76.3 18.0 %collective-permute-start.27 = (bf16[3,256,256]{2,1,0:T(8,128)(2,1)S(1)}, bf16[3,256,256]{2,1,0:T(8,128)(2,1)S(1)}, u32[]{:S(2)}, u32[]{:S(2)}) collective-permute-start(bf16[3,256,256]{2,1,0:T(8,128)(2,1)S(1)} %shard_map.79.refs_0_.refs_4_), channel_id=1, source_target_pairs={{0,30},{2,4},{4,2},{6,8},{8,6},{10,12},{12,10},{14,16},{16,14},{18... | collective-permute-start | bytes 1179656 | tf_op jit(solution)/shard_map/ppermute | solution.py:236
  91.2 6.9 %collective-permute-start.22 = (bf16[3,256,256]{2,1,0:T(8,128)(2,1)S(1)}, bf16[3,256,256]{2,1,0:T(8,128)(2,1)S(1)}, u32[]{:S(2)}, u32[]{:S(2)}) collective-permute-start(bf16[3,256,256]{2,1,0:T(8,128)(2,1)S(1)} %get-tuple-element.61.refs_1_.refs_5_), channel_id=1, source_target_pairs={{0,2},{2,0},{4,6},{6,4},{8,10},{10,8},{12,14},{14,12},{16,18},{18,... | collective-permute-start | bytes 1179656 | tf_op jit(solution)/shard_map/ppermute | solution.py:236
  96.1 18.2 %collective-permute-start.29 = (bf16[3,256,256]{2,1,0:T(8,128)(2,1)S(1)}, bf16[3,256,256]{2,1,0:T(8,128)(2,1)S(1)}, u32[]{:S(2)}, u32[]{:S(2)}) collective-permute-start(bf16[3,256,256]{2,1,0:T(8,128)(2,1)S(1)} %get-tuple-element.67.refs_0_.refs_4_), channel_id=1, source_target_pairs={{0,30},{2,4},{4,2},{6,8},{8,6},{10,12},{12,10},{14,16},{16,14},{18... | collective-permute-start | bytes 1179656 | tf_op jit(solution)/shard_map/ppermute | solution.py:236
  97.3 17.1 %collective-permute-start.30 = (bf16[3,256,256]{2,1,0:T(8,128)(2,1)S(1)}, bf16[3,256,256]{2,1,0:T(8,128)(2,1)S(1)}, u32[]{:S(2)}, u32[]{:S(2)}) collective-permute-start(bf16[3,256,256]{2,1,0:T(8,128)(2,1)S(1)} %get-tuple-element.68.refs_1_.refs_5_), channel_id=1, source_target_pairs={{0,2},{2,0},{4,6},{6,4},{8,10},{10,8},{12,14},{14,12},{16,18},{18,... | collective-permute-start | bytes 1179656 | tf_op jit(solution)/shard_map/ppermute | solution.py:236
  99.9 20.4 %collective-permute-start.23 = (bf16[3,256,256]{2,1,0:T(8,128)(2,1)S(1)}, bf16[3,256,256]{2,1,0:T(8,128)(2,1)S(1)}, u32[]{:S(2)}, u32[]{:S(2)}) collective-permute-start(bf16[3,256,256]{2,1,0:T(8,128)(2,1)S(1)} %get-tuple-element.62.refs_0_.refs_3_), channel_id=1, source_target_pairs={{0,30},{2,4},{4,2},{6,8},{8,6},{10,12},{12,10},{14,16},{16,14},{18... | collective-permute-start | bytes 1179656 | tf_op jit(solution)/shard_map/ppermute | solution.py:236
  100.1 20.2 %collective-permute-start.24 = (bf16[3,256,256]{2,1,0:T(8,128)(2,1)S(1)}, bf16[3,256,256]{2,1,0:T(8,128)(2,1)S(1)}, u32[]{:S(2)}, u32[]{:S(2)}) collective-permute-start(bf16[3,256,256]{2,1,0:T(8,128)(2,1)S(1)} %get-tuple-element.63.refs_1_.refs_3_), channel_id=1, source_target_pairs={{0,2},{2,0},{4,6},{6,4},{8,10},{10,8},{12,14},{14,12},{16,18},{18,... | collective-permute-start | bytes 1179656 | tf_op jit(solution)/shard_map/ppermute | solution.py:236
  116.2 8.3 %collective-permute-start.31 = (bf16[3,256,256]{2,1,0:T(8,128)(2,1)S(1)}, bf16[3,256,256]{2,1,0:T(8,128)(2,1)S(1)}, u32[]{:S(2)}, u32[]{:S(2)}) collective-permute-start(bf16[3,256,256]{2,1,0:T(8,128)(2,1)S(1)} %get-tuple-element.69.refs_0_), channel_id=1, source_target_pairs={{0,30},{2,4},{4,2},{6,8},{8,6},{10,12},{12,10},{14,16},{16,14},{18... | collective-permute-start | bytes 1179656 | tf_op jit(solution)/shard_map/ppermute | solution.py:236
  118.8 5.7 %collective-permute-start.32 = (bf16[3,256,256]{2,1,0:T(8,128)(2,1)S(1)}, bf16[3,256,256]{2,1,0:T(8,128)(2,1)S(1)}, u32[]{:S(2)}, u32[]{:S(2)}) collective-permute-start(bf16[3,256,256]{2,1,0:T(8,128)(2,1)S(1)} %get-tuple-element.70.refs_1_), channel_id=1, source_target_pairs={{0,2},{2,0},{4,6},{6,4},{8,10},{10,8},{12,14},{14,12},{16,18},{18,... | collective-permute-start | bytes 1179656 | tf_op jit(solution)/shard_map/ppermute | solution.py:236
  122.1 5.0 %collective-permute-start.26 = (bf16[3,256,256]{2,1,0:T(8,128)(2,1)S(1)}, bf16[3,256,256]{2,1,0:T(8,128)(2,1)S(1)}, u32[]{:S(2)}, u32[]{:S(2)}) collective-permute-start(bf16[3,256,256]{2,1,0:T(8,128)(2,1)S(1)} %get-tuple-element.65.refs_1_), channel_id=1, source_target_pairs={{0,2},{2,0},{4,6},{6,4},{8,10},{10,8},{12,14},{14,12},{16,18},{18,... | collective-permute-start | bytes 1179656 | tf_op jit(solution)/shard_map/ppermute | solution.py:236
  122.2 11.5 %collective-permute-start.25 = (bf16[3,256,256]{2,1,0:T(8,128)(2,1)S(1)}, bf16[3,256,256]{2,1,0:T(8,128)(2,1)S(1)}, u32[]{:S(2)}, u32[]{:S(2)}) collective-permute-start(bf16[3,256,256]{2,1,0:T(8,128)(2,1)S(1)} %get-tuple-element.64.refs_0_), channel_id=1, source_target_pairs={{0,30},{2,4},{4,2},{6,8},{8,6},{10,12},{12,10},{14,16},{16,14},{18... | collective-permute-start | bytes 1179656 | tf_op jit(solution)/shard_map/ppermute | solution.py:236
  (8 other events, 63.1 us)

commit v8 on v6

--- a/solution.py
+++ b/solution.py
@@ -238,7 +238,7 @@
 
 def bits_of(elems):
     bits = [1 << b for b in range(elems.bit_length() - 1)]
-    return bits[1:2] + bits[:1:-1] + bits[:1]
+    return bits[1:2] + bits[2:] + bits[:1]
 
 
 def owners_of(elems):

time: 136 us -> 136 us (level)
  waiting for transfers between devices: 64 us -> 69.3 us
  starting transfers between devices: 40 us -> 35.1 us
    ppermute x33, waiting for transfers between devices: 64 us -> 69.3 us  [exchange(): lax.ppermute(array, axis, [(i, partner(i)) for i in range(lax.axis_size(a...]
    ppermute x33, starting transfers between devices: 40 us -> 35.1 us  [exchange(): lax.ppermute(array, axis, [(i, partner(i)) for i in range(lax.axis_size(a...]
  transfers between devices with their start and end apart: 33 -> 33, of which waited for: 12 -> 14; matrix products, arithmetic and copies ran while one was open for 1% -> 1% of each run, Pallas kernels for 20% -> 20%
where the time goes in v8:
time: 136 us
  waiting for transfers between devices  69.3 us (51%)
  starting transfers between devices  35.1 us (26%)
  Pallas kernels  29 us (21%)
  local copies, waits for them, and re-layouts  2.03 us (1%)
    ppermute x33, waiting for transfers between devices, exchange(): lax.ppermute(array, axis, [(i, partner(i)) for i in range(lax.axis_size(a...  69.3 us
    ppermute x33, starting transfers between devices, exchange(): lax.ppermute(array, axis, [(i, partner(i)) for i in range(lax.axis_size(a...  35.1 us
    pallas_call x13, Pallas kernels, apply_step(): pl.pallas_call(functools.partial(step_kernel, sides, firsts, out_column,...  25.5 us
  transfers between devices with their start and end apart: 33, of which 14 were waited for; matrix products, arithmetic and copies ran while one was open for 1% of the time, Pallas kernels for 20%

profile of v8, /device:TPU:1, one launch (start us, length us, event | category | flops | bytes accessed | tf_op | source)
XLA Modules:
  0.0 135.8 jit_solution(7215410569129905329)
XLA Ops:
  1.4 2.6 %collective-permute-start = (bf16[3,256,256]{2,1,0:T(8,128)(2,1)S(1)}, bf16[3,256,256]{2,1,0:T(8,128)(2,1)S(1)}, u32[]{:S(2)}, u32[]{:S(2)}) collective-permute-start(bf16[3,256,256]{2,1,0:T(8,128)(2,1)S(1)} %get-tuple-element.72.refs_0_.refs_4_), channel_id=1, source_target_pairs={{0,30},{2,4},{4,2},{6,8},{8,6},{10,12},{12,10},{14,16},{16,14},{18... | collective-permute-start | bytes 1179656 | tf_op jit(solution)/shard_map/ppermute | solution.py:236
  6.2 3.9 %collective-permute-start.5 = (bf16[3,256,256]{2,1,0:T(8,128)(2,1)S(1)}, bf16[3,256,256]{2,1,0:T(8,128)(2,1)S(1)}, u32[]{:S(2)}, u32[]{:S(2)}) collective-permute-start(bf16[3,256,256]{2,1,0:T(8,128)(2,1)S(1)} %get-tuple-element.40.refs_0_.refs_4_), channel_id=1, source_target_pairs={{0,30},{2,4},{4,2},{6,8},{8,6},{10,12},{12,10},{14,16},{16,14},{18... | collective-permute-start | bytes 1179656 | tf_op jit(solution)/shard_map/ppermute | solution.py:236
  10.1 8.6 %collective-permute-done.2.refs_5_ = bf16[64,512]{1,0:T(8,128)(2,1)S(1)} collective-permute-done((bf16[64,512]{1,0:T(8,128)(2,1)}, bf16[64,512]{1,0:T(8,128)(2,1)S(1)}, u32[]{:S(2)}, u32[]{:S(2)}) %collective-permute-start.2) | collective-permute-done | bytes 65568 | tf_op jit(solution)/shard_map/ppermute | solution.py:236
  18.7 2.0 %shard_map.64 = (bf16[3,256,256]{2,1,0:T(8,128)(2,1)S(1)}, bf16[3,256,256]{2,1,0:T(8,128)(2,1)S(1)}, bf16[128,512]{1,0:T(8,128)(2,1)S(1)}) custom-call(s32[1]{0:T(128)} %bitcast.odd_ref, s32[6,5]{1,0:T(8,128)S(1)} %copy-done.4, bf16[6,5,256,256]{3,2,1,0:T(8,128)(2,1)S(1)} %copy-done.1, bf16[3,256,256]{2,1,0:T(8,128)(2,1)S(1)} %get-tuple-element.72.refs_0_.refs_4_, ...), custom_call_target="tpu_custom_call" | custom-call | flops 4000000000 | bytes 1024 | tf_op jit(solution)/shard_map/pallas_call | solution.py:145
  22.5 3.6 %collective-permute-start.4 = (bf16[3,256,256]{2,1,0:T(8,128)(2,1)S(1)}, bf16[3,256,256]{2,1,0:T(8,128)(2,1)S(1)}, u32[]{:S(2)}, u32[]{:S(2)}) collective-permute-start(bf16[3,256,256]{2,1,0:T(8,128)(2,1)S(1)} %get-tuple-element.39.refs_1_.refs_5_), channel_id=1, source_target_pairs={{0,2},{2,0},{4,6},{6,4},{8,10},{10,8},{12,14},{14,12},{16,18},{18,... | collective-permute-start | bytes 1179656 | tf_op jit(solution)/shard_map/ppermute | solution.py:236
  26.1 1.8 %shard_map.66 = (bf16[3,256,256]{2,1,0:T(8,128)(2,1)S(1)}, bf16[3,256,256]{2,1,0:T(8,128)(2,1)S(1)}) custom-call(s32[1]{0:T(128)} %bitcast.odd_ref, s32[6,5]{1,0:T(8,128)S(1)} %copy-done.4, bf16[6,5,256,256]{3,2,1,0:T(8,128)(2,1)S(1)} %copy-done.1, bf16[3,256,256]{2,1,0:T(8,128)(2,1)S(1)} %get-tuple-element.40.refs_0_.refs_4_, ...), custom_call_target="tpu_custom_call" | custom-call | flops 4000000000 | bytes 1024 | tf_op jit(solution)/shard_map/pallas_call | solution.py:145
  28.7 6.9 %collective-permute-done.3.refs_2_ = bf16[3,256,256]{2,1,0:T(8,128)(2,1)S(1)} collective-permute-done((bf16[3,256,256]{2,1,0:T(8,128)(2,1)S(1)}, bf16[3,256,256]{2,1,0:T(8,128)(2,1)S(1)}, u32[]{:S(2)}, u32[]{:S(2)}) %collective-permute-start.3) | collective-permute-done | bytes 393248 | tf_op jit(solution)/shard_map/ppermute | solution.py:236
  35.7 1.8 %shard_map.67 = (bf16[3,256,256]{2,1,0:T(8,128)(2,1)S(1)}, bf16[3,256,256]{2,1,0:T(8,128)(2,1)S(1)}) custom-call(s32[1]{0:T(128)} %bitcast.odd_ref, s32[6,5]{1,0:T(8,128)S(1)} %copy-done.4, bf16[6,5,256,256]{3,2,1,0:T(8,128)(2,1)S(1)} %copy-done.1, bf16[3,256,256]{2,1,0:T(8,128)(2,1)S(1)} %get-tuple-element.38.refs_4_.refs_0_, ...), custom_call_target="tpu_custom_call" | custom-call | flops 4000000000 | bytes 1024 | tf_op jit(solution)/shard_map/pallas_call | solution.py:145
  37.5 2.5 %collective-permute-start.7 = (bf16[3,256,256]{2,1,0:T(8,128)(2,1)S(1)}, bf16[3,256,256]{2,1,0:T(8,128)(2,1)S(1)}, u32[]{:S(2)}, u32[]{:S(2)}) collective-permute-start(bf16[3,256,256]{2,1,0:T(8,128)(2,1)S(1)} %get-tuple-element.43.refs_8_.refs_0_), channel_id=1, source_target_pairs={{0,30},{2,4},{4,2},{6,8},{8,6},{10,12},{12,10},{14,16},{16,14},{18... | collective-permute-start | bytes 1179656 | tf_op jit(solution)/shard_map/ppermute | solution.py:236
  40.1 4.8 %collective-permute-done.9.refs_2_ = bf16[3,256,256]{2,1,0:T(8,128)(2,1)S(1)} collective-permute-done((bf16[3,256,256]{2,1,0:T(8,128)(2,1)S(1)}, bf16[3,256,256]{2,1,0:T(8,128)(2,1)S(1)}, u32[]{:S(2)}, u32[]{:S(2)}) %collective-permute-start.9) | collective-permute-done | bytes 393248 | tf_op jit(solution)/shard_map/ppermute | solution.py:236
  44.9 2.3 %shard_map.68 = (bf16[3,256,256]{2,1,0:T(8,128)(2,1)S(1)}, bf16[3,256,256]{2,1,0:T(8,128)(2,1)S(1)}, bf16[256,512]{1,0:T(8,128)(2,1)S(1)}) custom-call(s32[1]{0:T(128)} %bitcast.odd_ref, s32[6,5]{1,0:T(8,128)S(1)} %copy-done.4, bf16[6,5,256,256]{3,2,1,0:T(8,128)(2,1)S(1)} %copy-done.1, bf16[3,256,256]{2,1,0:T(8,128)(2,1)S(1)} %get-tuple-element.42.refs_6_.refs_0_.refs_4_, ...), custom_call_target="tpu_custom_call" | custom-call | flops 4000000000 | bytes 1024 | tf_op jit(solution)/shard_map/pallas_call | solution.py:145
  49.0 4.3 %collective-permute-done.7.refs_2_ = bf16[3,256,256]{2,1,0:T(8,128)(2,1)S(1)} collective-permute-done((bf16[3,256,256]{2,1,0:T(8,128)(2,1)S(1)}, bf16[3,256,256]{2,1,0:T(8,128)(2,1)S(1)}, u32[]{:S(2)}, u32[]{:S(2)}) %collective-permute-start.7) | collective-permute-done | bytes 393248 | tf_op jit(solution)/shard_map/ppermute | solution.py:236
  53.3 1.8 %shard_map.69 = (bf16[3,256,256]{2,1,0:T(8,128)(2,1)S(1)}, bf16[3,256,256]{2,1,0:T(8,128)(2,1)S(1)}) custom-call(s32[1]{0:T(128)} %bitcast.odd_ref, s32[6,5]{1,0:T(8,128)S(1)} %copy-done.4, bf16[6,5,256,256]{3,2,1,0:T(8,128)(2,1)S(1)} %copy-done.1, bf16[3,256,256]{2,1,0:T(8,128)(2,1)S(1)} %get-tuple-element.43.refs_8_.refs_0_, ...), custom_call_target="tpu_custom_call" | custom-call | flops 4000000000 | bytes 1024 | tf_op jit(solution)/shard_map/pallas_call | solution.py:145
  55.1 1.8 %collective-permute-start.14 = (bf16[3,256,256]{2,1,0:T(8,128)(2,1)S(1)}, bf16[3,256,256]{2,1,0:T(8,128)(2,1)S(1)}, u32[]{:S(2)}, u32[]{:S(2)}) collective-permute-start(bf16[3,256,256]{2,1,0:T(8,128)(2,1)S(1)} %get-tuple-element.48.refs_6_.refs_0_), channel_id=1, source_target_pairs={{0,1},{1,0},{2,3},{3,2},{4,5},{5,4},{6,7},{7,6},{8,9},{9,8},{10,11... | collective-permute-start | bytes 1179656 | tf_op jit(solution)/shard_map/ppermute | solution.py:236
  56.9 3.3 %collective-permute-start.16 = (bf16[256,512]{1,0:T(8,128)(2,1)S(1)}, bf16[256,512]{1,0:T(8,128)(2,1)S(1)}, u32[]{:S(2)}, u32[]{:S(2)}) collective-permute-start(bf16[256,512]{1,0:T(8,128)(2,1)S(1)} %get-tuple-element.52.refs_0_), channel_id=1, source_target_pairs={{0,16},{2,18},{4,20},{6,22},{8,24},{10,26},{12,28},{14,30},{16,0},... | collective-permute-start | bytes 786440 | tf_op jit(solution)/shard_map/ppermute | solution.py:236
  60.2 1.8 %shard_map.70 = (bf16[3,256,256]{2,1,0:T(8,128)(2,1)S(1)}, bf16[3,256,256]{2,1,0:T(8,128)(2,1)S(1)}) custom-call(s32[1]{0:T(128)} %bitcast.odd_ref, s32[6,5]{1,0:T(8,128)S(1)} %copy-done.4, bf16[6,5,256,256]{3,2,1,0:T(8,128)(2,1)S(1)} %copy-done.1, bf16[3,256,256]{2,1,0:T(8,128)(2,1)S(1)} %get-tuple-element.47.refs_6_.refs_0_, ...), custom_call_target="tpu_custom_call" | custom-call | flops 4000000000 | bytes 1024 | tf_op jit(solution)/shard_map/pallas_call | solution.py:145
  62.4 5.6 %collective-permute-done.16.refs_1_ = bf16[256,512]{1,0:T(8,128)(2,1)S(1)} collective-permute-done((bf16[256,512]{1,0:T(8,128)(2,1)S(1)}, bf16[256,512]{1,0:T(8,128)(2,1)S(1)}, u32[]{:S(2)}, u32[]{:S(2)}) %collective-permute-start.16) | collective-permute-done | bytes 262176 | tf_op jit(solution)/shard_map/ppermute | solution.py:236
  67.9 3.2 %collective-permute-done.15.refs_2_.refs_4_.refs_3_ = bf16[3,256,256]{2,1,0:T(8,128)(2,1)S(1)} collective-permute-done((bf16[3,256,256]{2,1,0:T(8,128)(2,1)S(1)}, bf16[3,256,256]{2,1,0:T(8,128)(2,1)S(1)}, u32[]{:S(2)}, u32[]{:S(2)}) %collective-permute-start.15) | collective-permute-done | bytes 393248 | tf_op jit(solution)/shard_map/ppermute | solution.py:236
  76.9 5.4 %collective-permute-done.19.refs_0_ = bf16[3,256,256]{2,1,0:T(8,128)(2,1)S(1)} collective-permute-done((bf16[3,256,256]{2,1,0:T(8,128)(2,1)S(1)}, bf16[3,256,256]{2,1,0:T(8,128)(2,1)S(1)}, u32[]{:S(2)}, u32[]{:S(2)}) %collective-permute-start.19) | collective-permute-done | bytes 393248 | tf_op jit(solution)/shard_map/ppermute | solution.py:236
  82.3 6.9 %collective-permute-done.20.refs_1_ = bf16[3,256,256]{2,1,0:T(8,128)(2,1)S(1)} collective-permute-done((bf16[3,256,256]{2,1,0:T(8,128)(2,1)S(1)}, bf16[3,256,256]{2,1,0:T(8,128)(2,1)S(1)}, u32[]{:S(2)}, u32[]{:S(2)}) %collective-permute-start.20) | collective-permute-done | bytes 393248 | tf_op jit(solution)/shard_map/ppermute | solution.py:236
  91.7 2.7 %collective-permute-done.27.refs_2_ = bf16[3,256,256]{2,1,0:T(8,128)(2,1)S(1)} collective-permute-done((bf16[3,256,256]{2,1,0:T(8,128)(2,1)S(1)}, bf16[3,256,256]{2,1,0:T(8,128)(2,1)S(1)}, u32[]{:S(2)}, u32[]{:S(2)}) %collective-permute-start.27) | collective-permute-done | bytes 393248 | tf_op jit(solution)/shard_map/ppermute | solution.py:236
  94.3 1.8 %shard_map.80 = (bf16[3,256,256]{2,1,0:T(8,128)(2,1)S(1)}, bf16[3,256,256]{2,1,0:T(8,128)(2,1)S(1)}) custom-call(s32[1]{0:T(128)} %bitcast.odd_ref, s32[6,5]{1,0:T(8,128)S(1)} %copy-done.4, bf16[6,5,256,256]{3,2,1,0:T(8,128)(2,1)S(1)} %copy-done.2, bf16[3,256,256]{2,1,0:T(8,128)(2,1)S(1)} %shard_map.79.refs_0_.refs_4_, ...), custom_call_target="tpu_custom_call" | custom-call | flops 4000000000 | bytes 1024 | tf_op jit(solution)/shard_map/pallas_call | solution.py:145
  98.1 1.8 %shard_map.77 = (bf16[3,256,256]{2,1,0:T(8,128)(2,1)S(1)}, bf16[3,256,256]{2,1,0:T(8,128)(2,1)S(1)}) custom-call(s32[1]{0:T(128)} %bitcast.odd_ref, s32[6,5]{1,0:T(8,128)S(1)} %copy-done.4, bf16[6,5,256,256]{3,2,1,0:T(8,128)(2,1)S(1)} %copy-done.2, bf16[3,256,256]{2,1,0:T(8,128)(2,1)S(1)} %shard_map.74.refs_0_.refs_4_, ...), custom_call_target="tpu_custom_call" | custom-call | flops 4000000000 | bytes 1024 | tf_op jit(solution)/shard_map/pallas_call | solution.py:145
  100.1 1.8 %collective-permute-start.24 = (bf16[3,256,256]{2,1,0:T(8,128)(2,1)S(1)}, bf16[3,256,256]{2,1,0:T(8,128)(2,1)S(1)}, u32[]{:S(2)}, u32[]{:S(2)}) collective-permute-start(bf16[3,256,256]{2,1,0:T(8,128)(2,1)S(1)} %get-tuple-element.63.refs_1_.refs_3_), channel_id=1, source_target_pairs={{0,2},{2,0},{4,6},{6,4},{8,10},{10,8},{12,14},{14,12},{16,18},{18,... | collective-permute-start | bytes 1179656 | tf_op jit(solution)/shard_map/ppermute | solution.py:236
  101.9 12.5 %collective-permute-done.29.refs_2_ = bf16[3,256,256]{2,1,0:T(8,128)(2,1)S(1)} collective-permute-done((bf16[3,256,256]{2,1,0:T(8,128)(2,1)S(1)}, bf16[3,256,256]{2,1,0:T(8,128)(2,1)S(1)}, u32[]{:S(2)}, u32[]{:S(2)}) %collective-permute-start.29) | collective-permute-done | bytes 393248 | tf_op jit(solution)/shard_map/ppermute | solution.py:236
  114.4 1.8 %shard_map.81 = (bf16[3,256,256]{2,1,0:T(8,128)(2,1)S(1)}, bf16[3,256,256]{2,1,0:T(8,128)(2,1)S(1)}) custom-call(s32[1]{0:T(128)} %bitcast.odd_ref, s32[6,5]{1,0:T(8,128)S(1)} %copy-done.4, bf16[6,5,256,256]{3,2,1,0:T(8,128)(2,1)S(1)} %copy-done.2, bf16[3,256,256]{2,1,0:T(8,128)(2,1)S(1)} %get-tuple-element.67.refs_0_.refs_4_, ...), custom_call_target="tpu_custom_call" | custom-call | flops 4000000000 | bytes 1024 | tf_op jit(solution)/shard_map/pallas_call | solution.py:145
  116.2 2.5 %collective-permute-start.31 = (bf16[3,256,256]{2,1,0:T(8,128)(2,1)S(1)}, bf16[3,256,256]{2,1,0:T(8,128)(2,1)S(1)}, u32[]{:S(2)}, u32[]{:S(2)}) collective-permute-start(bf16[3,256,256]{2,1,0:T(8,128)(2,1)S(1)} %get-tuple-element.69.refs_0_), channel_id=1, source_target_pairs={{0,30},{2,4},{4,2},{6,8},{8,6},{10,12},{12,10},{14,16},{16,14},{18... | collective-permute-start | bytes 1179656 | tf_op jit(solution)/shard_map/ppermute | solution.py:236
  120.3 1.8 %shard_map.78 = (bf16[3,256,256]{2,1,0:T(8,128)(2,1)S(1)}, bf16[3,256,256]{2,1,0:T(8,128)(2,1)S(1)}) custom-call(s32[1]{0:T(128)} %bitcast.odd_ref, s32[6,5]{1,0:T(8,128)S(1)} %copy-done.4, bf16[6,5,256,256]{3,2,1,0:T(8,128)(2,1)S(1)} %copy-done.2, bf16[3,256,256]{2,1,0:T(8,128)(2,1)S(1)} %get-tuple-element.62.refs_0_.refs_3_, ...), custom_call_target="tpu_custom_call" | custom-call | flops 4000000000 | bytes 1024 | tf_op jit(solution)/shard_map/pallas_call | solution.py:145
  124.5 2.6 %shard_map.82.refs_4_ = bf16[6,256,512]{2,1,0:T(8,128)(2,1)} custom-call(s32[1]{0:T(128)} %bitcast.odd_ref, s32[6,5]{1,0:T(8,128)S(1)} %copy-done.4, bf16[6,5,256,256]{3,2,1,0:T(8,128)(2,1)S(1)} %copy-done.2, bf16[3,256,256]{2,1,0:T(8,128)(2,1)S(1)} %get-tuple-element.69.refs_0_, bf16[3,256,256]{2,1,0:T(8,128)(2,1)S(1)} %get-tuple-element.70.refs_1_, ...), custom_call_target="tpu_custom_call" | custom-call | flops 4000000000 | bytes 1024 | tf_op jit(solution)/shard_map/pallas_call | solution.py:145
  127.1 2.0 %shard_map.83.refs_4_ = bf16[6,256,512]{2,1,0:T(8,128)(2,1)} custom-call(s32[1]{0:T(128)} %bitcast.odd_ref, s32[6,5]{1,0:T(8,128)S(1)} %copy-done.4, bf16[6,5,256,256]{3,2,1,0:T(8,128)(2,1)S(1)} %copy-done.2, bf16[3,256,256]{2,1,0:T(8,128)(2,1)S(1)} %get-tuple-element.64.refs_0_, ...), custom_call_target="tpu_custom_call", output_to_operand_aliasing={{}: (7, {})} | custom-call | flops 4000000000 | bytes 1024 | tf_op jit(solution)/shard_map/pallas_call | solution.py:145
  129.1 4.5 %collective-permute-done.25.refs_2_ = bf16[3,256,256]{2,1,0:T(8,128)(2,1)S(1)} collective-permute-done((bf16[3,256,256]{2,1,0:T(8,128)(2,1)S(1)}, bf16[3,256,256]{2,1,0:T(8,128)(2,1)S(1)}, u32[]{:S(2)}, u32[]{:S(2)}) %collective-permute-start.25) | collective-permute-done | bytes 393248 | tf_op jit(solution)/shard_map/ppermute | solution.py:236
  133.7 2.0 %shard_map.84 = bf16[6,256,512]{2,1,0:T(8,128)(2,1)} custom-call(s32[1]{0:T(128)} %bitcast.odd_ref, s32[6,5]{1,0:T(8,128)S(1)} %copy-done.4, bf16[6,5,256,256]{3,2,1,0:T(8,128)(2,1)S(1)} %copy-done.2, bf16[3,256,256]{2,1,0:T(8,128)(2,1)S(1)} %get-tuple-element.64.refs_0_, ...), custom_call_target="tpu_custom_call", output_to_operand_aliasing={{}: (7, {})} | custom-call | flops 4000000000 | bytes 1024 | tf_op jit(solution)/shard_map/pallas_call | solution.py:145
  (75 shorter events, 22.5 us)
Async XLA Ops:
  1.3 4.8 %collective-permute-start.1 = (bf16[3,256,256]{2,1,0:T(8,128)(2,1)S(1)}, bf16[3,256,256]{2,1,0:T(8,128)(2,1)S(1)}, u32[]{:S(2)}, u32[]{:S(2)}) collective-permute-start(bf16[3,256,256]{2,1,0:T(8,128)(2,1)S(1)} %get-tuple-element.71.refs_1_.refs_5_), channel_id=1, source_target_pairs={{0,2},{2,0},{4,6},{6,4},{8,10},{10,8},{12,14},{14,12},{16,18},{18,... | collective-permute-start | bytes 1179656 | tf_op jit(solution)/shard_map/ppermute | solution.py:236
  1.4 17.3 %collective-permute-start = (bf16[3,256,256]{2,1,0:T(8,128)(2,1)S(1)}, bf16[3,256,256]{2,1,0:T(8,128)(2,1)S(1)}, u32[]{:S(2)}, u32[]{:S(2)}) collective-permute-start(bf16[3,256,256]{2,1,0:T(8,128)(2,1)S(1)} %get-tuple-element.72.refs_0_.refs_4_), channel_id=1, source_target_pairs={{0,30},{2,4},{4,2},{6,8},{8,6},{10,12},{12,10},{14,16},{16,14},{18... | collective-permute-start | bytes 1179656 | tf_op jit(solution)/shard_map/ppermute | solution.py:236
  4.1 14.7 %collective-permute-start.2 = (bf16[64,512]{1,0:T(8,128)(2,1)}, bf16[64,512]{1,0:T(8,128)(2,1)S(1)}, u32[]{:S(2)}, u32[]{:S(2)}) collective-permute-start(bf16[64,512]{1,0:T(8,128)(2,1)} %refs_4_.1), channel_id=1, source_target_pairs={{0,4},{2,6},{4,0},{6,2},{8,12},{10,14},{12,8},{14,10},{16,20},{18,... | collective-permute-start | bytes 196616 | tf_op jit(solution)/shard_map/ppermute | solution.py:236
  6.2 19.9 %collective-permute-start.5 = (bf16[3,256,256]{2,1,0:T(8,128)(2,1)S(1)}, bf16[3,256,256]{2,1,0:T(8,128)(2,1)S(1)}, u32[]{:S(2)}, u32[]{:S(2)}) collective-permute-start(bf16[3,256,256]{2,1,0:T(8,128)(2,1)S(1)} %get-tuple-element.40.refs_0_.refs_4_), channel_id=1, source_target_pairs={{0,30},{2,4},{4,2},{6,8},{8,6},{10,12},{12,10},{14,16},{16,14},{18... | collective-permute-start | bytes 1179656 | tf_op jit(solution)/shard_map/ppermute | solution.py:236
  10.1 16.0 %collective-permute-start.6 = (bf16[3,256,256]{2,1,0:T(8,128)(2,1)S(1)}, bf16[3,256,256]{2,1,0:T(8,128)(2,1)S(1)}, u32[]{:S(2)}, u32[]{:S(2)}) collective-permute-start(bf16[3,256,256]{2,1,0:T(8,128)(2,1)S(1)} %get-tuple-element.41.refs_1_.refs_5_), channel_id=1, source_target_pairs={{0,2},{2,0},{4,6},{6,4},{8,10},{10,8},{12,14},{14,12},{16,18},{18,... | collective-permute-start | bytes 1179656 | tf_op jit(solution)/shard_map/ppermute | solution.py:236
  20.8 14.9 %collective-permute-start.3 = (bf16[3,256,256]{2,1,0:T(8,128)(2,1)S(1)}, bf16[3,256,256]{2,1,0:T(8,128)(2,1)S(1)}, u32[]{:S(2)}, u32[]{:S(2)}) collective-permute-start(bf16[3,256,256]{2,1,0:T(8,128)(2,1)S(1)} %get-tuple-element.38.refs_4_.refs_0_), channel_id=1, source_target_pairs={{0,30},{2,4},{4,2},{6,8},{8,6},{10,12},{12,10},{14,16},{16,14},{18... | collective-permute-start | bytes 1179656 | tf_op jit(solution)/shard_map/ppermute | solution.py:236
  22.5 13.2 %collective-permute-start.4 = (bf16[3,256,256]{2,1,0:T(8,128)(2,1)S(1)}, bf16[3,256,256]{2,1,0:T(8,128)(2,1)S(1)}, u32[]{:S(2)}, u32[]{:S(2)}) collective-permute-start(bf16[3,256,256]{2,1,0:T(8,128)(2,1)S(1)} %get-tuple-element.39.refs_1_.refs_5_), channel_id=1, source_target_pairs={{0,2},{2,0},{4,6},{6,4},{8,10},{10,8},{12,14},{14,12},{16,18},{18,... | collective-permute-start | bytes 1179656 | tf_op jit(solution)/shard_map/ppermute | solution.py:236
  27.9 12.2 %collective-permute-start.10 = (bf16[3,256,256]{2,1,0:T(8,128)(2,1)S(1)}, bf16[3,256,256]{2,1,0:T(8,128)(2,1)S(1)}, u32[]{:S(2)}, u32[]{:S(2)}) collective-permute-start(bf16[3,256,256]{2,1,0:T(8,128)(2,1)S(1)} %get-tuple-element.45.refs_1_.refs_5_), channel_id=1, source_target_pairs={{0,2},{2,0},{4,6},{6,4},{8,10},{10,8},{12,14},{14,12},{16,18},{18,... | collective-permute-start | bytes 1179656 | tf_op jit(solution)/shard_map/ppermute | solution.py:236
  28.0 16.9 %collective-permute-start.9 = (bf16[3,256,256]{2,1,0:T(8,128)(2,1)S(1)}, bf16[3,256,256]{2,1,0:T(8,128)(2,1)S(1)}, u32[]{:S(2)}, u32[]{:S(2)}) collective-permute-start(bf16[3,256,256]{2,1,0:T(8,128)(2,1)S(1)} %get-tuple-element.42.refs_6_.refs_0_.refs_4_), channel_id=1, source_target_pairs={{0,30},{2,4},{4,2},{6,8},{8,6},{10,12},{12,10},{14,16},{16,14},{18... | collective-permute-start | bytes 1179656 | tf_op jit(solution)/shard_map/ppermute | solution.py:236
  28.0 12.0 %collective-permute-start.11 = (bf16[128,512]{1,0:T(8,128)(2,1)S(1)}, bf16[128,512]{1,0:T(8,128)(2,1)S(1)}, u32[]{:S(2)}, u32[]{:S(2)}) collective-permute-start(bf16[128,512]{1,0:T(8,128)(2,1)S(1)} %get-tuple-element.46.refs_6_), channel_id=1, source_target_pairs={{0,8},{2,10},{4,12},{6,14},{8,0},{10,2},{12,4},{14,6},{16,24},{18,... | collective-permute-start | bytes 393224 | tf_op jit(solution)/shard_map/ppermute | solution.py:236
  37.5 15.8 %collective-permute-start.7 = (bf16[3,256,256]{2,1,0:T(8,128)(2,1)S(1)}, bf16[3,256,256]{2,1,0:T(8,128)(2,1)S(1)}, u32[]{:S(2)}, u32[]{:S(2)}) collective-permute-start(bf16[3,256,256]{2,1,0:T(8,128)(2,1)S(1)} %get-tuple-element.43.refs_8_.refs_0_), channel_id=1, source_target_pairs={{0,30},{2,4},{4,2},{6,8},{8,6},{10,12},{12,10},{14,16},{16,14},{18... | collective-permute-start | bytes 1179656 | tf_op jit(solution)/shard_map/ppermute | solution.py:236
  40.0 13.3 %collective-permute-start.8 = (bf16[3,256,256]{2,1,0:T(8,128)(2,1)S(1)}, bf16[3,256,256]{2,1,0:T(8,128)(2,1)S(1)}, u32[]{:S(2)}, u32[]{:S(2)}) collective-permute-start(bf16[3,256,256]{2,1,0:T(8,128)(2,1)S(1)} %get-tuple-element.44.refs_1_), channel_id=1, source_target_pairs={{0,2},{2,0},{4,6},{6,4},{8,10},{10,8},{12,14},{14,12},{16,18},{18,... | collective-permute-start | bytes 1179656 | tf_op jit(solution)/shard_map/ppermute | solution.py:236
  47.2 13.0 %collective-permute-start.12 = (bf16[3,256,256]{2,1,0:T(8,128)(2,1)S(1)}, bf16[3,256,256]{2,1,0:T(8,128)(2,1)S(1)}, u32[]{:S(2)}, u32[]{:S(2)}) collective-permute-start(bf16[3,256,256]{2,1,0:T(8,128)(2,1)S(1)} %get-tuple-element.47.refs_6_.refs_0_), channel_id=1, source_target_pairs={{0,30},{2,4},{4,2},{6,8},{8,6},{10,12},{12,10},{14,16},{16,14},{18... | collective-permute-start | bytes 1179656 | tf_op jit(solution)/shard_map/ppermute | solution.py:236
  49.0 11.3 %collective-permute-start.13 = (bf16[3,256,256]{2,1,0:T(8,128)(2,1)S(1)}, bf16[3,256,256]{2,1,0:T(8,128)(2,1)S(1)}, u32[]{:S(2)}, u32[]{:S(2)}) collective-permute-start(bf16[3,256,256]{2,1,0:T(8,128)(2,1)S(1)} %get-tuple-element.49.refs_1_), channel_id=1, source_target_pairs={{0,2},{2,0},{4,6},{6,4},{8,10},{10,8},{12,14},{14,12},{16,18},{18,... | collective-permute-start | bytes 1179656 | tf_op jit(solution)/shard_map/ppermute | solution.py:236
  55.1 12.8 %collective-permute-start.14 = (bf16[3,256,256]{2,1,0:T(8,128)(2,1)S(1)}, bf16[3,256,256]{2,1,0:T(8,128)(2,1)S(1)}, u32[]{:S(2)}, u32[]{:S(2)}) collective-permute-start(bf16[3,256,256]{2,1,0:T(8,128)(2,1)S(1)} %get-tuple-element.48.refs_6_.refs_0_), channel_id=1, source_target_pairs={{0,1},{1,0},{2,3},{3,2},{4,5},{5,4},{6,7},{7,6},{8,9},{9,8},{10,11... | collective-permute-start | bytes 1179656 | tf_op jit(solution)/shard_map/ppermute | solution.py:236
  56.9 11.0 %collective-permute-start.16 = (bf16[256,512]{1,0:T(8,128)(2,1)S(1)}, bf16[256,512]{1,0:T(8,128)(2,1)S(1)}, u32[]{:S(2)}, u32[]{:S(2)}) collective-permute-start(bf16[256,512]{1,0:T(8,128)(2,1)S(1)} %get-tuple-element.52.refs_0_), channel_id=1, source_target_pairs={{0,16},{2,18},{4,20},{6,22},{8,24},{10,26},{12,28},{14,30},{16,0},... | collective-permute-start | bytes 786440 | tf_op jit(solution)/shard_map/ppermute | solution.py:236
  62.1 9.1 %collective-permute-start.15 = (bf16[3,256,256]{2,1,0:T(8,128)(2,1)S(1)}, bf16[3,256,256]{2,1,0:T(8,128)(2,1)S(1)}, u32[]{:S(2)}, u32[]{:S(2)}) collective-permute-start(bf16[3,256,256]{2,1,0:T(8,128)(2,1)S(1)} %get-tuple-element.50.refs_1_), channel_id=1, source_target_pairs={{0,1},{1,0},{2,3},{3,2},{4,5},{5,4},{6,7},{7,6},{8,9},{9,8},{10,11... | collective-permute-start | bytes 1179656 | tf_op jit(solution)/shard_map/ppermute | solution.py:236
  62.3 10.2 %collective-permute-start.17 = (bf16[256,512]{1,0:T(8,128)(2,1)S(1)}, bf16[256,512]{1,0:T(8,128)(2,1)S(1)}, u32[]{:S(2)}, u32[]{:S(2)}) collective-permute-start(bf16[256,512]{1,0:T(8,128)(2,1)S(1)} %get-tuple-element.52.refs_0_), channel_id=1, source_target_pairs={{0,2},{2,0},{4,6},{6,4},{8,10},{10,8},{12,14},{14,12},{16,18},{18,... | collective-permute-start | bytes 786440 | tf_op jit(solution)/shard_map/ppermute | solution.py:236
  67.9 4.7 %collective-permute-start.18 = (bf16[256,512]{1,0:T(8,128)(2,1)S(1)}, bf16[256,512]{1,0:T(8,128)(2,1)S(1)}, u32[]{:S(2)}, u32[]{:S(2)}) collective-permute-start(bf16[256,512]{1,0:T(8,128)(2,1)S(1)} %collective-permute-done.16.refs_1_), channel_id=1, source_target_pairs={{0,2},{2,0},{4,6},{6,4},{8,10},{10,8},{12,14},{14,12},{16,18},{18,... | collective-permute-start | bytes 786440 | tf_op jit(solution)/shard_map/ppermute | solution.py:236
  71.1 11.2 %collective-permute-start.19 = (bf16[3,256,256]{2,1,0:T(8,128)(2,1)S(1)}, bf16[3,256,256]{2,1,0:T(8,128)(2,1)S(1)}, u32[]{:S(2)}, u32[]{:S(2)}) collective-permute-start(bf16[3,256,256]{2,1,0:T(8,128)(2,1)S(1)} %get-tuple-element.57.refs_5_.refs_0_), channel_id=1, source_target_pairs={{0,1},{1,0},{2,3},{3,2},{4,5},{5,4},{6,7},{7,6},{8,9},{9,8},{10,11... | collective-permute-start | bytes 1179656 | tf_op jit(solution)/shard_map/ppermute | solution.py:236
  72.4 16.8 %collective-permute-start.20 = (bf16[3,256,256]{2,1,0:T(8,128)(2,1)S(1)}, bf16[3,256,256]{2,1,0:T(8,128)(2,1)S(1)}, u32[]{:S(2)}, u32[]{:S(2)}) collective-permute-start(bf16[3,256,256]{2,1,0:T(8,128)(2,1)S(1)} %get-tuple-element.58.refs_1_), channel_id=1, source_target_pairs={{0,1},{1,0},{2,3},{3,2},{4,5},{5,4},{6,7},{7,6},{8,9},{9,8},{10,11... | collective-permute-start | bytes 1179656 | tf_op jit(solution)/shard_map/ppermute | solution.py:236
  74.4 15.7 %collective-permute-start.21 = (bf16[3,256,256]{2,1,0:T(8,128)(2,1)S(1)}, bf16[3,256,256]{2,1,0:T(8,128)(2,1)S(1)}, u32[]{:S(2)}, u32[]{:S(2)}) collective-permute-start(bf16[3,256,256]{2,1,0:T(8,128)(2,1)S(1)} %shard_map.74.refs_0_.refs_4_), channel_id=1, source_target_pairs={{0,30},{2,4},{4,2},{6,8},{8,6},{10,12},{12,10},{14,16},{16,14},{18... | collective-permute-start | bytes 1179656 | tf_op jit(solution)/shard_map/ppermute | solution.py:236
  76.3 18.0 %collective-permute-start.27 = (bf16[3,256,256]{2,1,0:T(8,128)(2,1)S(1)}, bf16[3,256,256]{2,1,0:T(8,128)(2,1)S(1)}, u32[]{:S(2)}, u32[]{:S(2)}) collective-permute-start(bf16[3,256,256]{2,1,0:T(8,128)(2,1)S(1)} %shard_map.79.refs_0_.refs_4_), channel_id=1, source_target_pairs={{0,30},{2,4},{4,2},{6,8},{8,6},{10,12},{12,10},{14,16},{16,14},{18... | collective-permute-start | bytes 1179656 | tf_op jit(solution)/shard_map/ppermute | solution.py:236
  91.2 6.9 %collective-permute-start.22 = (bf16[3,256,256]{2,1,0:T(8,128)(2,1)S(1)}, bf16[3,256,256]{2,1,0:T(8,128)(2,1)S(1)}, u32[]{:S(2)}, u32[]{:S(2)}) collective-permute-start(bf16[3,256,256]{2,1,0:T(8,128)(2,1)S(1)} %get-tuple-element.61.refs_1_.refs_5_), channel_id=1, source_target_pairs={{0,2},{2,0},{4,6},{6,4},{8,10},{10,8},{12,14},{14,12},{16,18},{18,... | collective-permute-start | bytes 1179656 | tf_op jit(solution)/shard_map/ppermute | solution.py:236
  96.2 18.2 %collective-permute-start.29 = (bf16[3,256,256]{2,1,0:T(8,128)(2,1)S(1)}, bf16[3,256,256]{2,1,0:T(8,128)(2,1)S(1)}, u32[]{:S(2)}, u32[]{:S(2)}) collective-permute-start(bf16[3,256,256]{2,1,0:T(8,128)(2,1)S(1)} %get-tuple-element.67.refs_0_.refs_4_), channel_id=1, source_target_pairs={{0,30},{2,4},{4,2},{6,8},{8,6},{10,12},{12,10},{14,16},{16,14},{18... | collective-permute-start | bytes 1179656 | tf_op jit(solution)/shard_map/ppermute | solution.py:236
  97.3 17.1 %collective-permute-start.30 = (bf16[3,256,256]{2,1,0:T(8,128)(2,1)S(1)}, bf16[3,256,256]{2,1,0:T(8,128)(2,1)S(1)}, u32[]{:S(2)}, u32[]{:S(2)}) collective-permute-start(bf16[3,256,256]{2,1,0:T(8,128)(2,1)S(1)} %get-tuple-element.68.refs_1_.refs_5_), channel_id=1, source_target_pairs={{0,2},{2,0},{4,6},{6,4},{8,10},{10,8},{12,14},{14,12},{16,18},{18,... | collective-permute-start | bytes 1179656 | tf_op jit(solution)/shard_map/ppermute | solution.py:236
  99.9 20.4 %collective-permute-start.23 = (bf16[3,256,256]{2,1,0:T(8,128)(2,1)S(1)}, bf16[3,256,256]{2,1,0:T(8,128)(2,1)S(1)}, u32[]{:S(2)}, u32[]{:S(2)}) collective-permute-start(bf16[3,256,256]{2,1,0:T(8,128)(2,1)S(1)} %get-tuple-element.62.refs_0_.refs_3_), channel_id=1, source_target_pairs={{0,30},{2,4},{4,2},{6,8},{8,6},{10,12},{12,10},{14,16},{16,14},{18... | collective-permute-start | bytes 1179656 | tf_op jit(solution)/shard_map/ppermute | solution.py:236
  100.1 20.2 %collective-permute-start.24 = (bf16[3,256,256]{2,1,0:T(8,128)(2,1)S(1)}, bf16[3,256,256]{2,1,0:T(8,128)(2,1)S(1)}, u32[]{:S(2)}, u32[]{:S(2)}) collective-permute-start(bf16[3,256,256]{2,1,0:T(8,128)(2,1)S(1)} %get-tuple-element.63.refs_1_.refs_3_), channel_id=1, source_target_pairs={{0,2},{2,0},{4,6},{6,4},{8,10},{10,8},{12,14},{14,12},{16,18},{18,... | collective-permute-start | bytes 1179656 | tf_op jit(solution)/shard_map/ppermute | solution.py:236
  116.2 8.3 %collective-permute-start.31 = (bf16[3,256,256]{2,1,0:T(8,128)(2,1)S(1)}, bf16[3,256,256]{2,1,0:T(8,128)(2,1)S(1)}, u32[]{:S(2)}, u32[]{:S(2)}) collective-permute-start(bf16[3,256,256]{2,1,0:T(8,128)(2,1)S(1)} %get-tuple-element.69.refs_0_), channel_id=1, source_target_pairs={{0,30},{2,4},{4,2},{6,8},{8,6},{10,12},{12,10},{14,16},{16,14},{18... | collective-permute-start | bytes 1179656 | tf_op jit(solution)/shard_map/ppermute | solution.py:236
  118.8 5.7 %collective-permute-start.32 = (bf16[3,256,256]{2,1,0:T(8,128)(2,1)S(1)}, bf16[3,256,256]{2,1,0:T(8,128)(2,1)S(1)}, u32[]{:S(2)}, u32[]{:S(2)}) collective-permute-start(bf16[3,256,256]{2,1,0:T(8,128)(2,1)S(1)} %get-tuple-element.70.refs_1_), channel_id=1, source_target_pairs={{0,2},{2,0},{4,6},{6,4},{8,10},{10,8},{12,14},{14,12},{16,18},{18,... | collective-permute-start | bytes 1179656 | tf_op jit(solution)/shard_map/ppermute | solution.py:236
  122.1 5.0 %collective-permute-start.26 = (bf16[3,256,256]{2,1,0:T(8,128)(2,1)S(1)}, bf16[3,256,256]{2,1,0:T(8,128)(2,1)S(1)}, u32[]{:S(2)}, u32[]{:S(2)}) collective-permute-start(bf16[3,256,256]{2,1,0:T(8,128)(2,1)S(1)} %get-tuple-element.65.refs_1_), channel_id=1, source_target_pairs={{0,2},{2,0},{4,6},{6,4},{8,10},{10,8},{12,14},{14,12},{16,18},{18,... | collective-permute-start | bytes 1179656 | tf_op jit(solution)/shard_map/ppermute | solution.py:236
  122.2 11.5 %collective-permute-start.25 = (bf16[3,256,256]{2,1,0:T(8,128)(2,1)S(1)}, bf16[3,256,256]{2,1,0:T(8,128)(2,1)S(1)}, u32[]{:S(2)}, u32[]{:S(2)}) collective-permute-start(bf16[3,256,256]{2,1,0:T(8,128)(2,1)S(1)} %get-tuple-element.64.refs_0_), channel_id=1, source_target_pairs={{0,30},{2,4},{4,2},{6,8},{8,6},{10,12},{12,10},{14,16},{16,14},{18... | collective-permute-start | bytes 1179656 | tf_op jit(solution)/shard_map/ppermute | solution.py:236
  (8 other events, 63.1 us)
